TPU v7x, 32 devices: a whole 2x2x4 slice. The times are simulated.
32 devices in a mesh: replica: 8 (over y, x, core), fsdp: 4 (over z).
Axes of the slice: x: 2, y: 2, z: 4, core: 2. Of those that a mesh axis runs over, the one named last changes fastest.
Arguments:
- tokens: bfloat16 [8192, 2048], P(('replica', 'fsdp')), may hold values from -6 to 6
- segment_ids: int32 [8, 1024], P('replica'), may hold values from 0 to 4, as said below
- attention_gain: bfloat16 [2048], P('fsdp'), may hold values from 0.5 to 1.5
- query_weight: bfloat16 [2048, 2048], P('fsdp'), may hold values from -0.1875 to 0.1875
- key_weight: bfloat16 [2048, 256], P('fsdp'), may hold values from -0.1875 to 0.1875
- value_weight: bfloat16 [2048, 256], P('fsdp'), may hold values from -0.125 to 0.125
- output_weight: bfloat16 [2048, 2048], P('fsdp'), may hold values from -0.5 to 0.5
- feed_gain: bfloat16 [2048], P('fsdp'), may hold values from 0.5 to 1.5
- gate_weight: bfloat16 [2048, 5632], P('fsdp'), may hold values from -0.125 to 0.125
- up_weight: bfloat16 [2048, 5632], P('fsdp'), may hold values from -0.125 to 0.125
- down_weight: bfloat16 [5632, 2048], P('fsdp'), may hold values from -0.15625 to 0.15625
- cotangent: bfloat16 [8192, 2048], P(('replica', 'fsdp')), may hold values from -6 to 6
Outputs:
- activations: bfloat16 [8192, 2048], P(('replica', 'fsdp'))
- input_grad: bfloat16 [8192, 2048], P(('replica', 'fsdp'))
- attention_gain_grad: float32 [2048], P('fsdp')
- query_grad: float32 [2048, 2048], P('fsdp')
- key_grad: float32 [2048, 256], P('fsdp')
- value_grad: float32 [2048, 256], P('fsdp')
- output_grad: float32 [2048, 2048], P('fsdp')
- feed_gain_grad: float32 [2048], P('fsdp')
- gate_grad: float32 [2048, 5632], P('fsdp')
- up_grad: float32 [2048, 5632], P('fsdp')
- down_grad: float32 [5632, 2048], P('fsdp')
Inputs may be any that keep to these rules, and one draw needn't show every extreme that they name: `segment_ids`: in each row the document numbers start at 0 and rise by 0 or 1 from one token to the next. Every document has 60 to 800 tokens, except the last of a row, which is cut at the row's end and may be shorter. The first document of every row has exactly 800 tokens.
All inputs are finite; a program needn't handle non-finite values.
Results may differ from a plain program's by a relative error of at most 0.023.
Values may be sent and summed in bfloat16 or wider, within the bound.
A program may use at most 448 MiB of HBM per device.

v0:
```python
import math

import jax
import jax.numpy as jnp
from jax import lax
from jax.sharding import PartitionSpec as P

HEADS = 32
KV_HEADS = 4
HEAD_DIM = 64


EPSILON = 1e-05
NEGATIVE = -1e30


def inverse_rms(values):
    return lax.rsqrt(jnp.mean(values * values, axis=1, keepdims=True) + EPSILON)


def rope_tables(positions, head_dim):
    half_dim = head_dim // 2
    freq_rates = jnp.exp(jnp.arange(half_dim, dtype=jnp.float32) * (-math.log(10000.0) / half_dim))
    angles = positions.astype(jnp.float32)[:, None] * freq_rates[None, :]
    return (jnp.cos(angles), jnp.sin(angles))


def rotate(tensor, cosine_table, sine_table):
    half_dim = tensor.shape[-1] // 2
    lower_half = tensor[..., :half_dim]
    upper_half = tensor[..., half_dim:]
    cos_part = cosine_table[:, None, :]
    sin_part = sine_table[:, None, :]
    return jnp.concatenate(
        [
            lower_half * cos_part - upper_half * sin_part,
            upper_half * cos_part + lower_half * sin_part,
        ],
        axis=-1,
    )


def unrotate(tensor, cosine_table, sine_table):
    half_dim = tensor.shape[-1] // 2
    lower_half = tensor[..., :half_dim]
    upper_half = tensor[..., half_dim:]
    cos_part = cosine_table[:, None, :]
    sin_part = sine_table[:, None, :]
    return jnp.concatenate(
        [
            lower_half * cos_part + upper_half * sin_part,
            upper_half * cos_part - lower_half * sin_part,
        ],
        axis=-1,
    )


def times_transposed(left_side, right_side):
    return lax.dot_general(
        left_side, right_side, (((1,), (1,)), ((), ())), preferred_element_type=jnp.float32
    )


def transposed_times(left_side, right_side):
    return lax.dot_general(
        left_side, right_side, (((0,), (0,)), ((), ())), preferred_element_type=jnp.float32
    )


def probabilities(raw_scores, allowed, log_total):
    masked = jnp.where(allowed, raw_scores, NEGATIVE)
    return jnp.where(allowed, jnp.exp(masked - log_total), 0.0)


def owner_rows(left_side, right_side):
    return lax.psum_scatter(
        transposed_times(left_side, right_side).astype(jnp.bfloat16),
        "fsdp",
        scatter_dimension=0,
        tiled=True,
    ).astype(jnp.float32)


def per_device(
    tokens,
    segment_ids,
    attention_gain,
    query_weight,
    key_weight,
    value_weight,
    output_weight,
    feed_gain,
    gate_weight,
    up_weight,
    down_weight,
    cotangent,
):
    tok_count, model_width = tokens.shape
    query_width = query_weight.shape[1]
    key_width = key_weight.shape[1]
    feed_width = gate_weight.shape[1]
    group_ratio = HEADS // KV_HEADS
    score_scale = HEAD_DIM ** (-0.5)
    block_index = lax.axis_index("fsdp")
    first_token = block_index * tok_count
    row_ids = segment_ids[0]
    row_length = row_ids.shape[0]
    places = jnp.arange(row_length, dtype=jnp.int32)
    fresh_start = jnp.concatenate([jnp.ones((1,), dtype=jnp.bool_), row_ids[1:] != row_ids[:-1]])
    positions = places - lax.cummax(jnp.where(fresh_start, places, 0), axis=0)
    own_ids = lax.dynamic_slice_in_dim(row_ids, first_token, tok_count)
    own_positions = lax.dynamic_slice_in_dim(positions, first_token, tok_count)
    query_places = first_token + jnp.arange(tok_count, dtype=jnp.int32)
    allowed = (own_ids[:, None] == row_ids[None, :]) & (places[None, :] <= query_places[:, None])
    cosine_table, sine_table = rope_tables(own_positions, HEAD_DIM)
    tok_float = tokens.astype(jnp.float32)
    scale_in = inverse_rms(tok_float)
    normed_in = tok_float * scale_in
    gain_piece = lax.all_gather(attention_gain, "fsdp", axis=0, tiled=True)
    query_piece = lax.all_gather(query_weight, "fsdp", axis=0, tiled=True)
    key_piece = lax.all_gather(key_weight, "fsdp", axis=0, tiled=True)
    value_piece = lax.all_gather(value_weight, "fsdp", axis=0, tiled=True)
    columns = normed_in
    hidden_cols = (columns * gain_piece.astype(jnp.float32)).astype(jnp.bfloat16)
    query_acc = jnp.dot(hidden_cols, query_piece, preferred_element_type=jnp.float32)
    key_acc = jnp.dot(hidden_cols, key_piece, preferred_element_type=jnp.float32)
    value_acc = jnp.dot(hidden_cols, value_piece, preferred_element_type=jnp.float32)
    hidden_in = hidden_cols
    gain_in = gain_piece
    query_rot = rotate(
        query_acc.reshape(tok_count, HEADS, HEAD_DIM), cosine_table, sine_table
    ).astype(jnp.bfloat16)
    query_rot = query_rot.reshape(tok_count, KV_HEADS, group_ratio, HEAD_DIM)
    key_rot = (
        rotate(key_acc.reshape(tok_count, KV_HEADS, HEAD_DIM), cosine_table, sine_table)
        .astype(jnp.bfloat16)
        .reshape(tok_count, key_width)
    )
    value_low = value_acc.astype(jnp.bfloat16)
    key_row, value_row = (
        lax.all_gather(key_rot, "fsdp", axis=0, tiled=True),
        lax.all_gather(value_low, "fsdp", axis=0, tiled=True),
    )
    key_heads = key_row.reshape(row_length, KV_HEADS, HEAD_DIM).transpose(1, 0, 2)
    value_heads = value_row.reshape(row_length, KV_HEADS, HEAD_DIM).transpose(1, 0, 2)
    query_heads = query_rot.transpose(1, 0, 2, 3)

    def head_forward(items):
        query_part, key_part, value_part = items
        raw_scores = (
            jnp.einsum("qrd,kd->rqk", query_part, key_part, preferred_element_type=jnp.float32)
            * score_scale
        )
        masked = jnp.where(allowed, raw_scores, NEGATIVE)
        row_top = jnp.max(masked, axis=-1, keepdims=True)
        row_total = jnp.sum(
            jnp.where(allowed, jnp.exp(masked - row_top), 0.0), axis=-1, keepdims=True
        )
        log_total = row_top + jnp.log(row_total)
        softmax_rows = probabilities(raw_scores, allowed, log_total).astype(jnp.bfloat16)
        mixed_part = jnp.einsum(
            "rqk,kd->qrd", softmax_rows, value_part, preferred_element_type=jnp.float32
        )
        return (mixed_part, log_total)

    mixed_parts, log_totals = lax.map(head_forward, (query_heads, key_heads, value_heads))
    mixed_heads = (
        mixed_parts.transpose(1, 0, 2, 3).reshape(tok_count, query_width).astype(jnp.bfloat16)
    )
    columns = mixed_heads
    branch_out = jnp.dot(
        columns,
        lax.all_gather(output_weight, "fsdp", axis=0, tiled=True),
        preferred_element_type=jnp.float32,
    )
    middle = tok_float + branch_out
    scale_mid = inverse_rms(middle)
    normed_mid = middle * scale_mid
    gain_piece = lax.all_gather(feed_gain, "fsdp", axis=0, tiled=True)
    gate_piece = lax.all_gather(gate_weight, "fsdp", axis=0, tiled=True)
    up_piece = lax.all_gather(up_weight, "fsdp", axis=0, tiled=True)
    columns = normed_mid
    hidden_cols = (columns * gain_piece.astype(jnp.float32)).astype(jnp.bfloat16)
    gate_acc = jnp.dot(hidden_cols, gate_piece, preferred_element_type=jnp.float32)
    up_acc = jnp.dot(hidden_cols, up_piece, preferred_element_type=jnp.float32)
    gate_sig = jax.nn.sigmoid(gate_acc)
    gate_silu = gate_acc * gate_sig
    inner_act = (gate_silu * up_acc).astype(jnp.bfloat16)
    columns = inner_act
    feed_out = jnp.dot(
        columns,
        lax.all_gather(down_weight, "fsdp", axis=0, tiled=True),
        preferred_element_type=jnp.float32,
    )
    activations = (middle + feed_out).astype(jnp.bfloat16)
    grad_out = cotangent.astype(jnp.float32)
    grad_inner = times_transposed(
        cotangent, lax.all_gather(down_weight, "fsdp", axis=0, tiled=True)
    )
    grad_gate = (grad_inner * up_acc * gate_sig * (1.0 + gate_acc * (1.0 - gate_sig))).astype(
        jnp.bfloat16
    )
    grad_up = (grad_inner * gate_silu).astype(jnp.bfloat16)
    columns = times_transposed(
        grad_gate, lax.all_gather(gate_weight, "fsdp", axis=0, tiled=True)
    ) + times_transposed(grad_up, lax.all_gather(up_weight, "fsdp", axis=0, tiled=True))
    grad_hidden_mid = columns
    gain_mid_term = jnp.sum(grad_hidden_mid * normed_mid, axis=0)
    grad_normed_mid = grad_hidden_mid * gain_piece.astype(jnp.float32)
    grad_middle = grad_out + scale_mid * (
        grad_normed_mid - normed_mid * jnp.mean(grad_normed_mid * normed_mid, axis=1, keepdims=True)
    )
    grad_branch = grad_middle.astype(jnp.bfloat16)
    grad_mixed = times_transposed(
        grad_branch, lax.all_gather(output_weight, "fsdp", axis=0, tiled=True)
    ).astype(jnp.bfloat16)
    grad_mixed_heads = grad_mixed.reshape(tok_count, KV_HEADS, group_ratio, HEAD_DIM).transpose(
        1, 0, 2, 3
    )

    def head_backward(items):
        query_part, key_part, value_part, grad_part, log_total = items
        raw_again = (
            jnp.einsum("qrd,kd->rqk", query_part, key_part, preferred_element_type=jnp.float32)
            * score_scale
        )
        probs_again = probabilities(raw_again, allowed, log_total)
        probs_low = probs_again.astype(jnp.bfloat16)
        grad_probs = jnp.einsum(
            "qrd,kd->rqk", grad_part, value_part, preferred_element_type=jnp.float32
        )
        row_delta = jnp.sum(grad_probs * probs_again, axis=-1, keepdims=True)
        grad_scores = (probs_again * (grad_probs - row_delta)).astype(jnp.bfloat16)
        grad_query_part = (
            jnp.einsum("rqk,kd->qrd", grad_scores, key_part, preferred_element_type=jnp.float32)
            * score_scale
        )
        grad_key_part = (
            jnp.einsum("rqk,qrd->kd", grad_scores, query_part, preferred_element_type=jnp.float32)
            * score_scale
        )
        grad_value_part = jnp.einsum(
            "rqk,qrd->kd", probs_low, grad_part, preferred_element_type=jnp.float32
        )
        return (grad_query_part, grad_key_part, grad_value_part)

    grad_query_parts, grad_key_parts, grad_value_parts = lax.map(
        head_backward, (query_heads, key_heads, value_heads, grad_mixed_heads, log_totals)
    )
    grad_query_rot = grad_query_parts.transpose(1, 0, 2, 3)
    grad_key_row = grad_key_parts.transpose(1, 0, 2).reshape(row_length, key_width)
    grad_value_row = grad_value_parts.transpose(1, 0, 2).reshape(row_length, key_width)
    grad_key_rot, grad_value_sum = (
        lax.psum_scatter(
            grad_key_row.astype(jnp.bfloat16), "fsdp", scatter_dimension=0, tiled=True
        ).astype(jnp.float32),
        lax.psum_scatter(
            grad_value_row.astype(jnp.bfloat16), "fsdp", scatter_dimension=0, tiled=True
        ).astype(jnp.float32),
    )
    grad_value = grad_value_sum.astype(jnp.bfloat16)
    grad_query = (
        unrotate(grad_query_rot.reshape(tok_count, HEADS, HEAD_DIM), cosine_table, sine_table)
        .reshape(tok_count, query_width)
        .astype(jnp.bfloat16)
    )
    grad_key = (
        unrotate(grad_key_rot.reshape(tok_count, KV_HEADS, HEAD_DIM), cosine_table, sine_table)
        .reshape(tok_count, key_width)
        .astype(jnp.bfloat16)
    )
    query_piece = lax.all_gather(query_weight, "fsdp", axis=0, tiled=True)
    key_piece = lax.all_gather(key_weight, "fsdp", axis=0, tiled=True)
    value_piece = lax.all_gather(value_weight, "fsdp", axis=0, tiled=True)
    columns = (
        times_transposed(grad_query, query_piece)
        + times_transposed(grad_key, key_piece)
        + times_transposed(grad_value, value_piece)
    )
    gain_in_term = jnp.sum(columns * normed_in, axis=0)
    grad_normed_in = columns * gain_in.astype(jnp.float32)
    grad_tokens = grad_middle + scale_in * (
        grad_normed_in - normed_in * jnp.mean(grad_normed_in * normed_in, axis=1, keepdims=True)
    )
    input_grad = grad_tokens.astype(jnp.bfloat16)
    projection_rows = owner_rows(
        hidden_in, jnp.concatenate([grad_query, grad_key, grad_value], axis=1)
    )
    output_rows = owner_rows(mixed_heads, grad_branch)
    feed_rows = owner_rows(hidden_cols, jnp.concatenate([grad_gate, grad_up], axis=1))
    down_rows_grad = owner_rows(inner_act, cotangent)
    gain_in_rows, gain_mid_rows = (
        lax.psum_scatter(gain_in_term, "fsdp", scatter_dimension=0, tiled=True),
        lax.psum_scatter(gain_mid_term, "fsdp", scatter_dimension=0, tiled=True),
    )
    summed = (
        lax.psum(gain_in_rows.astype(jnp.bfloat16), "replica").astype(jnp.float32),
        lax.psum(projection_rows.astype(jnp.bfloat16), "replica").astype(jnp.float32),
        lax.psum(output_rows.astype(jnp.bfloat16), "replica").astype(jnp.float32),
        lax.psum(gain_mid_rows.astype(jnp.bfloat16), "replica").astype(jnp.float32),
        lax.psum(feed_rows.astype(jnp.bfloat16), "replica").astype(jnp.float32),
        lax.psum(down_rows_grad.astype(jnp.bfloat16), "replica").astype(jnp.float32),
    )
    gain_in_grad, projection_sum, output_sum, gain_mid_grad, feed_sum, down_sum = summed
    query_grad = projection_sum[:, :query_width]
    key_grad = projection_sum[:, query_width : query_width + key_width]
    value_grad = projection_sum[:, query_width + key_width :]
    gate_grad = feed_sum[:, :feed_width]
    up_grad = feed_sum[:, feed_width:]
    return (
        activations,
        input_grad,
        gain_in_grad,
        query_grad,
        key_grad,
        value_grad,
        output_sum,
        gain_mid_grad,
        gate_grad,
        up_grad,
        down_sum,
    )


def solution(mesh):
    in_specs = (
        P(("replica", "fsdp"), None),
        P("replica", None),
        P("fsdp"),
        P("fsdp", None),
        P("fsdp", None),
        P("fsdp", None),
        P("fsdp", None),
        P("fsdp"),
        P("fsdp", None),
        P("fsdp", None),
        P("fsdp", None),
        P(("replica", "fsdp"), None),
    )
    out_specs = (
        P(("replica", "fsdp"), None),
        P(("replica", "fsdp"), None),
        P("fsdp"),
        P("fsdp", None),
        P("fsdp", None),
        P("fsdp", None),
        P("fsdp", None),
        P("fsdp"),
        P("fsdp", None),
        P("fsdp", None),
        P("fsdp", None),
    )
    return jax.shard_map(
        per_device, mesh=mesh, in_specs=in_specs, out_specs=out_specs, check_vma=False
    )
```

profile of v0, /device:TPU:0, one launch (start us, length us, event | category | flops | bytes accessed | tf_op | source)
XLA Modules:
  0.0 3540.8 jit_solution(3284955656895021576)
XLA Ops:
  12.0 13.7 all-gather
  26.3 12.0 all-gather.1
  42.1 19.3 all_gather.42
  62.4 9.8 all-gather.12.cloned.1.call-done
  74.2 17.6 all_gather.44
  91.7 133.0 %all-gather.14.cloned.1.call-done = bf16[2048,2048]{1,0:T(8,128)(2,1)} async-done(((bf16[512,2048]{1,0:T(8,128)(2,1)}), bf16[2048,2048]{1,0:T(8,128)(2,1)}) %all-gather.14.cloned.1.call-update) | async-done | bytes 8388624 | tf_op jit(solution)/shard_map/all_gather | solution.py:120
  224.7 6.8 fusion.89
  232.0 31.0 while.30
  236.8 3.1 fusion.174
  244.5 3.1 fusion.174
  252.2 3.1 fusion.174
  259.9 3.1 fusion.174
  263.0 111.7 %all-gather.16.cloned.1.call-done = bf16[2048,2048]{1,0:T(8,128)(2,1)} async-done(((bf16[512,2048]{1,0:T(8,128)(2,1)}), bf16[2048,2048]{1,0:T(8,128)(2,1)}) %all-gather.16.cloned.1.call-update) | async-done | bytes 8388624 | tf_op jit(solution)/shard_map/all_gather | solution.py:173
  374.7 6.2 multiply_reduce_fusion.2
  381.2 384.3 %all-gather.18.cloned.1.call-done = bf16[2048,5632]{1,0:T(8,128)(2,1)} async-done(((bf16[512,5632]{1,0:T(8,128)(2,1)}), bf16[2048,5632]{1,0:T(8,128)(2,1)}) %all-gather.18.cloned.1.call-update) | async-done | bytes 23068688 | tf_op jit(solution)/shard_map/all_gather | solution.py:180
  765.5 14.5 fusion.96
  780.0 376.3 %all-gather.20.cloned.1.call-done = bf16[2048,5632]{1,0:T(8,128)(2,1)} async-done(((bf16[512,5632]{1,0:T(8,128)(2,1)}), bf16[2048,5632]{1,0:T(8,128)(2,1)}) %all-gather.20.cloned.1.call-update) | async-done | bytes 23068688 | tf_op jit(solution)/shard_map/all_gather | solution.py:181
  1156.3 13.8 fusion.97
  1170.1 377.2 %all-gather.22.cloned.1.call-done = bf16[5632,2048]{1,0:T(8,128)(2,1)} async-done(((bf16[1408,2048]{1,0:T(8,128)(2,1)}), bf16[5632,2048]{1,0:T(8,128)(2,1)}) %all-gather.22.cloned.1.call-update) | async-done | bytes 23068688 | tf_op jit(solution)/shard_map/all_gather | solution.py:192
  1547.4 25.8 multiply_convert_fusion
  1573.1 12.5 fusion.98
  1585.6 13.8 multiply_reduce_fusion
  1599.4 2.8 multiply_add_fusion
  1602.2 6.7 convolution_convert_fusion.4
  1610.4 105.2 %while.31 = (s32[]{:T(128)}, f32[4,256,8,64]{1,3,2,0:T(8,128)}, bf16[4,1024,64]{1,2,0:T(8,128)(2,1)}, bf16[4,1024,64]{1,2,0:T(8,128)(2,1)}, bf16[4,1024,64]{1,2,...) while((s32[]{:T(128)}, f32[4,256,8,64]{1,3,2,0:T(8,128)}, ...), condition=%wide.region_11.12_spmd.clone.clone, body=%wide.region_9.11_spmd.clone.sunk.clone | while | flops 1364129792 | bytes 145673520 | solution.py:247
  1613.5 7.5 fusion.185
  1621.0 7.1 fusion.186
  1628.1 2.7 fusion.187
  1630.8 3.0 fusion.188
  1633.8 2.4 fusion.189
  1639.7 7.5 fusion.185
  1647.2 7.1 fusion.186
  1654.3 2.7 fusion.187
  1657.0 3.0 fusion.188
  1665.9 7.5 fusion.185
  1673.4 7.1 fusion.186
  1680.5 2.7 fusion.187
  1683.2 3.0 fusion.188
  1692.1 7.5 fusion.185
  1699.6 7.1 fusion.186
  1706.6 2.7 fusion.187
  1709.4 3.0 fusion.188
  1712.4 2.4 fusion.189
  1716.5 7.0 convolution_convert_fusion.3
  1727.2 8.5 reduce-scatter.7.cloned.1.call-done
  1736.8 21.2 reduce-scatter.9.cloned.1.call-done
  1758.0 7.3 convolution_convert_fusion.2
  1765.4 12.7 convolution_convert_fusion.1
  1778.1 21.2 convolution_convert_fusion
  1799.4 104.1 %reduce-scatter.13.cloned.1.call-done = bf16[512,2048]{1,0:T(8,128)(2,1)} async-done(((bf16[2048,2048]{1,0:T(8,128)(2,1)}), bf16[512,2048]{1,0:T(8,128)(2,1)}) %reduce-scatter.13.cloned.1.call-update) | async-done | bytes 2097168 | tf_op jit(solution)/shard_map/reduce_scatter | solution.py:76
  1903.4 181.7 %reduce-scatter.11.cloned.1.call-done = bf16[512,2560]{1,0:T(8,128)(2,1)} async-done(((bf16[2048,2560]{1,0:T(8,128)(2,1)}), bf16[512,2560]{1,0:T(8,128)(2,1)}) %reduce-scatter.11.cloned.1.call-update) | async-done | bytes 2621456 | tf_op jit(solution)/shard_map/reduce_scatter | solution.py:76
  2085.2 383.9 %reduce-scatter.17.cloned.1.call-done = bf16[1408,2048]{1,0:T(8,128)(2,1)} async-done(((bf16[5632,2048]{1,0:T(8,128)(2,1)}), bf16[1408,2048]{1,0:T(8,128)(2,1)}) %reduce-scatter.17.cloned.1.call-update) | async-done | bytes 5767184 | tf_op jit(solution)/shard_map/reduce_scatter | solution.py:76
  2469.1 757.8 %reduce-scatter.15.cloned.1.call-done = bf16[512,11264]{1,0:T(8,128)(2,1)} async-done(((bf16[2048,11264]{1,0:T(8,128)(2,1)}), bf16[512,11264]{1,0:T(8,128)(2,1)}) %reduce-scatter.15.cloned.1.call-update) | async-done | bytes 11534352 | tf_op jit(solution)/shard_map/reduce_scatter | solution.py:76
  3228.8 6.2 fusion.99
  3235.0 13.8 fusion.70
  3252.4 19.3 all-reduce.2
  3271.8 12.5 all-reduce.3
  3285.5 3.2 fusion.76
  3288.6 219.3 %all-reduce.7.cloned.1.call-done = (bf16[512,2560]{1,0:T(8,128)(2,1)}, bf16[512,2048]{1,0:T(8,128)(2,1)}, bf16[512,11264]{1,0:T(8,128)(2,1)}, bf16[1408,2048]{1,0:T(8,128)(2,1)}) async-done(((bf16[512,2560]{1,0:T(8,128)(2,1)}, bf16[512,2048]{1,0:T(8,128)(2,1)}, bf16[512,11264]{1,0:T(8,128)(2,1)}, bf16[1408,2048]{1,0:T(8,128)(2,1)}), (bf16[512,2560]{1,0:T(8,128)(2,1)}, bf16[512,2048]{1,0:T(8,128)(2,1)}, ...) | async-done | bytes 22020112 | tf_op jit(solution)/shard_map/psum | solution.py:298
  3508.0 4.4 slice.80
  3512.4 2.8 fusion.95
  3515.2 4.3 convert_element_type.177
  3519.5 8.5 fusion.94
  3528.0 6.0 convert_element_type.183
  (211 shorter events, 62.6 us)
Async XLA Ops:
  7.2 33.2 all-gather.10.cloned.1.call-start
  7.9 64.3 %all-gather.12.cloned.1.call-start = ((), (), s32[]{:S(2)}) async-start(), calls=%async_computation.7 | async-start | bytes 1310720 | tf_op jit(solution)/shard_map/all_gather | solution.py:121
  8.7 216.0 %all-gather.14.cloned.1.call-start = ((), (), s32[]{:S(2)}) async-start(), calls=%async_computation.8 | async-start | bytes 10485760 | tf_op jit(solution)/shard_map/all_gather | solution.py:120
  9.4 365.3 %all-gather.16.cloned.1.call-start = ((), (), s32[]{:S(2)}) async-start(), calls=%async_computation.9 | async-start | bytes 10485760 | tf_op jit(solution)/shard_map/all_gather | solution.py:173
  10.0 755.5 %all-gather.18.cloned.1.call-start = ((), (), s32[]{:S(2)}) async-start(), calls=%async_computation.10 | async-start | bytes 28835840 | tf_op jit(solution)/shard_map/all_gather | solution.py:180
  10.6 1145.8 %all-gather.20.cloned.1.call-start = ((), (), s32[]{:S(2)}) async-start(), calls=%async_computation.11 | async-start | bytes 28835840 | tf_op jit(solution)/shard_map/all_gather | solution.py:181
  11.1 0.9 copy-start.29
  11.1 14.6 copy-start.20
  11.2 15.1 copy-start.30
  11.2 27.6 copy-start.3
  11.2 1536.2 %all-gather.22.cloned.1.call-start = ((), (), s32[]{:S(2)}) async-start(), calls=%async_computation.12 | async-start | bytes 28835840 | tf_op jit(solution)/shard_map/all_gather | solution.py:192
  11.9 1723.8 %reduce-scatter.7.cloned.1.call-start = ((), (), s32[]{:S(2)}) async-start(), calls=%async_computation.13 | async-start | bytes 655360 | tf_op jit(solution)/shard_map/reduce_scatter | solution.py:254
  25.7 199.0 %copy-start.24 = (f32[4,1,512]{2,1,0:T(1,128)}, f32[4,1,512]{2,1,0:T(1,128)S(1)}, u32[]{:S(2)}) copy-start(f32[4,1,512]{2,1,0:T(1,128)S(1)} %convert_element_type.184) | copy-start | bytes 24580
  39.1 185.6 %copy-start.26 = (f32[256]{0:T(256)}, f32[256]{0:T(256)S(1)}, u32[]{:S(2)}) copy-start(f32[256]{0:T(256)S(1)} %add_rsqrt_fusion.1) | copy-start | bytes 3076
  39.3 192.3 %copy-start.16 = (f32[256,32]{0,1:T(8,128)}, f32[256,32]{0,1:T(8,128)S(1)}, u32[]{:S(2)}) copy-start(f32[256,32]{0,1:T(8,128)S(1)} %get-tuple-element.235) | copy-start | bytes 98308
  39.3 192.3 %copy-start.18 = (f32[256,32]{0,1:T(8,128)}, f32[256,32]{0,1:T(8,128)S(1)}, u32[]{:S(2)}) copy-start(f32[256,32]{0,1:T(8,128)S(1)} %get-tuple-element.236) | copy-start | bytes 98308
  263.0 111.7 %copy-start.7 = (bf16[4,256,8,64]{1,3,2,0:T(8,128)(2,1)}, bf16[4,256,8,64]{1,3,2,0:T(8,128)(2,1)S(1)}, u32[]{:S(2)}) copy-start(bf16[4,256,8,64]{1,3,2,0:T(8,128)(2,1)S(1)} %get-tuple-element.103) | copy-start | bytes 3145732
  263.0 111.7 %copy-start.10 = (bf16[4,256,8,64]{1,3,2,0:T(8,128)(2,1)}, bf16[4,256,8,64]{1,3,2,0:T(8,128)(2,1)S(1)}, u32[]{:S(2)}) copy-start(bf16[4,256,8,64]{1,3,2,0:T(8,128)(2,1)S(1)} %get-tuple-element.528) | copy-start | bytes 3145732
  380.9 1204.8 %copy-start.5 = (f32[256,2048]{1,0:T(8,128)}, f32[256,2048]{1,0:T(8,128)S(1)}, u32[]{:S(2)}) copy-start(f32[256,2048]{1,0:T(8,128)S(1)} %get-tuple-element.238) | copy-start | bytes 6291460
  381.2 384.3 %copy-start.13 = (bf16[256,2048]{1,0:T(8,128)(2,1)}, bf16[256,2048]{1,0:T(8,128)(2,1)S(1)}, u32[]{:S(2)}) copy-start(bf16[256,2048]{1,0:T(8,128)(2,1)S(1)} %multiply_convert_fusion.3) | copy-start | bytes 3145732
  780.0 767.3 %copy-start.12 = (bf16[256,2048]{1,0:T(8,128)(2,1)S(1)}, bf16[256,2048]{1,0:T(8,128)(2,1)}, u32[]{:S(2)}) copy-start(bf16[256,2048]{1,0:T(8,128)(2,1)} %param.27) | copy-start | bytes 3145732
  1610.8 2.3 copy-start.8
  1613.2 7.8 copy-start.1
  1628.1 5.8 copy-start
  1630.8 3.1 copy-start.22
  1633.8 3.2 copy-start.9
  1636.2 0.8 copy-start.23
  1637.1 2.3 copy-start.8
  1639.4 7.8 copy-start.1
  1654.2 5.8 copy-start
  1657.0 3.1 copy-start.22
  1660.0 3.2 copy-start.9
  1662.4 0.8 copy-start.23
  1663.3 2.3 copy-start.8
  1665.6 7.8 copy-start.1
  1680.4 5.8 copy-start
  1683.2 3.1 copy-start.22
  1686.2 3.2 copy-start.9
  1688.6 0.8 copy-start.23
  1689.4 2.3 copy-start.8
  1691.8 7.8 copy-start.1
  1706.6 5.8 copy-start
  1709.4 3.1 copy-start.22
  1712.4 3.2 copy-start.9
  1714.8 0.8 copy-start.23
  1715.7 42.3 %reduce-scatter.9.cloned.1.call-start = ((), (), s32[]{:S(2)}) async-start(), calls=%async_computation.14 | async-start | bytes 655360 | tf_op jit(solution)/shard_map/reduce_scatter | solution.py:257
  1716.4 187.0 %reduce-scatter.13.cloned.1.call-start = ((), (), s32[]{:S(2)}) async-start(), calls=%async_computation.16 | async-start | bytes 10485760 | tf_op jit(solution)/shard_map/reduce_scatter | solution.py:76
  1723.4 0.8 copy-start.19
  1723.5 361.7 %reduce-scatter.11.cloned.1.call-start = ((), (), s32[]{:S(2)}) async-start(), calls=%async_computation.15 | async-start | bytes 13107200 | tf_op jit(solution)/shard_map/reduce_scatter | solution.py:76
  1724.2 33.7 copy-start.4
  1724.2 33.7 copy-start.25
  1724.2 33.7 copy-start.27
  1765.3 703.8 %reduce-scatter.17.cloned.1.call-start = ((), (), s32[]{:S(2)}) async-start(), calls=%async_computation.18 | async-start | bytes 28835840 | tf_op jit(solution)/shard_map/reduce_scatter | solution.py:76
  1778.1 1448.8 %reduce-scatter.15.cloned.1.call-start = ((), (), s32[]{:S(2)}) async-start(), calls=%async_computation.17 | async-start | bytes 57671680 | tf_op jit(solution)/shard_map/reduce_scatter | solution.py:76
  1799.3 1708.6 %all-reduce.7.cloned.1.call-start = ((), (), s32[]{:S(2)}) async-start(), calls=%async_computation.19 | async-start | bytes 44040192 | tf_op jit(solution)/shard_map/psum | solution.py:298
  3228.7 6.3 copy-start.6
  3228.7 6.3 copy-start.11
  3235.0 13.8 copy-start.15
  3248.8 1.3 copy-start.14
  3248.8 1.3 copy-start.21
  3250.1 2.3 copy-start.28
  3508.0 11.5 copy-start.2
  3515.2 12.8 slice-start
  3519.5 8.5 slice-start.1
  (2 other events, 1.4 us)
Sparse Core Ops, SparseCore 0:
  9.6 30.7 all-gather.9
  42.0 30.2 all-gather.11
  73.8 150.8 all-gather.13
  226.1 148.5 all-gather.15
  376.1 389.3 all-gather.17
  766.9 389.3 all-gather.19
  1157.9 389.3 all-gather.21
  1715.8 19.9 reduce-scatter.6
  1738.1 19.8 reduce-scatter.8
  1760.7 142.6 reduce-scatter.12
  1906.4 178.7 reduce-scatter.10
  2087.4 381.6 reduce-scatter.16
  2471.6 755.2 reduce-scatter.14
  3230.9 276.9 all-reduce.6
where the time goes:
time: 3550 us; the launch traced here: 3540 us
  waiting for transfers between devices  3080 us (87%)
  matrix products  268 us (8%)
  blocking collectives  94.3 us (3%)
  other arithmetic  61.7 us (2%)
    reduce_scatter x4, waiting for transfers between devices, owner_rows(): lax.psum_scatter(transposed_times(left_side, right_side).astype(jnp.bfloa...  1430 us
    all_gather x1, waiting for transfers between devices, per_device(): gate_piece = lax.all_gather(gate_weight, 'fsdp', axis=0, tiled=True)  384 us
    all_gather x1, waiting for transfers between devices, per_device(): lax.all_gather(down_weight, 'fsdp', axis=0, tiled=True)  377 us
    all_gather x1, waiting for transfers between devices, per_device(): up_piece = lax.all_gather(up_weight, 'fsdp', axis=0, tiled=True)  376 us
    psum x1, waiting for transfers between devices, per_device(): lax.psum(projection_rows.astype(jnp.bfloat16), 'replica')  219 us
    all_gather x1, waiting for transfers between devices, per_device(): query_piece = lax.all_gather(query_weight, 'fsdp', axis=0, tiled=True)  133 us
    all_gather x1, waiting for transfers between devices, per_device(): lax.all_gather(output_weight, 'fsdp', axis=0, tiled=True)  112 us
  transfers between devices with their start and end apart: 14, of which 14 were waited for; matrix products, arithmetic and copies ran while one was open for 4% of the time, Pallas kernels for 0%

commit v1 on v0

v1 whole, which is shorter than its diff:
```python
import math

import jax
import jax.numpy as jnp
from jax import lax
from jax.sharding import PartitionSpec as P

HEADS = 32
KV_HEADS = 4
HEAD_DIM = 64
EPSILON = 1e-05
NEGATIVE = -1e30
R = "replica"
F = "fsdp"


def inverse_rms(values):
    return lax.rsqrt(jnp.mean(values * values, axis=1, keepdims=True) + EPSILON)


def rope_tables(positions):
    half_dim = HEAD_DIM // 2
    freq_rates = jnp.exp(jnp.arange(half_dim, dtype=jnp.float32) * (-math.log(10000.0) / half_dim))
    angles = positions.astype(jnp.float32)[:, None] * freq_rates[None, :]
    return (jnp.cos(angles), jnp.sin(angles))


def rotate(tensor, cosine_table, sine_table, sign):
    half_dim = HEAD_DIM // 2
    low, up = tensor[..., :half_dim], tensor[..., half_dim:]
    cos_part = cosine_table[:, None, :]
    sin_part = sine_table[:, None, :] * sign
    return jnp.concatenate(
        [low * cos_part - up * sin_part, up * cos_part + low * sin_part], axis=-1
    )


def dot(a, b, ca=1, cb=0):
    return lax.dot_general(a, b, (((ca,), (cb,)), ((), ())), preferred_element_type=jnp.float32)


def plane_gather(x):
    return lax.all_gather(x, R, axis=0, tiled=True)


def plane_scatter(x):
    return lax.psum_scatter(x, R, scatter_dimension=0, tiled=True)


def line_gather(x):
    return lax.all_gather(x, F, axis=0, tiled=True)


def line_scatter(x):
    return lax.psum_scatter(x, F, scatter_dimension=0, tiled=True)


def per_device(
    tokens,
    segment_ids,
    attention_gain,
    query_weight,
    key_weight,
    value_weight,
    output_weight,
    feed_gain,
    gate_weight,
    up_weight,
    down_weight,
    cotangent,
):
    f32, bf16 = jnp.float32, jnp.bfloat16
    planes, width = lax.axis_size(F), lax.axis_size(R)
    r, z = lax.axis_index(R), lax.axis_index(F)
    tok, model = tokens.shape
    length = segment_ids.shape[1]
    all_tok = width * tok
    heads = HEADS // width
    group = HEADS // KV_HEADS
    qw = heads * HEAD_DIM
    kv = (r * heads) // group
    feed = gate_weight.shape[1]
    piece = feed // (width * planes)
    hidden_units = piece * planes
    scale = HEAD_DIM ** (-0.5)

    def cols(weight, first, count):
        return lax.dynamic_slice_in_dim(weight, first, count, 1)

    def feed_cols(weight):
        return [cols(weight, p * (feed // planes) + r * piece, piece) for p in range(planes)]

    w_qkv = line_gather(
        jnp.concatenate(
            [
                cols(query_weight, r * qw, qw),
                cols(key_weight, kv * HEAD_DIM, HEAD_DIM),
                cols(value_weight, kv * HEAD_DIM, HEAD_DIM),
            ],
            axis=1,
        )
    )
    w_out = lax.all_to_all(
        line_gather(cols(output_weight, r * (model // width), model // width)),
        R,
        split_axis=0,
        concat_axis=1,
        tiled=True,
    )
    w_feed = line_gather(jnp.concatenate(feed_cols(gate_weight) + feed_cols(up_weight), axis=1))
    w_gate, w_up = w_feed[:, :hidden_units], w_feed[:, hidden_units:]
    w_down = line_gather(lax.dynamic_slice_in_dim(down_weight, r * piece, piece, 0))
    gains = lax.all_gather(jnp.stack([attention_gain, feed_gain]), F, axis=1, tiled=True)
    gain_in, gain_mid = gains[0].astype(f32), gains[1].astype(f32)

    ids = lax.all_gather(segment_ids, R, axis=0, tiled=True)
    places = jnp.arange(length, dtype=jnp.int32)
    fresh = jnp.concatenate(
        [jnp.ones((width, 1), dtype=jnp.bool_), ids[:, 1:] != ids[:, :-1]], axis=1
    )
    positions = places[None] - lax.cummax(jnp.where(fresh, places[None], 0), axis=1)
    own_ids = lax.dynamic_slice_in_dim(ids, z * tok, tok, 1)
    own_positions = lax.dynamic_slice_in_dim(positions, z * tok, tok, 1).reshape(all_tok)
    own_places = z * tok + jnp.arange(tok, dtype=jnp.int32)
    allowed = (own_ids[:, :, None] == ids[:, None, :]) & (
        places[None, None, :] <= own_places[None, :, None]
    )
    cosine, sine = rope_tables(own_positions)

    tok_float = tokens.astype(f32)
    scale_in = inverse_rms(tok_float)
    normed_in = tok_float * scale_in
    hidden_in = plane_gather((normed_in * gain_in).astype(bf16))
    qkv = dot(hidden_in, w_qkv)
    query = rotate(qkv[:, :qw].reshape(all_tok, heads, HEAD_DIM), cosine, sine, 1.0).astype(bf16)
    key = rotate(qkv[:, None, qw : qw + HEAD_DIM], cosine, sine, 1.0).astype(bf16)[:, 0]
    value = qkv[:, qw + HEAD_DIM :].astype(bf16)
    kv_rows = (
        lax.all_gather(jnp.concatenate([key, value], axis=1), F, axis=0, tiled=False)
        .reshape(planes, width, tok, 2 * HEAD_DIM)
        .transpose(1, 0, 2, 3)
        .reshape(width, length, 2 * HEAD_DIM)
    )
    key_rows, value_rows = kv_rows[..., :HEAD_DIM], kv_rows[..., HEAD_DIM:]
    query_rows = query.reshape(width, tok, heads, HEAD_DIM)

    def one_forward(items):
        q, k, v, mask = items
        raw = jnp.einsum("qhd,kd->hqk", q, k, preferred_element_type=f32) * scale
        masked = jnp.where(mask, raw, NEGATIVE)
        top = jnp.max(masked, axis=-1, keepdims=True)
        total = jnp.sum(jnp.where(mask, jnp.exp(masked - top), 0.0), axis=-1, keepdims=True)
        log_total = top + jnp.log(total)
        probs = jnp.where(mask, jnp.exp(masked - log_total), 0.0).astype(bf16)
        return jnp.einsum("hqk,kd->qhd", probs, v, preferred_element_type=f32), log_total

    mixed, log_totals = lax.map(one_forward, (query_rows, key_rows, value_rows, allowed))
    mixed = mixed.reshape(all_tok, qw).astype(bf16)
    branch = plane_scatter(dot(mixed, w_out).astype(bf16)).astype(f32)
    middle = tok_float + branch
    scale_mid = inverse_rms(middle)
    normed_mid = middle * scale_mid

    hidden_mid = plane_gather((normed_mid * gain_mid).astype(bf16))
    cot_all = plane_gather(cotangent)
    gate_acc = dot(hidden_mid, w_gate)
    up_acc = dot(hidden_mid, w_up)
    gate_sig = jax.nn.sigmoid(gate_acc)
    gate_silu = gate_acc * gate_sig
    inner_act = (gate_silu * up_acc).astype(bf16)
    feed_out = plane_scatter(dot(inner_act, w_down).astype(bf16)).astype(f32)
    activations = (middle + feed_out).astype(bf16)
    grad_inner = dot(cot_all, w_down, 1, 1)
    grad_gate = (grad_inner * up_acc * gate_sig * (1.0 + gate_acc * (1.0 - gate_sig))).astype(bf16)
    grad_up = (grad_inner * gate_silu).astype(bf16)
    grad_hidden_mid = plane_scatter(
        (dot(grad_gate, w_gate, 1, 1) + dot(grad_up, w_up, 1, 1)).astype(bf16)
    ).astype(f32)
    feed_rows = line_scatter(
        jnp.concatenate([dot(hidden_mid, grad_gate, 0, 0), dot(hidden_mid, grad_up, 0, 0)], axis=1)
        .astype(bf16)
    )
    down_rows = line_scatter(dot(inner_act, cot_all, 0, 0).astype(bf16))
    gain_mid_term = jnp.sum(grad_hidden_mid * normed_mid, axis=0)
    grad_normed_mid = grad_hidden_mid * gain_mid
    grad_middle = cotangent.astype(f32) + scale_mid * (
        grad_normed_mid - normed_mid * jnp.mean(grad_normed_mid * normed_mid, axis=1, keepdims=True)
    )

    grad_branch = plane_gather(grad_middle.astype(bf16))
    grad_mixed = dot(grad_branch, w_out, 1, 1).astype(bf16)
    out_part = dot(mixed, grad_branch, 0, 0).astype(bf16)
    out_rows = line_scatter(
        lax.all_to_all(out_part, R, split_axis=1, concat_axis=0, tiled=True)
    )

    def one_backward(items):
        q, k, v, g, mask, log_total = items
        raw = jnp.einsum("qhd,kd->hqk", q, k, preferred_element_type=f32) * scale
        probs = jnp.where(mask, jnp.exp(jnp.where(mask, raw, NEGATIVE) - log_total), 0.0)
        probs_low = probs.astype(bf16)
        grad_probs = jnp.einsum("qhd,kd->hqk", g, v, preferred_element_type=f32)
        delta = jnp.sum(grad_probs * probs, axis=-1, keepdims=True)
        grad_scores = (probs * (grad_probs - delta)).astype(bf16)
        gq = jnp.einsum("hqk,kd->qhd", grad_scores, k, preferred_element_type=f32) * scale
        gk = jnp.einsum("hqk,qhd->kd", grad_scores, q, preferred_element_type=f32) * scale
        gv = jnp.einsum("hqk,qhd->kd", probs_low, g, preferred_element_type=f32)
        return gq, jnp.concatenate([gk, gv], axis=-1).astype(bf16)

    gq, gkv = lax.map(
        one_backward,
        (
            query_rows,
            key_rows,
            value_rows,
            grad_mixed.reshape(width, tok, heads, HEAD_DIM),
            allowed,
            log_totals,
        ),
    )
    gkv = gkv.reshape(width, planes, tok, 2 * HEAD_DIM).transpose(1, 0, 2, 3)
    gkv = line_scatter(gkv.reshape(planes * all_tok, 2 * HEAD_DIM)).astype(f32)
    grad_qkv = jnp.concatenate(
        [
            rotate(gq.reshape(all_tok, heads, HEAD_DIM), cosine, sine, -1.0).reshape(all_tok, qw),
            rotate(gkv[:, None, :HEAD_DIM], cosine, sine, -1.0)[:, 0],
            gkv[:, HEAD_DIM:],
        ],
        axis=1,
    ).astype(bf16)
    grad_hidden_in = plane_scatter(dot(grad_qkv, w_qkv, 1, 1).astype(bf16)).astype(f32)
    qkv_rows = line_scatter(dot(hidden_in, grad_qkv, 0, 0).astype(bf16))
    gain_in_term = jnp.sum(grad_hidden_in * normed_in, axis=0)
    grad_normed_in = grad_hidden_in * gain_in
    input_grad = (
        grad_middle
        + scale_in
        * (
            grad_normed_in
            - normed_in * jnp.mean(grad_normed_in * normed_in, axis=1, keepdims=True)
        )
    ).astype(bf16)

    gain_terms = lax.psum(
        lax.psum_scatter(
            jnp.stack([gain_in_term, gain_mid_term]), F, scatter_dimension=1, tiled=True
        ),
        R,
    )
    rows = model // planes

    def spread(x):
        x = plane_gather(x)
        return x.reshape(width, x.shape[0] // width, x.shape[1])

    down_grad = spread(down_rows).reshape(feed // planes, model).astype(f32)
    feed_all = spread(feed_rows).reshape(width, rows, 2, planes, piece)
    feed_all = feed_all.transpose(2, 1, 3, 0, 4).reshape(2, rows, feed).astype(f32)
    out_grad = spread(out_rows).transpose(1, 0, 2).reshape(output_weight.shape).astype(f32)
    qkv_all = spread(qkv_rows)
    query_grad = qkv_all[..., :qw].transpose(1, 0, 2).reshape(query_weight.shape).astype(f32)
    kv_all = qkv_all[..., qw:].astype(f32).reshape(KV_HEADS, width // KV_HEADS, rows, 2, HEAD_DIM)
    kv_all = kv_all.sum(axis=1).transpose(2, 1, 0, 3).reshape(2, rows, KV_HEADS * HEAD_DIM)
    return (
        activations,
        input_grad,
        gain_terms[0],
        query_grad,
        kv_all[0],
        kv_all[1],
        out_grad,
        gain_terms[1],
        feed_all[0],
        feed_all[1],
        down_grad,
    )


def solution(mesh):
    tok = P((R, F), None)
    row = P(F, None)
    in_specs = (tok, P(R, None), P(F), row, row, row, row, P(F), row, row, row, tok)
    out_specs = (tok, tok, P(F), row, row, row, row, P(F), row, row, row)
    return jax.shard_map(
        per_device, mesh=mesh, in_specs=in_specs, out_specs=out_specs, check_vma=False
    )
```

time: 3550 us -> 1630 us (0.46)
  waiting for transfers between devices: 3080 us -> 980 us
  local copies, waits for them, and re-layouts: 24.7 us -> 237 us
  blocking collectives: 94.3 us -> 36.2 us
    reduce_scatter x6 -> x9, waiting for transfers between devices: 1460 us -> 434 us  [the longest x4 232 us: plane_scatter(): return lax.psum_scatter(x, R, scatter_dimension=0, tiled=True)]
    all_gather x7 -> x13, waiting for transfers between devices: 1390 us -> 499 us  [the longest x8 306 us: plane_gather(): return lax.all_gather(x, R, axis=0, tiled=True)]
    psum x1 -> x0, waiting for transfers between devices: 219 us -> none  [per_device(): lax.psum(projection_rows.astype(jnp.bfloat16), 'replica')]
    unnamed x61 -> x96, local copies, waits for them, and re-layouts: 2.92 us -> 77.9 us
    dynamic_update_slice x0 -> x16, local copies, waits for them, and re-layouts: none -> 57.7 us  [per_device(): lax.map(one_forward, (query_rows, key_rows, value_rows, allowed))]
    all_gather x4 -> x2, blocking collectives: 62.5 us -> 22.7 us  [the longest x1 13.7 us: per_device(): lax.all_gather(jnp.stack([attention_gain, feed_gain]), F, axis=1, tiled=T...]
    dot_general x46 -> x71, matrix products: 268 us -> 265 us  [the longest x15 147 us: dot(): lax.dot_general(a, b, (((ca,), (cb,)), ((), ())), preferred_element_type=...]
  transfers between devices with their start and end apart: 14 -> 25, of which waited for: 14 -> 22; matrix products, arithmetic and copies ran while one was open for 4% -> 16% of each run, Pallas kernels for 0% -> 0%
where the time goes in v1:
time: 1630 us; the launch traced here: 1620 us
  waiting for transfers between devices  980 us (60%)
  matrix products  265 us (16%)
  local copies, waits for them, and re-layouts  237 us (15%)
  other arithmetic  79.4 us (5%)
  blocking collectives  36.2 us (2%)
    all_gather x8, waiting for transfers between devices, plane_gather(): return lax.all_gather(x, R, axis=0, tiled=True)  306 us
    reduce_scatter x4, waiting for transfers between devices, plane_scatter(): return lax.psum_scatter(x, R, scatter_dimension=0, tiled=True)  232 us
    reduce_scatter x5, waiting for transfers between devices, line_scatter(): return lax.psum_scatter(x, F, scatter_dimension=0, tiled=True)  202 us
    all_gather x4, waiting for transfers between devices, line_gather(): return lax.all_gather(x, F, axis=0, tiled=True)  171 us
    dot_general x15, matrix products, dot(): lax.dot_general(a, b, (((ca,), (cb,)), ((), ())), preferred_element_type=...  147 us
    unnamed x96, local copies, waits for them, and re-layouts  77.9 us
    dynamic_update_slice x16, local copies, waits for them, and re-layouts, per_device(): lax.map(one_forward, (query_rows, key_rows, value_rows, allowed))  57.7 us
  transfers between devices with their start and end apart: 25, of which 22 were waited for; matrix products, arithmetic and copies ran while one was open for 16% of the time, Pallas kernels for 0%

profile of v1, /device:TPU:0, one launch (start us, length us, event | category | flops | bytes accessed | tf_op | source)
XLA Modules:
  0.0 1623.2 jit_solution(11792320276419491319)
XLA Ops:
  12.2 13.7 all_gather.48
  29.4 9.1 all-gather.1
  41.5 9.3 all-gather.18.cloned.1.call-done
  50.8 55.7 %all-gather.16.cloned.1.call-done = bf16[2048,2048]{1,0:T(8,128)(2,1)} async-done(((bf16[256,2048]{1,0:T(8,128)(2,1)}), bf16[2048,2048]{1,0:T(8,128)(2,1)}) %all-gather.16.cloned.1.call-update) | async-done | bytes 8388624 | tf_op jit(solution)/shard_map/all_gather | solution.py:43
  106.5 6.4 fusion.118
  116.9 19.7 %all-gather.20.cloned.1.call-done = bf16[2048,256]{1,0:T(8,128)(2,1)} async-done(((bf16[512,256]{1,0:T(8,128)(2,1)}), bf16[2048,256]{1,0:T(8,128)(2,1)}) %all-gather.20.cloned.1.call-update) | async-done | bytes 1048592 | tf_op jit(solution)/shard_map/all_gather | solution.py:51
  136.6 3.7 all-to-all-start
  142.7 3.9 compare_and_fusion
  146.6 9.1 all-to-all-done
  161.9 22.2 %all-gather.40.cloned.1.call-done = bf16[8192,128]{0,1:T(8,128)(2,1)} async-done(((bf16[2048,128]{0,1:T(8,128)(2,1)}), bf16[8192,128]{0,1:T(8,128)(2,1)}) %all-gather.40.cloned.1.call-update) | async-done | bytes 2097168 | tf_op jit(solution)/shard_map/all_gather | solution.py:139
  193.2 52.6 %while.24 = (s32[]{:T(128)}, bf16[8,256,4,64]{1,3,2,0:T(8,128)(2,1)}, f32[8,4,256,1]{2,1,3,0:T(4,128)S(1)}, bf16[8,1024,64]{1,2,0:T(8,128)(2,1)}, pred[8,256,102...) while((s32[]{:T(128)}, ...), condition=%wide.region_6.7_spmd, body=%wide.region_3.6_spmd.sunk | while | flops 282065920 | bytes 14583909 | solution.py:157
  248.1 5.8 convolution_convert_fusion.2
  259.5 64.5 %reduce-scatter.13.cloned.1.call-done = bf16[256,2048]{1,0:T(8,128)(2,1)} async-done(((bf16[2048,2048]{1,0:T(8,128)(2,1)}), bf16[256,2048]{1,0:T(8,128)(2,1)}) %reduce-scatter.13.cloned.1.call-update) | async-done | bytes 1048592 | tf_op jit(solution)/shard_map/reduce_scatter | solution.py:47
  331.2 101.6 %all-gather.24.cloned.1.call-done = bf16[2048,1408]{1,0:T(8,128)(2,1)} async-done(((bf16[512,1408]{1,0:T(8,128)(2,1)}), bf16[2048,1408]{1,0:T(8,128)(2,1)}) %all-gather.24.cloned.1.call-update) | async-done | bytes 5767184 | tf_op jit(solution)/shard_map/all_gather | solution.py:51
  432.8 55.3 %all-gather.22.cloned.1.call-done = bf16[2048,2048]{1,0:T(8,128)(2,1)} async-done(((bf16[256,2048]{1,0:T(8,128)(2,1)}), bf16[2048,2048]{1,0:T(8,128)(2,1)}) %all-gather.22.cloned.1.call-update) | async-done | bytes 8388624 | tf_op jit(solution)/shard_map/all_gather | solution.py:43
  488.2 11.3 fusion.72
  499.5 9.7 fusion.68
  509.2 40.4 %all-gather.26.cloned.1.call-done = bf16[704,2048]{1,0:T(8,128)(2,1)} async-done(((bf16[176,2048]{1,0:T(8,128)(2,1)}), bf16[704,2048]{1,0:T(8,128)(2,1)}) %all-gather.26.cloned.1.call-update) | async-done | bytes 2883600 | tf_op jit(solution)/shard_map/all_gather | solution.py:51
  549.6 55.2 %all-gather.28.cloned.1.call-done = bf16[2048,2048]{1,0:T(8,128)(2,1)} async-done(((bf16[256,2048]{1,0:T(8,128)(2,1)}), bf16[2048,2048]{1,0:T(8,128)(2,1)}) %all-gather.28.cloned.1.call-update) | async-done | bytes 8388624 | tf_op jit(solution)/shard_map/all_gather | solution.py:43
  604.8 15.1 fusion.61
  619.9 14.3 fusion.70
  634.2 15.6 add_convert_fusion
  649.8 71.4 %reduce-scatter.17.cloned.1.call-done = bf16[256,2048]{1,0:T(8,128)(2,1)} async-done(((bf16[2048,2048]{1,0:T(8,128)(2,1)}), bf16[256,2048]{1,0:T(8,128)(2,1)}) %reduce-scatter.17.cloned.1.call-update) | async-done | bytes 1048592 | tf_op jit(solution)/shard_map/reduce_scatter | solution.py:47
  726.7 54.0 %all-gather.30.cloned.1.call-done = bf16[2048,2048]{1,0:T(8,128)(2,1)} async-done(((bf16[256,2048]{1,0:T(8,128)(2,1)}), bf16[2048,2048]{1,0:T(8,128)(2,1)}) %all-gather.30.cloned.1.call-update) | async-done | bytes 8388624 | tf_op jit(solution)/shard_map/all_gather | solution.py:43
  780.7 6.0 convolution_convert_fusion.8
  789.7 169.6 %while.25 = (s32[]{:T(128)}, f32[8,256,4,64]{1,0,3,2:T(8,128)}, bf16[8,1024,128]{1,2,0:T(8,128)(2,1)}, bf16[8,1024,64]{1,2,0:T(8,128)(2,1)}, pred[8,256,1024]{1,...) while((s32[]{:T(128)}, f32[8,256,4,64]{1,0,3,2:T(8,128)}, ...), condition=%wide.region_14.15_spmd, body=%wide.region_12.14_spmd.sunk | while | flops 682359808 | bytes 52058284 | solution.py:210
  798.6 6.9 dynamic_update_slice.25
  819.8 6.9 dynamic_update_slice.25
  841.0 6.9 dynamic_update_slice.25
  862.2 6.9 dynamic_update_slice.25
  883.4 6.9 dynamic_update_slice.25
  904.6 6.9 dynamic_update_slice.25
  925.8 6.9 dynamic_update_slice.25
  947.0 6.9 dynamic_update_slice.25
  967.9 10.8 convolution_convert_fusion.5
  978.8 9.6 convolution_convert_fusion.3
  988.4 8.6 convolution_convert_fusion.4
  1001.6 5.8 convolution_convert_fusion.7
  1008.4 3.7 all-to-all-start.1
  1015.2 12.2 all-to-all-done.1
  1031.0 9.1 convolution_convert_fusion.6
  1040.3 30.0 %reduce-scatter.29.cloned.1.call-done = bf16[176,2048]{1,0:T(8,128)(2,1)} async-done(((bf16[704,2048]{1,0:T(8,128)(2,1)}), bf16[176,2048]{1,0:T(8,128)(2,1)}) %reduce-scatter.29.cloned.1.call-update) | async-done | bytes 720912 | tf_op jit(solution)/shard_map/reduce_scatter | solution.py:55
  1070.3 104.9 %reduce-scatter.27.cloned.1.call-done = bf16[512,1408]{0,1:T(8,128)(2,1)} async-done(((bf16[2048,1408]{0,1:T(8,128)(2,1)}), bf16[512,1408]{0,1:T(8,128)(2,1)}) %reduce-scatter.27.cloned.1.call-update) | async-done | bytes 1441808 | tf_op jit(solution)/shard_map/reduce_scatter | solution.py:55
  1175.3 30.4 %reduce-scatter.25.cloned.1.call-done = bf16[512,256]{1,0:T(8,128)(2,1)} async-done(((bf16[2048,256]{1,0:T(8,128)(2,1)}), bf16[512,256]{1,0:T(8,128)(2,1)}) %reduce-scatter.25.cloned.1.call-update) | async-done | bytes 262160 | tf_op jit(solution)/shard_map/reduce_scatter | solution.py:55
  1205.8 36.6 %reduce-scatter.23.cloned.1.call-done = bf16[512,384]{1,0:T(8,128)(2,1)} async-done(((bf16[2048,384]{1,0:T(8,128)(2,1)}), bf16[512,384]{1,0:T(8,128)(2,1)}) %reduce-scatter.23.cloned.1.call-update) | async-done | bytes 393232 | tf_op jit(solution)/shard_map/reduce_scatter | solution.py:55
  1242.5 8.2 convolution_convert_fusion
  1252.8 10.8 convolution_convert_fusion.1
  1263.6 22.9 %all-gather.38.cloned.1.call-done = bf16[1408,2048]{1,0:T(8,128)(2,1)} async-done(((bf16[176,2048]{1,0:T(8,128)(2,1)}), bf16[1408,2048]{1,0:T(8,128)(2,1)}) %all-gather.38.cloned.1.call-update) | async-done | bytes 5767184 | tf_op jit(solution)/shard_map/all_gather | solution.py:43
  1286.5 8.7 convert_element_type.185
  1295.2 63.0 %all-gather.36.cloned.1.call-done = bf16[4096,1408]{0,1:T(8,128)(2,1)} async-done(((bf16[512,1408]{0,1:T(8,128)(2,1)}), bf16[4096,1408]{0,1:T(8,128)(2,1)}) %all-gather.36.cloned.1.call-update) | async-done | bytes 11534352 | tf_op jit(solution)/shard_map/all_gather | solution.py:43
  1358.1 7.1 convert_element_type.191
  1365.2 27.7 %copy.129 = f32[176,8,8,512]{3,2,1,0:T(8,128)} copy(f32[176,8,8,512]{3,1,2,0:T(8,128)S(1)} %bitcast.311) | data formatting | bytes 46137344
  1392.9 22.1 %copy.135 = f32[8,512,2,4,176]{1,4,0,3,2:T(8,128)S(1)} copy(f32[8,512,2,4,176]{1,0,4,3,2:T(8,128)} %bitcast.312) | data formatting | bytes 46137344 | tf_op jit(solution)/shard_map/convert_element_type | solution.py:258
  1415.0 8.5 fusion.114
  1423.5 12.2 copy.98
  1435.7 12.6 copy.99
  1448.3 4.0 convert_bitcast_fusion
  1452.3 5.3 copy.93
  1457.6 5.4 copy.97
  1472.1 24.8 %reduce-scatter.21.cloned.1.call-done = bf16[256,2048]{1,0:T(8,128)(2,1)} async-done(((bf16[2048,2048]{1,0:T(8,128)(2,1)}), bf16[256,2048]{1,0:T(8,128)(2,1)}) %reduce-scatter.21.cloned.1.call-update) | async-done | bytes 1048592 | tf_op jit(solution)/shard_map/reduce_scatter | solution.py:47
  1500.4 71.6 %reduce-scatter.15.cloned.1.call-done = bf16[256,2048]{1,0:T(8,128)(2,1)} async-done(((bf16[2048,2048]{1,0:T(8,128)(2,1)}), bf16[256,2048]{1,0:T(8,128)(2,1)}) %reduce-scatter.15.cloned.1.call-update) | async-done | bytes 1048592 | tf_op jit(solution)/shard_map/reduce_scatter | solution.py:47
  1572.0 5.5 fusion.79
  1577.5 23.9 %reduce-scatter.31.cloned.1.call-done = f32[512,2]{1,0:T(8,128)} async-done(((f32[2048,2]{1,0:T(8,128)}), f32[512,2]{1,0:T(8,128)}) %reduce-scatter.31.cloned.1.call-update) | async-done | bytes 4112
  1602.5 13.4 psum.7
  (349 shorter events, 259.9 us)
Async XLA Ops:
  7.2 18.7 %copy-start.3 = (bf16[256,2048]{1,0:T(8,128)(2,1)S(1)}, bf16[256,2048]{1,0:T(8,128)(2,1)}, u32[]{:S(2)}) copy-start(bf16[256,2048]{1,0:T(8,128)(2,1)} %param.16) | copy-start | bytes 3145732
  7.2 43.6 %all-gather.18.cloned.1.call-start = ((), (), s32[]{:S(2)}) async-start(), calls=%async_computation.13 | async-start | bytes 1966080 | tf_op jit(solution)/shard_map/all_gather | solution.py:51
  10.8 18.6 %copy-start.32 = (s32[1,1024]{1,0:T(1,128)S(1)}, s32[1,1024]{1,0:T(1,128)}, u32[]{:S(2)}) copy-start(s32[1,1024]{1,0:T(1,128)} %param.17) | copy-start | bytes 12292
  10.8 95.7 %all-gather.16.cloned.1.call-start = ((), (), s32[]{:S(2)}) async-start(), calls=%async_computation.12 | async-start | bytes 9437184 | tf_op jit(solution)/shard_map/all_gather | solution.py:43
  26.2 86.7 %copy-start.26 = (f32[256]{0:T(256)}, f32[256]{0:T(256)S(1)}, u32[]{:S(2)}) copy-start(f32[256]{0:T(256)S(1)} %add_rsqrt_fusion.1) | copy-start | bytes 3076
  26.2 86.7 %copy-start.21 = (f32[1,2048]{1,0:T(1,128)}, f32[1,2048]{1,0:T(1,128)S(1)}, u32[]{:S(2)}) copy-start(f32[1,2048]{1,0:T(1,128)S(1)} %get-tuple-element.266) | copy-start | bytes 24580
  26.2 697.8 %copy-start.17 = (f32[1,2048]{1,0:T(1,128)}, f32[1,2048]{1,0:T(1,128)S(1)}, u32[]{:S(2)}) copy-start(f32[1,2048]{1,0:T(1,128)S(1)} %get-tuple-element.265) | copy-start | bytes 24580
  27.6 109.1 %all-gather.20.cloned.1.call-start = ((), (), s32[]{:S(2)}) async-start(), calls=%async_computation.14 | async-start | bytes 1310720 | tf_op jit(solution)/shard_map/all_gather | solution.py:51
  29.3 154.8 %all-gather.40.cloned.1.call-start = ((), (), s32[]{:S(2)}) async-start(), calls=%async_computation.33 | async-start | bytes 2621440 | tf_op jit(solution)/shard_map/all_gather | solution.py:139
  29.4 111.5 %copy-start.30 = (f32[32]{0:T(128)}, f32[32]{0:T(128)S(1)}, u32[]{:S(2)}) copy-start(f32[32]{0:T(128)S(1)} %multiply_exponential_fusion) | copy-start | bytes 388
  41.5 99.4 %copy-start.19 = (f32[1,2,8,128]{3,1,2,0:T(2,128)}, f32[1,2,8,128]{3,1,2,0:T(2,128)S(1)}, u32[]{:S(2)}) copy-start(f32[1,2,8,128]{3,1,2,0:T(2,128)S(1)} %copy.123) | copy-start | bytes 24580
  136.6 19.1 %all-to-all-start = ((bf16[8,256,256]{2,1,0:T(8,128)(2,1)}), bf16[8,256,256]{2,1,0:T(8,128)(2,1)S(1)}, u32[]{:S(2)}, u32[]{:S(2)}) async-start(bf16[8,256,256]{2,1,0:T(8,128)(2,1)} %bitcast.343), calls=%async_computation | async-start | bytes 2097152 | tf_op jit(solution)/shard_map/all_to_all | solution.py:103
  140.3 183.7 %reduce-scatter.13.cloned.1.call-start = ((), (), s32[]{:S(2)}) async-start(), calls=%async_computation.15 | async-start | bytes 9437184 | tf_op jit(solution)/shard_map/reduce_scatter | solution.py:47
  142.7 16.4 %copy-start.14 = (f32[2048,32]{0,1:T(8,128)}, f32[2048,32]{0,1:T(8,128)S(1)}, u32[]{:S(2)}) copy-start(f32[2048,32]{0,1:T(8,128)S(1)} %get-tuple-element.264) | copy-start | bytes 786436
  156.7 2.5 slice-start
  245.8 2.2 copy-start.13
  248.0 5.8 copy-start.9
  253.9 178.9 %all-gather.24.cloned.1.call-start = ((), (), s32[]{:S(2)}) async-start(), calls=%async_computation.17 | async-start | bytes 7208960 | tf_op jit(solution)/shard_map/all_gather | solution.py:51
  259.2 228.9 %all-gather.22.cloned.1.call-start = ((), (), s32[]{:S(2)}) async-start(), calls=%async_computation.16 | async-start | bytes 9437184 | tf_op jit(solution)/shard_map/all_gather | solution.py:43
  325.7 398.4 %copy-start.24 = (f32[256]{0:T(256)}, f32[256]{0:T(256)S(1)}, u32[]{:S(2)}) copy-start(f32[256]{0:T(256)S(1)} %add_rsqrt_fusion) | copy-start | bytes 3076
  328.3 221.3 %all-gather.26.cloned.1.call-start = ((), (), s32[]{:S(2)}) async-start(), calls=%async_computation.18 | async-start | bytes 3604480 | tf_op jit(solution)/shard_map/all_gather | solution.py:51
  330.4 274.4 %all-gather.28.cloned.1.call-start = ((), (), s32[]{:S(2)}) async-start(), calls=%async_computation.20 | async-start | bytes 9437184 | tf_op jit(solution)/shard_map/all_gather | solution.py:43
  331.1 390.1 %reduce-scatter.17.cloned.1.call-start = ((), (), s32[]{:S(2)}) async-start(), calls=%async_computation.21 | async-start | bytes 9437184 | tf_op jit(solution)/shard_map/reduce_scatter | solution.py:47
  488.2 11.3 copy-start.33
  488.2 11.3 copy-start.34
  619.8 14.3 copy-start.37
  619.8 14.3 copy-start.36
  649.7 71.5 %copy-start.5 = (bf16[256,2048]{1,0:T(8,128)(2,1)S(1)}, bf16[256,2048]{1,0:T(8,128)(2,1)}, u32[]{:S(2)}) copy-start(bf16[256,2048]{1,0:T(8,128)(2,1)} %reduce-scatter.13.cloned.1.call-done) | copy-start | bytes 3145732
  649.8 74.3 %copy-start.6 = (bf16[256,2048]{1,0:T(8,128)(2,1)S(1)}, bf16[256,2048]{1,0:T(8,128)(2,1)}, u32[]{:S(2)}) copy-start(bf16[256,2048]{1,0:T(8,128)(2,1)} %param.27) | copy-start | bytes 3145732
  649.8 130.9 %all-gather.30.cloned.1.call-start = ((), (), s32[]{:S(2)}) async-start(), calls=%async_computation.22 | async-start | bytes 9437184 | tf_op jit(solution)/shard_map/all_gather | solution.py:43
  721.2 2.9 copy-start.7
  724.1 2.1 copy-start.28
  726.2 302.5 %reduce-scatter.19.cloned.1.call-start = ((), (), s32[]{:S(2)}) async-start(), calls=%async_computation.23 | async-start | bytes 2621440 | tf_op jit(solution)/shard_map/reduce_scatter | solution.py:55
  794.9 2.0 copy-start.2
  816.1 2.0 copy-start.2
  837.3 2.0 copy-start.2
  858.5 2.0 copy-start.2
  879.7 2.0 copy-start.2
  964.9 3.0 copy-start.39
  967.7 102.6 %reduce-scatter.29.cloned.1.call-start = ((), (), s32[]{:S(2)}) async-start(), calls=%async_computation.31 | async-start | bytes 3604480 | tf_op jit(solution)/shard_map/reduce_scatter | solution.py:55
  978.7 196.5 %reduce-scatter.27.cloned.1.call-start = ((), (), s32[]{:S(2)}) async-start(), calls=%async_computation.29 | async-start | bytes 7208960 | tf_op jit(solution)/shard_map/reduce_scatter | solution.py:55
  978.8 9.6 copy-start.38
  1008.4 5.5 copy-start.15
  1008.4 19.0 %all-to-all-start.1 = ((bf16[256,8,256]{2,0,1:T(8,128)(2,1)}), bf16[256,8,256]{2,0,1:T(8,128)(2,1)S(1)}, u32[]{:S(2)}, u32[]{:S(2)}) async-start(bf16[256,8,256]{2,0,1:T(8,128)(2,1)} %bitcast.251), calls=%async_computation.7 | async-start | bytes 2097152 | tf_op jit(solution)/shard_map/all_to_all | solution.py:194
  1012.1 193.6 %reduce-scatter.25.cloned.1.call-start = ((), (), s32[]{:S(2)}) async-start(), calls=%async_computation.27 | async-start | bytes 1310720 | tf_op jit(solution)/shard_map/reduce_scatter | solution.py:55
  1015.1 14.7 copy-start.20
  1015.1 14.7 copy-start.31
  1028.4 214.0 %reduce-scatter.23.cloned.1.call-start = ((), (), s32[]{:S(2)}) async-start(), calls=%async_computation.25 | async-start | bytes 1966080 | tf_op jit(solution)/shard_map/reduce_scatter | solution.py:55
  1040.2 246.3 %all-gather.38.cloned.1.call-start = ((), (), s32[]{:S(2)}) async-start(), calls=%async_computation.32 | async-start | bytes 6488064 | tf_op jit(solution)/shard_map/all_gather | solution.py:43
  1070.3 287.9 %all-gather.36.cloned.1.call-start = ((), (), s32[]{:S(2)}) async-start(), calls=%async_computation.30 | async-start | bytes 12976128 | tf_op jit(solution)/shard_map/all_gather | solution.py:43
  1175.2 273.1 %all-gather.34.cloned.1.call-start = ((), (), s32[]{:S(2)}) async-start(), calls=%async_computation.28 | async-start | bytes 2359296 | tf_op jit(solution)/shard_map/all_gather | solution.py:43
  1205.7 257.3 %all-gather.32.cloned.1.call-start = ((), (), s32[]{:S(2)}) async-start(), calls=%async_computation.26 | async-start | bytes 3538944 | tf_op jit(solution)/shard_map/all_gather | solution.py:43
  1242.4 254.4 %reduce-scatter.21.cloned.1.call-start = ((), (), s32[]{:S(2)}) async-start(), calls=%async_computation.24 | async-start | bytes 9437184 | tf_op jit(solution)/shard_map/reduce_scatter | solution.py:47
  1250.7 2.1 copy-start.35
  1250.7 321.2 %reduce-scatter.15.cloned.1.call-start = ((), (), s32[]{:S(2)}) async-start(), calls=%async_computation.19 | async-start | bytes 9437184 | tf_op jit(solution)/shard_map/reduce_scatter | solution.py:47
  1263.6 337.8 %reduce-scatter.31.cloned.1.call-start = ((), (), s32[]{:S(2)}) async-start(), calls=%async_computation.34 | async-start | bytes 1310720
  1469.7 27.1 %copy-start.4 = (bf16[256,2048]{1,0:T(8,128)(2,1)S(1)}, bf16[256,2048]{1,0:T(8,128)(2,1)}, u32[]{:S(2)}) copy-start(bf16[256,2048]{1,0:T(8,128)(2,1)} %param.16) | copy-start | bytes 3145732
  1469.8 27.1 %copy-start.22 = (f32[1,2048]{1,0:T(1,128)S(1)}, f32[1,2048]{1,0:T(1,128)}, u32[]{:S(2)}) copy-start(f32[1,2048]{1,0:T(1,128)} %copy-done.21) | copy-start | bytes 24580
  1469.8 27.1 %copy-start.27 = (f32[256]{0:T(256)S(1)}, f32[256]{0:T(256)}, u32[]{:S(2)}) copy-start(f32[256]{0:T(256)} %copy-done.26) | copy-start | bytes 3076
  1470.0 28.9 %copy-start.23 = (f32[2048]{0:T(1024)S(1)}, f32[2048]{0:T(1024)}, u32[]{:S(2)}) copy-start(f32[2048]{0:T(1024)} %get-tuple-element.191) | copy-start | bytes 24580
  1471.1 100.9 %copy-start.18 = (f32[1,2048]{1,0:T(1,128)S(1)}, f32[1,2048]{1,0:T(1,128)}, u32[]{:S(2)}) copy-start(f32[1,2048]{1,0:T(1,128)} %copy-done.17) | copy-start | bytes 24580
  1471.1 100.9 %copy-start.25 = (f32[256]{0:T(256)S(1)}, f32[256]{0:T(256)}, u32[]{:S(2)}) copy-start(f32[256]{0:T(256)} %copy-done.24) | copy-start | bytes 3076
  1471.1 100.9 %copy-start.29 = (f32[256]{0:T(256)S(1)}, f32[256]{0:T(256)}, u32[]{:S(2)}) copy-start(f32[256]{0:T(256)} %copy-done.28) | copy-start | bytes 3076
  1500.3 116.2 %copy-start.1 = (bf16[512,2048]{1,0:T(8,128)(2,1)S(1)}, bf16[512,2048]{1,0:T(8,128)(2,1)}, u32[]{:S(2)}) copy-start(bf16[512,2048]{1,0:T(8,128)(2,1)} %param.19) | copy-start | bytes 6291460
  (9 other events, 13.4 us)
Sparse Core Ops, SparseCore 0:
  10.9 39.8 all-gather.17
  53.2 53.2 all-gather.15
  108.7 27.9 all-gather.19
  138.6 45.4 all-gather.39
  254.0 69.9 reduce-scatter.12
  326.1 106.6 all-gather.23
  435.4 52.6 all-gather.21
  490.4 59.1 all-gather.25
  551.7 53.0 all-gather.27
  649.9 71.3 reduce-scatter.16
  726.3 54.3 all-gather.29
  967.8 43.8 reduce-scatter.18
  1014.7 55.4 reduce-scatter.28
  1073.1 102.1 reduce-scatter.26
  1178.0 27.6 reduce-scatter.24
  1208.4 33.9 reduce-scatter.22
  1244.2 42.2 all-gather.37
  1288.2 69.8 all-gather.35
  1360.0 27.8 all-gather.33
  1389.7 32.3 all-gather.31
  1425.5 71.2 reduce-scatter.20
  1500.7 71.2 reduce-scatter.14
  1574.3 27.1 reduce-scatter.30

commit v2 on v1

--- a/solution.py
+++ b/solution.py
@@ -1,8 +1,11 @@
+import functools
 import math
 
 import jax
 import jax.numpy as jnp
 from jax import lax
+from jax.experimental import pallas as pl
+from jax.experimental.pallas import tpu as pltpu
 from jax.sharding import PartitionSpec as P
 
 HEADS = 32
@@ -12,6 +15,9 @@
 NEGATIVE = -1e30
 R = "replica"
 F = "fsdp"
+MESH = pl.DeviceIdType.MESH
+DMA = pltpu.SemaphoreType.DMA
+ANY = pl.BlockSpec(memory_space=pl.ANY)
 
 
 def inverse_rms(values):
@@ -39,12 +45,188 @@
     return lax.dot_general(a, b, (((ca,), (cb,)), ((), ())), preferred_element_type=jnp.float32)
 
 
-def plane_gather(x):
-    return lax.all_gather(x, R, axis=0, tiled=True)
-
-
-def plane_scatter(x):
-    return lax.psum_scatter(x, R, scatter_dimension=0, tiled=True)
+def remote(src, dst, sems, index, device):
+    return pltpu.make_async_remote_copy(
+        src_ref=src,
+        dst_ref=dst,
+        send_sem=sems[0].at[index],
+        recv_sem=sems[1].at[index],
+        device_id={R: device},
+        device_id_type=MESH,
+    )
+
+
+def greet(*devices):
+    barrier = pltpu.get_barrier_semaphore()
+    for device in devices:
+        pl.semaphore_signal(barrier, inc=1, device_id={R: device}, device_id_type=MESH)
+    pl.semaphore_wait(barrier, len(devices))
+
+
+def gather_kernel(chunks, x, out, local_sem, to_x, at_x, to_y, at_y, to_far, at_far, to_sib, at_sib):
+    me = lax.axis_index(R)
+    sibling, beside_x, beside_y, across = me + 1 - 2 * lax.rem(me, 2), me ^ 2, me ^ 4, me ^ 6
+    size = x.shape[0] // chunks
+    half = chunks // 2
+    greet(sibling, beside_x, beside_y)
+    own = pltpu.make_async_copy(x, out.at[me], local_sem)
+    own.start()
+
+    def copy(owner, chunk, device, sems, index):
+        part = pl.ds(chunk * size, size)
+        src = x.at[part] if owner is me else out.at[owner, part]
+        return remote(src, out.at[owner, part], sems, index, device)
+
+    x_sems, y_sems, far_sems, sib_sems = (to_x, at_x), (to_y, at_y), (to_far, at_far), (to_sib, at_sib)
+    x_copies, y_copies, far_copies, sib_copies = [], [], [], []
+    for i in range(chunks):
+        j = (i + half) % chunks
+        x_copies.append(copy(me, i, beside_x, x_sems, i))
+        y_copies.append(copy(me, j, beside_y, y_sems, j))
+        x_copies[-1].start()
+        y_copies[-1].start()
+    for i in range(chunks):
+        sib_copies.append(copy(me, i, sibling, sib_sems, (0, i)))
+        sib_copies[-1].start()
+    for i in range(chunks):
+        j = (i + half) % chunks
+        x_copies[i].wait_recv()
+        if i < half:
+            far_copies.append((i, copy(beside_x, i, beside_y, far_sems, i)))
+            far_copies[-1][1].start()
+        sib_copies.append(copy(beside_x, i, sibling, sib_sems, (1, i)))
+        sib_copies[-1].start()
+        y_copies[i].wait_recv()
+        if j >= half:
+            far_copies.append((j, copy(beside_y, j, beside_x, far_sems, j)))
+            far_copies[-1][1].start()
+        sib_copies.append(copy(beside_y, j, sibling, sib_sems, (2, j)))
+        sib_copies[-1].start()
+    for i, far in far_copies:
+        far.wait_recv()
+        sib_copies.append(copy(across, i, sibling, sib_sems, (3, i)))
+        sib_copies[-1].start()
+    for sent in sib_copies:
+        sent.wait()
+    for sent in x_copies + y_copies + [far for _, far in far_copies]:
+        sent.wait_send()
+    own.wait()
+
+
+def scatter_kernel(
+    chunks, part, out, own, from_sib, give, got, give_far, got_far, total,
+    own_sem, out_sem, to_sib, at_sib, to_near, at_near, to_far, at_far,
+):
+    f32, bf16 = jnp.float32, jnp.bfloat16
+    me = lax.axis_index(R)
+    flip = 1 - 2 * lax.rem(me, 2)
+    sibling, beside_x, beside_y = me + flip, me ^ 2, me ^ 4
+    rows = out.shape[0]
+    size = rows // chunks
+    half = chunks // 2
+    owners = [me, beside_x, beside_y, me ^ 6]
+    order = [c for j in range(half) for c in (j, half + j)]
+
+    def rows_of(device, j):
+        return part.at[pl.ds(pl.multiple_of(device * rows + j * size, 16), size)]
+
+    def own_copy(d, j):
+        return pltpu.make_async_copy(rows_of(owners[d], j), own.at[d, j], own_sem.at[d, j])
+
+    def sib_copy(d, j):
+        return remote(rows_of(owners[d] + flip, j), from_sib.at[d, j], (to_sib, at_sib), (d, j), sibling)
+
+    def near_copy(j):
+        device = beside_x if j < half else beside_y
+        return remote(give.at[j], got.at[j], (to_near, at_near), j, device)
+
+    def far_copy(j):
+        device = beside_y if j < half else beside_x
+        return remote(give_far.at[j], got_far.at[j], (to_far, at_far), j, device)
+
+    def out_copy(j):
+        return pltpu.make_async_copy(total.at[j], out.at[pl.ds(j * size, size)], out_sem.at[j])
+
+    def summed(d, j):
+        own_copy(d, j).wait()
+        sib_copy(d, j).wait_recv()
+        return own[d, j].astype(f32) + from_sib[d, j].astype(f32)
+
+    for j in order:
+        for d in (1, 2, 3, 0):
+            own_copy(d, j).start()
+    greet(sibling, beside_x, beside_y)
+    for j in order:
+        for d in (1, 3, 2, 0) if j < half else (2, 3, 1, 0):
+            sib_copy(d, j).start()
+    for j in order:
+        give[j, 0] = summed(1 if j < half else 2, j).astype(bf16)
+        give[j, 1] = summed(3, j).astype(bf16)
+        near_copy(j).start()
+    for j in order:
+        passed = summed(2 if j < half else 1, j)
+        kept = summed(0, j)
+        near_copy(j).wait_recv()
+        give_far[j] = (passed + got[j, 1].astype(f32)).astype(bf16)
+        far_copy(j).start()
+        total[j] = kept + got[j, 0].astype(f32)
+    for j in order:
+        far_copy(j).wait_recv()
+        total[j] = total[j] + got_far[j].astype(f32)
+        out_copy(j).start()
+    for j in order:
+        out_copy(j).wait()
+        near_copy(j).wait_send()
+        far_copy(j).wait_send()
+        for d in range(4):
+            sib_copy(d, j).wait_send()
+
+
+def plane_gather(x, call, chunks=4):
+    width = lax.axis_size(R)
+    if width != 8:
+        return lax.all_gather(x, R, axis=0, tiled=True)
+    out = pl.pallas_call(
+        functools.partial(gather_kernel, chunks),
+        out_shape=jax.ShapeDtypeStruct((width,) + x.shape, x.dtype),
+        in_specs=[ANY],
+        out_specs=ANY,
+        scratch_shapes=[DMA] + [DMA((chunks,))] * 6 + [DMA((4, chunks))] * 2,
+        compiler_params=pltpu.CompilerParams(collective_id=call, has_side_effects=True),
+    )(x)
+    return out.reshape((width * x.shape[0],) + x.shape[1:])
+
+
+def plane_scatter(x, call, chunks=4):
+    width = lax.axis_size(R)
+    if width != 8:
+        return lax.psum_scatter(x, R, scatter_dimension=0, tiled=True).astype(jnp.float32)
+    rows, columns = x.shape[0] // width, x.shape[1]
+    size = rows // chunks
+    bf16 = jnp.bfloat16
+    return pl.pallas_call(
+        functools.partial(scatter_kernel, chunks),
+        out_shape=jax.ShapeDtypeStruct((rows, columns), jnp.float32),
+        in_specs=[ANY],
+        out_specs=ANY,
+        scratch_shapes=[
+            pltpu.VMEM((4, chunks, size, columns), bf16),
+            pltpu.VMEM((4, chunks, size, columns), bf16),
+            pltpu.VMEM((chunks, 2, size, columns), bf16),
+            pltpu.VMEM((chunks, 2, size, columns), bf16),
+            pltpu.VMEM((chunks, size, columns), bf16),
+            pltpu.VMEM((chunks, size, columns), bf16),
+            pltpu.VMEM((chunks, size, columns), jnp.float32),
+            DMA((4, chunks)),
+            DMA((chunks,)),
+            DMA((4, chunks)),
+            DMA((4, chunks)),
+        ]
+        + [DMA((chunks,))] * 4,
+        compiler_params=pltpu.CompilerParams(
+            collective_id=call, has_side_effects=True, vmem_limit_bytes=32 << 20
+        ),
+    )(x)
 
 
 def line_gather(x):
@@ -130,7 +312,7 @@
     tok_float = tokens.astype(f32)
     scale_in = inverse_rms(tok_float)
     normed_in = tok_float * scale_in
-    hidden_in = plane_gather((normed_in * gain_in).astype(bf16))
+    hidden_in = plane_gather((normed_in * gain_in).astype(bf16), 0)
     qkv = dot(hidden_in, w_qkv)
     query = rotate(qkv[:, :qw].reshape(all_tok, heads, HEAD_DIM), cosine, sine, 1.0).astype(bf16)
     key = rotate(qkv[:, None, qw : qw + HEAD_DIM], cosine, sine, 1.0).astype(bf16)[:, 0]
@@ -156,26 +338,26 @@
 
     mixed, log_totals = lax.map(one_forward, (query_rows, key_rows, value_rows, allowed))
     mixed = mixed.reshape(all_tok, qw).astype(bf16)
-    branch = plane_scatter(dot(mixed, w_out).astype(bf16)).astype(f32)
+    branch = plane_scatter(dot(mixed, w_out).astype(bf16), 1)
     middle = tok_float + branch
     scale_mid = inverse_rms(middle)
     normed_mid = middle * scale_mid
 
-    hidden_mid = plane_gather((normed_mid * gain_mid).astype(bf16))
-    cot_all = plane_gather(cotangent)
+    hidden_mid = plane_gather((normed_mid * gain_mid).astype(bf16), 2)
+    cot_all = plane_gather(cotangent, 3)
     gate_acc = dot(hidden_mid, w_gate)
     up_acc = dot(hidden_mid, w_up)
     gate_sig = jax.nn.sigmoid(gate_acc)
     gate_silu = gate_acc * gate_sig
     inner_act = (gate_silu * up_acc).astype(bf16)
-    feed_out = plane_scatter(dot(inner_act, w_down).astype(bf16)).astype(f32)
+    feed_out = plane_scatter(dot(inner_act, w_down).astype(bf16), 4)
     activations = (middle + feed_out).astype(bf16)
     grad_inner = dot(cot_all, w_down, 1, 1)
     grad_gate = (grad_inner * up_acc * gate_sig * (1.0 + gate_acc * (1.0 - gate_sig))).astype(bf16)
     grad_up = (grad_inner * gate_silu).astype(bf16)
     grad_hidden_mid = plane_scatter(
-        (dot(grad_gate, w_gate, 1, 1) + dot(grad_up, w_up, 1, 1)).astype(bf16)
-    ).astype(f32)
+        (dot(grad_gate, w_gate, 1, 1) + dot(grad_up, w_up, 1, 1)).astype(bf16), 5
+    )
     feed_rows = line_scatter(
         jnp.concatenate([dot(hidden_mid, grad_gate, 0, 0), dot(hidden_mid, grad_up, 0, 0)], axis=1)
         .astype(bf16)
@@ -187,7 +369,7 @@
         grad_normed_mid - normed_mid * jnp.mean(grad_normed_mid * normed_mid, axis=1, keepdims=True)
     )
 
-    grad_branch = plane_gather(grad_middle.astype(bf16))
+    grad_branch = plane_gather(grad_middle.astype(bf16), 6)
     grad_mixed = dot(grad_branch, w_out, 1, 1).astype(bf16)
     out_part = dot(mixed, grad_branch, 0, 0).astype(bf16)
     out_rows = line_scatter(
@@ -228,7 +410,7 @@
         ],
         axis=1,
     ).astype(bf16)
-    grad_hidden_in = plane_scatter(dot(grad_qkv, w_qkv, 1, 1).astype(bf16)).astype(f32)
+    grad_hidden_in = plane_scatter(dot(grad_qkv, w_qkv, 1, 1).astype(bf16), 7)
     qkv_rows = line_scatter(dot(hidden_in, grad_qkv, 0, 0).astype(bf16))
     gain_in_term = jnp.sum(grad_hidden_in * normed_in, axis=0)
     grad_normed_in = grad_hidden_in * gain_in
@@ -249,15 +431,15 @@
     )
     rows = model // planes
 
-    def spread(x):
-        x = plane_gather(x)
+    def spread(x, call):
+        x = plane_gather(x, call, 2)
         return x.reshape(width, x.shape[0] // width, x.shape[1])
 
-    down_grad = spread(down_rows).reshape(feed // planes, model).astype(f32)
-    feed_all = spread(feed_rows).reshape(width, rows, 2, planes, piece)
+    down_grad = spread(down_rows, 8).reshape(feed // planes, model).astype(f32)
+    feed_all = spread(feed_rows, 9).reshape(width, rows, 2, planes, piece)
     feed_all = feed_all.transpose(2, 1, 3, 0, 4).reshape(2, rows, feed).astype(f32)
-    out_grad = spread(out_rows).transpose(1, 0, 2).reshape(output_weight.shape).astype(f32)
-    qkv_all = spread(qkv_rows)
+    out_grad = spread(out_rows, 10).transpose(1, 0, 2).reshape(output_weight.shape).astype(f32)
+    qkv_all = spread(qkv_rows, 11)
     query_grad = qkv_all[..., :qw].transpose(1, 0, 2).reshape(query_weight.shape).astype(f32)
     kv_all = qkv_all[..., qw:].astype(f32).reshape(KV_HEADS, width // KV_HEADS, rows, 2, HEAD_DIM)
     kv_all = kv_all.sum(axis=1).transpose(2, 1, 0, 3).reshape(2, rows, KV_HEADS * HEAD_DIM)

time: 1630 us -> 1120 us (0.69)
  waiting for transfers between devices: 980 us -> 39.2 us
  Pallas kernels: 0 us -> 436 us
    pallas_call x0 -> x12, Pallas kernels: none -> 436 us  [the longest x8 271 us: plane_gather(): pl.pallas_call(functools.partial(gather_kernel, chunks), out_shape=jax.Sh...]
    all_gather x8 -> x0, waiting for transfers between devices: 306 us -> none  [plane_gather(): return lax.all_gather(x, R, axis=0, tiled=True)]
    reduce_scatter x4 -> x0, waiting for transfers between devices: 232 us -> none  [plane_scatter(): return lax.psum_scatter(x, R, scatter_dimension=0, tiled=True)]
    reduce_scatter x5, waiting for transfers between devices: 202 us -> 15.8 us  [line_scatter(): return lax.psum_scatter(x, F, scatter_dimension=0, tiled=True)]
    all_gather x4, waiting for transfers between devices: 171 us -> 0.05 us  [line_gather(): return lax.all_gather(x, F, axis=0, tiled=True)]
    unnamed x24 -> x12, waiting for transfers between devices: 25 us -> 0.18 us
    unnamed x96 -> x100, local copies, waits for them, and re-layouts: 77.9 us -> 53.9 us
    all_gather x1, waiting for transfers between devices: 22.2 us -> 0.01 us  [per_device(): lax.all_gather(jnp.concatenate([key, value], axis=1), F, axis=0, tiled=Fa...]
  transfers between devices with their start and end apart: 25 -> 13, of which waited for: 22 -> 3; matrix products, arithmetic and copies ran while one was open for 16% -> 23% of each run, Pallas kernels for 0% -> 27%
where the time goes in v2:
time: 1120 us; the launch traced here: 1110 us
  Pallas kernels  436 us (39%)
  matrix products  257 us (23%)
  local copies, waits for them, and re-layouts  246 us (22%)
  other arithmetic  72.8 us (6%)
  waiting for transfers between devices  39.2 us (4%)
  blocking collectives  36.3 us (3%)
  between operations  15.1 us (1%)
    pallas_call x8, Pallas kernels, plane_gather(): pl.pallas_call(functools.partial(gather_kernel, chunks), out_shape=jax.Sh...  271 us
    pallas_call x4, Pallas kernels, plane_scatter(): pl.pallas_call(functools.partial(scatter_kernel, chunks), out_shape=jax.S...  165 us
    dot_general x15, matrix products, dot(): lax.dot_general(a, b, (((ca,), (cb,)), ((), ())), preferred_element_type=...  140 us
    dynamic_update_slice x16, local copies, waits for them, and re-layouts, per_device(): lax.map(one_forward, (query_rows, key_rows, value_rows, allowed))  58 us
    unnamed x100, local copies, waits for them, and re-layouts  53.9 us
    slice x2, local copies, waits for them, and re-layouts, per_device(): feed_all[1]  26.4 us
    dot_general x8, matrix products, one_backward(): gv = jnp.einsum('hqk,qhd->kd', probs_low, g, preferred_element_type=f32)  23.5 us
  transfers between devices with their start and end apart: 13, of which 3 were waited for; matrix products, arithmetic and copies ran while one was open for 23% of the time, Pallas kernels for 27%

profile of v2, /device:TPU:0, one launch (start us, length us, event | category | flops | bytes accessed | tf_op | source)
XLA Modules:
  0.0 1112.2 jit_solution(6979267906060251470)
XLA Ops:
  12.7 13.7 %all_gather.24 = bf16[2,2048]{1,0:T(2,128)(2,1)S(1)} all-gather(bf16[2,512]{1,0:T(2,128)(2,1)S(1)} %pad_maximum_fusion.9), channel_id=1, replica_groups=mesh['replica'=8,'fsdp'=4] {'fsdp'}, dimensions={1}, use_global_device_ids=true | all-gather | bytes 10240 | tf_op jit(solution)/shard_map/all_gather | solution.py:295
  28.0 39.3 %shard_map.203 = bf16[8,256,2048]{2,1,0:T(8,128)(2,1)} custom-call(bf16[256,2048]{1,0:T(8,128)(2,1)} %fusion.74.x), custom_call_target="tpu_custom_call" | custom-call | tf_op jit(solution)/shard_map/pallas_call | solution.py:189
  67.4 9.1 all-gather.1
  79.5 6.4 fusion.111
  97.4 39.4 %shard_map.207 = bf16[8,256,2048]{2,1,0:T(8,128)(2,1)} custom-call(bf16[256,2048]{1,0:T(8,128)(2,1)} %x.3), custom_call_target="tpu_custom_call" | custom-call | tf_op jit(solution)/shard_map/pallas_call | solution.py:189
  136.8 3.9 compare_and_fusion
  140.7 4.5 all-to-all-start
  149.6 11.0 all-to-all-done
  167.3 3.2 reshape.389
  172.1 52.6 %while.24 = (s32[]{:T(128)}, bf16[8,256,4,64]{1,3,2,0:T(8,128)(2,1)}, f32[8,4,256,1]{2,1,3,0:T(4,128)S(1)}, bf16[8,1024,64]{1,2,0:T(8,128)(2,1)}, pred[8,256,102...) while((s32[]{:T(128)}, ...), condition=%wide.region_6.7_spmd, body=%wide.region_3.6_spmd.sunk | while | flops 282065920 | bytes 14583909 | solution.py:339
  230.3 40.2 %shard_map.204 = f32[256,2048]{1,0:T(8,128)S(1)} custom-call(bf16[2048,2048]{1,0:T(8,128)(2,1)S(1)} %convolution_convert_fusion.2.part), custom_call_target="tpu_custom_call" | custom-call | tf_op jit(solution)/shard_map/pallas_call | solution.py:207
  273.3 40.0 %shard_map.205 = bf16[8,256,2048]{2,1,0:T(8,128)(2,1)} custom-call(bf16[256,2048]{1,0:T(8,128)(2,1)} %multiply_convert_fusion.1.x), custom_call_target="tpu_custom_call" | custom-call | tf_op jit(solution)/shard_map/pallas_call | solution.py:189
  313.4 11.3 %fusion.72 = f32[2048,704]{0,1:T(8,128)} fusion(bf16[2048,2048]{1,0:T(8,128)(2,1)} %bitcast.321, bf16[2048,1408]{1,0:T(8,128)(2,1)} %all-gather.12.cloned.1.call-done), kind=kOutput, calls=%fused_computation.100 | convolution fusion | flops 5905580032 | bytes 17301504 | tf_op jit(solution)/shard_map/dot_general | solution.py:45
  324.7 9.7 fusion.68
  334.4 15.7 %fusion.61 = (bf16[2048,704]{0,1:T(8,128)(2,1)}, bf16[2048,704]{0,1:T(8,128)(2,1)S(1)}, bf16[2048,704]{0,1:T(8,128)(2,1)}) fusion(f32[2048,704]{0,1:T(8,128)} %fusion.72, f32[2048,704]{0,1:T(8,128)} %fusion.68, bf16[704,2048]{1,0:T(8,128)(2,1)} %all-gather.14.cloned.1.call-done, bf16[2048,2048]{1,0:T(8,128)(2,1)} %bitcast.319), kind=kOutput, calls=%fused_computation.78 | convolution fusion | flops 5927206912 | bytes 31457280 | tf_op jit(solution)/shard_map/dot_general | solution.py:45
  350.2 13.2 %fusion.70 = f32[2048,2048]{1,0:T(8,128)} fusion(bf16[2048,704]{0,1:T(8,128)(2,1)S(1)} %get-tuple-element.265, bf16[2048,1408]{1,0:T(8,128)(2,1)} %all-gather.12.cloned.1.call-done), kind=kOutput, calls=%fused_computation.98 | convolution fusion | flops 5905580032 | bytes 22806528 | tf_op jit(solution)/shard_map/dot_general | solution.py:45
  363.4 13.2 %add_convert_fusion.part = bf16[2048,2048]{1,0:T(8,128)(2,1)S(1)} fusion(f32[2048,2048]{1,0:T(8,128)} %fusion.70, bf16[2048,704]{0,1:T(8,128)(2,1)} %get-tuple-element.264, bf16[2048,1408]{1,0:T(8,128)(2,1)} %all-gather.12.cloned.1.call-done), kind=kOutput, calls=%fused_computation.66 | convolution fusion | flops 5913968640 | bytes 31195136 | tf_op jit(solution)/shard_map/dot_general | solution.py:45
  376.6 41.5 %shard_map.208 = f32[256,2048]{1,0:T(8,128)S(1)} custom-call(bf16[2048,2048]{1,0:T(8,128)(2,1)S(1)} %add_convert_fusion.part), custom_call_target="tpu_custom_call" | custom-call | tf_op jit(solution)/shard_map/pallas_call | solution.py:207
  421.7 39.1 %shard_map.209 = bf16[8,256,2048]{2,1,0:T(8,128)(2,1)} custom-call(bf16[256,2048]{1,0:T(8,128)(2,1)} %fusion.106.x), custom_call_target="tpu_custom_call" | custom-call | tf_op jit(solution)/shard_map/pallas_call | solution.py:189
  460.8 5.7 convolution_convert_fusion.8
  468.4 169.2 %while.25 = (s32[]{:T(128)}, f32[8,256,4,64]{1,0,3,2:T(8,128)}, bf16[8,1024,128]{1,2,0:T(8,128)(2,1)}, bf16[8,1024,64]{1,2,0:T(8,128)(2,1)}, pred[8,256,1024]{1,...) while((s32[]{:T(128)}, f32[8,256,4,64]{1,0,3,2:T(8,128)}, ...), condition=%wide.region_11.12_spmd, body=%wide.region_9.11_spmd.sunk | while | flops 682359808 | bytes 52058284 | solution.py:392
  477.3 7.0 dynamic_update_slice.25
  498.4 7.0 dynamic_update_slice.25
  519.6 7.0 dynamic_update_slice.25
  540.7 7.0 dynamic_update_slice.25
  561.9 7.0 dynamic_update_slice.25
  583.0 7.0 dynamic_update_slice.25
  604.2 7.0 dynamic_update_slice.25
  625.3 7.0 dynamic_update_slice.25
  637.7 3.7 reshape.397
  646.5 5.7 convolution_convert_fusion.7
  653.2 3.7 all-to-all-start.1
  660.1 12.2 %all-to-all-done.1 = bf16[256,8,256]{2,0,1:T(8,128)(2,1)S(1)} async-done(((bf16[256,8,256]{2,0,1:T(8,128)(2,1)}), bf16[256,8,256]{2,0,1:T(8,128)(2,1)S(1)}, u32[]{:S(2)}, u32[]{:S(2)}) %all-to-all-start.1) | async-done | bytes 1048608 | tf_op jit(solution)/shard_map/all_to_all | solution.py:376
  673.3 15.8 %reduce-scatter.9.cloned.1.call-done = bf16[2048,128]{0,1:T(8,128)(2,1)} async-done(((bf16[8192,128]{0,1:T(8,128)(2,1)}), bf16[2048,128]{0,1:T(8,128)(2,1)}) %reduce-scatter.9.cloned.1.call-update) | async-done | bytes 524304 | tf_op jit(solution)/shard_map/reduce_scatter | solution.py:237
  692.3 6.2 convolution_convert_fusion.part
  698.5 41.4 %shard_map.210 = f32[256,2048]{1,0:T(8,128)S(1)} custom-call(bf16[2048,2048]{1,0:T(8,128)(2,1)S(1)} %convolution_convert_fusion.part), custom_call_target="tpu_custom_call" | custom-call | tf_op jit(solution)/shard_map/pallas_call | solution.py:207
  742.0 10.6 convolution_convert_fusion.5
  752.9 9.5 convolution_convert_fusion.6
  762.5 10.5 convolution_convert_fusion.3
  773.0 4.6 copy.138
  777.6 10.5 convolution_convert_fusion.4
  788.1 4.6 copy.137
  792.7 7.2 pad_maximum_fusion
  799.9 9.3 convolution_convert_fusion.1.part
  809.2 41.7 %shard_map.206 = f32[256,2048]{1,0:T(8,128)S(1)} custom-call(bf16[2048,2048]{1,0:T(8,128)(2,1)S(1)} %convolution_convert_fusion.1.part), custom_call_target="tpu_custom_call" | custom-call | tf_op jit(solution)/shard_map/pallas_call | solution.py:207
  851.0 13.3 %shard_map.212 = bf16[8,512,256]{2,1,0:T(8,128)(2,1)} custom-call(bf16[512,256]{1,0:T(8,128)(2,1)} %reduce-scatter.13.cloned.1.call-done.x), custom_call_target="tpu_custom_call" | custom-call | tf_op jit(solution)/shard_map/pallas_call | solution.py:189
  864.3 4.0 convert_bitcast_fusion
  868.3 5.4 copy.136
  873.7 5.5 copy.145
  879.3 5.6 fusion.79
  885.9 13.6 %psum.7 = f32[2,512]{1,0:T(2,128)S(1)} all-reduce(f32[2,512]{1,0:T(2,128)S(1)} %copy.156), channel_id=1, replica_groups=mesh['replica'=8,'fsdp'=4] {'replica'}, use_global_device_ids=true, to_apply=%region_17.18 | all-reduce | flops 1024 | bytes 8192 | tf_op jit(solution)/shard_map/psum | solution.py:426
  900.1 28.8 %shard_map.214 = bf16[8,176,2048]{2,1,0:T(8,128)(2,1)} custom-call(bf16[176,2048]{1,0:T(8,128)(2,1)} %reduce-scatter.17.cloned.1.call-done.x), custom_call_target="tpu_custom_call" | custom-call | tf_op jit(solution)/shard_map/pallas_call | solution.py:189
  928.9 8.7 bitcast_convert_fusion
  937.6 17.9 %shard_map.211 = bf16[8,512,384]{2,1,0:T(8,128)(2,1)} custom-call(bf16[512,384]{1,0:T(8,128)(2,1)} %reduce-scatter.11.cloned.1.call-done.x), custom_call_target="tpu_custom_call" | custom-call | tf_op jit(solution)/shard_map/pallas_call | solution.py:189
  955.5 4.0 convert_bitcast_fusion.1
  959.5 5.5 copy.133
  965.0 5.3 copy.142
  974.2 53.1 %shard_map.213 = bf16[8,512,1408]{2,1,0:T(8,128)(2,1)} custom-call(bf16[512,1408]{1,0:T(8,128)(2,1)} %reduce-scatter.15.cloned.1.call-done.x), custom_call_target="tpu_custom_call" | custom-call | tf_op jit(solution)/shard_map/pallas_call | solution.py:189
  1027.4 17.0 %copy.139 = f32[8,512,1408]{1,2,0:T(8,128)} copy(bf16[8,512,1408]{2,1,0:T(8,128)(2,1)} %shard_map.213) | data formatting | bytes 34603008 | tf_op jit(solution)/shard_map/convert_element_type | solution.py:440
  1044.3 15.7 %fusion.107 = (f32[1,512,4,8,176]{1,4,2,0,3:T(8,128)}, f32[1,512,4,8,176]{1,4,2,0,3:T(8,128)}) fusion(f32[2,512,4,8,176]{1,4,2,0,3:T(8,128)} %bitcast.312), kind=kLoop, calls=%fused_computation.196 | loop fusion | bytes 46137344 | tf_op jit(solution)/shard_map/slice | solution.py:456
  1060.0 10.8 copy.140
  1070.8 11.9 %copy.146 = f32[512,5632]{1,0:T(8,128)} copy(f32[512,5632]{0,1:T(8,128)} %bitcast.313) | data formatting | bytes 23068672
  1082.7 10.8 copy.141
  1093.5 12.1 %copy.147 = f32[512,5632]{1,0:T(8,128)} copy(f32[512,5632]{0,1:T(8,128)} %bitcast.314) | data formatting | bytes 23068672
  (331 shorter events, 234.7 us)
Async XLA Ops:
  7.2 1.6 copy-start
  7.2 5.4 copy-start.38
  7.2 5.5 copy-start.39
  7.2 19.2 %copy-start.9 = (bf16[256,2048]{1,0:T(8,128)(2,1)S(1)}, bf16[256,2048]{1,0:T(8,128)(2,1)}, u32[]{:S(2)}) copy-start(bf16[256,2048]{1,0:T(8,128)(2,1)} %param.16) | copy-start | bytes 3145732
  7.2 72.3 %all-gather.8.cloned.1.call-start = ((), (), s32[]{:S(2)}) async-start(), calls=%async_computation.8 | async-start | bytes 1966080 | tf_op jit(solution)/shard_map/all_gather | solution.py:233
  10.8 129.9 %all-gather.10.cloned.1.call-start = ((), (), s32[]{:S(2)}) async-start(), calls=%async_computation.9 | async-start | bytes 1310720 | tf_op jit(solution)/shard_map/all_gather | solution.py:233
  12.6 150.4 %all-gather.16.cloned.1.call-start = ((), (), s32[]{:S(2)}) async-start(), calls=%async_computation.17 | async-start | bytes 2621440 | tf_op jit(solution)/shard_map/all_gather | solution.py:321
  12.6 133.0 %copy-start.35 = (f32[32]{0:T(128)}, f32[32]{0:T(128)S(1)}, u32[]{:S(2)}) copy-start(f32[32]{0:T(128)S(1)} %multiply_exponential_fusion) | copy-start | bytes 388
  26.4 40.9 %copy-start.27 = (f32[1,2048]{1,0:T(1,128)}, f32[1,2048]{1,0:T(1,128)S(1)}, u32[]{:S(2)}) copy-start(f32[1,2048]{1,0:T(1,128)S(1)} %get-tuple-element.295) | copy-start | bytes 24580
  26.4 392.3 %copy-start.23 = (f32[1,2048]{1,0:T(1,128)}, f32[1,2048]{1,0:T(1,128)S(1)}, u32[]{:S(2)}) copy-start(f32[1,2048]{1,0:T(1,128)S(1)} %get-tuple-element.294) | copy-start | bytes 24580
  26.7 40.6 %copy-start.31 = (f32[256]{0:T(256)}, f32[256]{0:T(256)S(1)}, u32[]{:S(2)}) copy-start(f32[256]{0:T(256)S(1)} %add_rsqrt_fusion.1) | copy-start | bytes 3076
  28.0 39.4 %copy-start.37 = (s32[1,1024]{1,0:T(1,128)S(1)}, s32[1,1024]{1,0:T(1,128)}, u32[]{:S(2)}) copy-start(s32[1,1024]{1,0:T(1,128)} %param.17) | copy-start | bytes 12292
  79.4 66.2 %copy-start.25 = (f32[1,2,8,128]{3,1,2,0:T(2,128)}, f32[1,2,8,128]{3,1,2,0:T(2,128)S(1)}, u32[]{:S(2)}) copy-start(f32[1,2,8,128]{3,1,2,0:T(2,128)S(1)} %copy.170) | copy-start | bytes 24580
  85.9 1.7 copy-start.13
  89.6 223.8 %all-gather.12.cloned.1.call-start = ((), (), s32[]{:S(2)}) async-start(), calls=%async_computation.10 | async-start | bytes 7208960 | tf_op jit(solution)/shard_map/all_gather | solution.py:233
  95.0 239.5 %all-gather.14.cloned.1.call-start = ((), (), s32[]{:S(2)}) async-start(), calls=%async_computation.11 | async-start | bytes 3604480 | tf_op jit(solution)/shard_map/all_gather | solution.py:233
  140.7 6.7 slice-start
  140.7 20.0 %all-to-all-start = ((bf16[8,256,256]{2,1,0:T(8,128)(2,1)}), bf16[8,256,256]{2,1,0:T(8,128)(2,1)}, u32[]{:S(2)}, u32[]{:S(2)}) async-start(bf16[8,256,256]{2,1,0:T(8,128)(2,1)} %bitcast.346), calls=%async_computation | async-start | bytes 2097152 | tf_op jit(solution)/shard_map/all_to_all | solution.py:285
  145.3 543.8 %reduce-scatter.9.cloned.1.call-start = ((), (), s32[]{:S(2)}) async-start(), calls=%async_computation.12 | async-start | bytes 2621440 | tf_op jit(solution)/shard_map/reduce_scatter | solution.py:237
  147.4 0.7 copy-start.19
  224.7 3.2 copy-start.17
  226.9 1.0 copy-start.14
  270.8 1.3 copy-start.7
  270.8 147.9 %copy-start.29 = (f32[256]{0:T(256)}, f32[256]{0:T(256)S(1)}, u32[]{:S(2)}) copy-start(f32[256]{0:T(256)S(1)} %add_rsqrt_fusion) | copy-start | bytes 3076
  313.4 11.3 %copy-start.12 = (bf16[8,256,2048]{2,1,0:T(8,128)(2,1)S(1)}, bf16[8,256,2048]{2,1,0:T(8,128)(2,1)}, u32[]{:S(2)}) copy-start(bf16[8,256,2048]{2,1,0:T(8,128)(2,1)} %shard_map.205) | copy-start | bytes 25165828
  313.4 11.3 %copy-start.40 = (bf16[2048,1408]{1,0:T(8,128)(2,1)S(1)}, bf16[2048,1408]{1,0:T(8,128)(2,1)}, u32[]{:S(2)}) copy-start(bf16[2048,1408]{1,0:T(8,128)(2,1)} %all-gather.12.cloned.1.call-done) | copy-start | bytes 17301508
  350.2 13.2 %copy-start.41 = (bf16[2048,704]{0,1:T(8,128)(2,1)}, bf16[2048,704]{0,1:T(8,128)(2,1)S(1)}, u32[]{:S(2)}) copy-start(bf16[2048,704]{0,1:T(8,128)(2,1)S(1)} %get-tuple-element.265) | copy-start | bytes 8650756
  376.6 41.5 %copy-start.8 = (f32[256,2048]{1,0:T(8,128)S(1)}, f32[256,2048]{1,0:T(8,128)}, u32[]{:S(2)}) copy-start(f32[256,2048]{1,0:T(8,128)} %copy-done.7) | copy-start | bytes 6291460
  418.1 1.4 copy-start.2
  418.1 2.0 copy-start.11
  420.1 1.6 copy-start.33
  421.7 39.1 %copy-start.18 = (bf16[256,8,256]{0,2,1:T(8,128)(2,1)S(1)}, bf16[256,8,256]{0,2,1:T(8,128)(2,1)}, u32[]{:S(2)}) copy-start(bf16[256,8,256]{0,2,1:T(8,128)(2,1)} %copy.127) | copy-start | bytes 3145732
  473.6 2.0 copy-start.6
  494.7 2.0 copy-start.6
  515.9 2.0 copy-start.6
  537.0 2.0 copy-start.6
  558.2 2.0 copy-start.6
  579.4 2.0 copy-start.6
  600.5 2.0 copy-start.6
  621.7 2.0 copy-start.6
  643.7 2.8 copy-start.15
  653.2 5.5 copy-start.20
  653.2 19.0 %all-to-all-start.1 = ((bf16[256,8,256]{2,0,1:T(8,128)(2,1)}), bf16[256,8,256]{2,0,1:T(8,128)(2,1)S(1)}, u32[]{:S(2)}, u32[]{:S(2)}) async-start(bf16[256,8,256]{2,0,1:T(8,128)(2,1)} %bitcast.253), calls=%async_computation.3 | async-start | bytes 2097152 | tf_op jit(solution)/shard_map/all_to_all | solution.py:376
  656.9 194.0 %reduce-scatter.13.cloned.1.call-start = ((), (), s32[]{:S(2)}) async-start(), calls=%async_computation.14 | async-start | bytes 1310720 | tf_op jit(solution)/shard_map/reduce_scatter | solution.py:237
  660.0 30.2 %copy-start.26 = (f32[1,2,8,128]{3,1,2,0:T(2,128)S(1)}, f32[1,2,8,128]{3,1,2,0:T(2,128)}, u32[]{:S(2)}) copy-start(f32[1,2,8,128]{3,1,2,0:T(2,128)} %copy-done.25) | copy-start | bytes 24580
  660.0 30.2 %copy-start.36 = (f32[32]{0:T(128)S(1)}, f32[32]{0:T(128)}, u32[]{:S(2)}) copy-start(f32[32]{0:T(128)} %copy-done.35) | copy-start | bytes 388
  660.1 31.5 %copy-start.21 = (bf16[2048,4,64]{0,2,1:T(8,128)(2,1)}, bf16[2048,4,64]{0,2,1:T(8,128)(2,1)S(1)}, u32[]{:S(2)}) copy-start(bf16[2048,4,64]{0,2,1:T(8,128)(2,1)S(1)} %pad_maximum_fusion.3) | copy-start | bytes 3145732
  672.3 1.0 copy-start.16
  673.3 211.6 %reduce-scatter.19.cloned.1.call-start = ((), (), s32[]{:S(2)}) async-start(), calls=%async_computation.18 | async-start | bytes 1310720
  691.6 0.7 copy-start.22
  698.5 41.4 %copy-start.10 = (bf16[256,2048]{1,0:T(8,128)(2,1)S(1)}, bf16[256,2048]{1,0:T(8,128)(2,1)}, u32[]{:S(2)}) copy-start(bf16[256,2048]{1,0:T(8,128)(2,1)} %param.16) | copy-start | bytes 3145732
  698.5 41.4 %copy-start.28 = (f32[1,2048]{1,0:T(1,128)S(1)}, f32[1,2048]{1,0:T(1,128)}, u32[]{:S(2)}) copy-start(f32[1,2048]{1,0:T(1,128)} %copy-done.27) | copy-start | bytes 24580
  698.5 41.4 %copy-start.32 = (f32[256]{0:T(256)S(1)}, f32[256]{0:T(256)}, u32[]{:S(2)}) copy-start(f32[256]{0:T(256)} %copy-done.31) | copy-start | bytes 3076
  739.9 12.7 %copy-start.4 = (f32[256,2048]{1,0:T(8,128)}, f32[256,2048]{1,0:T(8,128)S(1)}, u32[]{:S(2)}) copy-start(f32[256,2048]{1,0:T(8,128)S(1)} %shard_map.210) | copy-start | bytes 6291460
  742.0 158.1 %reduce-scatter.17.cloned.1.call-start = ((), (), s32[]{:S(2)}) async-start(), calls=%async_computation.16 | async-start | bytes 3604480 | tf_op jit(solution)/shard_map/reduce_scatter | solution.py:237
  752.6 185.0 %reduce-scatter.11.cloned.1.call-start = ((), (), s32[]{:S(2)}) async-start(), calls=%async_computation.13 | async-start | bytes 1966080 | tf_op jit(solution)/shard_map/reduce_scatter | solution.py:237
  762.4 211.8 %reduce-scatter.15.cloned.1.call-start = ((), (), s32[]{:S(2)}) async-start(), calls=%async_computation.15 | async-start | bytes 7208960 | tf_op jit(solution)/shard_map/reduce_scatter | solution.py:237
  850.9 17.4 %copy-start.5 = (f32[256,2048]{1,0:T(8,128)}, f32[256,2048]{1,0:T(8,128)S(1)}, u32[]{:S(2)}) copy-start(f32[256,2048]{1,0:T(8,128)S(1)} %shard_map.206) | copy-start | bytes 6291460
  873.7 5.5 copy-start.3
  873.7 5.5 copy-start.24
  873.7 5.5 copy-start.30
  873.7 5.5 copy-start.34
  1093.4 12.1 %copy-start.1 = (bf16[512,2048]{1,0:T(8,128)(2,1)S(1)}, bf16[512,2048]{1,0:T(8,128)(2,1)}, u32[]{:S(2)}) copy-start(bf16[512,2048]{1,0:T(8,128)(2,1)} %param.19) | copy-start | bytes 6291460
Sparse Core Ops, SparseCore 0:
  10.9 39.8 all-gather.7
  52.9 26.7 all-gather.9
  89.7 44.6 all-gather.15
  136.4 105.4 all-gather.11
  243.9 57.4 all-gather.13
  646.6 42.4 reduce-scatter.8
  692.0 26.4 reduce-scatter.12
  742.1 25.8 reduce-scatter.18
  770.4 54.8 reduce-scatter.16
  827.6 35.1 reduce-scatter.10
  865.7 101.2 reduce-scatter.14

commit v3 on v2

v3 whole, which is shorter than its diff:
```python
import functools
import math

import jax
import jax.numpy as jnp
from jax import lax
from jax.experimental import pallas as pl
from jax.experimental.pallas import tpu as pltpu
from jax.sharding import PartitionSpec as P

HEADS = 32
KV_HEADS = 4
HEAD_DIM = 64
EPSILON = 1e-05
NEGATIVE = -1e30
R = "replica"
F = "fsdp"
MESH = pl.DeviceIdType.MESH
DMA = pltpu.SemaphoreType.DMA
ANY = pl.BlockSpec(memory_space=pl.ANY)
KEY_BLOCK = 256
QUERY_BLOCK = 128
PARTS = 2


def inverse_rms(values):
    return lax.rsqrt(jnp.mean(values * values, axis=1, keepdims=True) + EPSILON)


def rope_tables(positions):
    half_dim = HEAD_DIM // 2
    freq_rates = jnp.exp(jnp.arange(half_dim, dtype=jnp.float32) * (-math.log(10000.0) / half_dim))
    angles = positions.astype(jnp.float32)[:, None] * freq_rates[None, :]
    return (jnp.cos(angles), jnp.sin(angles))


def rotate(tensor, cosine_table, sine_table, sign):
    half_dim = HEAD_DIM // 2
    low, up = tensor[..., :half_dim], tensor[..., half_dim:]
    cos_part = cosine_table[:, None, :]
    sin_part = sine_table[:, None, :] * sign
    return jnp.concatenate(
        [low * cos_part - up * sin_part, up * cos_part + low * sin_part], axis=-1
    )


def dot(a, b, ca=1, cb=0):
    return lax.dot_general(a, b, (((ca,), (cb,)), ((), ())), preferred_element_type=jnp.float32)


def remote(src, dst, sems, index, device):
    return pltpu.make_async_remote_copy(
        src_ref=src,
        dst_ref=dst,
        send_sem=sems[0].at[index],
        recv_sem=sems[1].at[index],
        device_id={R: device},
        device_id_type=MESH,
    )


def greet(*devices):
    barrier = pltpu.get_barrier_semaphore()
    for device in devices:
        pl.semaphore_signal(barrier, inc=1, device_id={R: device}, device_id_type=MESH)
    pl.semaphore_wait(barrier, len(devices))


class Gather:
    @staticmethod
    def scratch(count):
        return [DMA((count,))] * 6 + [DMA((4, count))] * 2

    def __init__(self, items, sems):
        self.items, self.count = items, len(items)
        self.half = self.count // 2
        self.me = lax.axis_index(R)
        self.sibling, self.x, self.y = self.me + 1 - 2 * lax.rem(self.me, 2), self.me ^ 2, self.me ^ 4
        self.across = self.me ^ 6
        self.sems = sems
        self.copies = {}

    def send(self, kind, i, owner, device):
        own, slot = self.items[i]
        sems = self.sems[2 * min(kind, 3) : 2 * min(kind, 3) + 2]
        index = i if kind < 3 else (kind - 3, i)
        src = own if owner is self.me else slot(owner)
        copy = remote(src, slot(owner), sems, index, device)
        copy.start()
        self.copies[kind, i] = copy

    def start(self):
        for i in range(self.count):
            self.send(0, i, self.me, self.x)
            j = (i + self.half) % self.count
            self.send(1, j, self.me, self.y)
        for i in range(self.count):
            self.send(3, i, self.me, self.sibling)

    def relay(self, i):
        j = (i + self.half) % self.count
        self.copies[0, i].wait_recv()
        if i < self.half:
            self.send(2, i, self.x, self.y)
        self.send(4, i, self.x, self.sibling)
        self.copies[1, j].wait_recv()
        if j >= self.half:
            self.send(2, j, self.y, self.x)
        self.send(5, j, self.y, self.sibling)

    def finish(self):
        for i in range(self.half):
            for j in (i, self.half + i):
                if j < self.count and (2, j) in self.copies and (6, j) not in self.copies:
                    self.copies[2, j].wait_recv()
                    self.send(6, j, self.across, self.sibling)
        for i in range(self.count):
            if (6, i) not in self.copies:
                self.copies[2, i].wait_recv()
                self.send(6, i, self.across, self.sibling)
        for (kind, _), copy in self.copies.items():
            if kind < 3:
                copy.wait_send()
            else:
                copy.wait()


def row_items(x, out, chunks):
    size = x.shape[0] // chunks

    def item(i):
        part = pl.ds(i * size, size)
        return x.at[part], lambda owner: out.at[owner, part]

    return [item(i) for i in range(chunks)]


def gather_kernel(chunks, x, out, local_sem, *sems):
    gather = Gather(row_items(x, out, chunks), sems)
    greet(gather.sibling, gather.x, gather.y)
    own = pltpu.make_async_copy(x, out.at[gather.me], local_sem)
    own.start()
    gather.start()
    for i in range(chunks):
        gather.relay(i)
    gather.finish()
    own.wait()


def enter_kernel(chunks, tokens, gains, ids, hidden, all_gains, all_ids, own, own_sem, to_z, at_z, *sems):
    f32 = jnp.float32
    planes = all_gains.shape[0]
    z = lax.axis_index(F)
    items = row_items(own, hidden, chunks) + [(ids, lambda owner: all_ids.at[owner])]
    gather = Gather(items, sems)
    others = [lax.rem(z + i, planes) for i in range(1, planes)]
    barrier = pltpu.get_barrier_semaphore()
    for other in others:
        pl.semaphore_signal(barrier, inc=1, device_id={F: other}, device_id_type=MESH)
    for device in (gather.sibling, gather.x, gather.y):
        pl.semaphore_signal(barrier, inc=1, device_id={R: device}, device_id_type=MESH)
    pl.semaphore_wait(barrier, planes + 2)
    copies = [
        pltpu.make_async_remote_copy(
            src_ref=gains,
            dst_ref=all_gains.at[z],
            send_sem=to_z.at[i],
            recv_sem=at_z.at[i],
            device_id={F: other},
            device_id_type=MESH,
        )
        for i, other in enumerate(others)
    ]
    for copy in copies:
        copy.start()
    all_gains[z] = gains[...]
    all_ids[gather.me] = ids[...]
    size = tokens.shape[0] // chunks
    scales = [
        inverse_rms(tokens[i * size : (i + 1) * size, :].astype(f32)) for i in range(chunks)
    ]
    for copy in copies:
        copy.wait()
    gain = jnp.concatenate([all_gains[p, 0:1] for p in range(planes)], axis=1)
    for i in range(chunks):
        part = slice(i * size, (i + 1) * size)
        own[part, :] = (tokens[part, :].astype(f32) * scales[i] * gain).astype(jnp.bfloat16)
    kept = pltpu.make_async_copy(own, hidden.at[gather.me], own_sem)
    kept.start()
    gather.start()
    for i in range(gather.count):
        gather.relay(i)
    gather.finish()
    kept.wait()


def turn(x, cosine, sine):
    half_dim = HEAD_DIM // 2
    low = lax.rem(lax.broadcasted_iota(jnp.int32, x.shape, 1), HEAD_DIM) < half_dim
    swapped = jnp.where(low, pltpu.roll(x, 2 * HEAD_DIM - half_dim, 1), pltpu.roll(x, half_dim, 1))
    return x * cosine + swapped * sine


def turn_keys(x, cosine, sine):
    is_key = lax.broadcasted_iota(jnp.int32, x.shape, 1) < HEAD_DIM
    return jnp.where(is_key, turn(x, cosine, sine), x)


def along_line(src, dst, sems, index, plane):
    return pltpu.make_async_remote_copy(
        src_ref=src,
        dst_ref=dst,
        send_sem=sems[0].at[index],
        recv_sem=sems[1].at[index],
        device_id={F: plane},
        device_id_type=MESH,
    )


def project_kernel(
    chunks, hidden, weight, cosine, sine, cotangent, query, kv, cot_all,
    own, own_sem, cot_sem, to_line, at_line, to_sib, at_sib, *sems,
):
    bf16 = jnp.bfloat16
    planes = kv.shape[1]
    z = lax.axis_index(F)
    tok = cotangent.shape[0]
    width = kv.shape[0]
    count = width // 2
    gather = Gather(row_items(cotangent, cot_all, chunks), sems)
    core = lax.rem(gather.me, 2)
    mine = pl.ds(core * count, count)
    above, below = lax.rem(z + 1, planes), lax.rem(z + planes - 1, planes)
    barrier = pltpu.get_barrier_semaphore()
    for other in (above, below):
        pl.semaphore_signal(barrier, inc=1, device_id={F: other}, device_id_type=MESH)
    for device in (gather.sibling, gather.x, gather.y):
        pl.semaphore_signal(barrier, inc=1, device_id={R: device}, device_id_type=MESH)
    pl.semaphore_wait(barrier, 5)
    kept_cot = pltpu.make_async_copy(cotangent, cot_all.at[gather.me], cot_sem)
    kept_cot.start()
    gather.start()

    def tile(i, carry):
        s = lax.rem(core * count + i, width)
        rows = pl.ds(pl.multiple_of(s * tok, tok), tok)
        acc = dot(hidden[rows, :], weight[...])
        c, n = cosine[rows, :], sine[rows, :]
        columns = acc.shape[1] - 2 * HEAD_DIM
        for first in range(0, columns, 2 * HEAD_DIM):
            part = slice(first, first + 2 * HEAD_DIM)
            query[rows, part] = turn(acc[:, part], c, n).astype(bf16)
        own[s] = turn_keys(acc[:, columns:], c, n).astype(bf16)
        return carry

    def up(step):
        slot = z - step
        src = own.at[mine] if step == 0 else kv.at[mine, slot]
        return along_line(src, kv.at[mine, slot], (to_line, at_line), step, above)

    def came(step):
        slot = z - step
        return along_line(kv.at[mine, slot], kv.at[mine, slot], (to_line, at_line), step - 1, above)

    def across(step):
        slot = z - step
        return remote(kv.at[mine, slot], kv.at[mine, slot], (to_sib, at_sib), step, gather.sibling)

    lax.fori_loop(0, count, tile, 0)

    @pl.when(z < planes - 1)
    def _():
        up(0).start()

    lax.fori_loop(count, width, tile, 0)
    kept = pltpu.make_async_copy(own, kv.at[:, z], own_sem)
    kept.start()
    done = 0
    for step in range(1, planes):

        @pl.when(z >= step)
        def _():
            came(step).wait_recv()

            @pl.when(z < planes - 1)
            def _():
                up(step).start()

            across(step).start()

        while done < chunks * step // planes:
            gather.relay(done)
            done += 1
    for i in range(done, chunks):
        gather.relay(i)
    gather.finish()
    for step in range(planes):

        @pl.when((z >= step) & (z < planes - 1))
        def _():
            up(step).wait_send()

        if step:

            @pl.when(z >= step)
            def _():
                across(step).wait()

    kept.wait()
    kept_cot.wait()


def return_kernel(
    grad_kv, grad_q, cosine, sine, grad_qkv,
    own, from_sib, inbox, outbox, own_sem, to_sib, at_sib, to_line, at_line,
):
    f32, bf16 = jnp.float32, jnp.bfloat16
    planes, count, tok = inbox.shape[0], inbox.shape[1], inbox.shape[2]
    z, me = lax.axis_index(F), lax.axis_index(R)
    core = lax.rem(me, 2)
    sibling = me + 1 - 2 * core
    above, below = lax.rem(z + 1, planes), lax.rem(z + planes - 1, planes)
    columns = grad_q.shape[1]
    barrier = pltpu.get_barrier_semaphore()
    for other in (above, below):
        pl.semaphore_signal(barrier, inc=1, device_id={F: other}, device_id_type=MESH)
    pl.semaphore_signal(barrier, inc=1, device_id={R: sibling}, device_id_type=MESH)

    def block(half, b):
        return grad_kv.at[pl.ds(half * count, count), pl.ds(b * tok, tok)]

    def load(b):
        return pltpu.make_async_copy(block(core, b), own.at[b], own_sem.at[b])

    def trade(b):
        return remote(block(1 - core, b), from_sib.at[b], (to_sib, at_sib), b, sibling)

    def down(b):
        return along_line(outbox.at[b], inbox.at[b], (to_line, at_line), b, below)

    for b in range(planes):

        @pl.when(b <= z)
        def _():
            load(b).start()

    pl.semaphore_wait(barrier, 3)
    for b in range(planes):

        @pl.when(b <= z)
        def _():
            trade(b).start()

    def queries(s, carry):
        rows = pl.ds(pl.multiple_of(s * tok, tok), tok)
        c, n = cosine[rows, :], -sine[rows, :]
        for first in range(0, columns, 2 * HEAD_DIM):
            part = slice(first, first + 2 * HEAD_DIM)
            grad_qkv[rows, part] = turn(grad_q[rows, part], c, n).astype(bf16)
        grad_qkv[rows, columns:] = jnp.zeros((tok, 2 * HEAD_DIM), bf16)
        return carry

    for b in range(planes):

        @pl.when(b <= z)
        def _():
            load(b).wait()
            trade(b).wait_recv()

            @pl.when(z < planes - 1)
            def _():
                down(b).wait_recv()

        @pl.when((b < z) & (z < planes - 1))
        def _():
            outbox[b] = (
                own[b].astype(f32) + from_sib[b].astype(f32) + inbox[b].astype(f32)
            ).astype(bf16)

        @pl.when((b < z) & (z == planes - 1))
        def _():
            outbox[b] = (own[b].astype(f32) + from_sib[b].astype(f32)).astype(bf16)

        @pl.when(b < z)
        def _():
            down(b).start()

        if b == 0:
            lax.fori_loop(0, 2 * count, queries, 0)

    def keys(i, carry):
        s = core * count + i
        rows = pl.ds(pl.multiple_of(s * tok, tok), tok)
        total = own[z, i].astype(f32) + from_sib[z, i].astype(f32)
        total = total + jnp.where(z < planes - 1, inbox[z, i].astype(f32), 0.0)
        grad_qkv[rows, columns:] = turn_keys(total, cosine[rows, :], -sine[rows, :]).astype(bf16)
        return carry

    lax.fori_loop(0, count, keys, 0)
    for b in range(planes):

        @pl.when(b <= z)
        def _():
            trade(b).wait_send()

        @pl.when(b < z)
        def _():
            down(b).wait_send()


class Scatter:
    @staticmethod
    def scratch(rows, columns, chunks):
        bf16, size = jnp.bfloat16, rows // chunks
        return [
            pltpu.VMEM((5, rows, columns), bf16),
            pltpu.VMEM((4, rows, columns), bf16),
            pltpu.VMEM((chunks, 2, size, columns), bf16),
            pltpu.VMEM((chunks, size, columns), bf16),
            pltpu.VMEM((chunks, size, columns), jnp.float32),
            DMA((4,)),
            DMA((4,)),
            DMA((chunks, 2)),
            DMA((chunks, 2)),
            DMA((chunks,)),
            DMA((chunks,)),
            DMA((chunks,)),
        ]

    def __init__(self, out, chunks, refs):
        self.out, self.chunks, self.half = out, chunks, chunks // 2
        self.own, self.sib, self.got, self.got_far, self.total = refs[:5]
        self.sib_sems, self.near_sems, self.far_sems = refs[5:7], refs[7:9], refs[9:11]
        self.out_sem = refs[11]
        self.me = lax.axis_index(R)
        self.sibling, self.x, self.y = self.me + 1 - 2 * lax.rem(self.me, 2), self.me ^ 2, self.me ^ 4
        self.size = out.shape[0] // chunks

    def owner(self, i):
        return (self.me ^ (6 - 2 * (i // 2))) ^ (1 - lax.rem(i, 2))

    def trade(self, d):
        return remote(self.own.at[4], self.sib.at[d], self.sib_sems, d, self.sibling)

    def put(self, i, value):
        d = 3 - i // 2
        for_sibling = lax.rem(i, 2) == 0

        @pl.when(for_sibling & (i >= 2))
        def _():
            self.trade(d + 1).wait_send()

        self.own[jnp.where(for_sibling, 4, d)] = value

        @pl.when(for_sibling)
        def _():
            self.trade(d).start()

    def arrived(self, d):
        self.trade(d).wait_recv()

    def part(self, j):
        return pl.ds(j * self.size, self.size)

    def summed(self, d, j):
        part = self.part(j)
        return self.own[d, part].astype(jnp.float32) + self.sib[d, part].astype(jnp.float32)

    def near_copies(self, j):
        device, d = (self.x, 1) if j < self.half else (self.y, 2)
        return [
            remote(self.own.at[e, self.part(j)], self.got.at[j, n], self.near_sems, (j, n), device)
            for n, e in enumerate((d, 3))
        ]

    def far_copy(self, j):
        device, d = (self.y, 2) if j < self.half else (self.x, 1)
        return remote(self.own.at[d, self.part(j)], self.got_far.at[j], self.far_sems, j, device)

    def out_copy(self, j):
        return pltpu.make_async_copy(self.total.at[j], self.out.at[self.part(j)], self.out_sem.at[j])

    def near(self, j):
        for e in (1 if j < self.half else 2, 3):
            self.own[e, self.part(j)] = self.summed(e, j).astype(jnp.bfloat16)
        for copy in self.near_copies(j):
            copy.start()

    def far(self, j):
        for copy in self.near_copies(j):
            copy.wait_recv()
        d = 2 if j < self.half else 1
        passed = self.summed(d, j) + self.got[j, 1].astype(jnp.float32)
        self.own[d, self.part(j)] = passed.astype(jnp.bfloat16)
        self.far_copy(j).start()
        self.total[j] = self.summed(0, j) + self.got[j, 0].astype(jnp.float32)

    def last(self, j):
        self.far_copy(j).wait_recv()
        self.total[j] = self.total[j] + self.got_far[j].astype(jnp.float32)
        self.out_copy(j).start()

    def finish(self):
        self.trade(0).wait_send()
        for j in range(self.chunks):
            self.out_copy(j).wait()
            self.far_copy(j).wait_send()
            for copy in self.near_copies(j):
                copy.wait_send()


def feed_kernel(
    chunks, hidden, cotangent, w_feed, w_down, out_part, grad_hidden, feed_part, down_part,
    hidden_in, cot_in, grads, inner_turned, out_stage, column_in, feed_stage, down_stage,
    in_sems, out_sem, column_sems, feed_sem, down_sem, *refs,
):
    f32, bf16 = jnp.float32, jnp.bfloat16
    width, tok, model = hidden.shape
    units = w_down.shape[0]
    scatter = Scatter(grad_hidden, chunks, refs)
    half = chunks // 2

    def loads(i):
        slot, owner = lax.rem(i, 2), scatter.owner(i)
        return [
            pltpu.make_async_copy(hidden.at[owner], hidden_in.at[slot], in_sems.at[0, slot]),
            pltpu.make_async_copy(cotangent.at[owner], cot_in.at[slot], in_sems.at[1, slot]),
        ]

    def out_copy(i):
        return pltpu.make_async_copy(out_stage, out_part.at[scatter.owner(i)], out_sem)

    for i in (0, 1):
        for copy in loads(i):
            copy.start()
    greet(scatter.sibling, scatter.x, scatter.y)

    def block(i, carry):
        slot = lax.rem(i, 2)
        rows = pl.ds(pl.multiple_of(i * tok, tok), tok)
        for copy in loads(i):
            copy.wait()
        acc = dot(hidden_in[slot], w_feed[...])
        gate, up = acc[:, :units], acc[:, units:]
        gate_sig = 1.0 / (1.0 + jnp.exp(-gate))
        gate_silu = gate * gate_sig
        inner = (gate_silu * up).astype(bf16)
        inner_turned[i] = inner.T
        grad_inner = dot(cot_in[slot], w_down[...], 1, 1)
        grad_gate = grad_inner * up * gate_sig * (1.0 + gate * (1.0 - gate_sig))
        both = jnp.concatenate([grad_gate, grad_inner * gate_silu], axis=1).astype(bf16)
        grads[rows, :] = both
        scatter.put(i, dot(both, w_feed[...], 1, 1).astype(bf16))

        @pl.when(i >= 1)
        def _():
            out_copy(i - 1).wait()

        out_stage[...] = dot(inner, w_down[...]).astype(bf16)
        out_copy(i).start()

        @pl.when(i + 2 < width)
        def _():
            for copy in loads(i + 2):
                copy.start()

        @pl.when(i == 4)
        def _():
            scatter.arrived(3)
            scatter.arrived(2)
            for j in range(half, chunks):
                scatter.near(j)

        @pl.when(i == 6)
        def _():
            scatter.arrived(1)
            for j in range(half):
                scatter.near(j)

        return carry

    tiles = model // tok

    def column_loads(n, source, tile):
        slot = lax.rem(n, 2)
        part = pl.ds(pl.multiple_of(tile * tok, tok), tok)
        return [
            pltpu.make_async_copy(
                source.at[scatter.owner(i), :, part],
                column_in.at[slot, pl.ds(i * tok, tok)],
                column_sems.at[slot, i],
            )
            for i in range(width)
        ]

    def start_columns(n):
        @pl.when(n < tiles)
        def _():
            for copy in column_loads(n, hidden, n):
                copy.start()

        @pl.when((n >= tiles) & (n < 2 * tiles))
        def _():
            for copy in column_loads(n, cotangent, n - tiles):
                copy.start()

    def feed_copy(n):
        rows = pl.ds(pl.multiple_of(n * tok, tok), tok)
        slot = lax.rem(n, 2)
        return pltpu.make_async_copy(feed_stage.at[slot], feed_part.at[rows], feed_sem.at[slot])

    def down_copy(n):
        part = pl.ds(pl.multiple_of((n - tiles) * tok, tok), tok)
        slot = lax.rem(n, 2)
        return pltpu.make_async_copy(down_stage.at[slot], down_part.at[:, part], down_sem.at[slot])

    def feed_tile(n, carry):
        slot = lax.rem(n, 2)
        for copy in column_loads(n, hidden, n):
            copy.wait()

        @pl.when(n >= 2)
        def _():
            feed_copy(n - 2).wait()

        feed_stage[slot] = dot(column_in[slot], grads[...], 0, 0).astype(bf16)
        feed_copy(n).start()
        start_columns(n + 2)

        @pl.when(n == 1)
        def _():
            for j in range(half, chunks):
                scatter.far(j)

        @pl.when(n == 4)
        def _():
            for j in range(half):
                scatter.far(j)

        return carry

    def down_tile(n, carry):
        slot = lax.rem(n, 2)
        for copy in column_loads(n, cotangent, n - tiles):
            copy.wait()

        @pl.when(n >= tiles + 2)
        def _():
            down_copy(n - 2).wait()

        acc = dot(inner_turned[0], column_in[slot, :tok])
        for i in range(1, width):
            acc = acc + dot(inner_turned[i], column_in[slot, i * tok : (i + 1) * tok])
        down_stage[slot] = acc.astype(bf16)
        down_copy(n).start()
        start_columns(n + 2)
        return carry

    for n in (0, 1):
        for copy in column_loads(n, hidden, n):
            copy.start()
    lax.fori_loop(0, width, block, 0)
    scatter.arrived(0)
    lax.fori_loop(0, tiles, feed_tile, 0)
    for j in range(half, chunks):
        scatter.last(j)
    lax.fori_loop(tiles, 2 * tiles, down_tile, 0)
    for j in range(half):
        scatter.last(j)
    scatter.finish()
    out_copy(width - 1).wait()
    for n in (tiles - 2, tiles - 1):
        feed_copy(n).wait()
        down_copy(n + tiles).wait()


def feed_forward(hidden, cotangent, w_feed, w_down, call, chunks=4):
    width, tok, model = hidden.shape
    units = w_down.shape[0]
    bf16 = jnp.bfloat16
    vmem = pl.BlockSpec(memory_space=pltpu.VMEM)
    return pl.pallas_call(
        functools.partial(feed_kernel, chunks),
        out_shape=[
            jax.ShapeDtypeStruct((width, tok, model), bf16),
            jax.ShapeDtypeStruct((tok, model), jnp.float32),
            jax.ShapeDtypeStruct((model, 2 * units), bf16),
            jax.ShapeDtypeStruct((units, model), bf16),
        ],
        in_specs=[ANY, ANY, vmem, vmem],
        out_specs=[ANY] * 4,
        scratch_shapes=[
            pltpu.VMEM((2, tok, model), bf16),
            pltpu.VMEM((2, tok, model), bf16),
            pltpu.VMEM((width * tok, 2 * units), bf16),
            pltpu.VMEM((width, units, tok), bf16),
            pltpu.VMEM((tok, model), bf16),
            pltpu.VMEM((2, width * tok, tok), bf16),
            pltpu.VMEM((2, tok, 2 * units), bf16),
            pltpu.VMEM((2, units, tok), bf16),
            DMA((2, 2)),
            DMA,
            DMA((2, width)),
            DMA((2,)),
            DMA((2,)),
        ]
        + Scatter.scratch(tok, model, chunks),
        compiler_params=pltpu.CompilerParams(
            collective_id=call, has_side_effects=True, vmem_limit_bytes=60 << 20
        ),
    )(hidden, cotangent, w_feed, w_down)


def enter(tokens, gains, ids, call, chunks=4):
    planes, rows = lax.axis_size(F), lax.axis_size(R)
    tok, model = tokens.shape
    vmem = pl.BlockSpec(memory_space=pltpu.VMEM)
    return pl.pallas_call(
        functools.partial(enter_kernel, chunks),
        out_shape=[
            jax.ShapeDtypeStruct((rows, tok, model), jnp.bfloat16),
            jax.ShapeDtypeStruct((planes,) + gains.shape, jnp.float32),
            jax.ShapeDtypeStruct((rows,) + ids.shape, jnp.int32),
        ],
        in_specs=[vmem] * 3,
        out_specs=[ANY, vmem, vmem],
        scratch_shapes=[pltpu.VMEM((tok, model), jnp.bfloat16), DMA]
        + [DMA((planes - 1,))] * 2
        + Gather.scratch(chunks + 1),
        compiler_params=pltpu.CompilerParams(
            collective_id=call, has_side_effects=True, vmem_limit_bytes=32 << 20
        ),
    )(tokens, gains, ids)


def project(hidden, weight, cosine, sine, cotangent, call, chunks=4):
    planes, width = lax.axis_size(F), lax.axis_size(R)
    tok, model = cotangent.shape
    bf16 = jnp.bfloat16
    vmem = pl.BlockSpec(memory_space=pltpu.VMEM)
    return pl.pallas_call(
        functools.partial(project_kernel, chunks),
        out_shape=[
            jax.ShapeDtypeStruct((width * tok, weight.shape[1] - 2 * HEAD_DIM), bf16),
            jax.ShapeDtypeStruct((width, planes, tok, 2 * HEAD_DIM), bf16),
            jax.ShapeDtypeStruct((width, tok, model), bf16),
        ],
        in_specs=[vmem] * 4 + [ANY],
        out_specs=[vmem, ANY, ANY],
        scratch_shapes=[pltpu.VMEM((width, tok, 2 * HEAD_DIM), bf16), DMA, DMA]
        + [DMA((planes,))] * 4
        + Gather.scratch(chunks),
        compiler_params=pltpu.CompilerParams(
            collective_id=call, has_side_effects=True, vmem_limit_bytes=40 << 20
        ),
    )(hidden, weight, cosine, sine, cotangent)


def return_keys(grad_kv, grad_q, cosine, sine, call):
    planes, width = lax.axis_size(F), lax.axis_size(R)
    bf16 = jnp.bfloat16
    tok = grad_kv.shape[1] // planes
    vmem = pl.BlockSpec(memory_space=pltpu.VMEM)
    blocks = pltpu.VMEM((planes, width // 2, tok, 2 * HEAD_DIM), bf16)
    return pl.pallas_call(
        return_kernel,
        out_shape=jax.ShapeDtypeStruct((grad_q.shape[0], grad_q.shape[1] + 2 * HEAD_DIM), bf16),
        in_specs=[ANY] + [vmem] * 3,
        out_specs=vmem,
        scratch_shapes=[blocks] * 4 + [DMA((planes,))] * 5,
        compiler_params=pltpu.CompilerParams(
            collective_id=call, has_side_effects=True, vmem_limit_bytes=40 << 20
        ),
    )(grad_kv, grad_q, cosine, sine)


def scatter_kernel(
    chunks, part, out, own, from_sib, give, got, give_far, got_far, total,
    own_sem, out_sem, to_sib, at_sib, to_near, at_near, to_far, at_far,
):
    f32, bf16 = jnp.float32, jnp.bfloat16
    me = lax.axis_index(R)
    flip = 1 - 2 * lax.rem(me, 2)
    sibling, beside_x, beside_y = me + flip, me ^ 2, me ^ 4
    rows = out.shape[0]
    size = rows // chunks
    half = chunks // 2
    owners = [me, beside_x, beside_y, me ^ 6]
    order = [c for j in range(half) for c in (j, half + j)]

    def rows_of(device, j):
        return part.at[pl.ds(pl.multiple_of(device * rows + j * size, 16), size)]

    def own_copy(d, j):
        return pltpu.make_async_copy(rows_of(owners[d], j), own.at[d, j], own_sem.at[d, j])

    def sib_copy(d, j):
        return remote(rows_of(owners[d] + flip, j), from_sib.at[d, j], (to_sib, at_sib), (d, j), sibling)

    def near_copy(j):
        device = beside_x if j < half else beside_y
        return remote(give.at[j], got.at[j], (to_near, at_near), j, device)

    def far_copy(j):
        device = beside_y if j < half else beside_x
        return remote(give_far.at[j], got_far.at[j], (to_far, at_far), j, device)

    def out_copy(j):
        return pltpu.make_async_copy(total.at[j], out.at[pl.ds(j * size, size)], out_sem.at[j])

    def summed(d, j):
        own_copy(d, j).wait()
        sib_copy(d, j).wait_recv()
        return own[d, j].astype(f32) + from_sib[d, j].astype(f32)

    for j in order:
        for d in (1, 2, 3, 0):
            own_copy(d, j).start()
    greet(sibling, beside_x, beside_y)
    for j in order:
        for d in (1, 3, 2, 0) if j < half else (2, 3, 1, 0):
            sib_copy(d, j).start()
    for j in order:
        give[j, 0] = summed(1 if j < half else 2, j).astype(bf16)
        give[j, 1] = summed(3, j).astype(bf16)
        near_copy(j).start()
    for j in order:
        passed = summed(2 if j < half else 1, j)
        kept = summed(0, j)
        near_copy(j).wait_recv()
        give_far[j] = (passed + got[j, 1].astype(f32)).astype(bf16)
        far_copy(j).start()
        total[j] = kept + got[j, 0].astype(f32)
    for j in order:
        far_copy(j).wait_recv()
        total[j] = total[j] + got_far[j].astype(f32)
        out_copy(j).start()
    for j in order:
        out_copy(j).wait()
        near_copy(j).wait_send()
        far_copy(j).wait_send()
        for d in range(4):
            sib_copy(d, j).wait_send()


def plane_gather(x, call, chunks=4):
    width = lax.axis_size(R)
    if width != 8:
        return lax.all_gather(x, R, axis=0, tiled=True)
    out = pl.pallas_call(
        functools.partial(gather_kernel, chunks),
        out_shape=jax.ShapeDtypeStruct((width,) + x.shape, x.dtype),
        in_specs=[ANY],
        out_specs=ANY,
        scratch_shapes=[DMA] + Gather.scratch(chunks),
        compiler_params=pltpu.CompilerParams(collective_id=call, has_side_effects=True),
    )(x)
    return out.reshape((width * x.shape[0],) + x.shape[1:])


def plane_scatter(x, call, chunks=4):
    width = lax.axis_size(R)
    if width != 8:
        return lax.psum_scatter(x, R, scatter_dimension=0, tiled=True).astype(jnp.float32)
    rows, columns = x.shape[0] // width, x.shape[1]
    size = rows // chunks
    bf16 = jnp.bfloat16
    return pl.pallas_call(
        functools.partial(scatter_kernel, chunks),
        out_shape=jax.ShapeDtypeStruct((rows, columns), jnp.float32),
        in_specs=[ANY],
        out_specs=ANY,
        scratch_shapes=[
            pltpu.VMEM((4, chunks, size, columns), bf16),
            pltpu.VMEM((4, chunks, size, columns), bf16),
            pltpu.VMEM((chunks, 2, size, columns), bf16),
            pltpu.VMEM((chunks, 2, size, columns), bf16),
            pltpu.VMEM((chunks, size, columns), bf16),
            pltpu.VMEM((chunks, size, columns), bf16),
            pltpu.VMEM((chunks, size, columns), jnp.float32),
            DMA((4, chunks)),
            DMA((chunks,)),
            DMA((4, chunks)),
            DMA((4, chunks)),
        ]
        + [DMA((chunks,))] * 4,
        compiler_params=pltpu.CompilerParams(
            collective_id=call, has_side_effects=True, vmem_limit_bytes=32 << 20
        ),
    )(x)


def line_gather(x):
    return lax.all_gather(x, F, axis=0, tiled=True)


def line_scatter(x):
    return lax.psum_scatter(x, F, scatter_dimension=0, tiled=True)


def heads_to_rows(block, heads):
    parts = [block[:, h * HEAD_DIM : (h + 1) * HEAD_DIM] for h in range(heads)]
    rows = jnp.concatenate(parts, axis=0)
    return jnp.concatenate([rows, jnp.zeros_like(rows)], axis=1)


def rows_to_heads(columns, heads):
    count = columns.shape[1] // heads
    return jnp.concatenate([columns[:, h * count : (h + 1) * count].T for h in range(heads)], axis=1)


def visible(block_index, starts, places):
    keys = block_index * KEY_BLOCK + lax.broadcasted_iota(jnp.int32, (KEY_BLOCK, starts.shape[1]), 0)
    return (keys >= starts) & (keys <= places)


def attention_kernel(heads, low, high, q, kv, starts, places, mixed, log_total):
    f32, bf16 = jnp.float32, jnp.bfloat16
    step = pl.program_id(0) * pl.num_programs(1) + pl.program_id(1)
    queries = heads_to_rows(q[...] * bf16(HEAD_DIM**-0.5), heads)
    first = jnp.concatenate([starts[0]] * heads, axis=1)
    place = jnp.concatenate([places[0]] * heads, axis=1)
    columns = queries.shape[0]

    def block(index, carry):
        top, total, acc = carry
        rows = kv[0, pl.ds(pl.multiple_of(index * KEY_BLOCK, KEY_BLOCK), KEY_BLOCK), :]
        scores = jnp.where(visible(index, first, place), dot(rows, queries, 1, 1), NEGATIVE)
        new_top = jnp.maximum(top, jnp.max(scores, axis=0, keepdims=True))
        weights = jnp.exp(scores - new_top)
        fade = jnp.exp(top - new_top)
        total = total * fade + jnp.sum(weights, axis=0, keepdims=True)
        acc = acc * fade + dot(rows, weights.astype(bf16), 0, 0)
        return new_top, total, acc

    top, total, acc = lax.fori_loop(
        low[step],
        high[step],
        block,
        (
            jnp.full((1, columns), NEGATIVE, f32),
            jnp.zeros((1, columns), f32),
            jnp.zeros((2 * HEAD_DIM, columns), f32),
        ),
    )
    mixed[...] = rows_to_heads(acc[HEAD_DIM:] / total, heads).astype(bf16)
    log_total[0] = top + jnp.log(total)


def attention_back_kernel(
    heads, low, high, q, kv, starts, places, grad, mixed, log_total, grad_q, grad_kv, sums
):
    f32, bf16 = jnp.float32, jnp.bfloat16
    step = pl.program_id(0) * pl.num_programs(1) + pl.program_id(1)
    queries = heads_to_rows(q[...] * bf16(HEAD_DIM**-0.5), heads)
    grads = heads_to_rows(grad[...], heads)
    first = jnp.concatenate([starts[0]] * heads, axis=1)
    place = jnp.concatenate([places[0]] * heads, axis=1)
    columns = queries.shape[0]
    products = grads.astype(f32) * heads_to_rows(mixed[...], heads).astype(f32)
    delta = lax.dot_general(
        jnp.ones((8, 2 * HEAD_DIM), f32),
        products,
        (((1,), (1,)), ((), ())),
        precision=lax.Precision.HIGHEST,
        preferred_element_type=f32,
    )[:1]
    level = log_total[0]
    upper = pltpu.roll(grads.astype(f32), HEAD_DIM, 1).astype(bf16)

    @pl.when(pl.program_id(1) == 0)
    def _():
        sums[...] = jnp.zeros_like(sums)

    def block(index, acc):
        part = pl.ds(pl.multiple_of(index * KEY_BLOCK, KEY_BLOCK), KEY_BLOCK)
        rows = kv[0, part, :]
        scores = dot(rows, queries, 1, 1)
        probs = jnp.where(visible(index, first, place), jnp.exp(scores - level), 0.0)
        grad_probs = dot(rows, upper, 1, 1)
        grad_scores = (probs * (grad_probs - delta)).astype(bf16)
        sums[part, :] += dot(grad_scores, queries) + dot(probs.astype(bf16), upper)
        return acc + dot(rows, grad_scores, 0, 0)

    acc = lax.fori_loop(low[step], high[step], block, jnp.zeros((2 * HEAD_DIM, columns), f32))
    grad_q[...] = rows_to_heads(acc[:HEAD_DIM] * HEAD_DIM**-0.5, heads)

    @pl.when(pl.program_id(1) == PARTS - 1)
    def _():
        grad_kv[0] = sums[...].astype(bf16)


def attention_call(kernel, heads, low, high, arrays, outs, scratch=()):
    blocks = {
        "tokens": lambda shape: pl.BlockSpec((QUERY_BLOCK, shape[1]), lambda s, b, *_: (s * PARTS + b, 0)),
        "row": lambda shape: pl.BlockSpec((1,) + shape[1:], lambda s, b, *_: (s * PARTS + b, 0, 0)),
        "sequence": lambda shape: pl.BlockSpec((1,) + shape[1:], lambda s, b, *_: (s, 0, 0)),
    }
    return pl.pallas_call(
        functools.partial(kernel, heads),
        grid_spec=pltpu.PrefetchScalarGridSpec(
            num_scalar_prefetch=2,
            grid=(low.shape[0] // PARTS, PARTS),
            in_specs=[blocks[kind](x.shape) for kind, x in arrays],
            out_specs=[blocks[kind](x.shape) for kind, x in outs],
            scratch_shapes=scratch,
        ),
        out_shape=[x for _, x in outs],
        compiler_params=pltpu.CompilerParams(vmem_limit_bytes=32 << 20),
    )(low, high, *[x for _, x in arrays])


def join_feed_kernel(planes, piece, x, gate, up):
    width = x.shape[0]
    for kind, out in enumerate((gate, up)):
        for p in range(planes):
            for r in range(width):
                first = (kind * planes + p) * piece
                to = (p * width + r) * piece
                out[:, to : to + piece] = x[r, :, first : first + piece].astype(jnp.float32)


def join_attention_kernel(sharers, qkv, o, query, key, value, out):
    f32 = jnp.float32
    width, qw, ow = qkv.shape[0], qkv.shape[2] - 2 * HEAD_DIM, o.shape[2]
    for r in range(width):
        query[:, r * qw : (r + 1) * qw] = qkv[r, :, :qw].astype(f32)
        out[:, r * ow : (r + 1) * ow] = o[r].astype(f32)
    for head in range(width // sharers):
        both = sum(qkv[head * sharers + i, :, qw:].astype(f32) for i in range(sharers))
        to = slice(head * HEAD_DIM, (head + 1) * HEAD_DIM)
        key[:, to] = both[:, :HEAD_DIM]
        value[:, to] = both[:, HEAD_DIM:]


def join_call(kernel, arrays, outs, block=64):
    rows = arrays[0].shape[1]
    return pl.pallas_call(
        kernel,
        grid=(rows // block,),
        in_specs=[pl.BlockSpec((x.shape[0], block, x.shape[2]), lambda i: (0, i, 0)) for x in arrays],
        out_specs=[pl.BlockSpec((block, columns), lambda i: (i, 0)) for columns in outs],
        out_shape=[jax.ShapeDtypeStruct((rows, columns), jnp.float32) for columns in outs],
        compiler_params=pltpu.CompilerParams(vmem_limit_bytes=32 << 20),
    )(*arrays)


def per_device(
    tokens,
    segment_ids,
    attention_gain,
    query_weight,
    key_weight,
    value_weight,
    output_weight,
    feed_gain,
    gate_weight,
    up_weight,
    down_weight,
    cotangent,
):
    f32, bf16 = jnp.float32, jnp.bfloat16
    planes, width = lax.axis_size(F), lax.axis_size(R)
    r, z = lax.axis_index(R), lax.axis_index(F)
    tok, model = tokens.shape
    length = segment_ids.shape[1]
    all_tok = width * tok
    plane_kernels = width == 8
    heads = HEADS // width
    group = HEADS // KV_HEADS
    qw = heads * HEAD_DIM
    kv = (r * heads) // group
    feed = gate_weight.shape[1]
    piece = feed // (width * planes)
    hidden_units = piece * planes

    def cols(weight, first, count):
        return lax.dynamic_slice_in_dim(weight, first, count, 1)

    def feed_cols(weight):
        return [cols(weight, p * (feed // planes) + r * piece, piece) for p in range(planes)]

    w_qkv = line_gather(
        jnp.concatenate(
            [
                cols(query_weight, r * qw, qw),
                cols(key_weight, kv * HEAD_DIM, HEAD_DIM),
                cols(value_weight, kv * HEAD_DIM, HEAD_DIM),
            ],
            axis=1,
        )
    )
    w_out = lax.all_to_all(
        line_gather(cols(output_weight, r * (model // width), model // width)),
        R,
        split_axis=0,
        concat_axis=1,
        tiled=True,
    )
    w_feed = line_gather(jnp.concatenate(feed_cols(gate_weight) + feed_cols(up_weight), axis=1))
    w_down = line_gather(lax.dynamic_slice_in_dim(down_weight, r * piece, piece, 0))
    own_gains = jnp.stack([attention_gain, feed_gain]).astype(f32)
    tok_float = tokens.astype(f32)
    scale_in = inverse_rms(tok_float)
    normed_in = tok_float * scale_in
    if plane_kernels:
        hidden_in, gains, ids = enter(
            tokens, jnp.pad(own_gains, ((0, 6), (0, 0))), segment_ids.reshape(8, length // 8), 0
        )
        hidden_in = hidden_in.reshape(all_tok, model)
        gains = gains[:, :2].transpose(1, 0, 2).reshape(2, model)
        ids = ids.reshape(width, length)
    else:
        gains = lax.all_gather(own_gains, F, axis=1, tiled=True)
        hidden_in = lax.all_gather((normed_in * gains[0]).astype(bf16), R, axis=0, tiled=True)
        ids = lax.all_gather(segment_ids, R, axis=0, tiled=True)
    gain_in, gain_mid = gains[0], gains[1]

    places = jnp.arange(length, dtype=jnp.int32)
    fresh = jnp.concatenate(
        [jnp.ones((width, 1), dtype=jnp.bool_), ids[:, 1:] != ids[:, :-1]], axis=1
    )
    positions = places[None] - lax.cummax(jnp.where(fresh, places[None], 0), axis=1)
    own_positions = lax.dynamic_slice_in_dim(positions, z * tok, tok, 1).reshape(all_tok)
    own_places = z * tok + jnp.arange(all_tok, dtype=jnp.int32) % tok
    own_starts = own_places - own_positions
    steps = all_tok // QUERY_BLOCK
    starts = own_starts.reshape(steps, 1, QUERY_BLOCK)
    query_places = own_places.reshape(steps, 1, QUERY_BLOCK)
    low = starts[:, 0, 0] // KEY_BLOCK
    high = query_places[:, 0, QUERY_BLOCK - 1] // KEY_BLOCK + 1
    cosine, sine = rope_tables(own_positions)

    if plane_kernels:
        wide_cosine = jnp.concatenate([cosine] * 4, axis=1)
        wide_sine = jnp.concatenate([-sine, sine] * 2, axis=1)
        query, kv_rows, cot_all = project(hidden_in, w_qkv, wide_cosine, wide_sine, cotangent, 3)
        kv_rows = kv_rows.reshape(width, length, 2 * HEAD_DIM)
        cot_all = cot_all.reshape(all_tok, model)
    else:
        qkv = dot(hidden_in, w_qkv)
        query = rotate(qkv[:, :qw].reshape(all_tok, heads, HEAD_DIM), cosine, sine, 1.0)
        query = query.astype(bf16).reshape(all_tok, qw)
        key = rotate(qkv[:, None, qw : qw + HEAD_DIM], cosine, sine, 1.0).astype(bf16)[:, 0]
        value = qkv[:, qw + HEAD_DIM :].astype(bf16)
        kv_rows = (
            lax.all_gather(jnp.concatenate([key, value], axis=1), F, axis=0, tiled=False)
            .reshape(planes, width, tok, 2 * HEAD_DIM)
            .transpose(1, 0, 2, 3)
            .reshape(width, length, 2 * HEAD_DIM)
        )
        cot_all = lax.all_gather(cotangent, R, axis=0, tiled=True)
    common = [("tokens", query), ("sequence", kv_rows), ("row", starts), ("row", query_places)]
    mixed, log_totals = attention_call(
        attention_kernel,
        heads,
        low,
        high,
        common,
        [
            ("tokens", jax.ShapeDtypeStruct((all_tok, qw), bf16)),
            ("row", jax.ShapeDtypeStruct((steps, 1, heads * QUERY_BLOCK), f32)),
        ],
    )
    branch = plane_scatter(dot(mixed, w_out).astype(bf16), 1)
    middle = tok_float + branch
    scale_mid = inverse_rms(middle)
    normed_mid = middle * scale_mid

    hidden_mid = plane_gather((normed_mid * gain_mid).astype(bf16), 2)
    if plane_kernels:
        out_part, grad_hidden_mid, feed_part, down_part = feed_forward(
            hidden_mid.reshape(width, tok, model),
            cot_all.reshape(width, tok, model),
            w_feed,
            w_down,
            5,
        )
        out_part = out_part.reshape(all_tok, model)
    else:
        w_gate, w_up = w_feed[:, :hidden_units], w_feed[:, hidden_units:]
        gate_acc = dot(hidden_mid, w_gate)
        up_acc = dot(hidden_mid, w_up)
        gate_sig = jax.nn.sigmoid(gate_acc)
        gate_silu = gate_acc * gate_sig
        inner_act = (gate_silu * up_acc).astype(bf16)
        out_part = dot(inner_act, w_down).astype(bf16)
        grad_inner = dot(cot_all, w_down, 1, 1)
        grad_gate = grad_inner * up_acc * gate_sig * (1.0 + gate_acc * (1.0 - gate_sig))
        grad_gate = grad_gate.astype(bf16)
        grad_up = (grad_inner * gate_silu).astype(bf16)
        feed_part = jnp.concatenate(
            [dot(hidden_mid, grad_gate, 0, 0), dot(hidden_mid, grad_up, 0, 0)], axis=1
        ).astype(bf16)
        down_part = dot(inner_act, cot_all, 0, 0).astype(bf16)
        grad_hidden_part = dot(grad_gate, w_gate, 1, 1) + dot(grad_up, w_up, 1, 1)
        grad_hidden_mid = plane_scatter(grad_hidden_part.astype(bf16), 5)
    feed_out = plane_scatter(out_part, 4)
    activations = (middle + feed_out).astype(bf16)
    feed_rows = line_scatter(feed_part)
    down_rows = line_scatter(down_part)
    gain_mid_term = jnp.sum(grad_hidden_mid * normed_mid, axis=0)
    grad_normed_mid = grad_hidden_mid * gain_mid
    grad_middle = cotangent.astype(f32) + scale_mid * (
        grad_normed_mid - normed_mid * jnp.mean(grad_normed_mid * normed_mid, axis=1, keepdims=True)
    )

    grad_branch = plane_gather(grad_middle.astype(bf16), 6)
    grad_mixed = dot(grad_branch, w_out, 1, 1).astype(bf16)
    out_part = dot(mixed, grad_branch, 0, 0).astype(bf16)
    out_rows = line_scatter(
        lax.all_to_all(out_part, R, split_axis=1, concat_axis=0, tiled=True)
    )

    grad_mixed, feed_rows = lax.optimization_barrier((grad_mixed, feed_rows))
    gq, gkv = attention_call(
        attention_back_kernel,
        heads,
        low,
        high,
        common + [("tokens", grad_mixed), ("tokens", mixed), ("row", log_totals)],
        [
            ("tokens", jax.ShapeDtypeStruct((all_tok, qw), f32)),
            ("sequence", jax.ShapeDtypeStruct((width, length, 2 * HEAD_DIM), bf16)),
        ],
        [pltpu.VMEM((length, 2 * HEAD_DIM), f32)],
    )
    if plane_kernels:
        grad_qkv = return_keys(gkv, gq, wide_cosine, wide_sine, 10)
    else:
        gkv = gkv.reshape(width, planes, tok, 2 * HEAD_DIM).transpose(1, 0, 2, 3)
        gkv = line_scatter(gkv.reshape(planes * all_tok, 2 * HEAD_DIM)).astype(f32)
        gq = rotate(gq.reshape(all_tok, heads, HEAD_DIM), cosine, sine, -1.0)
        gk = rotate(gkv[:, None, :HEAD_DIM], cosine, sine, -1.0)[:, 0]
        grad_qkv = jnp.concatenate([gq.reshape(all_tok, qw), gk, gkv[:, HEAD_DIM:]], axis=1)
        grad_qkv = grad_qkv.astype(bf16)
    hidden_part = dot(grad_qkv, w_qkv, 1, 1).astype(bf16)
    hidden_part, down_rows = lax.optimization_barrier((hidden_part, down_rows))
    grad_hidden_in = plane_scatter(hidden_part, 7)
    qkv_rows = line_scatter(dot(hidden_in, grad_qkv, 0, 0).astype(bf16))
    gain_in_term = jnp.sum(grad_hidden_in * normed_in, axis=0)
    grad_normed_in = grad_hidden_in * gain_in
    input_grad = (
        grad_middle
        + scale_in
        * (
            grad_normed_in
            - normed_in * jnp.mean(grad_normed_in * normed_in, axis=1, keepdims=True)
        )
    ).astype(bf16)

    gain_terms = lax.psum(
        lax.psum_scatter(
            jnp.stack([gain_in_term, gain_mid_term]), F, scatter_dimension=1, tiled=True
        ),
        R,
    )
    rows = model // planes

    def spread(x, call=None):
        x = lax.all_gather(x, R, axis=0, tiled=True) if call is None else plane_gather(x, call, 2)
        return x.reshape(width, x.shape[0] // width, x.shape[1])

    down_grad = spread(down_rows).reshape(feed // planes, model).astype(f32)
    gate_grad, up_grad = join_call(
        functools.partial(join_feed_kernel, planes, piece), [spread(feed_rows)], [feed, feed]
    )
    query_grad, key_grad, value_grad, out_grad = join_call(
        functools.partial(join_attention_kernel, width // KV_HEADS),
        [spread(qkv_rows, 9), spread(out_rows, 8)],
        [width * qw, KV_HEADS * HEAD_DIM, KV_HEADS * HEAD_DIM, model],
    )
    return (
        activations,
        input_grad,
        gain_terms[0],
        query_grad,
        key_grad,
        value_grad,
        out_grad,
        gain_terms[1],
        gate_grad,
        up_grad,
        down_grad,
    )


def solution(mesh):
    tok = P((R, F), None)
    row = P(F, None)
    in_specs = (tok, P(R, None), P(F), row, row, row, row, P(F), row, row, row, tok)
    out_specs = (tok, tok, P(F), row, row, row, row, P(F), row, row, row)
    return jax.shard_map(
        per_device, mesh=mesh, in_specs=in_specs, out_specs=out_specs, check_vma=False
    )
```

time: 1120 us -> 824 us (0.74)
  matrix products: 257 us -> 34.1 us
  local copies, waits for them, and re-layouts: 246 us -> 46.9 us
  Pallas kernels: 436 us -> 530 us
  waiting for transfers between devices: 39.2 us -> 118 us
  other arithmetic: 72.8 us -> 33 us
    pallas_call x0 -> x8, Pallas kernels: none -> 287 us  [the longest x1 93.8 us: feed_forward(): pl.pallas_call(functools.partial(feed_kernel, chunks), out_shape=[jax.Sha...]
    pallas_call x8 -> x4, Pallas kernels: 271 us -> 120 us  [plane_gather(): pl.pallas_call(functools.partial(gather_kernel, chunks), out_shape=jax.Sh...]
    dot_general x56 -> x0, matrix products: 117 us -> none  [the longest x8 23.5 us: one_backward(): gv = jnp.einsum('hqk,qhd->kd', probs_low, g, preferred_element_type=f32)]
    dot_general x15 -> x5, matrix products: 140 us -> 34.1 us  [dot(): lax.dot_general(a, b, (((ca,), (cb,)), ((), ())), preferred_element_type=...]
    dynamic_update_slice x16 -> x0, local copies, waits for them, and re-layouts: 58 us -> none  [per_device(): lax.map(one_forward, (query_rows, key_rows, value_rows, allowed))]
    all_gather x1 -> x2, waiting for transfers between devices: 0.01 us -> 53.2 us  [spread(): lax.all_gather(x, R, axis=0, tiled=True)]
    pallas_call x4 -> x3, Pallas kernels: 165 us -> 124 us  [plane_scatter(): pl.pallas_call(functools.partial(scatter_kernel, chunks), out_shape=jax.S...]
    slice x9 -> x4, local copies, waits for them, and re-layouts: 39.2 us -> 1.13 us  [the longest x1 0.44 us: per_device(): high = query_places[:, 0, QUERY_BLOCK - 1] // KEY_BLOCK + 1]
  transfers between devices with their start and end apart: 13 -> 12, of which waited for: 3 -> 3; matrix products, arithmetic and copies ran while one was open for 23% -> 10% of each run, Pallas kernels for 27% -> 52%
where the time goes in v3:
time: 824 us; the launch traced here: 815 us
  Pallas kernels  530 us (64%)
  waiting for transfers between devices  118 us (14%)
  local copies, waits for them, and re-layouts  46.9 us (6%)
  matrix products  34.1 us (4%)
  other arithmetic  33 us (4%)
  blocking collectives  32.2 us (4%)
  between operations  14.9 us (2%)
    pallas_call x3, Pallas kernels, plane_scatter(): pl.pallas_call(functools.partial(scatter_kernel, chunks), out_shape=jax.S...  124 us
    pallas_call x4, Pallas kernels, plane_gather(): pl.pallas_call(functools.partial(gather_kernel, chunks), out_shape=jax.Sh...  120 us
    pallas_call x1, Pallas kernels, feed_forward(): pl.pallas_call(functools.partial(feed_kernel, chunks), out_shape=[jax.Sha...  93.8 us
    pallas_call x1, Pallas kernels, return_keys(): pl.pallas_call(return_kernel, out_shape=jax.ShapeDtypeStruct((grad_q.shap...  55.1 us
    all_gather x2, waiting for transfers between devices, spread(): lax.all_gather(x, R, axis=0, tiled=True)  53.2 us
    pallas_call x1, Pallas kernels, enter(): pl.pallas_call(functools.partial(enter_kernel, chunks), out_shape=[jax.Sh...  46.3 us
    pallas_call x1, Pallas kernels, project(): pl.pallas_call(functools.partial(project_kernel, chunks), out_shape=[jax....  46.3 us
    reduce_scatter x4, waiting for transfers between devices, line_scatter(): return lax.psum_scatter(x, F, scatter_dimension=0, tiled=True)  39.6 us
  transfers between devices with their start and end apart: 12, of which 3 were waited for; matrix products, arithmetic and copies ran while one was open for 10% of the time, Pallas kernels for 52%

profile of v3, /device:TPU:0, one launch (start us, length us, event | category | flops | bytes accessed | tf_op | source)
XLA Modules:
  0.0 814.5 jit_solution(10722311208561104397)
XLA Ops:
  7.2 1.5 copy-done
  8.8 0.7 constant_dynamic-slice_fusion.9
  9.6 1.0 constant_dynamic-slice_fusion.12
  10.6 1.1 constant_dynamic-slice_fusion.10
  11.7 0.9 pad_maximum_fusion.2
  12.6 2.1 constant_dynamic-slice_fusion
  14.8 2.9 constant_dynamic-slice_fusion.1
  17.7 2.4 concatenate.19
  20.2 46.3 %shard_map.203 = (bf16[8,256,2048]{2,1,0:T(8,128)(2,1)S(1)}, f32[4,8,512]{2,1,0:T(8,128)S(1)}, s32[8,8,128]{2,1,0:T(8,128)S(1)}) custom-call(bf16[256,2048]{1,0:T(8,128)(2,1)S(1)} %copy-done.2, f32[8,512]{1,0:T(8,128)S(1)} %fusion.14.gains, s32[8,128]{1,0:T(8,128)S(1)} %bitcast.61), custom_call_target="tpu_custom_call" | custom-call | tf_op jit(solution)/shard_map/pallas_call | solution.py:718
  66.5 3.4 copy-done.11
  70.1 2.3 reduce-window.6
  73.9 4.3 all-to-all-start
  78.3 3.7 fusion.10
  82.0 1.7 pad_maximum_fusion
  83.7 1.6 copy-done.7
  85.3 1.4 copy-done.18
  86.7 46.3 %shard_map.204 = (bf16[2048,256]{1,0:T(8,128)(2,1)S(1)}, bf16[8,4,256,128]{3,2,1,0:T(8,128)(2,1)S(1)}, bf16[8,256,2048]{2,1,0:T(8,128)(2,1)}) custom-call(bf16[2048,2048]{1,0:T(8,128)(2,1)} %bitcast.56, bf16[2048,384]{1,0:T(8,128)(2,1)S(1)} %copy-done.18, f32[2048,128]{1,0:T(8,128)S(1)} %get-tuple-element.89.cosine, f32[2048,128]{1,0:T(8,128)S(1)} %get-tuple-element.90.sine, ...), custom_call_target="tpu_custom_call" | custom-call | tf_op jit(solution)/shard_map/pallas_call | solution.py:741
  133.0 13.1 %shard_map.205 = (bf16[2048,256]{1,0:T(8,128)(2,1)S(1)}, f32[16,1,512]{2,1,0:T(1,128)S(1)}) custom-call(s32[16]{0:T(128)S(1)} %and_select_fusion.2.low, s32[16]{0:T(128)S(1)} %fusion.17.high, bf16[2048,256]{1,0:T(8,128)(2,1)S(1)} %get-tuple-element.37.q, bf16[8,1024,128]{2,1,0:T(8,128)(2,1)S(1)} %bitcast.58, s32[16,1,128]{2,1,0:T(1,128)S(1)} %get-tuple-element.86.starts, ...), custom_call_target="tpu_custom_call" | custom-call | tf_op jit(solution)/shard_map/pallas_call | solution.py:999
  146.1 1.3 copy-done.12
  147.4 1.0 copy-done.16
  148.4 2.3 copy.30
  150.6 3.6 convolution_convert_fusion.1.part
  154.2 41.3 %shard_map.206 = f32[256,2048]{1,0:T(8,128)S(1)} custom-call(bf16[2048,2048]{1,0:T(8,128)(2,1)S(1)} %convolution_convert_fusion.1.part), custom_call_target="tpu_custom_call" | custom-call | tf_op jit(solution)/shard_map/pallas_call | solution.py:868
  196.0 1.3 copy-done.22
  197.3 1.2 multiply_convert_fusion.x
  198.5 39.2 %shard_map.207.hidden = bf16[8,256,2048]{2,1,0:T(8,128)(2,1)} custom-call(bf16[256,2048]{1,0:T(8,128)(2,1)} %multiply_convert_fusion.x), custom_call_target="tpu_custom_call" | custom-call | tf_op jit(solution)/shard_map/pallas_call | solution.py:850
  237.8 23.6 %all-gather.11.cloned.1.call-done.w_feed = bf16[2048,1408]{1,0:T(8,128)(2,1)} async-done(((bf16[512,1408]{1,0:T(8,128)(2,1)}), bf16[2048,1408]{1,0:T(8,128)(2,1)}) %all-gather.11.cloned.1.call-update) | async-done | bytes 5767184 | tf_op jit(solution)/shard_map/all_gather | solution.py:894
  261.4 93.8 %shard_map.208 = (bf16[8,256,2048]{2,1,0:T(8,128)(2,1)}, f32[256,2048]{1,0:T(8,128)}, bf16[2048,1408]{1,0:T(8,128)(2,1)}, bf16[704,2048]{1,0:T(8,128)(2,1)}) custom-call(bf16[8,256,2048]{2,1,0:T(8,128)(2,1)} %shard_map.207.hidden, bf16[8,256,2048]{2,1,0:T(8,128)(2,1)} %get-tuple-element.41.cotangent, ...), custom_call_target="tpu_custom_call" | custom-call | tf_op jit(solution)/shard_map/pallas_call | solution.py:682
  355.3 0.5 reduce-scatter.10.cloned.1.call-update
  355.9 3.0 multiply_reduce_fusion
  359.0 3.3 fusion.19.x
  362.3 39.3 %shard_map.210 = bf16[8,256,2048]{2,1,0:T(8,128)(2,1)} custom-call(bf16[256,2048]{1,0:T(8,128)(2,1)} %fusion.19.x), custom_call_target="tpu_custom_call" | custom-call | tf_op jit(solution)/shard_map/pallas_call | solution.py:850
  401.6 5.9 convolution_convert_fusion.3
  407.5 18.7 %all_to_all.38 = bf16[256,8,256]{2,0,1:T(8,128)(2,1)} all-to-all(bf16[256,8,256]{2,0,1:T(8,128)(2,1)S(1)} %bitcast.67), channel_id=1, replica_groups=mesh['replica'=8,'fsdp'=4] {'replica'}, dimensions={1} | all-to-all | bytes 2097152 | tf_op jit(solution)/shard_map/all_to_all | solution.py:1212
  426.3 6.9 convolution_convert_fusion.4.grad
  433.2 39.6 %reduce-scatter.8.cloned.1.call-done = bf16[512,1408]{1,0:T(8,128)(2,1)} async-done(((bf16[2048,1408]{1,0:T(8,128)(2,1)}), bf16[512,1408]{1,0:T(8,128)(2,1)}) %reduce-scatter.8.cloned.1.call-update) | async-done | bytes 1441808 | tf_op jit(solution)/shard_map/reduce_scatter | solution.py:898
  472.8 1.6 copy-done.13
  474.4 1.2 copy-done.17
  475.6 1.2 copy-done.20
  476.8 18.3 %shard_map.211 = (f32[2048,256]{1,0:T(8,128)S(1)}, bf16[8,1024,128]{2,1,0:T(8,128)(2,1)S(1)}) custom-call(s32[16]{0:T(128)S(1)} %and_select_fusion.2.low, s32[16]{0:T(128)S(1)} %fusion.17.high, bf16[2048,256]{1,0:T(8,128)(2,1)S(1)} %copy-done.17, bf16[8,1024,128]{2,1,0:T(8,128)(2,1)S(1)} %bitcast.59, s32[16,1,128]{2,1,0:T(1,128)S(1)} %get-tuple-element.86.starts, ...), custom_call_target="tpu_custom_call" | custom-call | tf_op jit(solution)/shard_map/pallas_call | solution.py:999
  495.1 55.1 %shard_map.212 = bf16[2048,384]{1,0:T(8,128)(2,1)} custom-call(bf16[8,1024,128]{2,1,0:T(8,128)(2,1)S(1)} %get-tuple-element.47.grad_kv, f32[2048,256]{1,0:T(8,128)S(1)} %get-tuple-element.48.grad_q, f32[2048,128]{1,0:T(8,128)S(1)} %get-tuple-element.89.cosine, f32[2048,128]{1,0:T(8,128)S(1)} %copy-done.6), custom_call_target="tpu_custom_call" | custom-call | tf_op jit(solution)/shard_map/pallas_call | solution.py:765
  550.3 8.2 %convolution_convert_fusion.part = bf16[2048,2048]{1,0:T(8,128)(2,1)} fusion(bf16[2048,384]{1,0:T(8,128)(2,1)} %shard_map.212, bf16[2048,384]{1,0:T(8,128)(2,1)S(1)} %copy-done.19), kind=kOutput, calls=%fused_computation | convolution fusion | flops 3225419776 | bytes 11534336 | tf_op jit(solution)/shard_map/dot_general | solution.py:48
  558.5 3.4 copy-done.10
  561.9 41.2 %shard_map.213 = f32[256,2048]{1,0:T(8,128)S(1)} custom-call(bf16[2048,2048]{1,0:T(8,128)(2,1)S(1)} %copy-done.10), custom_call_target="tpu_custom_call" | custom-call | tf_op jit(solution)/shard_map/pallas_call | solution.py:868
  603.2 0.7 fusion.8
  603.8 1.3 copy.32
  605.5 9.5 %convolution_convert_fusion.2 = bf16[2048,384]{1,0:T(8,128)(2,1)} fusion(bf16[2048,2048]{1,0:T(8,128)(2,1)} %bitcast.57, bf16[2048,384]{1,0:T(8,128)(2,1)} %shard_map.212), kind=kOutput, calls=%fused_computation.8 | convolution fusion | flops 3222011904 | bytes 11534336 | tf_op jit(solution)/shard_map/dot_general | solution.py:48
  615.1 0.5 all-gather.17.cloned.1.call-update
  615.7 0.7 all-gather.15.cloned.1.call-update
  616.4 3.4 copy-done.9
  619.8 41.2 %shard_map.209 = f32[256,2048]{1,0:T(8,128)S(1)} custom-call(bf16[2048,2048]{1,0:T(8,128)(2,1)S(1)} %bitcast.55), custom_call_target="tpu_custom_call" | custom-call | tf_op jit(solution)/shard_map/pallas_call | solution.py:868
  661.0 1.3 copy-done.15
  662.3 13.2 %shard_map.215.o = bf16[8,512,256]{2,1,0:T(8,128)(2,1)} custom-call(bf16[512,256]{1,0:T(8,128)(2,1)} %reduce-scatter.14.cloned.1.call-done.x), custom_call_target="tpu_custom_call" | custom-call | tf_op jit(solution)/shard_map/pallas_call | solution.py:850
  675.6 6.0 fusion.7
  681.6 1.2 copy.33
  682.8 13.5 %psum.7 = f32[2,512]{1,0:T(2,128)S(1)} all-reduce(f32[2,512]{1,0:T(2,128)S(1)} %copy.33), channel_id=1, replica_groups=mesh['replica'=8,'fsdp'=4] {'replica'}, use_global_device_ids=true, to_apply=%region_11.12 | all-reduce | flops 1024 | bytes 8192 | tf_op jit(solution)/shard_map/psum | solution.py:1252
  696.3 0.6 fusion.21
  696.9 28.1 %shard_map.214.qkv = bf16[8,512,384]{2,1,0:T(8,128)(2,1)} custom-call(bf16[512,384]{1,0:T(8,128)(2,1)} %reduce-scatter.12.cloned.1.call-done.x), custom_call_target="tpu_custom_call" | custom-call | tf_op jit(solution)/shard_map/pallas_call | solution.py:850
  725.1 1.9 copy-done.3
  727.0 4.8 shard_map.216
  731.8 9.3 %convert_element_type.62 = f32[1408,2048]{1,0:T(8,128)} convert(bf16[1408,2048]{1,0:T(8,128)(2,1)} %all-gather.17.cloned.1.call-done) | non-fusion elementwise | flops 2883584 | bytes 17301504 | tf_op jit(solution)/shard_map/convert_element_type | solution.py:1264
  741.1 53.2 %all-gather.15.cloned.1.call-done = bf16[4096,1408]{1,0:T(8,128)(2,1)} async-done(((bf16[512,1408]{1,0:T(8,128)(2,1)}), bf16[4096,1408]{1,0:T(8,128)(2,1)}) %all-gather.15.cloned.1.call-update) | async-done | bytes 11534352 | tf_op jit(solution)/shard_map/all_gather | solution.py:1261
  794.3 4.3 copy-done.4
  798.6 9.0 %shard_map.217 = (f32[512,5632]{1,0:T(8,128)}, f32[512,5632]{1,0:T(8,128)}) custom-call(bf16[8,512,1408]{2,1,0:T(8,128)(2,1)S(1)} %bitcast.54), custom_call_target="tpu_custom_call" | custom-call | tf_op jit(solution)/shard_map/pallas_call | solution.py:1038
  (94 shorter events, 3.5 us)
Async XLA Ops:
  7.2 1.6 copy-start
  7.2 66.7 %all-gather.9.cloned.1.call-start = ((), (), s32[]{:S(2)}) async-start(), calls=%async_computation.8 | async-start | bytes 1310720 | tf_op jit(solution)/shard_map/all_gather | solution.py:894
  9.5 74.2 %all-gather.7.cloned.1.call-start = ((), (), s32[]{:S(2)}) async-start(), calls=%async_computation.7 | async-start | bytes 1966080 | tf_op jit(solution)/shard_map/all_gather | solution.py:894
  12.6 225.2 %all-gather.13.cloned.1.call-start = ((), (), s32[]{:S(2)}) async-start(), calls=%async_computation.10 | async-start | bytes 3604480 | tf_op jit(solution)/shard_map/all_gather | solution.py:894
  14.7 246.7 %all-gather.11.cloned.1.call-start = ((), (), s32[]{:S(2)}) async-start(), calls=%async_computation.9 | async-start | bytes 7208960 | tf_op jit(solution)/shard_map/all_gather | solution.py:894
  17.7 2.4 copy-start.24
  17.7 2.5 copy-start.25
  17.7 2.5 copy-start.2
  17.7 2.5 copy-start.21
  66.5 3.4 copy-start.11
  73.9 74.4 %all-to-all-start = ((bf16[8,256,256]{2,1,0:T(8,128)(2,1)}), bf16[8,256,256]{2,1,0:T(8,128)(2,1)}, u32[]{:S(2)}, u32[]{:S(2)}) async-start(bf16[8,256,256]{2,1,0:T(8,128)(2,1)} %bitcast.70), calls=%async_computation | async-start | bytes 2097152 | tf_op jit(solution)/shard_map/all_to_all | solution.py:1093
  78.2 394.6 %reduce-scatter.8.cloned.1.call-start = ((), (), s32[]{:S(2)}) async-start(), calls=%async_computation.11 | async-start | bytes 7208960 | tf_op jit(solution)/shard_map/reduce_scatter | solution.py:898
  83.7 49.3 %copy-start.5 = (f32[2048,128]{1,0:T(8,128)}, f32[2048,128]{1,0:T(8,128)S(1)}, u32[]{:S(2)}) copy-start(f32[2048,128]{1,0:T(8,128)S(1)} %get-tuple-element.90.sine) | copy-start | bytes 3145732
  83.7 1.6 copy-start.7
  85.3 1.4 copy-start.18
  146.1 1.3 copy-start.12
  147.4 1.0 copy-start.16
  196.0 1.3 copy-start.22
  355.2 203.3 %reduce-scatter.10.cloned.1.call-start = ((), (), s32[]{:S(2)}) async-start(), calls=%async_computation.12 | async-start | bytes 3604480 | tf_op jit(solution)/shard_map/reduce_scatter | solution.py:898
  355.8 306.6 %reduce-scatter.14.cloned.1.call-start = ((), (), s32[]{:S(2)}) async-start(), calls=%async_computation.14 | async-start | bytes 1310720 | tf_op jit(solution)/shard_map/reduce_scatter | solution.py:898
  355.8 3.0 copy-start.8
  355.8 3.2 copy-start.23
  426.2 255.4 %reduce-scatter.16.cloned.1.call-start = ((), (), s32[]{:S(2)}) async-start(), calls=%async_computation.17 | async-start | bytes 1310720
  472.8 1.6 copy-start.13
  474.4 1.2 copy-start.17
  475.6 1.2 copy-start.20
  476.8 18.3 %copy-start.6 = (f32[2048,128]{1,0:T(8,128)S(1)}, f32[2048,128]{1,0:T(8,128)}, u32[]{:S(2)}) copy-start(f32[2048,128]{1,0:T(8,128)} %copy-done.5) | copy-start | bytes 3145732
  495.1 55.1 %copy-start.19 = (bf16[2048,384]{1,0:T(8,128)(2,1)S(1)}, bf16[2048,384]{1,0:T(8,128)(2,1)}, u32[]{:S(2)}) copy-start(bf16[2048,384]{1,0:T(8,128)(2,1)} %all-gather.7.cloned.1.call-done.weight) | copy-start | bytes 4718596
  558.5 3.4 copy-start.10
  605.2 91.7 %reduce-scatter.12.cloned.1.call-start = ((), (), s32[]{:S(2)}) async-start(), calls=%async_computation.13 | async-start | bytes 1966080 | tf_op jit(solution)/shard_map/reduce_scatter | solution.py:898
  615.0 116.7 %all-gather.17.cloned.1.call-start = ((), (), s32[]{:S(2)}) async-start(), calls=%async_computation.16 | async-start | bytes 6488064 | tf_op jit(solution)/shard_map/all_gather | solution.py:1261
  615.6 178.7 %all-gather.15.cloned.1.call-start = ((), (), s32[]{:S(2)}) async-start(), calls=%async_computation.15 | async-start | bytes 12976128 | tf_op jit(solution)/shard_map/all_gather | solution.py:1261
  616.4 3.4 copy-start.9
  661.0 1.3 copy-start.15
  681.6 43.5 %copy-start.14 = (bf16[8,512,256]{2,1,0:T(8,128)(2,1)S(1)}, bf16[8,512,256]{2,1,0:T(8,128)(2,1)}, u32[]{:S(2)}) copy-start(bf16[8,512,256]{2,1,0:T(8,128)(2,1)} %shard_map.215.o) | copy-start | bytes 6291460
  725.1 1.9 copy-start.3
  794.3 4.3 copy-start.4
  798.6 9.0 %copy-start.1 = (bf16[512,2048]{1,0:T(8,128)(2,1)S(1)}, bf16[512,2048]{1,0:T(8,128)(2,1)}, u32[]{:S(2)}) copy-start(bf16[512,2048]{1,0:T(8,128)(2,1)} %param.18) | copy-start | bytes 6291460
Sparse Core Ops, SparseCore 0:
  10.2 32.5 all-gather.8
  44.9 35.9 all-gather.6
  82.5 59.7 all-gather.12
  144.3 117.0 all-gather.10
  355.3 117.4 reduce-scatter.7
  475.0 69.5 reduce-scatter.9
  546.8 28.8 reduce-scatter.13
  605.3 25.7 reduce-scatter.15
  634.0 33.9 reduce-scatter.11
  669.7 53.9 all-gather.16
  725.6 68.6 all-gather.14

commit v4 on v3

--- a/solution.py
+++ b/solution.py
@@ -21,15 +21,17 @@
 KEY_BLOCK = 256
 QUERY_BLOCK = 128
 PARTS = 2
+FIRST_DOC = 800
 
 
 def inverse_rms(values):
     return lax.rsqrt(jnp.mean(values * values, axis=1, keepdims=True) + EPSILON)
 
 
-def rope_tables(positions):
+def rope_tables(positions, repeats=1):
     half_dim = HEAD_DIM // 2
-    freq_rates = jnp.exp(jnp.arange(half_dim, dtype=jnp.float32) * (-math.log(10000.0) / half_dim))
+    places = jnp.arange(repeats * half_dim, dtype=jnp.int32) % half_dim
+    freq_rates = jnp.exp(places.astype(jnp.float32) * (-math.log(10000.0) / half_dim))
     angles = positions.astype(jnp.float32)[:, None] * freq_rates[None, :]
     return (jnp.cos(angles), jnp.sin(angles))
 
@@ -89,12 +91,18 @@
         copy.start()
         self.copies[kind, i] = copy
 
-    def start(self):
-        for i in range(self.count):
+    def start(self, kept=()):
+        ready = [i for i in range(self.count) if i not in kept]
+        for i in ready:
             self.send(0, i, self.me, self.x)
-            j = (i + self.half) % self.count
-            self.send(1, j, self.me, self.y)
-        for i in range(self.count):
+            self.send(1, ready[(ready.index(i) + self.half) % len(ready)], self.me, self.y)
+        for i in ready:
+            self.send(3, i, self.me, self.sibling)
+
+    def start_kept(self, kept):
+        for i in kept:
+            self.send(0, i, self.me, self.x)
+            self.send(1, i, self.me, self.y)
             self.send(3, i, self.me, self.sibling)
 
     def relay(self, i):
@@ -253,14 +261,33 @@
         own[s] = turn_keys(acc[:, columns:], c, n).astype(bf16)
         return carry
 
+    class Group:
+        def __init__(self, make):
+            self.each = [make(i) for i in range(count)]
+
+        def __getattr__(self, name):
+            def call():
+                for copy in self.each:
+                    getattr(copy, name)()
+
+            return call
+
     def up(step):
         slot = z - step
-        src = own.at[mine] if step == 0 else kv.at[mine, slot]
-        return along_line(src, kv.at[mine, slot], (to_line, at_line), step, above)
+
+        def make(i):
+            dst = kv.at[core * count + i, slot]
+            src = own.at[core * count + i] if step == 0 else dst
+            return along_line(src, dst, (to_line, at_line), (step, i), above)
+
+        return Group(make)
 
     def came(step):
-        slot = z - step
-        return along_line(kv.at[mine, slot], kv.at[mine, slot], (to_line, at_line), step - 1, above)
+        def make(i):
+            dst = kv.at[core * count + i, z - step]
+            return along_line(dst, dst, (to_line, at_line), (step - 1, i), above)
+
+        return Group(make)
 
     def across(step):
         slot = z - step
@@ -310,102 +337,78 @@
     kept_cot.wait()
 
 
-def return_kernel(
-    grad_kv, grad_q, cosine, sine, grad_qkv,
-    own, from_sib, inbox, outbox, own_sem, to_sib, at_sib, to_line, at_line,
+def finish_kernel(
+    qkv, out_rows, terms, all_qkv, all_out, gains, own_gain, all_gains,
+    at_planes, own_sems, to_z, at_z, *sems,
 ):
+    planes = terms.shape[0]
+    z = lax.axis_index(F)
+    chunks = [x for pair in zip(row_items(qkv, all_qkv, 2), row_items(out_rows, all_out, 2)) for x in pair]
+    gather = Gather(chunks + [(own_gain, lambda owner: all_gains.at[owner])], sems)
+    me, last = gather.me, gather.count - 1
+    others = [lax.rem(z + i, planes) for i in range(1, planes)]
+    barrier = pltpu.get_barrier_semaphore()
+    for other in others:
+        pl.semaphore_signal(barrier, inc=1, device_id={F: other}, device_id_type=MESH)
+    for device in (gather.sibling, gather.x, gather.y):
+        pl.semaphore_signal(barrier, inc=1, device_id={R: device}, device_id_type=MESH)
+    pl.semaphore_wait(barrier, planes + 2)
+    copies = [
+        along_line(terms.at[other], at_planes.at[i], (to_z, at_z), i, other)
+        for i, other in enumerate(others)
+    ]
+    for copy in copies:
+        copy.start()
+    kept = [
+        pltpu.make_async_copy(qkv, all_qkv.at[me], own_sems.at[0]),
+        pltpu.make_async_copy(out_rows, all_out.at[me], own_sems.at[1]),
+    ]
+    for copy in kept:
+        copy.start()
+    gather.start((last,))
+    total = terms[z]
+    for i, copy in enumerate(copies):
+        copy.wait()
+        total = total + at_planes[i]
+    own_gain[...] = total
+    all_gains[me] = total
+    gather.start_kept((last,))
+    for i in range(gather.count):
+        gather.relay(i)
+    gather.finish()
+    total = all_gains[0]
+    for device in range(1, all_gains.shape[0]):
+        total = total + all_gains[device]
+    gains[...] = total
+    for copy in kept:
+        copy.wait()
+
+
+def finish(qkv, out_rows, terms, call):
+    planes, width = lax.axis_size(F), lax.axis_size(R)
     f32, bf16 = jnp.float32, jnp.bfloat16
-    planes, count, tok = inbox.shape[0], inbox.shape[1], inbox.shape[2]
-    z, me = lax.axis_index(F), lax.axis_index(R)
-    core = lax.rem(me, 2)
-    sibling = me + 1 - 2 * core
-    above, below = lax.rem(z + 1, planes), lax.rem(z + planes - 1, planes)
-    columns = grad_q.shape[1]
-    barrier = pltpu.get_barrier_semaphore()
-    for other in (above, below):
-        pl.semaphore_signal(barrier, inc=1, device_id={F: other}, device_id_type=MESH)
-    pl.semaphore_signal(barrier, inc=1, device_id={R: sibling}, device_id_type=MESH)
-
-    def block(half, b):
-        return grad_kv.at[pl.ds(half * count, count), pl.ds(b * tok, tok)]
-
-    def load(b):
-        return pltpu.make_async_copy(block(core, b), own.at[b], own_sem.at[b])
-
-    def trade(b):
-        return remote(block(1 - core, b), from_sib.at[b], (to_sib, at_sib), b, sibling)
-
-    def down(b):
-        return along_line(outbox.at[b], inbox.at[b], (to_line, at_line), b, below)
-
-    for b in range(planes):
-
-        @pl.when(b <= z)
-        def _():
-            load(b).start()
-
-    pl.semaphore_wait(barrier, 3)
-    for b in range(planes):
-
-        @pl.when(b <= z)
-        def _():
-            trade(b).start()
-
-    def queries(s, carry):
-        rows = pl.ds(pl.multiple_of(s * tok, tok), tok)
-        c, n = cosine[rows, :], -sine[rows, :]
-        for first in range(0, columns, 2 * HEAD_DIM):
-            part = slice(first, first + 2 * HEAD_DIM)
-            grad_qkv[rows, part] = turn(grad_q[rows, part], c, n).astype(bf16)
-        grad_qkv[rows, columns:] = jnp.zeros((tok, 2 * HEAD_DIM), bf16)
-        return carry
-
-    for b in range(planes):
-
-        @pl.when(b <= z)
-        def _():
-            load(b).wait()
-            trade(b).wait_recv()
-
-            @pl.when(z < planes - 1)
-            def _():
-                down(b).wait_recv()
-
-        @pl.when((b < z) & (z < planes - 1))
-        def _():
-            outbox[b] = (
-                own[b].astype(f32) + from_sib[b].astype(f32) + inbox[b].astype(f32)
-            ).astype(bf16)
-
-        @pl.when((b < z) & (z == planes - 1))
-        def _():
-            outbox[b] = (own[b].astype(f32) + from_sib[b].astype(f32)).astype(bf16)
-
-        @pl.when(b < z)
-        def _():
-            down(b).start()
-
-        if b == 0:
-            lax.fori_loop(0, 2 * count, queries, 0)
-
-    def keys(i, carry):
-        s = core * count + i
-        rows = pl.ds(pl.multiple_of(s * tok, tok), tok)
-        total = own[z, i].astype(f32) + from_sib[z, i].astype(f32)
-        total = total + jnp.where(z < planes - 1, inbox[z, i].astype(f32), 0.0)
-        grad_qkv[rows, columns:] = turn_keys(total, cosine[rows, :], -sine[rows, :]).astype(bf16)
-        return carry
-
-    lax.fori_loop(0, count, keys, 0)
-    for b in range(planes):
-
-        @pl.when(b <= z)
-        def _():
-            trade(b).wait_send()
-
-        @pl.when(b < z)
-        def _():
-            down(b).wait_send()
+    vmem = pl.BlockSpec(memory_space=pltpu.VMEM)
+    block = terms.shape[1:]
+    return pl.pallas_call(
+        finish_kernel,
+        out_shape=[
+            jax.ShapeDtypeStruct((width,) + qkv.shape, bf16),
+            jax.ShapeDtypeStruct((width,) + out_rows.shape, bf16),
+            jax.ShapeDtypeStruct(block, f32),
+        ],
+        in_specs=[ANY, ANY, vmem],
+        out_specs=[ANY, ANY, vmem],
+        scratch_shapes=[
+            pltpu.VMEM(block, f32),
+            pltpu.VMEM((width,) + block, f32),
+            pltpu.VMEM((planes - 1,) + block, f32),
+            DMA((2,)),
+            DMA((planes - 1,)),
+            DMA((planes - 1,)),
+        ]
+        + Gather.scratch(5),
+        compiler_params=pltpu.CompilerParams(collective_id=call, has_side_effects=True),
+    )(qkv, out_rows, terms)
 
 
 class Scatter:
@@ -417,14 +420,14 @@
             pltpu.VMEM((4, rows, columns), bf16),
             pltpu.VMEM((chunks, 2, size, columns), bf16),
             pltpu.VMEM((chunks, size, columns), bf16),
-            pltpu.VMEM((chunks, size, columns), jnp.float32),
+            pltpu.VMEM((2, size, columns), jnp.float32),
             DMA((4,)),
             DMA((4,)),
             DMA((chunks, 2)),
             DMA((chunks, 2)),
             DMA((chunks,)),
             DMA((chunks,)),
-            DMA((chunks,)),
+            DMA((2,)),
         ]
 
     def __init__(self, out, chunks, refs):
@@ -435,6 +438,8 @@
         self.me = lax.axis_index(R)
         self.sibling, self.x, self.y = self.me + 1 - 2 * lax.rem(self.me, 2), self.me ^ 2, self.me ^ 4
         self.size = out.shape[0] // chunks
+        self.order = [*range(self.half, chunks), *range(self.half)]
+        self.trades = None
 
     def owner(self, i):
         return (self.me ^ (6 - 2 * (i // 2))) ^ (1 - lax.rem(i, 2))
@@ -455,6 +460,21 @@
         @pl.when(for_sibling)
         def _():
             self.trade(d).start()
+
+    def take(self, part, sems):
+        self.loads, self.trades = {}, {}
+        for d in (3, 2, 1, 0):
+            self.loads[d] = pltpu.make_async_copy(part.at[self.me ^ (2 * d)], self.own.at[d], sems.at[d])
+            self.loads[d].start()
+        for d in (3, 2, 1, 0):
+            self.trades[d] = remote(
+                part.at[self.sibling ^ (2 * d)], self.sib.at[d], self.sib_sems, d, self.sibling
+            )
+            self.trades[d].start()
+
+    def taken(self, d):
+        self.loads[d].wait()
+        self.trades[d].wait_recv()
 
     def arrived(self, d):
         self.trade(d).wait_recv()
@@ -478,7 +498,10 @@
         return remote(self.own.at[d, self.part(j)], self.got_far.at[j], self.far_sems, j, device)
 
     def out_copy(self, j):
-        return pltpu.make_async_copy(self.total.at[j], self.out.at[self.part(j)], self.out_sem.at[j])
+        slot = self.order.index(j) % 2
+        return pltpu.make_async_copy(
+            self.total.at[slot], self.out.at[self.part(j)], self.out_sem.at[slot]
+        )
 
     def near(self, j):
         for e in (1 if j < self.half else 2, 3):
@@ -493,42 +516,102 @@
         passed = self.summed(d, j) + self.got[j, 1].astype(jnp.float32)
         self.own[d, self.part(j)] = passed.astype(jnp.bfloat16)
         self.far_copy(j).start()
-        self.total[j] = self.summed(0, j) + self.got[j, 0].astype(jnp.float32)
 
     def last(self, j):
         self.far_copy(j).wait_recv()
-        self.total[j] = self.total[j] + self.got_far[j].astype(jnp.float32)
+        turn = self.order.index(j)
+        if turn >= 2:
+            self.out_copy(self.order[turn - 2]).wait()
+        self.total[turn % 2] = (
+            self.summed(0, j)
+            + self.got[j, 0].astype(jnp.float32)
+            + self.got_far[j].astype(jnp.float32)
+        )
         self.out_copy(j).start()
 
     def finish(self):
-        self.trade(0).wait_send()
+        if self.trades is None:
+            self.trade(0).wait_send()
+        else:
+            for copy in self.trades.values():
+                copy.wait_send()
+        for j in self.order[-2:]:
+            self.out_copy(j).wait()
         for j in range(self.chunks):
-            self.out_copy(j).wait()
             self.far_copy(j).wait_send()
             for copy in self.near_copies(j):
                 copy.wait_send()
 
 
+def feed_in_kernel(hidden, cotangent, w_feed, acts, down_part, inner_turned):
+    width, _, tok = inner_turned.shape
+    units = w_feed.shape[1] // 2
+    i = pl.program_id(0)
+
+    @pl.when(i < width)
+    def _():
+        acc = dot(hidden[0], w_feed[...])
+        acts[0] = acc
+        gate, up = acc[:, :units], acc[:, units:]
+        inner_turned[i] = (gate / (1.0 + jnp.exp(-gate)) * up).astype(jnp.bfloat16).T
+
+    @pl.when(i >= width)
+    def _():
+        acc = dot(inner_turned[0], cotangent[0])
+        for s in range(1, width):
+            acc = acc + dot(inner_turned[s], cotangent[s])
+        down_part[...] = acc.astype(jnp.bfloat16)
+
+
+def feed_in(hidden, cotangent, w_feed):
+    width, tok, model = hidden.shape
+    units = w_feed.shape[1] // 2
+    tiles = model // tok
+    return pl.pallas_call(
+        feed_in_kernel,
+        grid=(width + tiles,),
+        out_shape=[
+            jax.ShapeDtypeStruct((width, tok, 2 * units), jnp.float32),
+            jax.ShapeDtypeStruct((units, model), jnp.bfloat16),
+        ],
+        in_specs=[
+            pl.BlockSpec((1, tok, model), lambda i: (jnp.minimum(i, width - 1), 0, 0)),
+            pl.BlockSpec((width, tok, tok), lambda i: (0, 0, jnp.maximum(i - width, 0))),
+            pl.BlockSpec(memory_space=pltpu.VMEM),
+        ],
+        out_specs=[
+            pl.BlockSpec((1, tok, 2 * units), lambda i: (jnp.minimum(i, width - 1), 0, 0)),
+            pl.BlockSpec((units, tok), lambda i: (0, jnp.maximum(i - width, 0))),
+        ],
+        scratch_shapes=[pltpu.VMEM((width, units, tok), jnp.bfloat16)],
+        compiler_params=pltpu.CompilerParams(vmem_limit_bytes=48 << 20),
+    )(hidden, cotangent, w_feed)
+
+
 def feed_kernel(
-    chunks, hidden, cotangent, w_feed, w_down, out_part, grad_hidden, feed_part, down_part,
-    hidden_in, cot_in, grads, inner_turned, out_stage, column_in, feed_stage, down_stage,
-    in_sems, out_sem, column_sems, feed_sem, down_sem, *refs,
+    chunks, hidden, cotangent, acts, w_feed, w_down, out_part, grad_hidden, feed_part,
+    acts_in, cot_in, grads, column_in, feed_stage, out_stage, in_sems, column_sems, feed_sem, out_sem,
+    *refs,
 ):
     f32, bf16 = jnp.float32, jnp.bfloat16
     width, tok, model = hidden.shape
     units = w_down.shape[0]
     scatter = Scatter(grad_hidden, chunks, refs)
     half = chunks // 2
+    first_half, second_half = range(half), range(half, chunks)
 
     def loads(i):
         slot, owner = lax.rem(i, 2), scatter.owner(i)
         return [
-            pltpu.make_async_copy(hidden.at[owner], hidden_in.at[slot], in_sems.at[0, slot]),
+            pltpu.make_async_copy(acts.at[owner], acts_in.at[slot], in_sems.at[0, slot]),
             pltpu.make_async_copy(cotangent.at[owner], cot_in.at[slot], in_sems.at[1, slot]),
         ]
 
     def out_copy(i):
-        return pltpu.make_async_copy(out_stage, out_part.at[scatter.owner(i)], out_sem)
+        slot = lax.rem(i, 2)
+        return pltpu.make_async_copy(
+            out_stage.at[slot], out_part.at[scatter.owner(i)], out_sem.at[slot]
+        )
 
     for i in (0, 1):
         for copy in loads(i):
@@ -540,23 +623,21 @@
         rows = pl.ds(pl.multiple_of(i * tok, tok), tok)
         for copy in loads(i):
             copy.wait()
-        acc = dot(hidden_in[slot], w_feed[...])
-        gate, up = acc[:, :units], acc[:, units:]
+        gate, up = acts_in[slot, :, :units], acts_in[slot, :, units:]
         gate_sig = 1.0 / (1.0 + jnp.exp(-gate))
         gate_silu = gate * gate_sig
         inner = (gate_silu * up).astype(bf16)
-        inner_turned[i] = inner.T
         grad_inner = dot(cot_in[slot], w_down[...], 1, 1)
         grad_gate = grad_inner * up * gate_sig * (1.0 + gate * (1.0 - gate_sig))
         both = jnp.concatenate([grad_gate, grad_inner * gate_silu], axis=1).astype(bf16)
         grads[rows, :] = both
         scatter.put(i, dot(both, w_feed[...], 1, 1).astype(bf16))
 
-        @pl.when(i >= 1)
-        def _():
-            out_copy(i - 1).wait()
-
-        out_stage[...] = dot(inner, w_down[...]).astype(bf16)
+        @pl.when(i >= 2)
+        def _():
+            out_copy(i - 2).wait()
+
+        out_stage[slot] = dot(inner, w_down[...]).astype(bf16)
         out_copy(i).start()
 
         @pl.when(i + 2 < width)
@@ -568,55 +649,39 @@
         def _():
             scatter.arrived(3)
             scatter.arrived(2)
-            for j in range(half, chunks):
+            for j in second_half:
                 scatter.near(j)
 
         @pl.when(i == 6)
         def _():
             scatter.arrived(1)
-            for j in range(half):
+            for j in first_half:
                 scatter.near(j)
 
         return carry
 
     tiles = model // tok
 
-    def column_loads(n, source, tile):
+    def column_loads(n):
         slot = lax.rem(n, 2)
-        part = pl.ds(pl.multiple_of(tile * tok, tok), tok)
+        part = pl.ds(pl.multiple_of(n * tok, tok), tok)
         return [
             pltpu.make_async_copy(
-                source.at[scatter.owner(i), :, part],
+                hidden.at[scatter.owner(i), :, part],
                 column_in.at[slot, pl.ds(i * tok, tok)],
                 column_sems.at[slot, i],
             )
             for i in range(width)
         ]
 
-    def start_columns(n):
-        @pl.when(n < tiles)
-        def _():
-            for copy in column_loads(n, hidden, n):
-                copy.start()
-
-        @pl.when((n >= tiles) & (n < 2 * tiles))
-        def _():
-            for copy in column_loads(n, cotangent, n - tiles):
-                copy.start()
-
     def feed_copy(n):
         rows = pl.ds(pl.multiple_of(n * tok, tok), tok)
         slot = lax.rem(n, 2)
         return pltpu.make_async_copy(feed_stage.at[slot], feed_part.at[rows], feed_sem.at[slot])
 
-    def down_copy(n):
-        part = pl.ds(pl.multiple_of((n - tiles) * tok, tok), tok)
-        slot = lax.rem(n, 2)
-        return pltpu.make_async_copy(down_stage.at[slot], down_part.at[:, part], down_sem.at[slot])
-
     def feed_tile(n, carry):
         slot = lax.rem(n, 2)
-        for copy in column_loads(n, hidden, n):
+        for copy in column_loads(n):
             copy.wait()
 
         @pl.when(n >= 2)
@@ -625,56 +690,40 @@
 
         feed_stage[slot] = dot(column_in[slot], grads[...], 0, 0).astype(bf16)
         feed_copy(n).start()
-        start_columns(n + 2)
-
-        @pl.when(n == 1)
-        def _():
-            for j in range(half, chunks):
+
+        @pl.when(n + 2 < tiles)
+        def _():
+            for copy in column_loads(n + 2):
+                copy.start()
+
+        @pl.when(n == 2)
+        def _():
+            for j in second_half:
                 scatter.far(j)
 
-        @pl.when(n == 4)
-        def _():
-            for j in range(half):
+        @pl.when(n == 5)
+        def _():
+            for j in first_half:
                 scatter.far(j)
 
         return carry
 
-    def down_tile(n, carry):
-        slot = lax.rem(n, 2)
-        for copy in column_loads(n, cotangent, n - tiles):
-            copy.wait()
-
-        @pl.when(n >= tiles + 2)
-        def _():
-            down_copy(n - 2).wait()
-
-        acc = dot(inner_turned[0], column_in[slot, :tok])
-        for i in range(1, width):
-            acc = acc + dot(inner_turned[i], column_in[slot, i * tok : (i + 1) * tok])
-        down_stage[slot] = acc.astype(bf16)
-        down_copy(n).start()
-        start_columns(n + 2)
-        return carry
-
     for n in (0, 1):
-        for copy in column_loads(n, hidden, n):
+        for copy in column_loads(n):
             copy.start()
     lax.fori_loop(0, width, block, 0)
     scatter.arrived(0)
     lax.fori_loop(0, tiles, feed_tile, 0)
-    for j in range(half, chunks):
-        scatter.last(j)
-    lax.fori_loop(tiles, 2 * tiles, down_tile, 0)
-    for j in range(half):
+    for j in scatter.order:
         scatter.last(j)
     scatter.finish()
-    out_copy(width - 1).wait()
+    for i in (width - 2, width - 1):
+        out_copy(i).wait()
     for n in (tiles - 2, tiles - 1):
         feed_copy(n).wait()
-        down_copy(n + tiles).wait()
-
-
-def feed_forward(hidden, cotangent, w_feed, w_down, call, chunks=4):
+
+
+def feed_forward(hidden, cotangent, acts, w_feed, w_down, call, chunks=4):
     width, tok, model = hidden.shape
     units = w_down.shape[0]
     bf16 = jnp.bfloat16
@@ -685,30 +734,240 @@
             jax.ShapeDtypeStruct((width, tok, model), bf16),
             jax.ShapeDtypeStruct((tok, model), jnp.float32),
             jax.ShapeDtypeStruct((model, 2 * units), bf16),
-            jax.ShapeDtypeStruct((units, model), bf16),
         ],
-        in_specs=[ANY, ANY, vmem, vmem],
-        out_specs=[ANY] * 4,
+        in_specs=[ANY, ANY, ANY, vmem, vmem],
+        out_specs=[ANY] * 3,
         scratch_shapes=[
-            pltpu.VMEM((2, tok, model), bf16),
+            pltpu.VMEM((2, tok, 2 * units), jnp.float32),
             pltpu.VMEM((2, tok, model), bf16),
             pltpu.VMEM((width * tok, 2 * units), bf16),
-            pltpu.VMEM((width, units, tok), bf16),
-            pltpu.VMEM((tok, model), bf16),
             pltpu.VMEM((2, width * tok, tok), bf16),
             pltpu.VMEM((2, tok, 2 * units), bf16),
-            pltpu.VMEM((2, units, tok), bf16),
+            pltpu.VMEM((2, tok, model), bf16),
             DMA((2, 2)),
-            DMA,
             DMA((2, width)),
             DMA((2,)),
             DMA((2,)),
         ]
         + Scatter.scratch(tok, model, chunks),
         compiler_params=pltpu.CompilerParams(
+            collective_id=call, has_side_effects=True, vmem_limit_bytes=62 << 20
+        ),
+    )(hidden, cotangent, acts, w_feed, w_down)
+
+
+def back_kernel(
+    chunks, heads, q, kv, starts, places, grad, mixed, log_total, cosine, sine, out_part, down_rows, w_part,
+    grad_qkv, feed_out, all_down, w_rows,
+    sums, grad_kv, from_sib, inbox, outbox, to_sib, at_sib, to_line, at_line, down_sem, w_sem,
+    to_all, at_all, load_sems, *refs,
+):
+    f32, bf16 = jnp.float32, jnp.bfloat16
+    planes, count, tok = inbox.shape[0], inbox.shape[1], inbox.shape[2]
+    width = 2 * count
+    columns = heads * HEAD_DIM
+    z, me = lax.axis_index(F), lax.axis_index(R)
+    core = lax.rem(me, 2)
+    above, below = lax.rem(z + 1, planes), lax.rem(z + planes - 1, planes)
+    scatter = Scatter(feed_out, chunks, refs[:12])
+    gather = Gather([(down_rows, lambda owner: all_down.at[owner])] * 1, refs[12:])
+    half = chunks // 2
+    barrier = pltpu.get_barrier_semaphore()
+    for other in (above, below):
+        pl.semaphore_signal(barrier, inc=1, device_id={F: other}, device_id_type=MESH)
+    peers = [me ^ distance for distance in range(1, width)]
+    for device in peers:
+        pl.semaphore_signal(barrier, inc=1, device_id={R: device}, device_id_type=MESH)
+    pl.semaphore_wait(barrier, 1 + width)
+    share = w_part.shape[1] // width
+
+    def share_of(device):
+        return w_part.at[:, pl.ds(pl.multiple_of(device * share, share), share)]
+
+    w_copies = [
+        remote(share_of(device), w_rows.at[me], (to_all, at_all), i, device)
+        for i, device in enumerate(peers)
+    ]
+    w_kept = pltpu.make_async_copy(share_of(me), w_rows.at[me], w_sem)
+    for copy in [w_kept] + w_copies:
+        copy.start()
+    scatter.take(out_part, load_sems)
+    kept = pltpu.make_async_copy(down_rows, all_down.at[me], down_sem)
+    kept.start()
+    parts = tok // QUERY_BLOCK
+
+    def step(n, carry):
+        s, sub = n // parts, lax.rem(n, parts)
+        rows = pl.ds(pl.multiple_of(n * QUERY_BLOCK, QUERY_BLOCK), QUERY_BLOCK)
+        queries = heads_to_rows(q[rows, :] * bf16(HEAD_DIM**-0.5), heads)
+        grads = heads_to_rows(grad[rows, :], heads)
+        first = jnp.concatenate([starts[n]] * heads, axis=1)
+        place = jnp.concatenate([places[n]] * heads, axis=1)
+        products = grads.astype(f32) * heads_to_rows(mixed[rows, :], heads).astype(f32)
+        delta = lax.dot_general(
+            jnp.ones((8, 2 * HEAD_DIM), f32),
+            products,
+            (((1,), (1,)), ((), ())),
+            precision=lax.Precision.HIGHEST,
+            preferred_element_type=f32,
+        )[:1]
+        level = log_total[n]
+        upper = pltpu.roll(grads.astype(f32), HEAD_DIM, 1).astype(bf16)
+
+        @pl.when(sub == 0)
+        def _():
+            sums[...] = jnp.zeros_like(sums)
+
+        def block(index, acc):
+            part = pl.ds(pl.multiple_of(index * KEY_BLOCK, KEY_BLOCK), KEY_BLOCK)
+            keys = kv[s, part, :]
+            scores = dot(keys, queries, 1, 1)
+            probs = jnp.where(visible(index, first, place), jnp.exp(scores - level), 0.0)
+            grad_probs = dot(keys, upper, 1, 1)
+            grad_scores = (probs * (grad_probs - delta)).astype(bf16)
+            sums[part, :] += dot(grad_scores, queries) + dot(probs.astype(bf16), upper)
+            return acc + dot(keys, grad_scores, 0, 0)
+
+        place_of_first = z * tok + sub * QUERY_BLOCK
+        low = jnp.where(place_of_first >= FIRST_DOC, FIRST_DOC // KEY_BLOCK, 0)
+        high = (place_of_first + QUERY_BLOCK - 1) // KEY_BLOCK + 1
+        acc = lax.fori_loop(low, high, block, jnp.zeros((2 * HEAD_DIM, queries.shape[0]), f32))
+        grad_q = rows_to_heads(acc[:HEAD_DIM] * HEAD_DIM**-0.5, heads)
+        c, n_sine = cosine[rows, :], -sine[rows, :]
+        for at in range(0, columns, 2 * HEAD_DIM):
+            part = slice(at, at + 2 * HEAD_DIM)
+            grad_qkv[rows, part] = turn(grad_q[:, part], c, n_sine).astype(bf16)
+        grad_qkv[rows, columns:] = jnp.zeros((QUERY_BLOCK, 2 * HEAD_DIM), bf16)
+
+        @pl.when(sub == parts - 1)
+        def _():
+            grad_kv[s] = sums[...].astype(bf16)
+
+        return carry
+
+    lax.fori_loop(0, width // 2, step, 0)
+    for d in (3, 2):
+        scatter.taken(d)
+    for j in range(half, chunks):
+        scatter.near(j)
+    scatter.taken(1)
+    for j in range(half):
+        scatter.near(j)
+    gather.start()
+    lax.fori_loop(width // 2, width * parts, step, 0)
+
+    def block_of(which, b):
+        return grad_kv.at[pl.ds(which * count, count), pl.ds(b * tok, tok)]
+
+    def trade(b):
+        return remote(block_of(1 - core, b), from_sib.at[b], (to_sib, at_sib), b, scatter.sibling)
+
+    def down(b):
+        return along_line(outbox.at[b], inbox.at[b], (to_line, at_line), b, below)
+
+    def own(b):
+        part = pl.ds(b * tok, tok)
+        return grad_kv[pl.ds(core * count, count), part, :].astype(f32) + from_sib[b].astype(f32)
+
+    for b in range(planes):
+
+        @pl.when(b <= z)
+        def _():
+            trade(b).start()
+
+    scatter.taken(0)
+    for b in range(planes):
+
+        @pl.when(b <= z)
+        def _():
+            trade(b).wait_recv()
+
+            @pl.when(z < planes - 1)
+            def _():
+                down(b).wait_recv()
+
+        @pl.when((b < z) & (z < planes - 1))
+        def _():
+            outbox[b] = (own(b) + inbox[b].astype(f32)).astype(bf16)
+
+        @pl.when((b < z) & (z == planes - 1))
+        def _():
+            outbox[b] = own(b).astype(bf16)
+
+        @pl.when(b < z)
+        def _():
+            down(b).start()
+
+        if b == 0:
+            for j in range(half, chunks):
+                scatter.far(j)
+        if b == 1:
+            gather.relay(0)
+            for j in range(half):
+                scatter.far(j)
+
+    def keys(i, carry):
+        rows = pl.ds(pl.multiple_of((core * count + i) * tok, tok), tok)
+        part = pl.ds(pl.multiple_of(z * tok, tok), tok)
+        total = grad_kv[core * count + i, part, :].astype(f32) + from_sib[z, i].astype(f32)
+        total = total + jnp.where(z < planes - 1, inbox[z, i].astype(f32), 0.0)
+        grad_qkv[rows, columns:] = turn_keys(total, cosine[rows, :], -sine[rows, :]).astype(bf16)
+        return carry
+
+    lax.fori_loop(0, count, keys, 0)
+    for j in scatter.order:
+        scatter.last(j)
+    gather.finish()
+    scatter.finish()
+    for b in range(planes):
+
+        @pl.when(b <= z)
+        def _():
+            trade(b).wait_send()
+
+        @pl.when(b < z)
+        def _():
+            down(b).wait_send()
+
+    for copy in [kept, w_kept] + w_copies:
+        copy.wait()
+
+
+def attention_back(
+    heads, q, kv, starts, places, grad, mixed, log_total, cosine, sine, out_part, down_rows, w_part, call,
+    chunks=4,
+):
+    planes, width = lax.axis_size(F), lax.axis_size(R)
+    f32, bf16 = jnp.float32, jnp.bfloat16
+    tok, model = out_part.shape[1:]
+    length = kv.shape[1]
+    vmem = pl.BlockSpec(memory_space=pltpu.VMEM)
+    blocks = pltpu.VMEM((planes, width // 2, tok, 2 * HEAD_DIM), bf16)
+    return pl.pallas_call(
+        functools.partial(back_kernel, chunks, heads),
+        out_shape=[
+            jax.ShapeDtypeStruct((q.shape[0], q.shape[1] + 2 * HEAD_DIM), bf16),
+            jax.ShapeDtypeStruct((tok, model), f32),
+            jax.ShapeDtypeStruct((width,) + down_rows.shape, bf16),
+            jax.ShapeDtypeStruct((width, w_part.shape[0], w_part.shape[1] // width), bf16),
+        ],
+        in_specs=[vmem] * 9 + [ANY] * 3,
+        out_specs=[vmem] + [ANY] * 3,
+        scratch_shapes=[
+            pltpu.VMEM((length, 2 * HEAD_DIM), f32),
+            pltpu.VMEM((width, length, 2 * HEAD_DIM), bf16),
+            blocks,
+            blocks,
+            blocks,
+        ]
+        + [DMA((planes,))] * 4
+        + [DMA, DMA, DMA((width - 1,)), DMA((width - 1,)), DMA((4,))]
+        + Scatter.scratch(tok, model, chunks)
+        + Gather.scratch(1),
+        compiler_params=pltpu.CompilerParams(
             collective_id=call, has_side_effects=True, vmem_limit_bytes=60 << 20
         ),
-    )(hidden, cotangent, w_feed, w_down)
+    )(q, kv, starts, places, grad, mixed, log_total, cosine, sine, out_part, down_rows, w_part)
 
 
 def enter(tokens, gains, ids, call, chunks=4):
@@ -748,30 +1007,13 @@
         in_specs=[vmem] * 4 + [ANY],
         out_specs=[vmem, ANY, ANY],
         scratch_shapes=[pltpu.VMEM((width, tok, 2 * HEAD_DIM), bf16), DMA, DMA]
-        + [DMA((planes,))] * 4
+        + [DMA((planes, width // 2))] * 2
+        + [DMA((planes,))] * 2
         + Gather.scratch(chunks),
         compiler_params=pltpu.CompilerParams(
             collective_id=call, has_side_effects=True, vmem_limit_bytes=40 << 20
         ),
     )(hidden, weight, cosine, sine, cotangent)
-
-
-def return_keys(grad_kv, grad_q, cosine, sine, call):
-    planes, width = lax.axis_size(F), lax.axis_size(R)
-    bf16 = jnp.bfloat16
-    tok = grad_kv.shape[1] // planes
-    vmem = pl.BlockSpec(memory_space=pltpu.VMEM)
-    blocks = pltpu.VMEM((planes, width // 2, tok, 2 * HEAD_DIM), bf16)
-    return pl.pallas_call(
-        return_kernel,
-        out_shape=jax.ShapeDtypeStruct((grad_q.shape[0], grad_q.shape[1] + 2 * HEAD_DIM), bf16),
-        in_specs=[ANY] + [vmem] * 3,
-        out_specs=vmem,
-        scratch_shapes=[blocks] * 4 + [DMA((planes,))] * 5,
-        compiler_params=pltpu.CompilerParams(
-            collective_id=call, has_side_effects=True, vmem_limit_bytes=40 << 20
-        ),
-    )(grad_kv, grad_q, cosine, sine)
 
 
 def scatter_kernel(
@@ -1080,25 +1322,21 @@
     def feed_cols(weight):
         return [cols(weight, p * (feed // planes) + r * piece, piece) for p in range(planes)]
 
-    w_qkv = line_gather(
+    w_attention = line_gather(
         jnp.concatenate(
             [
                 cols(query_weight, r * qw, qw),
                 cols(key_weight, kv * HEAD_DIM, HEAD_DIM),
                 cols(value_weight, kv * HEAD_DIM, HEAD_DIM),
+                cols(output_weight, r * (model // width), model // width),
             ],
             axis=1,
         )
     )
+    w_qkv = w_attention[:, : qw + 2 * HEAD_DIM]
     w_out = lax.all_to_all(
-        line_gather(cols(output_weight, r * (model // width), model // width)),
-        R,
-        split_axis=0,
-        concat_axis=1,
-        tiled=True,
+        w_attention[:, qw + 2 * HEAD_DIM :], R, split_axis=0, concat_axis=1, tiled=True
     )
-    w_feed = line_gather(jnp.concatenate(feed_cols(gate_weight) + feed_cols(up_weight), axis=1))
-    w_down = line_gather(lax.dynamic_slice_in_dim(down_weight, r * piece, piece, 0))
     own_gains = jnp.stack([attention_gain, feed_gain]).astype(f32)
     tok_float = tokens.astype(f32)
     scale_in = inverse_rms(tok_float)
@@ -1115,6 +1353,11 @@
         hidden_in = lax.all_gather((normed_in * gains[0]).astype(bf16), R, axis=0, tiled=True)
         ids = lax.all_gather(segment_ids, R, axis=0, tiled=True)
     gain_in, gain_mid = gains[0], gains[1]
+    gate_weight, up_weight, down_weight, ids = lax.optimization_barrier(
+        (gate_weight, up_weight, down_weight, ids)
+    )
+    w_feed = line_gather(jnp.concatenate(feed_cols(gate_weight) + feed_cols(up_weight), axis=1))
+    w_down = line_gather(lax.dynamic_slice_in_dim(down_weight, r * piece, piece, 0))
 
     places = jnp.arange(length, dtype=jnp.int32)
     fresh = jnp.concatenate(
@@ -1129,15 +1372,15 @@
     query_places = own_places.reshape(steps, 1, QUERY_BLOCK)
     low = starts[:, 0, 0] // KEY_BLOCK
     high = query_places[:, 0, QUERY_BLOCK - 1] // KEY_BLOCK + 1
-    cosine, sine = rope_tables(own_positions)
 
     if plane_kernels:
-        wide_cosine = jnp.concatenate([cosine] * 4, axis=1)
-        wide_sine = jnp.concatenate([-sine, sine] * 2, axis=1)
+        wide_cosine, wide_sine = rope_tables(own_positions, 4)
+        wide_sine = wide_sine * jnp.where(jnp.arange(2 * HEAD_DIM) // (HEAD_DIM // 2) % 2, 1.0, -1.0)
         query, kv_rows, cot_all = project(hidden_in, w_qkv, wide_cosine, wide_sine, cotangent, 3)
         kv_rows = kv_rows.reshape(width, length, 2 * HEAD_DIM)
         cot_all = cot_all.reshape(all_tok, model)
     else:
+        cosine, sine = rope_tables(own_positions)
         qkv = dot(hidden_in, w_qkv)
         query = rotate(qkv[:, :qw].reshape(all_tok, heads, HEAD_DIM), cosine, sine, 1.0)
         query = query.astype(bf16).reshape(all_tok, qw)
@@ -1169,14 +1412,12 @@
 
     hidden_mid = plane_gather((normed_mid * gain_mid).astype(bf16), 2)
     if plane_kernels:
-        out_part, grad_hidden_mid, feed_part, down_part = feed_forward(
-            hidden_mid.reshape(width, tok, model),
-            cot_all.reshape(width, tok, model),
-            w_feed,
-            w_down,
-            5,
+        hidden_blocks = hidden_mid.reshape(width, tok, model)
+        cot_blocks = cot_all.reshape(width, tok, model)
+        acts, down_part = feed_in(hidden_blocks, cot_blocks, w_feed)
+        out_part, grad_hidden_mid, feed_part = feed_forward(
+            hidden_blocks, cot_blocks, acts, w_feed, w_down, 5
         )
-        out_part = out_part.reshape(all_tok, model)
     else:
         w_gate, w_up = w_feed[:, :hidden_units], w_feed[:, hidden_units:]
         gate_acc = dot(hidden_mid, w_gate)
@@ -1195,10 +1436,9 @@
         down_part = dot(inner_act, cot_all, 0, 0).astype(bf16)
         grad_hidden_part = dot(grad_gate, w_gate, 1, 1) + dot(grad_up, w_up, 1, 1)
         grad_hidden_mid = plane_scatter(grad_hidden_part.astype(bf16), 5)
-    feed_out = plane_scatter(out_part, 4)
-    activations = (middle + feed_out).astype(bf16)
+        feed_out = plane_scatter(out_part, 4)
+    down_rows = line_scatter(down_part)
     feed_rows = line_scatter(feed_part)
-    down_rows = line_scatter(down_part)
     gain_mid_term = jnp.sum(grad_hidden_mid * normed_mid, axis=0)
     grad_normed_mid = grad_hidden_mid * gain_mid
     grad_middle = cotangent.astype(f32) + scale_mid * (
@@ -1207,37 +1447,54 @@
 
     grad_branch = plane_gather(grad_middle.astype(bf16), 6)
     grad_mixed = dot(grad_branch, w_out, 1, 1).astype(bf16)
-    out_part = dot(mixed, grad_branch, 0, 0).astype(bf16)
-    out_rows = line_scatter(
-        lax.all_to_all(out_part, R, split_axis=1, concat_axis=0, tiled=True)
-    )
-
-    grad_mixed, feed_rows = lax.optimization_barrier((grad_mixed, feed_rows))
-    gq, gkv = attention_call(
-        attention_back_kernel,
-        heads,
-        low,
-        high,
-        common + [("tokens", grad_mixed), ("tokens", mixed), ("row", log_totals)],
-        [
-            ("tokens", jax.ShapeDtypeStruct((all_tok, qw), f32)),
-            ("sequence", jax.ShapeDtypeStruct((width, length, 2 * HEAD_DIM), bf16)),
-        ],
-        [pltpu.VMEM((length, 2 * HEAD_DIM), f32)],
-    )
+    w_out_part = dot(mixed, grad_branch, 0, 0).astype(bf16)
+
     if plane_kernels:
-        grad_qkv = return_keys(gkv, gq, wide_cosine, wide_sine, 10)
+        grad_qkv, feed_out, down_all, w_out_part = attention_back(
+            heads,
+            query,
+            kv_rows,
+            starts,
+            query_places,
+            grad_mixed,
+            mixed,
+            log_totals,
+            wide_cosine,
+            wide_sine,
+            out_part,
+            down_rows,
+            w_out_part,
+            10,
+        )
+        w_out_part = w_out_part.reshape(width * qw, model // width)
     else:
+        gq, gkv = attention_call(
+            attention_back_kernel,
+            heads,
+            low,
+            high,
+            common + [("tokens", grad_mixed), ("tokens", mixed), ("row", log_totals)],
+            [
+                ("tokens", jax.ShapeDtypeStruct((all_tok, qw), f32)),
+                ("sequence", jax.ShapeDtypeStruct((width, length, 2 * HEAD_DIM), bf16)),
+            ],
+            [pltpu.VMEM((length, 2 * HEAD_DIM), f32)],
+        )
         gkv = gkv.reshape(width, planes, tok, 2 * HEAD_DIM).transpose(1, 0, 2, 3)
         gkv = line_scatter(gkv.reshape(planes * all_tok, 2 * HEAD_DIM)).astype(f32)
         gq = rotate(gq.reshape(all_tok, heads, HEAD_DIM), cosine, sine, -1.0)
         gk = rotate(gkv[:, None, :HEAD_DIM], cosine, sine, -1.0)[:, 0]
         grad_qkv = jnp.concatenate([gq.reshape(all_tok, qw), gk, gkv[:, HEAD_DIM:]], axis=1)
         grad_qkv = grad_qkv.astype(bf16)
+        down_all = lax.all_gather(down_rows, R, axis=0, tiled=True)
+        w_out_part = lax.all_to_all(w_out_part, R, split_axis=1, concat_axis=0, tiled=True)
+    out_rows = line_scatter(w_out_part)
+    activations = (middle + feed_out).astype(bf16)
     hidden_part = dot(grad_qkv, w_qkv, 1, 1).astype(bf16)
-    hidden_part, down_rows = lax.optimization_barrier((hidden_part, down_rows))
+    qkv_part = dot(hidden_in, grad_qkv, 0, 0).astype(bf16)
+    hidden_part, qkv_part, feed_rows = lax.optimization_barrier((hidden_part, qkv_part, feed_rows))
+    qkv_rows = line_scatter(qkv_part)
     grad_hidden_in = plane_scatter(hidden_part, 7)
-    qkv_rows = line_scatter(dot(hidden_in, grad_qkv, 0, 0).astype(bf16))
     gain_in_term = jnp.sum(grad_hidden_in * normed_in, axis=0)
     grad_normed_in = grad_hidden_in * gain_in
     input_grad = (
@@ -1249,25 +1506,23 @@
         )
     ).astype(bf16)
 
-    gain_terms = lax.psum(
-        lax.psum_scatter(
-            jnp.stack([gain_in_term, gain_mid_term]), F, scatter_dimension=1, tiled=True
-        ),
-        R,
-    )
     rows = model // planes
-
-    def spread(x, call=None):
-        x = lax.all_gather(x, R, axis=0, tiled=True) if call is None else plane_gather(x, call, 2)
-        return x.reshape(width, x.shape[0] // width, x.shape[1])
-
-    down_grad = spread(down_rows).reshape(feed // planes, model).astype(f32)
+    feed_all = plane_gather(feed_rows, 4, 2).reshape((width,) + feed_rows.shape)
+    terms = jnp.stack([gain_in_term, gain_mid_term])
+    if plane_kernels:
+        terms = jnp.pad(terms.reshape(2, planes, rows).transpose(1, 0, 2), ((0, 0), (0, 6), (0, 0)))
+        qkv_all, out_all, gain_terms = finish(qkv_rows, out_rows, terms, 9)
+    else:
+        qkv_all = lax.all_gather(qkv_rows, R, axis=0, tiled=False)
+        out_all = lax.all_gather(out_rows, R, axis=0, tiled=False)
+        gain_terms = lax.psum(lax.psum_scatter(terms, F, scatter_dimension=1, tiled=True), R)
+    down_grad = down_all.reshape(feed // planes, model).astype(f32)
     gate_grad, up_grad = join_call(
-        functools.partial(join_feed_kernel, planes, piece), [spread(feed_rows)], [feed, feed]
+        functools.partial(join_feed_kernel, planes, piece), [feed_all], [feed, feed]
     )
     query_grad, key_grad, value_grad, out_grad = join_call(
         functools.partial(join_attention_kernel, width // KV_HEADS),
-        [spread(qkv_rows, 9), spread(out_rows, 8)],
+        [qkv_all, out_all],
         [width * qw, KV_HEADS * HEAD_DIM, KV_HEADS * HEAD_DIM, model],
     )
     return (

time: 824 us -> 733 us (0.89)
  waiting for transfers between devices: 118 us -> 0.19 us
  Pallas kernels: 530 us -> 609 us
  blocking collectives: 32.2 us -> 0 us
    pallas_call x1 -> x3, Pallas kernels: 55.1 us -> 202 us  [the longest x1 144 us: attention_back(): pl.pallas_call(functools.partial(back_kernel, chunks, heads), out_shape=[...]
    all_gather x2 -> x0, waiting for transfers between devices: 53.2 us -> none  [spread(): lax.all_gather(x, R, axis=0, tiled=True)]
    pallas_call x3 -> x2, Pallas kernels: 124 us -> 82.7 us  [plane_scatter(): pl.pallas_call(functools.partial(scatter_kernel, chunks), out_shape=jax.S...]
    reduce_scatter x4, waiting for transfers between devices: 39.6 us -> 0.01 us  [line_scatter(): return lax.psum_scatter(x, F, scatter_dimension=0, tiled=True)]
    all_gather x4 -> x3, waiting for transfers between devices: 23.7 us -> 0.06 us  [line_gather(): return lax.all_gather(x, F, axis=0, tiled=True)]
    all_to_all x1 -> x0, blocking collectives: 18.7 us -> none  [per_device(): lax.all_to_all(out_part, R, split_axis=1, concat_axis=0, tiled=True)]
    pallas_call x2 -> x1, Pallas kernels: 31.4 us -> 13 us  [attention_call(): pl.pallas_call(functools.partial(kernel, heads), grid_spec=pltpu.Prefetch...]
    pallas_call x1, Pallas kernels: 93.8 us -> 76 us  [feed_forward(): pl.pallas_call(functools.partial(feed_kernel, chunks), out_shape=[jax.Sha...]
  transfers between devices with their start and end apart: 12 -> 8, of which waited for: 3 -> 0; matrix products, arithmetic and copies ran while one was open for 10% -> 9% of each run, Pallas kernels for 52% -> 79%
where the time goes in v4:
time: 733 us; the launch traced here: 726 us
  Pallas kernels  609 us (83%)
  local copies, waits for them, and re-layouts  40.1 us (5%)
  matrix products  31.7 us (4%)
  other arithmetic  25.1 us (3%)
  between operations  14.9 us (2%)
    pallas_call x1, Pallas kernels, attention_back(): pl.pallas_call(functools.partial(back_kernel, chunks, heads), out_shape=[...  144 us
    pallas_call x3, Pallas kernels, plane_gather(): pl.pallas_call(functools.partial(gather_kernel, chunks), out_shape=jax.Sh...  130 us
    pallas_call x2, Pallas kernels, plane_scatter(): pl.pallas_call(functools.partial(scatter_kernel, chunks), out_shape=jax.S...  82.7 us
    pallas_call x1, Pallas kernels, feed_forward(): pl.pallas_call(functools.partial(feed_kernel, chunks), out_shape=[jax.Sha...  76 us
    pallas_call x1, Pallas kernels, enter(): pl.pallas_call(functools.partial(enter_kernel, chunks), out_shape=[jax.Sh...  45.7 us
    pallas_call x1, Pallas kernels, project(): pl.pallas_call(functools.partial(project_kernel, chunks), out_shape=[jax....  45.6 us
    dot_general x5, matrix products, dot(): lax.dot_general(a, b, (((ca,), (cb,)), ((), ())), preferred_element_type=...  31.7 us
    pallas_call x1, Pallas kernels, feed_in(): pl.pallas_call(feed_in_kernel, grid=(width + tiles,), out_shape=[jax.Shap...  29.7 us
  transfers between devices with their start and end apart: 8, of which 0 were waited for; matrix products, arithmetic and copies ran while one was open for 9% of the time, Pallas kernels for 79%

profile of v4, /device:TPU:0, one launch (start us, length us, event | category | flops | bytes accessed | tf_op | source)
XLA Modules:
  0.0 726.0 jit_solution(17773639610262376655)
XLA Ops:
  7.3 1.2 constant_dynamic-slice_fusion.10
  8.5 1.1 constant_dynamic-slice_fusion.9
  9.6 1.0 pad_maximum_fusion
  10.7 45.7 %shard_map.203 = (bf16[8,256,2048]{2,1,0:T(8,128)(2,1)S(1)}, f32[4,8,512]{2,1,0:T(8,128)S(1)}, s32[8,8,128]{2,1,0:T(8,128)S(1)}) custom-call(bf16[256,2048]{1,0:T(8,128)(2,1)S(1)} %copy-done.1, f32[8,512]{1,0:T(8,128)S(1)} %fusion.14.gains, s32[8,128]{1,0:T(8,128)S(1)} %bitcast.54), custom_call_target="tpu_custom_call" | custom-call | tf_op jit(solution)/shard_map/pallas_call | solution.py:977
  56.5 3.4 copy-done.11
  59.9 2.9 constant_dynamic-slice_fusion.1
  62.8 2.4 concatenate.12
  65.2 2.0 constant_dynamic-slice_fusion
  67.3 0.1 slice_compare_fusion
  67.4 0.1 select_bitcast_fusion
  67.5 2.3 reduce-window.6
  69.7 0.3 slice_reduce_fusion
  70.0 0.2 reduce-window.9
  70.2 0.1 maximum_bitcast_fusion
  70.4 0.4 slice_reduce_fusion.1
  70.9 0.4 slice_reduce_fusion.2
  71.3 1.2 slice-done
  72.5 1.3 copy.23
  73.8 3.6 all-to-all-start
  77.5 3.7 fusion.10
  81.2 2.3 slice.57.weight
  83.6 0.1 copy-done.4
  83.7 45.6 %shard_map.204 = (bf16[2048,256]{1,0:T(8,128)(2,1)S(1)}, bf16[8,4,256,128]{3,2,1,0:T(8,128)(2,1)S(1)}, bf16[8,256,2048]{2,1,0:T(8,128)(2,1)}) custom-call(bf16[2048,2048]{1,0:T(8,128)(2,1)} %bitcast.51, bf16[2048,384]{1,0:T(8,128)(2,1)S(1)} %slice.57.weight, f32[2048,128]{1,0:T(8,128)S(1)} %get-tuple-element.101.cosine, ...), custom_call_target="tpu_custom_call" | custom-call | tf_op jit(solution)/shard_map/pallas_call | solution.py:1000
  129.4 13.0 %shard_map.205 = (bf16[2048,256]{1,0:T(8,128)(2,1)S(1)}, f32[16,1,512]{2,1,0:T(1,128)S(1)}) custom-call(s32[16]{0:T(128)S(1)} %get-tuple-element.104.low, s32[16]{0:T(128)S(1)} %get-tuple-element.105.high, bf16[2048,256]{1,0:T(8,128)(2,1)S(1)} %get-tuple-element.47.q, bf16[8,1024,128]{2,1,0:T(8,128)(2,1)S(1)} %bitcast.49, s32[16,1,128]{2,1,0:T(1,128)S(1)} %fusion.22.starts, ...), custom_call_target="tpu_custom_call" | custom-call | tf_op jit(solution)/shard_map/pallas_call | solution.py:1241
  142.4 1.3 copy-done.10
  143.7 1.0 copy-done.12
  144.7 0.6 copy-done.18
  145.3 2.4 convolution_convert_fusion.1.part
  147.7 41.2 %shard_map.206 = f32[256,2048]{1,0:T(8,128)S(1)} custom-call(bf16[2048,2048]{1,0:T(8,128)(2,1)S(1)} %convolution_convert_fusion.1.part), custom_call_target="tpu_custom_call" | custom-call | tf_op jit(solution)/shard_map/pallas_call | solution.py:1110
  189.0 0.5 multiply_reduce_fusion.2
  189.5 1.3 copy-done.21
  190.8 1.2 multiply_convert_fusion.x
  192.0 38.9 %shard_map.207.hidden = bf16[8,256,2048]{2,1,0:T(8,128)(2,1)} custom-call(bf16[256,2048]{1,0:T(8,128)(2,1)} %multiply_convert_fusion.x), custom_call_target="tpu_custom_call" | custom-call | tf_op jit(solution)/shard_map/pallas_call | solution.py:1092
  231.0 29.7 %shard_map.208 = (f32[8,256,1408]{2,1,0:T(8,128)}, bf16[704,2048]{1,0:T(8,128)(2,1)S(1)}) custom-call(bf16[8,256,2048]{2,1,0:T(8,128)(2,1)} %shard_map.207.hidden, bf16[8,256,2048]{2,1,0:T(8,128)(2,1)} %get-tuple-element.51.cotangent, bf16[2048,1408]{1,0:T(8,128)(2,1)} %all-gather.6.cloned.1.call-done.w_feed), custom_call_target="tpu_custom_call" | custom-call | tf_op jit(solution)/shard_map/pallas_call | solution.py:570
  260.7 1.6 copy-done.14
  262.3 0.0 reduce-scatter.7.cloned.1.call-start
  262.4 76.0 %shard_map.209 = (bf16[8,256,2048]{2,1,0:T(8,128)(2,1)}, f32[256,2048]{1,0:T(8,128)}, bf16[2048,1408]{1,0:T(8,128)(2,1)}) custom-call(bf16[8,256,2048]{2,1,0:T(8,128)(2,1)} %shard_map.207.hidden, bf16[8,256,2048]{2,1,0:T(8,128)(2,1)} %get-tuple-element.51.cotangent, f32[8,256,1408]{2,1,0:T(8,128)} %get-tuple-element.54.acts, ...), custom_call_target="tpu_custom_call" | custom-call | tf_op jit(solution)/shard_map/pallas_call | solution.py:731
  338.4 0.4 reduce-scatter.11.cloned.1.call-start
  338.9 1.1 copy-done.22
  340.0 2.3 multiply_reduce_fusion
  342.4 0.3 copy-done.24
  342.6 1.6 fusion.24.x
  344.3 38.9 %shard_map.210 = bf16[8,256,2048]{2,1,0:T(8,128)(2,1)} custom-call(bf16[256,2048]{1,0:T(8,128)(2,1)} %fusion.24.x), custom_call_target="tpu_custom_call" | custom-call | tf_op jit(solution)/shard_map/pallas_call | solution.py:1092
  383.2 6.8 convolution_convert_fusion.4.grad
  390.1 3.3 convolution_convert_fusion.3.w_part
  393.4 144.0 %shard_map.211 = (bf16[2048,384]{1,0:T(8,128)(2,1)}, f32[256,2048]{1,0:T(8,128)}, bf16[8,176,2048]{2,1,0:T(8,128)(2,1)}, bf16[8,256,256]{2,1,0:T(8,128)(2,1)}) custom-call(bf16[2048,256]{1,0:T(8,128)(2,1)} %copy-done.12, bf16[8,1024,128]{2,1,0:T(8,128)(2,1)} %bitcast.50, s32[16,1,128]{2,1,0:T(1,128)} %copy-done.17, s32[16,1,128]{2,1,0:T(1,128)} %copy-done.16, ...), custom_call_target="tpu_custom_call" | custom-call | tf_op jit(solution)/shard_map/pallas_call | solution.py:946
  537.4 0.2 reduce-scatter.9.cloned.1.call-start
  537.7 10.0 %convolution_convert_fusion.part = bf16[2048,2048]{1,0:T(8,128)(2,1)} fusion(bf16[2048,384]{1,0:T(8,128)(2,1)} %get-tuple-element.61, bf16[2048,640]{1,0:T(8,128)(2,1)} %all-gather.4.cloned.1.call-done), kind=kOutput, calls=%fused_computation | convolution fusion | flops 3225419776 | bytes 11534336 | tf_op jit(solution)/shard_map/dot_general | solution.py:50
  547.6 9.2 %convolution_convert_fusion.2 = bf16[2048,384]{1,0:T(8,128)(2,1)} fusion(bf16[2048,2048]{1,0:T(8,128)(2,1)} %bitcast.52, bf16[2048,384]{1,0:T(8,128)(2,1)S(1)} %copy-done.31), kind=kOutput, calls=%fused_computation.9 | convolution fusion | flops 3222011904 | bytes 11534336 | tf_op jit(solution)/shard_map/dot_general | solution.py:50
  556.8 8.7 %bitcast_convert_fusion = f32[1408,2048]{1,0:T(8,128)} fusion(bf16[8,176,2048]{2,1,0:T(8,128)(2,1)} %get-tuple-element.76), kind=kLoop, calls=%fused_computation.2 | loop fusion | flops 2883584 | bytes 17301504 | tf_op jit(solution)/shard_map/convert_element_type | solution.py:1519
  565.5 3.4 copy-done.9
  568.9 41.4 %shard_map.212 = f32[256,2048]{1,0:T(8,128)S(1)} custom-call(bf16[2048,2048]{1,0:T(8,128)(2,1)S(1)} %copy-done.9), custom_call_target="tpu_custom_call" | custom-call | tf_op jit(solution)/shard_map/pallas_call | solution.py:1110
  610.3 52.6 %shard_map.215.x = bf16[8,512,1408]{2,1,0:T(8,128)(2,1)} custom-call(bf16[512,1408]{1,0:T(8,128)(2,1)} %reduce-scatter.7.cloned.1.call-done.x), custom_call_target="tpu_custom_call" | custom-call | tf_op jit(solution)/shard_map/pallas_call | solution.py:1092
  663.0 4.3 copy-done
  667.2 9.1 %shard_map.216 = (f32[512,5632]{1,0:T(8,128)}, f32[512,5632]{1,0:T(8,128)}) custom-call(bf16[8,512,1408]{2,1,0:T(8,128)(2,1)S(1)} %copy-done), custom_call_target="tpu_custom_call" | custom-call | tf_op jit(solution)/shard_map/pallas_call | solution.py:1280
  676.3 0.7 fusion.8
  677.0 0.6 pad.13.terms
  677.7 0.6 copy-done.23
  678.3 2.6 fusion.7
  680.9 28.4 %shard_map.213 = (bf16[8,512,384]{2,1,0:T(8,128)(2,1)}, bf16[8,512,256]{2,1,0:T(8,128)(2,1)}, f32[8,512]{1,0:T(8,128)}) custom-call(bf16[512,384]{1,0:T(8,128)(2,1)} %reduce-scatter.9.cloned.1.call-done.qkv, bf16[512,256]{1,0:T(8,128)(2,1)} %reduce-scatter.11.cloned.1.call-done.out_rows, f32[4,8,512]{2,1,0:T(8,128)} %pad.13.terms), custom_call_target="tpu_custom_call" | custom-call | tf_op jit(solution)/shard_map/pallas_call | solution.py:392
  709.2 1.4 fusion.25
  710.6 1.9 copy-done.13
  712.5 1.6 copy-done.15
  714.1 4.8 shard_map.214
  (90 shorter events, 0.7 us)
Async XLA Ops:
  7.2 3.5 copy-start.29
  7.2 3.5 copy-start.30
  7.2 3.5 copy-start.1
  7.2 3.5 copy-start.19
  7.2 64.1 %all-gather.4.cloned.1.call-start = ((), (), s32[]{:S(2)}) async-start(), calls=%async_computation.5 | async-start | bytes 3276800 | tf_op jit(solution)/shard_map/all_gather | solution.py:1136
  10.6 220.4 %all-gather.6.cloned.1.call-start = ((), (), s32[]{:S(2)}) async-start(), calls=%async_computation.6 | async-start | bytes 7208960 | tf_op jit(solution)/shard_map/all_gather | solution.py:1136
  56.5 3.4 copy-start.11
  65.2 197.2 %all-gather.8.cloned.1.call-start = ((), (), s32[]{:S(2)}) async-start(), calls=%async_computation.7 | async-start | bytes 3604480 | tf_op jit(solution)/shard_map/all_gather | solution.py:1136
  70.4 59.0 %copy-start.16 = (s32[16,1,128]{2,1,0:T(1,128)}, s32[16,1,128]{2,1,0:T(1,128)S(1)}, u32[]{:S(2)}) copy-start(s32[16,1,128]{2,1,0:T(1,128)S(1)} %fusion.15.places) | copy-start | bytes 24580
  70.8 58.5 %copy-start.17 = (s32[16,1,128]{2,1,0:T(1,128)}, s32[16,1,128]{2,1,0:T(1,128)S(1)}, u32[]{:S(2)}) copy-start(s32[16,1,128]{2,1,0:T(1,128)S(1)} %fusion.22.starts) | copy-start | bytes 24580
  71.3 1.2 slice-start
  73.8 71.5 %all-to-all-start = ((bf16[8,256,256]{1,2,0:T(8,128)(2,1)}), bf16[8,256,256]{1,2,0:T(8,128)(2,1)S(1)}, u32[]{:S(2)}, u32[]{:S(2)}) async-start(bf16[8,256,256]{1,2,0:T(8,128)(2,1)} %copy.23), calls=%async_computation | async-start | bytes 2097152 | tf_op jit(solution)/shard_map/all_to_all | solution.py:1337
  77.4 316.0 %reduce-scatter.5.cloned.1.call-start = ((), (), s32[]{:S(2)}) async-start(), calls=%async_computation.8 | async-start | bytes 3604480 | tf_op jit(solution)/shard_map/reduce_scatter | solution.py:1140
  81.2 48.1 %copy-start.7 = (f32[2048,128]{1,0:T(8,128)}, f32[2048,128]{1,0:T(8,128)S(1)}, u32[]{:S(2)}) copy-start(f32[2048,128]{1,0:T(8,128)S(1)} %get-tuple-element.100.sine) | copy-start | bytes 3145732
  81.2 48.1 %copy-start.8 = (f32[2048,128]{1,0:T(8,128)}, f32[2048,128]{1,0:T(8,128)S(1)}, u32[]{:S(2)}) copy-start(f32[2048,128]{1,0:T(8,128)S(1)} %get-tuple-element.101.cosine) | copy-start | bytes 3145732
  81.2 2.5 copy-start.4
  142.4 1.3 copy-start.10
  143.7 1.0 copy-start.12
  144.7 0.6 copy-start.18
  145.3 2.4 copy-start.2
  145.3 2.4 copy-start.26
  189.5 1.3 copy-start.21
  260.7 1.6 copy-start.14
  262.3 294.5 %reduce-scatter.7.cloned.1.call-start = ((), (), s32[]{:S(2)}) async-start(), calls=%async_computation.9 | async-start | bytes 7208960 | tf_op jit(solution)/shard_map/reduce_scatter | solution.py:1140
  338.4 1.6 copy-start.22
  338.4 342.4 %reduce-scatter.11.cloned.1.call-start = ((), (), s32[]{:S(2)}) async-start(), calls=%async_computation.11 | async-start | bytes 1310720 | tf_op jit(solution)/shard_map/reduce_scatter | solution.py:1140
  340.0 2.3 copy-start.5
  340.0 2.6 copy-start.24
  344.3 38.9 %copy-start.27 = (bf16[8,256,256]{1,2,0:T(8,128)(2,1)S(1)}, bf16[8,256,256]{1,2,0:T(8,128)(2,1)}, u32[]{:S(2)}) copy-start(bf16[8,256,256]{1,2,0:T(8,128)(2,1)} %copy-done.26) | copy-start | bytes 3145732
  383.2 6.9 copy-start.3
  383.2 6.9 copy-start.20
  537.4 143.4 %reduce-scatter.9.cloned.1.call-start = ((), (), s32[]{:S(2)}) async-start(), calls=%async_computation.10 | async-start | bytes 1966080 | tf_op jit(solution)/shard_map/reduce_scatter | solution.py:1140
  537.7 10.0 %copy-start.31 = (bf16[2048,384]{1,0:T(8,128)(2,1)S(1)}, bf16[2048,384]{1,0:T(8,128)(2,1)}, u32[]{:S(2)}) copy-start(bf16[2048,384]{1,0:T(8,128)(2,1)} %get-tuple-element.61) | copy-start | bytes 4718596
  565.5 3.4 copy-start.9
  663.0 4.3 copy-start
  667.2 10.4 %copy-start.25 = (f32[256,2048]{1,0:T(8,128)S(1)}, f32[256,2048]{1,0:T(8,128)}, u32[]{:S(2)}) copy-start(f32[256,2048]{1,0:T(8,128)} %get-tuple-element.56) | copy-start | bytes 6291460
  667.2 10.4 %copy-start.28 = (f32[256,2048]{1,0:T(8,128)S(1)}, f32[256,2048]{1,0:T(8,128)}, u32[]{:S(2)}) copy-start(f32[256,2048]{1,0:T(8,128)} %get-tuple-element.60) | copy-start | bytes 6291460
  676.3 1.3 copy-start.6
  676.3 1.9 copy-start.23
  710.6 1.9 copy-start.13
  712.5 1.6 copy-start.15
Sparse Core Ops, SparseCore 0:
  10.7 57.4 all-gather.3
  70.4 106.9 all-gather.5
  178.9 72.2 all-gather.7
  262.4 101.0 reduce-scatter.4
  365.7 120.4 reduce-scatter.6
  537.5 24.3 reduce-scatter.10
  565.0 33.9 reduce-scatter.8

commit v5 on v4

--- a/solution.py
+++ b/solution.py
@@ -78,59 +78,68 @@
         self.half = self.count // 2
         self.me = lax.axis_index(R)
         self.sibling, self.x, self.y = self.me + 1 - 2 * lax.rem(self.me, 2), self.me ^ 2, self.me ^ 4
-        self.across = self.me ^ 6
         self.sems = sems
-        self.copies = {}
-
-    def send(self, kind, i, owner, device):
+
+    def copy(self, kind, i):
+        first = i < self.half
+        owner, device = {
+            0: (self.me, self.x),
+            1: (self.me, self.y),
+            2: (self.x, self.y) if first else (self.y, self.x),
+            3: (self.me, self.sibling),
+            4: (self.x, self.sibling),
+            5: (self.y, self.sibling),
+            6: (self.me ^ 6, self.sibling),
+        }[kind]
         own, slot = self.items[i]
         sems = self.sems[2 * min(kind, 3) : 2 * min(kind, 3) + 2]
-        index = i if kind < 3 else (kind - 3, i)
-        src = own if owner is self.me else slot(owner)
-        copy = remote(src, slot(owner), sems, index, device)
-        copy.start()
-        self.copies[kind, i] = copy
+        src = own if kind in (0, 1, 3) else slot(owner)
+        return remote(src, slot(owner), sems, i if kind < 3 else (kind - 3, i), device)
 
     def start(self, kept=()):
         ready = [i for i in range(self.count) if i not in kept]
+        for n, i in enumerate(ready):
+            self.copy(0, i).start()
+            self.copy(1, ready[(n + self.half) % len(ready)]).start()
         for i in ready:
-            self.send(0, i, self.me, self.x)
-            self.send(1, ready[(ready.index(i) + self.half) % len(ready)], self.me, self.y)
-        for i in ready:
-            self.send(3, i, self.me, self.sibling)
-
-    def start_kept(self, kept):
-        for i in kept:
-            self.send(0, i, self.me, self.x)
-            self.send(1, i, self.me, self.y)
-            self.send(3, i, self.me, self.sibling)
+            self.copy(3, i).start()
+
+    def start_items(self, items):
+        for i in items:
+            for kind in (0, 1, 3):
+                self.copy(kind, i).start()
+
+    def pass_on(self, kind, i):
+        self.copy(kind, i).wait_recv()
+        if kind < 2 and (i < self.half) == (kind == 0):
+            self.copy(2, i).start()
+        self.copy(kind + 4, i).start()
 
     def relay(self, i):
-        j = (i + self.half) % self.count
-        self.copies[0, i].wait_recv()
-        if i < self.half:
-            self.send(2, i, self.x, self.y)
-        self.send(4, i, self.x, self.sibling)
-        self.copies[1, j].wait_recv()
-        if j >= self.half:
-            self.send(2, j, self.y, self.x)
-        self.send(5, j, self.y, self.sibling)
+        self.pass_on(0, i)
+        self.pass_on(1, (i + self.half) % self.count)
+
+    def far(self):
+        for i in range(self.half):
+            self.pass_on(2, i)
+            self.pass_on(2, self.half + i)
+        for i in range(2 * self.half, self.count):
+            self.pass_on(2, i)
+
+    def from_sibling(self, kind):
+        for i in range(self.count):
+            self.copy(kind, i).wait_recv()
+
+    def wait_sends(self):
+        for i in range(self.count):
+            for kind in range(7):
+                self.copy(kind, i).wait_send()
 
     def finish(self):
-        for i in range(self.half):
-            for j in (i, self.half + i):
-                if j < self.count and (2, j) in self.copies and (6, j) not in self.copies:
-                    self.copies[2, j].wait_recv()
-                    self.send(6, j, self.across, self.sibling)
-        for i in range(self.count):
-            if (6, i) not in self.copies:
-                self.copies[2, i].wait_recv()
-                self.send(6, i, self.across, self.sibling)
-        for (kind, _), copy in self.copies.items():
-            if kind < 3:
-                copy.wait_send()
-            else:
-                copy.wait()
+        self.far()
+        for kind in range(3, 7):
+            self.from_sibling(kind)
+        self.wait_sends()
 
 
 def row_items(x, out, chunks):
@@ -307,11 +316,13 @@
 
         @pl.when(z >= step)
         def _():
-            came(step).wait_recv()
-
-            @pl.when(z < planes - 1)
-            def _():
-                up(step).start()
+            arriving, leaving = came(step), up(step)
+            for i in range(count):
+                arriving.each[i].wait_recv()
+
+                @pl.when(z < planes - 1)
+                def _():
+                    leaving.each[i].start()
 
             across(step).start()
 
@@ -372,7 +383,7 @@
         total = total + at_planes[i]
     own_gain[...] = total
     all_gains[me] = total
-    gather.start_kept((last,))
+    gather.start_items((last,))
     for i in range(gather.count):
         gather.relay(i)
     gather.finish()
@@ -486,12 +497,10 @@
         part = self.part(j)
         return self.own[d, part].astype(jnp.float32) + self.sib[d, part].astype(jnp.float32)
 
-    def near_copies(self, j):
+    def near_copy(self, j, n):
         device, d = (self.x, 1) if j < self.half else (self.y, 2)
-        return [
-            remote(self.own.at[e, self.part(j)], self.got.at[j, n], self.near_sems, (j, n), device)
-            for n, e in enumerate((d, 3))
-        ]
+        src = self.own.at[3 if n else d, self.part(j)]
+        return remote(src, self.got.at[j, n], self.near_sems, (j, n), device)
 
     def far_copy(self, j):
         device, d = (self.y, 2) if j < self.half else (self.x, 1)
@@ -503,89 +512,240 @@
             self.total.at[slot], self.out.at[self.part(j)], self.out_sem.at[slot]
         )
 
-    def near(self, j):
-        for e in (1 if j < self.half else 2, 3):
-            self.own[e, self.part(j)] = self.summed(e, j).astype(jnp.bfloat16)
-        for copy in self.near_copies(j):
-            copy.start()
+    def near(self, j, n):
+        e = 3 if n else (1 if j < self.half else 2)
+        self.own[e, self.part(j)] = self.summed(e, j).astype(jnp.bfloat16)
+        self.near_copy(j, n).start()
+
+    def progress(self, i):
+        @pl.when(i == 2)
+        def _():
+            self.arrived(3)
+            for j in self.order:
+                self.near(j, 1)
+
+        @pl.when(i == 4)
+        def _():
+            self.arrived(2)
+            for j in range(self.half, self.chunks):
+                self.near(j, 0)
+
+        @pl.when(i == 6)
+        def _():
+            self.arrived(1)
+            for j in range(self.half):
+                self.near(j, 0)
 
     def far(self, j):
-        for copy in self.near_copies(j):
-            copy.wait_recv()
+        for n in (0, 1):
+            self.near_copy(j, n).wait_recv()
         d = 2 if j < self.half else 1
         passed = self.summed(d, j) + self.got[j, 1].astype(jnp.float32)
         self.own[d, self.part(j)] = passed.astype(jnp.bfloat16)
         self.far_copy(j).start()
 
-    def last(self, j):
+    def result(self, j):
         self.far_copy(j).wait_recv()
-        turn = self.order.index(j)
-        if turn >= 2:
-            self.out_copy(self.order[turn - 2]).wait()
-        self.total[turn % 2] = (
+        return (
             self.summed(0, j)
             + self.got[j, 0].astype(jnp.float32)
             + self.got_far[j].astype(jnp.float32)
         )
+
+    def last(self, j):
+        total = self.result(j)
+        turn = self.order.index(j)
+        if turn >= 2:
+            self.out_copy(self.order[turn - 2]).wait()
+        self.total[turn % 2] = total
         self.out_copy(j).start()
 
-    def finish(self):
+    def finish(self, written=True):
         if self.trades is None:
             self.trade(0).wait_send()
         else:
             for copy in self.trades.values():
                 copy.wait_send()
-        for j in self.order[-2:]:
-            self.out_copy(j).wait()
+        if written:
+            for j in self.order[-2:]:
+                self.out_copy(j).wait()
         for j in range(self.chunks):
             self.far_copy(j).wait_send()
-            for copy in self.near_copies(j):
-                copy.wait_send()
-
-
-def feed_in_kernel(hidden, cotangent, w_feed, acts, down_part, inner_turned):
-    width, _, tok = inner_turned.shape
+            for n in (0, 1):
+                self.near_copy(j, n).wait_send()
+
+
+def middle_kernel(
+    chunks, mixed, w_out, tokens, gain, w_feed, cotangent, middle, hidden, acts, down_part,
+    blocks, act_stage, inner_turned, column_in, down_stage, out_sems, act_sems, column_sems, down_sem, *refs,
+):
+    f32, bf16 = jnp.float32, jnp.bfloat16
+    width, tok, _ = blocks.shape
+    scatter = Scatter(middle, chunks, refs[:12])
+    me = scatter.me
+    size = tok // chunks
+
+    def item(j):
+        part = pl.ds(j * size, size)
+        return blocks.at[me, part], lambda owner: blocks.at[owner, part]
+
+    gather = Gather([item(j) for j in range(chunks)], refs[12:])
+    greet(scatter.sibling, scatter.x, scatter.y)
+
+    def branch(i, carry):
+        rows = pl.ds(pl.multiple_of(scatter.owner(i) * tok, tok), tok)
+        scatter.put(i, dot(mixed[rows, :], w_out[...]).astype(bf16))
+        scatter.progress(i)
+        return carry
+
+    lax.fori_loop(0, width, branch, 0)
+    scatter.arrived(0)
+    for j in scatter.order:
+        scatter.far(j)
+    for j in scatter.order:
+        part = pl.ds(j * size, size)
+        total = tokens[part, :].astype(f32) + scatter.result(j)
+        middle[part, :] = total
+        blocks[me, part] = (total * inverse_rms(total) * gain[...]).astype(bf16)
+        gather.start_items((j,))
+
+    def hidden_copy(i):
+        return pltpu.make_async_copy(blocks.at[me ^ i], hidden.at[me ^ i], out_sems.at[i])
+
+    def act_copy(i):
+        slot = lax.rem(i, 2)
+        return pltpu.make_async_copy(act_stage.at[slot], acts.at[me ^ i], act_sems.at[slot])
+
+    def block(i, carry):
+        @pl.when(i == 1)
+        def _():
+            gather.from_sibling(3)
+
+        @pl.when(i == 2)
+        def _():
+            for j in scatter.order:
+                gather.pass_on(0, j)
+                gather.pass_on(1, j)
+
+        @pl.when(i == 3)
+        def _():
+            gather.from_sibling(4)
+
+        @pl.when(i == 5)
+        def _():
+            gather.from_sibling(5)
+
+        @pl.when(i == 6)
+        def _():
+            for j in scatter.order:
+                gather.pass_on(2, j)
+
+        @pl.when(i == 7)
+        def _():
+            gather.from_sibling(6)
+
+        @pl.when(i >= 2)
+        def _():
+            act_copy(i - 2).wait()
+
+        acc = dot(blocks[me ^ i], w_feed[...])
+        act_stage[lax.rem(i, 2)] = acc
+        act_copy(i).start()
+        hidden_copy(i).start()
+        gate, up = acc[:, :units], acc[:, units:]
+        inner_turned[i] = (gate / (1.0 + jnp.exp(-gate)) * up).astype(bf16).T
+        return carry
+
     units = w_feed.shape[1] // 2
-    i = pl.program_id(0)
-
-    @pl.when(i < width)
-    def _():
-        acc = dot(hidden[0], w_feed[...])
-        acts[0] = acc
-        gate, up = acc[:, :units], acc[:, units:]
-        inner_turned[i] = (gate / (1.0 + jnp.exp(-gate)) * up).astype(jnp.bfloat16).T
-
-    @pl.when(i >= width)
-    def _():
-        acc = dot(inner_turned[0], cotangent[0])
-        for s in range(1, width):
-            acc = acc + dot(inner_turned[s], cotangent[s])
-        down_part[...] = acc.astype(jnp.bfloat16)
-
-
-def feed_in(hidden, cotangent, w_feed):
-    width, tok, model = hidden.shape
+    tiles = tokens.shape[1] // tok
+
+    def column_loads(n):
+        slot = lax.rem(n, 2)
+        part = pl.ds(pl.multiple_of(n * tok, tok), tok)
+        return [
+            pltpu.make_async_copy(
+                cotangent.at[me ^ i, :, part],
+                column_in.at[slot, pl.ds(i * tok, tok)],
+                column_sems.at[slot, i],
+            )
+            for i in range(width)
+        ]
+
+    def down_copy(n):
+        part = pl.ds(pl.multiple_of(n * tok, tok), tok)
+        slot = lax.rem(n, 2)
+        return pltpu.make_async_copy(down_stage.at[slot], down_part.at[:, part], down_sem.at[slot])
+
+    def down_tile(n, carry):
+        slot = lax.rem(n, 2)
+        for copy in column_loads(n):
+            copy.wait()
+
+        @pl.when(n >= 2)
+        def _():
+            down_copy(n - 2).wait()
+
+        acc = dot(inner_turned[0], column_in[slot, :tok])
+        for i in range(1, width):
+            acc = acc + dot(inner_turned[i], column_in[slot, i * tok : (i + 1) * tok])
+        down_stage[slot] = acc.astype(bf16)
+        down_copy(n).start()
+
+        @pl.when(n + 2 < tiles)
+        def _():
+            for copy in column_loads(n + 2):
+                copy.start()
+
+        return carry
+
+    for n in (0, 1):
+        for copy in column_loads(n):
+            copy.start()
+    lax.fori_loop(0, width, block, 0)
+    lax.fori_loop(0, tiles, down_tile, 0)
+    for n in (tiles - 2, tiles - 1):
+        down_copy(n).wait()
+    gather.wait_sends()
+    scatter.finish(False)
+    for i in (width - 2, width - 1):
+        act_copy(i).wait()
+    for i in range(width):
+        hidden_copy(i).wait()
+
+
+def middle_layer(mixed, w_out, tokens, gain, w_feed, cotangent, call, chunks=4):
+    width = lax.axis_size(R)
+    tok, model = tokens.shape
+    bf16, f32 = jnp.bfloat16, jnp.float32
     units = w_feed.shape[1] // 2
-    tiles = model // tok
+    vmem = pl.BlockSpec(memory_space=pltpu.VMEM)
     return pl.pallas_call(
-        feed_in_kernel,
-        grid=(width + tiles,),
+        functools.partial(middle_kernel, chunks),
         out_shape=[
-            jax.ShapeDtypeStruct((width, tok, 2 * units), jnp.float32),
-            jax.ShapeDtypeStruct((units, model), jnp.bfloat16),
+            jax.ShapeDtypeStruct((tok, model), f32),
+            jax.ShapeDtypeStruct((width, tok, model), bf16),
+            jax.ShapeDtypeStruct((width, tok, 2 * units), f32),
+            jax.ShapeDtypeStruct((units, model), bf16),
         ],
-        in_specs=[
-            pl.BlockSpec((1, tok, model), lambda i: (jnp.minimum(i, width - 1), 0, 0)),
-            pl.BlockSpec((width, tok, tok), lambda i: (0, 0, jnp.maximum(i - width, 0))),
-            pl.BlockSpec(memory_space=pltpu.VMEM),
-        ],
-        out_specs=[
-            pl.BlockSpec((1, tok, 2 * units), lambda i: (jnp.minimum(i, width - 1), 0, 0)),
-            pl.BlockSpec((units, tok), lambda i: (0, jnp.maximum(i - width, 0))),
-        ],
-        scratch_shapes=[pltpu.VMEM((width, units, tok), jnp.bfloat16)],
-        compiler_params=pltpu.CompilerParams(vmem_limit_bytes=48 << 20),
-    )(hidden, cotangent, w_feed)
+        in_specs=[vmem] * 5 + [ANY],
+        out_specs=[vmem, ANY, ANY, ANY],
+        scratch_shapes=[
+            pltpu.VMEM((width, tok, model), bf16),
+            pltpu.VMEM((2, tok, 2 * units), f32),
+            pltpu.VMEM((width, units, tok), bf16),
+            pltpu.VMEM((2, width * tok, tok), bf16),
+            pltpu.VMEM((2, units, tok), bf16),
+            DMA((width,)),
+            DMA((2,)),
+            DMA((2, width)),
+            DMA((2,)),
+        ]
+        + Scatter.scratch(tok, model, chunks)
+        + Gather.scratch(chunks),
+        compiler_params=pltpu.CompilerParams(
+            collective_id=call, has_side_effects=True, vmem_limit_bytes=56 << 20
+        ),
+    )(mixed, w_out, tokens, gain, w_feed, cotangent)
 
 
 def feed_kernel(
@@ -645,19 +805,7 @@
             for copy in loads(i + 2):
                 copy.start()
 
-        @pl.when(i == 4)
-        def _():
-            scatter.arrived(3)
-            scatter.arrived(2)
-            for j in second_half:
-                scatter.near(j)
-
-        @pl.when(i == 6)
-        def _():
-            scatter.arrived(1)
-            for j in first_half:
-                scatter.near(j)
-
+        scatter.progress(i)
         return carry
 
     tiles = model // tok
@@ -846,13 +994,15 @@
         return carry
 
     lax.fori_loop(0, width // 2, step, 0)
-    for d in (3, 2):
-        scatter.taken(d)
+    scatter.taken(3)
+    for j in scatter.order:
+        scatter.near(j, 1)
+    scatter.taken(2)
     for j in range(half, chunks):
-        scatter.near(j)
+        scatter.near(j, 0)
     scatter.taken(1)
     for j in range(half):
-        scatter.near(j)
+        scatter.near(j, 0)
     gather.start()
     lax.fori_loop(width // 2, width * parts, step, 0)
 
@@ -968,6 +1118,54 @@
             collective_id=call, has_side_effects=True, vmem_limit_bytes=60 << 20
         ),
     )(q, kv, starts, places, grad, mixed, log_total, cosine, sine, out_part, down_rows, w_part)
+
+
+def hidden_kernel(chunks, grad_qkv, weight, feed_rows, grad_hidden, all_feed, feed_sem, *refs):
+    bf16 = jnp.bfloat16
+    scatter = Scatter(grad_hidden, chunks, refs[:12])
+    gather = Gather(row_items(feed_rows, all_feed, chunks), refs[12:])
+    tok = grad_hidden.shape[0]
+    columns = grad_qkv.shape[1]
+    greet(scatter.sibling, scatter.x, scatter.y)
+    kept = pltpu.make_async_copy(feed_rows, all_feed.at[scatter.me], feed_sem)
+    kept.start()
+    gather.start()
+
+    def block(i, carry):
+        rows = pl.ds(pl.multiple_of(scatter.owner(i) * tok, tok), tok)
+        scatter.put(i, dot(grad_qkv[rows, :], weight[:, :columns], 1, 1).astype(bf16))
+        scatter.progress(i)
+        return carry
+
+    lax.fori_loop(0, grad_qkv.shape[0] // tok, block, 0)
+    scatter.arrived(0)
+    for i in range(chunks):
+        gather.relay(i)
+    for j in scatter.order:
+        scatter.far(j)
+    gather.finish()
+    for j in scatter.order:
+        scatter.last(j)
+    scatter.finish()
+    kept.wait()
+
+
+def scatter_hidden(grad_qkv, weight, feed_rows, tok, call, chunks=4):
+    width, model = lax.axis_size(R), weight.shape[0]
+    vmem = pl.BlockSpec(memory_space=pltpu.VMEM)
+    return pl.pallas_call(
+        functools.partial(hidden_kernel, chunks),
+        out_shape=[
+            jax.ShapeDtypeStruct((tok, model), jnp.float32),
+            jax.ShapeDtypeStruct((width,) + feed_rows.shape, jnp.bfloat16),
+        ],
+        in_specs=[vmem, vmem, ANY],
+        out_specs=[ANY, ANY],
+        scratch_shapes=[DMA] + Scatter.scratch(tok, model, chunks) + Gather.scratch(chunks),
+        compiler_params=pltpu.CompilerParams(
+            collective_id=call, has_side_effects=True, vmem_limit_bytes=40 << 20
+        ),
+    )(grad_qkv, weight, feed_rows)
 
 
 def enter(tokens, gains, ids, call, chunks=4):
@@ -1405,21 +1603,23 @@
             ("row", jax.ShapeDtypeStruct((steps, 1, heads * QUERY_BLOCK), f32)),
         ],
     )
-    branch = plane_scatter(dot(mixed, w_out).astype(bf16), 1)
-    middle = tok_float + branch
+    if plane_kernels:
+        cot_blocks = cot_all.reshape(width, tok, model)
+        middle, hidden_blocks, acts, down_part = middle_layer(
+            mixed, w_out, tokens, gain_mid[None], w_feed, cot_blocks, 1
+        )
+    else:
+        middle = tok_float + plane_scatter(dot(mixed, w_out).astype(bf16), 1)
     scale_mid = inverse_rms(middle)
     normed_mid = middle * scale_mid
 
-    hidden_mid = plane_gather((normed_mid * gain_mid).astype(bf16), 2)
     if plane_kernels:
-        hidden_blocks = hidden_mid.reshape(width, tok, model)
-        cot_blocks = cot_all.reshape(width, tok, model)
-        acts, down_part = feed_in(hidden_blocks, cot_blocks, w_feed)
         out_part, grad_hidden_mid, feed_part = feed_forward(
             hidden_blocks, cot_blocks, acts, w_feed, w_down, 5
         )
     else:
         w_gate, w_up = w_feed[:, :hidden_units], w_feed[:, hidden_units:]
+        hidden_mid = plane_gather((normed_mid * gain_mid).astype(bf16), 2)
         gate_acc = dot(hidden_mid, w_gate)
         up_acc = dot(hidden_mid, w_up)
         gate_sig = jax.nn.sigmoid(gate_acc)
@@ -1490,11 +1690,14 @@
         w_out_part = lax.all_to_all(w_out_part, R, split_axis=1, concat_axis=0, tiled=True)
     out_rows = line_scatter(w_out_part)
     activations = (middle + feed_out).astype(bf16)
-    hidden_part = dot(grad_qkv, w_qkv, 1, 1).astype(bf16)
     qkv_part = dot(hidden_in, grad_qkv, 0, 0).astype(bf16)
-    hidden_part, qkv_part, feed_rows = lax.optimization_barrier((hidden_part, qkv_part, feed_rows))
+    grad_qkv, qkv_part, feed_rows = lax.optimization_barrier((grad_qkv, qkv_part, feed_rows))
     qkv_rows = line_scatter(qkv_part)
-    grad_hidden_in = plane_scatter(hidden_part, 7)
+    if plane_kernels:
+        grad_hidden_in, feed_all = scatter_hidden(grad_qkv, w_attention, feed_rows, tok, 7)
+    else:
+        grad_hidden_in = plane_scatter(dot(grad_qkv, w_qkv, 1, 1).astype(bf16), 7)
+        feed_all = lax.all_gather(feed_rows, R, axis=0, tiled=False)
     gain_in_term = jnp.sum(grad_hidden_in * normed_in, axis=0)
     grad_normed_in = grad_hidden_in * gain_in
     input_grad = (
@@ -1507,7 +1710,6 @@
     ).astype(bf16)
 
     rows = model // planes
-    feed_all = plane_gather(feed_rows, 4, 2).reshape((width,) + feed_rows.shape)
     terms = jnp.stack([gain_in_term, gain_mid_term])
     if plane_kernels:
         terms = jnp.pad(terms.reshape(2, planes, rows).transpose(1, 0, 2), ((0, 0), (0, 6), (0, 0)))

time: 733 us -> 679 us (0.926)
  Pallas kernels: 609 us -> 543 us
  waiting for transfers between devices: 0.19 us -> 29.2 us
  matrix products: 31.7 us -> 20 us
    pallas_call x3 -> x1, Pallas kernels: 130 us -> 38.4 us  [plane_gather(): pl.pallas_call(functools.partial(gather_kernel, chunks), out_shape=jax.Sh...]
    pallas_call x3 -> x2, Pallas kernels: 112 us -> 179 us  [the longest x1 94.5 us: middle_layer(): pl.pallas_call(functools.partial(middle_kernel, chunks), out_shape=[jax.S...]
    pallas_call x1, Pallas kernels: 144 us -> 112 us  [attention_back(): pl.pallas_call(functools.partial(back_kernel, chunks, heads), out_shape=[...]
    all_gather x3, waiting for transfers between devices: 0.06 us -> 29.1 us  [line_gather(): return lax.all_gather(x, F, axis=0, tiled=True)]
    dot_general x5 -> x3, matrix products: 31.7 us -> 20 us  [dot(): lax.dot_general(a, b, (((ca,), (cb,)), ((), ())), preferred_element_type=...]
    pallas_call x1, Pallas kernels: 76 us -> 68.2 us  [feed_forward(): pl.pallas_call(functools.partial(feed_kernel, chunks), out_shape=[jax.Sha...]
  transfers between devices with their start and end apart: 8 -> 8, of which waited for: 0 -> 1; matrix products, arithmetic and copies ran while one was open for 9% -> 8% of each run, Pallas kernels for 79% -> 76%
where the time goes in v5:
time: 679 us; the launch traced here: 672 us
  Pallas kernels  543 us (80%)
  local copies, waits for them, and re-layouts  36.5 us (5%)
  waiting for transfers between devices  29.2 us (4%)
  other arithmetic  22.4 us (3%)
  matrix products  20 us (3%)
  between operations  14.9 us (2%)
    pallas_call x1, Pallas kernels, attention_back(): pl.pallas_call(functools.partial(back_kernel, chunks, heads), out_shape=[...  112 us
    pallas_call x1, Pallas kernels, middle_layer(): pl.pallas_call(functools.partial(middle_kernel, chunks), out_shape=[jax.S...  94.5 us
    pallas_call x1, Pallas kernels, scatter_hidden(): pl.pallas_call(functools.partial(hidden_kernel, chunks), out_shape=[jax.S...  84.7 us
    pallas_call x1, Pallas kernels, feed_forward(): pl.pallas_call(functools.partial(feed_kernel, chunks), out_shape=[jax.Sha...  68.2 us
    pallas_call x1, Pallas kernels, enter(): pl.pallas_call(functools.partial(enter_kernel, chunks), out_shape=[jax.Sh...  45.7 us
    pallas_call x1, Pallas kernels, project(): pl.pallas_call(functools.partial(project_kernel, chunks), out_shape=[jax....  45.5 us
    pallas_call x1, Pallas kernels, plane_gather(): pl.pallas_call(functools.partial(gather_kernel, chunks), out_shape=jax.Sh...  38.4 us
    all_gather x3, waiting for transfers between devices, line_gather(): return lax.all_gather(x, F, axis=0, tiled=True)  29.1 us
  transfers between devices with their start and end apart: 8, of which 1 were waited for; matrix products, arithmetic and copies ran while one was open for 8% of the time, Pallas kernels for 76%

profile of v5, /device:TPU:0, one launch (start us, length us, event | category | flops | bytes accessed | tf_op | source)
XLA Modules:
  0.0 671.9 jit_solution(4754538351564281970)
XLA Ops:
  7.2 0.0 all-gather.4.cloned.1.call-start
  7.3 1.2 constant_dynamic-slice_fusion.10
  8.5 1.1 constant_dynamic-slice_fusion.9
  9.6 1.0 pad_maximum_fusion
  10.6 0.0 all-gather.6.cloned.1.call-start
  10.7 45.7 %shard_map.203 = (bf16[8,256,2048]{2,1,0:T(8,128)(2,1)S(1)}, f32[4,8,512]{2,1,0:T(8,128)S(1)}, s32[8,8,128]{2,1,0:T(8,128)S(1)}) custom-call(bf16[256,2048]{1,0:T(8,128)(2,1)S(1)} %copy-done, f32[8,512]{1,0:T(8,128)S(1)} %fusion.14.gains, s32[8,128]{1,0:T(8,128)S(1)} %bitcast.52), custom_call_target="tpu_custom_call" | custom-call | tf_op jit(solution)/shard_map/pallas_call | solution.py:1175
  56.5 3.4 copy-done.12
  59.9 2.9 constant_dynamic-slice_fusion.1
  62.8 2.4 concatenate.12
  65.2 0.0 all-gather.8.cloned.1.call-start
  65.2 2.1 constant_dynamic-slice_fusion
  67.3 0.1 slice_compare_fusion
  67.4 0.1 select_bitcast_fusion
  67.5 2.3 reduce-window.6
  69.8 0.3 slice_reduce_fusion
  70.1 0.2 reduce-window.9
  70.2 0.1 maximum_bitcast_fusion
  70.5 0.4 slice_reduce_fusion.2
  70.8 0.5 slice_reduce_fusion.1
  71.3 0.0 all-gather.4.cloned.1.call-done.weight
  71.3 2.3 slice.61
  73.6 4.5 all-to-all-start
  78.1 0.0 reduce-scatter.5.cloned.1.call-start
  78.2 0.6 fusion.25
  78.8 3.7 fusion.10
  82.6 0.2 slice.60.weight
  82.8 1.8 copy-done.7
  84.6 45.5 %shard_map.204 = (bf16[2048,256]{1,0:T(8,128)(2,1)S(1)}, bf16[8,4,256,128]{3,2,1,0:T(8,128)(2,1)S(1)}, bf16[8,256,2048]{2,1,0:T(8,128)(2,1)}) custom-call(bf16[2048,2048]{1,0:T(8,128)(2,1)} %bitcast.49, bf16[2048,384]{1,0:T(8,128)(2,1)S(1)} %slice.60.weight, f32[2048,128]{1,0:T(8,128)S(1)} %get-tuple-element.106.cosine, ...), custom_call_target="tpu_custom_call" | custom-call | tf_op jit(solution)/shard_map/pallas_call | solution.py:1198
  130.1 13.0 %shard_map.205 = (bf16[2048,256]{1,0:T(8,128)(2,1)S(1)}, f32[16,1,512]{2,1,0:T(1,128)S(1)}) custom-call(s32[16]{0:T(128)S(1)} %get-tuple-element.109.low, s32[16]{0:T(128)S(1)} %get-tuple-element.110.high, bf16[2048,256]{1,0:T(8,128)(2,1)S(1)} %get-tuple-element.51.q, bf16[8,1024,128]{2,1,0:T(8,128)(2,1)S(1)} %bitcast.47, s32[16,1,128]{2,1,0:T(1,128)S(1)} %fusion.22.starts, ...), custom_call_target="tpu_custom_call" | custom-call | tf_op jit(solution)/shard_map/pallas_call | solution.py:1439
  143.1 1.0 copy-done.2
  144.1 1.3 copy-done.11
  145.4 0.6 copy-done.20
  146.0 2.3 copy.25
  148.4 29.0 %all-gather.6.cloned.1.call-done.w_feed = bf16[2048,1408]{1,0:T(8,128)(2,1)} async-done(((bf16[512,1408]{1,0:T(8,128)(2,1)}), bf16[2048,1408]{1,0:T(8,128)(2,1)}) %all-gather.6.cloned.1.call-update) | async-done | bytes 5767184 | tf_op jit(solution)/shard_map/all_gather | solution.py:1334
  177.4 94.5 %shard_map.206 = (f32[256,2048]{1,0:T(8,128)}, bf16[8,256,2048]{2,1,0:T(8,128)(2,1)}, f32[8,256,1408]{2,1,0:T(8,128)}, bf16[704,2048]{1,0:T(8,128)(2,1)}) custom-call(bf16[2048,256]{1,0:T(8,128)(2,1)} %copy-done.2, bf16[256,2048]{1,0:T(8,128)(2,1)} %bitcast.56, bf16[256,2048]{1,0:T(8,128)(2,1)} %tokens.3, f32[1,2048]{1,0:T(1,128)} %bitcast.60, ...), custom_call_target="tpu_custom_call" | custom-call | tf_op jit(solution)/shard_map/pallas_call | solution.py:722
  271.9 0.0 reduce-scatter.7.cloned.1.call-start
  272.0 68.2 %shard_map.207 = (bf16[8,256,2048]{2,1,0:T(8,128)(2,1)}, f32[256,2048]{1,0:T(8,128)}, bf16[2048,1408]{1,0:T(8,128)(2,1)}) custom-call(bf16[8,256,2048]{2,1,0:T(8,128)(2,1)} %get-tuple-element.59.hidden, bf16[8,256,2048]{2,1,0:T(8,128)(2,1)} %get-tuple-element.57.cotangent, f32[8,256,1408]{2,1,0:T(8,128)} %get-tuple-element.60.acts, ...), custom_call_target="tpu_custom_call" | custom-call | tf_op jit(solution)/shard_map/pallas_call | solution.py:879
  340.3 0.5 reduce-scatter.11.cloned.1.call-start
  340.8 1.0 copy-done.23
  341.8 0.2 multiply_reduce_fusion.2
  342.0 0.6 copy-done.25
  342.6 0.7 multiply_reduce_fusion
  343.3 0.5 copy-done.8
  343.8 1.6 fusion.23.x
  345.5 38.4 %shard_map.208 = bf16[8,256,2048]{2,1,0:T(8,128)(2,1)} custom-call(bf16[256,2048]{1,0:T(8,128)(2,1)} %fusion.23.x), custom_call_target="tpu_custom_call" | custom-call | tf_op jit(solution)/shard_map/pallas_call | solution.py:1290
  383.9 7.0 %convolution_convert_fusion.1.w_part = bf16[256,2048]{1,0:T(8,128)(2,1)} fusion(bf16[2048,256]{1,0:T(8,128)(2,1)S(1)} %copy-done.3, bf16[2048,2048]{1,0:T(8,128)(2,1)} %bitcast.53), kind=kOutput, calls=%fused_computation.7 | convolution fusion | flops 2148007936 | bytes 10485760 | tf_op jit(solution)/shard_map/dot_general | solution.py:50
  390.9 3.4 convolution_convert_fusion.2.grad
  394.2 111.9 %shard_map.209 = (bf16[2048,384]{1,0:T(8,128)(2,1)}, f32[256,2048]{1,0:T(8,128)}, bf16[8,176,2048]{2,1,0:T(8,128)(2,1)}, bf16[8,256,256]{2,1,0:T(8,128)(2,1)}) custom-call(bf16[2048,256]{1,0:T(8,128)(2,1)} %copy-done.13, bf16[8,1024,128]{2,1,0:T(8,128)(2,1)} %bitcast.48, s32[16,1,128]{2,1,0:T(1,128)} %copy-done.19, s32[16,1,128]{2,1,0:T(1,128)} %copy-done.18, ...), custom_call_target="tpu_custom_call" | custom-call | tf_op jit(solution)/shard_map/pallas_call | solution.py:1096
  506.2 0.2 reduce-scatter.9.cloned.1.call-start
  506.4 0.3 fusion.9
  506.7 9.7 %convolution_convert_fusion = bf16[2048,384]{1,0:T(8,128)(2,1)} fusion(bf16[2048,2048]{1,0:T(8,128)(2,1)} %bitcast.50, bf16[2048,384]{1,0:T(8,128)(2,1)} %get-tuple-element.69.grad_qkv), kind=kOutput, calls=%fused_computation.1 | convolution fusion | flops 3222011904 | bytes 11534336 | tf_op jit(solution)/shard_map/dot_general | solution.py:50
  516.5 8.9 %bitcast_convert_fusion = f32[1408,2048]{1,0:T(8,128)} fusion(bf16[8,176,2048]{2,1,0:T(8,128)(2,1)} %get-tuple-element.84), kind=kLoop, calls=%fused_computation | loop fusion | flops 2883584 | bytes 17301504 | tf_op jit(solution)/shard_map/convert_element_type | solution.py:1721
  525.4 84.7 %shard_map.210 = (f32[256,2048]{1,0:T(8,128)S(1)}, bf16[8,512,1408]{2,1,0:T(8,128)(2,1)}) custom-call(bf16[2048,384]{1,0:T(8,128)(2,1)S(1)} %copy-done.16, bf16[2048,640]{1,0:T(8,128)(2,1)S(1)} %copy-done.6, bf16[512,1408]{1,0:T(8,128)(2,1)S(1)} %copy-done.17), custom_call_target="tpu_custom_call" | custom-call | tf_op jit(solution)/shard_map/pallas_call | solution.py:1156
  610.1 4.3 copy-done.4
  614.3 9.1 %shard_map.213 = (f32[512,5632]{1,0:T(8,128)}, f32[512,5632]{1,0:T(8,128)}) custom-call(bf16[8,512,1408]{2,1,0:T(8,128)(2,1)S(1)} %copy-done.4), custom_call_target="tpu_custom_call" | custom-call | tf_op jit(solution)/shard_map/pallas_call | solution.py:1478
  623.4 0.7 fusion.8
  624.1 0.6 pad.13.terms
  624.8 0.3 copy-done.24
  625.0 2.5 fusion.7
  627.6 27.6 %shard_map.211 = (bf16[8,512,384]{2,1,0:T(8,128)(2,1)}, bf16[8,512,256]{2,1,0:T(8,128)(2,1)}, f32[8,512]{1,0:T(8,128)}) custom-call(bf16[512,384]{1,0:T(8,128)(2,1)} %reduce-scatter.9.cloned.1.call-done.qkv, bf16[512,256]{1,0:T(8,128)(2,1)} %reduce-scatter.11.cloned.1.call-done.out_rows, f32[4,8,512]{2,1,0:T(8,128)} %pad.13.terms), custom_call_target="tpu_custom_call" | custom-call | tf_op jit(solution)/shard_map/pallas_call | solution.py:403
  655.1 1.4 fusion.24
  656.5 1.9 copy-done.14
  658.4 1.6 copy-done.15
  660.0 4.8 shard_map.212
  (84 shorter events, 0.4 us)
Async XLA Ops:
  7.2 3.5 copy-start.30
  7.2 3.5 copy-start.31
  7.2 3.5 copy-start.21
  7.2 3.5 copy-start
  7.2 64.1 %all-gather.4.cloned.1.call-start = ((), (), s32[]{:S(2)}) async-start(), calls=%async_computation.5 | async-start | bytes 3276800 | tf_op jit(solution)/shard_map/all_gather | solution.py:1334
  10.6 166.8 %all-gather.6.cloned.1.call-start = ((), (), s32[]{:S(2)}) async-start(), calls=%async_computation.6 | async-start | bytes 7208960 | tf_op jit(solution)/shard_map/all_gather | solution.py:1334
  56.5 3.4 copy-start.12
  65.2 206.8 %all-gather.8.cloned.1.call-start = ((), (), s32[]{:S(2)}) async-start(), calls=%async_computation.7 | async-start | bytes 3604480 | tf_op jit(solution)/shard_map/all_gather | solution.py:1334
  70.4 59.7 %copy-start.18 = (s32[16,1,128]{2,1,0:T(1,128)}, s32[16,1,128]{2,1,0:T(1,128)S(1)}, u32[]{:S(2)}) copy-start(s32[16,1,128]{2,1,0:T(1,128)S(1)} %fusion.15.places) | copy-start | bytes 24580
  70.5 59.6 %copy-start.19 = (s32[16,1,128]{2,1,0:T(1,128)}, s32[16,1,128]{2,1,0:T(1,128)S(1)}, u32[]{:S(2)}) copy-start(s32[16,1,128]{2,1,0:T(1,128)S(1)} %fusion.22.starts) | copy-start | bytes 24580
  73.6 8.9 %copy-start.5 = (bf16[2048,640]{1,0:T(8,128)(2,1)S(1)}, bf16[2048,640]{1,0:T(8,128)(2,1)}, u32[]{:S(2)}) copy-start(bf16[2048,640]{1,0:T(8,128)(2,1)} %all-gather.4.cloned.1.call-done.weight) | copy-start | bytes 7864324
  73.6 72.4 %all-to-all-start = ((bf16[8,256,256]{2,1,0:T(8,128)(2,1)}), bf16[8,256,256]{2,1,0:T(8,128)(2,1)}, u32[]{:S(2)}, u32[]{:S(2)}) async-start(bf16[8,256,256]{2,1,0:T(8,128)(2,1)} %bitcast.55), calls=%async_computation | async-start | bytes 2097152 | tf_op jit(solution)/shard_map/all_to_all | solution.py:1535
  78.1 316.1 %reduce-scatter.5.cloned.1.call-start = ((), (), s32[]{:S(2)}) async-start(), calls=%async_computation.8 | async-start | bytes 3604480 | tf_op jit(solution)/shard_map/reduce_scatter | solution.py:1338
  82.6 47.5 %copy-start.9 = (f32[2048,128]{1,0:T(8,128)}, f32[2048,128]{1,0:T(8,128)S(1)}, u32[]{:S(2)}) copy-start(f32[2048,128]{1,0:T(8,128)S(1)} %get-tuple-element.105.sine) | copy-start | bytes 3145732
  82.6 47.5 %copy-start.10 = (f32[2048,128]{1,0:T(8,128)}, f32[2048,128]{1,0:T(8,128)S(1)}, u32[]{:S(2)}) copy-start(f32[2048,128]{1,0:T(8,128)S(1)} %get-tuple-element.106.cosine) | copy-start | bytes 3145732
  82.6 2.0 copy-start.7
  130.1 18.3 %copy-start.13 = (bf16[2048,256]{1,0:T(8,128)(2,1)}, bf16[2048,256]{1,0:T(8,128)(2,1)S(1)}, u32[]{:S(2)}) copy-start(bf16[2048,256]{1,0:T(8,128)(2,1)S(1)} %get-tuple-element.51.q) | copy-start | bytes 3145732
  143.1 1.0 copy-start.2
  144.1 1.3 copy-start.11
  145.4 0.6 copy-start.20
  271.9 244.5 %reduce-scatter.7.cloned.1.call-start = ((), (), s32[]{:S(2)}) async-start(), calls=%async_computation.9 | async-start | bytes 7208960 | tf_op jit(solution)/shard_map/reduce_scatter | solution.py:1338
  340.2 1.6 copy-start.23
  340.2 1.8 copy-start.29
  340.3 287.3 %reduce-scatter.11.cloned.1.call-start = ((), (), s32[]{:S(2)}) async-start(), calls=%async_computation.11 | async-start | bytes 1310720 | tf_op jit(solution)/shard_map/reduce_scatter | solution.py:1338
  340.8 1.8 copy-start.25
  342.6 1.2 copy-start.8
  345.5 38.4 %copy-start.3 = (bf16[2048,256]{1,0:T(8,128)(2,1)S(1)}, bf16[2048,256]{1,0:T(8,128)(2,1)}, u32[]{:S(2)}) copy-start(bf16[2048,256]{1,0:T(8,128)(2,1)} %copy-done.2) | copy-start | bytes 3145732
  383.9 7.0 %copy-start.22 = (bf16[8,256,2048]{2,1,0:T(8,128)(2,1)S(1)}, bf16[8,256,2048]{2,1,0:T(8,128)(2,1)}, u32[]{:S(2)}) copy-start(bf16[8,256,2048]{2,1,0:T(8,128)(2,1)} %shard_map.208) | copy-start | bytes 25165828
  383.9 7.0 %copy-start.27 = (bf16[8,32,8,256]{3,2,0,1:T(8,128)(2,1)S(1)}, bf16[8,32,8,256]{3,2,0,1:T(8,128)(2,1)}, u32[]{:S(2)}) copy-start(bf16[8,32,8,256]{3,2,0,1:T(8,128)(2,1)} %copy.25) | copy-start | bytes 3145732
  394.2 112.2 %copy-start.1 = (bf16[256,2048]{1,0:T(8,128)(2,1)S(1)}, bf16[256,2048]{1,0:T(8,128)(2,1)}, u32[]{:S(2)}) copy-start(bf16[256,2048]{1,0:T(8,128)(2,1)} %tokens.3) | copy-start | bytes 3145732
  506.2 121.4 %reduce-scatter.9.cloned.1.call-start = ((), (), s32[]{:S(2)}) async-start(), calls=%async_computation.10 | async-start | bytes 1966080 | tf_op jit(solution)/shard_map/reduce_scatter | solution.py:1338
  516.5 8.9 %copy-start.6 = (bf16[2048,640]{1,0:T(8,128)(2,1)S(1)}, bf16[2048,640]{1,0:T(8,128)(2,1)}, u32[]{:S(2)}) copy-start(bf16[2048,640]{1,0:T(8,128)(2,1)} %all-gather.4.cloned.1.call-done.weight) | copy-start | bytes 7864324
  516.5 8.9 %copy-start.16 = (bf16[2048,384]{1,0:T(8,128)(2,1)S(1)}, bf16[2048,384]{1,0:T(8,128)(2,1)}, u32[]{:S(2)}) copy-start(bf16[2048,384]{1,0:T(8,128)(2,1)} %get-tuple-element.69.grad_qkv) | copy-start | bytes 4718596
  516.5 8.9 %copy-start.17 = (bf16[512,1408]{1,0:T(8,128)(2,1)S(1)}, bf16[512,1408]{1,0:T(8,128)(2,1)}, u32[]{:S(2)}) copy-start(bf16[512,1408]{1,0:T(8,128)(2,1)} %reduce-scatter.7.cloned.1.call-done.feed_rows) | copy-start | bytes 4325380
  610.0 4.3 copy-start.4
  614.3 10.4 %copy-start.26 = (f32[256,2048]{1,0:T(8,128)S(1)}, f32[256,2048]{1,0:T(8,128)}, u32[]{:S(2)}) copy-start(f32[256,2048]{1,0:T(8,128)} %get-tuple-element.62) | copy-start | bytes 6291460
  614.3 10.4 %copy-start.28 = (f32[256,2048]{1,0:T(8,128)S(1)}, f32[256,2048]{1,0:T(8,128)}, u32[]{:S(2)}) copy-start(f32[256,2048]{1,0:T(8,128)} %get-tuple-element.66) | copy-start | bytes 6291460
  623.4 1.6 copy-start.24
  656.5 1.9 copy-start.14
  658.4 1.6 copy-start.15
Sparse Core Ops, SparseCore 0:
  10.7 57.4 all-gather.3
  70.4 106.9 all-gather.5
  179.0 72.2 all-gather.7
  272.0 68.1 reduce-scatter.4
  342.4 113.9 reduce-scatter.6
  506.3 24.4 reduce-scatter.10
  533.8 33.9 reduce-scatter.8

commit v6 on v5

--- a/solution.py
+++ b/solution.py
@@ -235,8 +235,9 @@
 
 
 def project_kernel(
-    chunks, hidden, weight, cosine, sine, cotangent, query, kv, cot_all,
-    own, own_sem, cot_sem, to_line, at_line, to_sib, at_sib, *sems,
+    chunks, hidden, weight, cosine, sine, cotangent, w_cols, query, kv, cot_all, w_out,
+    own, hidden_in, hidden_sems, own_sem, cot_sem, w_sem, to_all, at_all, to_line, at_line, to_sib, at_sib,
+    *sems,
 ):
     bf16 = jnp.bfloat16
     planes = kv.shape[1]
@@ -248,20 +249,50 @@
     core = lax.rem(gather.me, 2)
     mine = pl.ds(core * count, count)
     above, below = lax.rem(z + 1, planes), lax.rem(z + planes - 1, planes)
+    me = gather.me
+    peers = [me ^ distance for distance in range(1, width)]
+
+    def hidden_load(i):
+        slot = lax.rem(i, 2)
+        block = hidden.at[lax.rem(core * count + i, width)]
+        return pltpu.make_async_copy(block, hidden_in.at[slot], hidden_sems.at[slot])
+
+    for i in (0, 1):
+        hidden_load(i).start()
     barrier = pltpu.get_barrier_semaphore()
     for other in (above, below):
         pl.semaphore_signal(barrier, inc=1, device_id={F: other}, device_id_type=MESH)
-    for device in (gather.sibling, gather.x, gather.y):
+    for device in peers:
         pl.semaphore_signal(barrier, inc=1, device_id={R: device}, device_id_type=MESH)
-    pl.semaphore_wait(barrier, 5)
+    pl.semaphore_wait(barrier, 1 + width)
+    rows = w_out.shape[0]
+    share = w_out.shape[1] // width
+    to = w_out.at[:, pl.ds(pl.multiple_of(me * share, share), share)]
+
+    def rows_of(device):
+        part = pl.ds(pl.multiple_of(device * rows, rows), rows)
+        return w_cols.at[part, pl.ds(w_cols.shape[1] - share, share)]
+
+    w_copies = [
+        remote(rows_of(device), to, (to_all, at_all), i, device) for i, device in enumerate(peers)
+    ]
+    w_kept = pltpu.make_async_copy(rows_of(me), to, w_sem)
     kept_cot = pltpu.make_async_copy(cotangent, cot_all.at[gather.me], cot_sem)
     kept_cot.start()
     gather.start()
+    for copy in [w_kept] + w_copies:
+        copy.start()
 
     def tile(i, carry):
         s = lax.rem(core * count + i, width)
         rows = pl.ds(pl.multiple_of(s * tok, tok), tok)
-        acc = dot(hidden[rows, :], weight[...])
+        hidden_load(i).wait()
+        acc = dot(hidden_in[lax.rem(i, 2)], weight[:, : query.shape[1] + 2 * HEAD_DIM])
+
+        @pl.when(i + 2 < width)
+        def _():
+            hidden_load(i + 2).start()
+
         c, n = cosine[rows, :], sine[rows, :]
         columns = acc.shape[1] - 2 * HEAD_DIM
         for first in range(0, columns, 2 * HEAD_DIM):
@@ -344,8 +375,8 @@
             def _():
                 across(step).wait()
 
-    kept.wait()
-    kept_cot.wait()
+    for copy in [kept, kept_cot, w_kept] + w_copies:
+        copy.wait()
 
 
 def finish_kernel(
@@ -575,21 +606,11 @@
                 self.near_copy(j, n).wait_send()
 
 
-def middle_kernel(
-    chunks, mixed, w_out, tokens, gain, w_feed, cotangent, middle, hidden, acts, down_part,
-    blocks, act_stage, inner_turned, column_in, down_stage, out_sems, act_sems, column_sems, down_sem, *refs,
-):
+def branch_kernel(chunks, mixed, w_out, tokens, middle, *refs):
     f32, bf16 = jnp.float32, jnp.bfloat16
-    width, tok, _ = blocks.shape
-    scatter = Scatter(middle, chunks, refs[:12])
-    me = scatter.me
+    scatter = Scatter(middle, chunks, refs)
+    tok = tokens.shape[0]
     size = tok // chunks
-
-    def item(j):
-        part = pl.ds(j * size, size)
-        return blocks.at[me, part], lambda owner: blocks.at[owner, part]
-
-    gather = Gather([item(j) for j in range(chunks)], refs[12:])
     greet(scatter.sibling, scatter.x, scatter.y)
 
     def branch(i, carry):
@@ -598,66 +619,33 @@
         scatter.progress(i)
         return carry
 
-    lax.fori_loop(0, width, branch, 0)
+    lax.fori_loop(0, mixed.shape[0] // tok, branch, 0)
     scatter.arrived(0)
     for j in scatter.order:
         scatter.far(j)
     for j in scatter.order:
         part = pl.ds(j * size, size)
-        total = tokens[part, :].astype(f32) + scatter.result(j)
-        middle[part, :] = total
-        blocks[me, part] = (total * inverse_rms(total) * gain[...]).astype(bf16)
-        gather.start_items((j,))
-
-    def hidden_copy(i):
-        return pltpu.make_async_copy(blocks.at[me ^ i], hidden.at[me ^ i], out_sems.at[i])
-
-    def act_copy(i):
-        slot = lax.rem(i, 2)
-        return pltpu.make_async_copy(act_stage.at[slot], acts.at[me ^ i], act_sems.at[slot])
-
-    def block(i, carry):
-        @pl.when(i == 1)
-        def _():
-            gather.from_sibling(3)
-
-        @pl.when(i == 2)
-        def _():
-            for j in scatter.order:
-                gather.pass_on(0, j)
-                gather.pass_on(1, j)
-
-        @pl.when(i == 3)
-        def _():
-            gather.from_sibling(4)
-
-        @pl.when(i == 5)
-        def _():
-            gather.from_sibling(5)
-
-        @pl.when(i == 6)
-        def _():
-            for j in scatter.order:
-                gather.pass_on(2, j)
-
-        @pl.when(i == 7)
-        def _():
-            gather.from_sibling(6)
-
-        @pl.when(i >= 2)
-        def _():
-            act_copy(i - 2).wait()
-
-        acc = dot(blocks[me ^ i], w_feed[...])
-        act_stage[lax.rem(i, 2)] = acc
-        act_copy(i).start()
-        hidden_copy(i).start()
-        gate, up = acc[:, :units], acc[:, units:]
-        inner_turned[i] = (gate / (1.0 + jnp.exp(-gate)) * up).astype(bf16).T
-        return carry
-
+        middle[part, :] = tokens[part, :].astype(f32) + scatter.result(j)
+    scatter.finish(False)
+
+
+def middle_kernel(
+    chunks, middle, gain, w_feed, cotangent, hidden, acts, down_part,
+    blocks, act_stage, inner_turned, column_in, down_stage, out_sems, act_sems, column_sems, down_sem, *sems,
+):
+    f32, bf16 = jnp.float32, jnp.bfloat16
+    width, tok, _ = blocks.shape
+    me = lax.axis_index(R)
+    size = tok // chunks
+
+    def item(j):
+        part = pl.ds(j * size, size)
+        return blocks.at[me, part], lambda owner: blocks.at[owner, part]
+
+    gather = Gather([item(j) for j in range(chunks)], sems)
     units = w_feed.shape[1] // 2
-    tiles = tokens.shape[1] // tok
+    tiles = middle.shape[1] // tok
+    order = [*range(chunks // 2, chunks), *range(chunks // 2)]
 
     def column_loads(n):
         slot = lax.rem(n, 2)
@@ -671,6 +659,63 @@
             for i in range(width)
         ]
 
+    for n in (0, 1):
+        for copy in column_loads(n):
+            copy.start()
+    greet(gather.sibling, gather.x, gather.y)
+    for j in order:
+        part = pl.ds(j * size, size)
+        total = middle[part, :]
+        blocks[me, part] = (total * inverse_rms(total) * gain[...]).astype(bf16)
+        gather.start_items((j,))
+
+    def hidden_copy(i):
+        return pltpu.make_async_copy(blocks.at[me ^ i], hidden.at[me ^ i], out_sems.at[i])
+
+    def act_copy(i):
+        slot = lax.rem(i, 2)
+        return pltpu.make_async_copy(act_stage.at[slot], acts.at[me ^ i], act_sems.at[slot])
+
+    def block(i, carry):
+        @pl.when(i == 1)
+        def _():
+            gather.from_sibling(3)
+
+        @pl.when(i == 2)
+        def _():
+            for j in order:
+                gather.pass_on(0, j)
+                gather.pass_on(1, j)
+
+        @pl.when(i == 3)
+        def _():
+            gather.from_sibling(4)
+
+        @pl.when(i == 5)
+        def _():
+            gather.from_sibling(5)
+
+        @pl.when(i == 6)
+        def _():
+            for j in order:
+                gather.pass_on(2, j)
+
+        @pl.when(i == 7)
+        def _():
+            gather.from_sibling(6)
+
+        @pl.when(i >= 2)
+        def _():
+            act_copy(i - 2).wait()
+
+        acc = dot(blocks[me ^ i], w_feed[...])
+        act_stage[lax.rem(i, 2)] = acc
+        act_copy(i).start()
+        hidden_copy(i).start()
+        gate, up = acc[:, :units], acc[:, units:]
+        inner_turned[i] = (gate / (1.0 + jnp.exp(-gate)) * up).astype(bf16).T
+        return carry
+
     def down_copy(n):
         part = pl.ds(pl.multiple_of(n * tok, tok), tok)
         slot = lax.rem(n, 2)
@@ -698,37 +743,46 @@
 
         return carry
 
-    for n in (0, 1):
-        for copy in column_loads(n):
-            copy.start()
     lax.fori_loop(0, width, block, 0)
     lax.fori_loop(0, tiles, down_tile, 0)
     for n in (tiles - 2, tiles - 1):
         down_copy(n).wait()
     gather.wait_sends()
-    scatter.finish(False)
     for i in (width - 2, width - 1):
         act_copy(i).wait()
     for i in range(width):
         hidden_copy(i).wait()
 
 
-def middle_layer(mixed, w_out, tokens, gain, w_feed, cotangent, call, chunks=4):
+def branch_layer(mixed, w_out, tokens, call, chunks=4):
+    vmem = pl.BlockSpec(memory_space=pltpu.VMEM)
+    return pl.pallas_call(
+        functools.partial(branch_kernel, chunks),
+        out_shape=jax.ShapeDtypeStruct(tokens.shape, jnp.float32),
+        in_specs=[vmem] * 3,
+        out_specs=vmem,
+        scratch_shapes=Scatter.scratch(*tokens.shape, chunks),
+        compiler_params=pltpu.CompilerParams(
+            collective_id=call, has_side_effects=True, vmem_limit_bytes=40 << 20
+        ),
+    )(mixed, w_out, tokens)
+
+
+def middle_layer(middle, gain, w_feed, cotangent, call, chunks=4):
     width = lax.axis_size(R)
-    tok, model = tokens.shape
+    tok, model = middle.shape
     bf16, f32 = jnp.bfloat16, jnp.float32
     units = w_feed.shape[1] // 2
     vmem = pl.BlockSpec(memory_space=pltpu.VMEM)
     return pl.pallas_call(
         functools.partial(middle_kernel, chunks),
         out_shape=[
-            jax.ShapeDtypeStruct((tok, model), f32),
             jax.ShapeDtypeStruct((width, tok, model), bf16),
             jax.ShapeDtypeStruct((width, tok, 2 * units), f32),
             jax.ShapeDtypeStruct((units, model), bf16),
         ],
-        in_specs=[vmem] * 5 + [ANY],
-        out_specs=[vmem, ANY, ANY, ANY],
+        in_specs=[vmem] * 3 + [ANY],
+        out_specs=[ANY] * 3,
         scratch_shapes=[
             pltpu.VMEM((width, tok, model), bf16),
             pltpu.VMEM((2, tok, 2 * units), f32),
@@ -740,12 +794,11 @@
             DMA((2, width)),
             DMA((2,)),
         ]
-        + Scatter.scratch(tok, model, chunks)
         + Gather.scratch(chunks),
         compiler_params=pltpu.CompilerParams(
             collective_id=call, has_side_effects=True, vmem_limit_bytes=56 << 20
         ),
-    )(mixed, w_out, tokens, gain, w_feed, cotangent)
+    )(middle, gain, w_feed, cotangent)
 
 
 def feed_kernel(
@@ -905,10 +958,10 @@
 
 
 def back_kernel(
-    chunks, heads, q, kv, starts, places, grad, mixed, log_total, cosine, sine, out_part, down_rows, w_part,
-    grad_qkv, feed_out, all_down, w_rows,
+    chunks, heads, q, kv, starts, places, grad, mixed, log_total, cosine, sine, hidden, out_part, down_rows, w_part,
+    grad_qkv, weight_part, feed_out, all_down, w_rows,
     sums, grad_kv, from_sib, inbox, outbox, to_sib, at_sib, to_line, at_line, down_sem, w_sem,
-    to_all, at_all, load_sems, *refs,
+    to_all, at_all, column_in, weight_stage, column_sems, weight_sem, load_sems, *refs,
 ):
     f32, bf16 = jnp.float32, jnp.bfloat16
     planes, count, tok = inbox.shape[0], inbox.shape[1], inbox.shape[2]
@@ -918,8 +971,7 @@
     core = lax.rem(me, 2)
     above, below = lax.rem(z + 1, planes), lax.rem(z + planes - 1, planes)
     scatter = Scatter(feed_out, chunks, refs[:12])
-    gather = Gather([(down_rows, lambda owner: all_down.at[owner])] * 1, refs[12:])
-    half = chunks // 2
+    gather = Gather(row_items(down_rows, all_down, 1), refs[12:])
     barrier = pltpu.get_barrier_semaphore()
     for other in (above, below):
         pl.semaphore_signal(barrier, inc=1, device_id={F: other}, device_id_type=MESH)
@@ -939,7 +991,6 @@
     w_kept = pltpu.make_async_copy(share_of(me), w_rows.at[me], w_sem)
     for copy in [w_kept] + w_copies:
         copy.start()
-    scatter.take(out_part, load_sems)
     kept = pltpu.make_async_copy(down_rows, all_down.at[me], down_sem)
     kept.start()
     parts = tok // QUERY_BLOCK
@@ -991,33 +1042,40 @@
         def _():
             grad_kv[s] = sums[...].astype(bf16)
 
+        @pl.when(n == 3)
+        def _():
+            scatter.taken(3)
+            for j in scatter.order:
+                scatter.near(j, 1)
+            scatter.taken(2)
+            for j in scatter.order[: chunks // 2]:
+                scatter.near(j, 0)
+            scatter.taken(1)
+            for j in scatter.order[chunks // 2 :]:
+                scatter.near(j, 0)
+
+        @pl.when(n == 11)
+        def _():
+            gather.relay(0)
+
         return carry
 
-    lax.fori_loop(0, width // 2, step, 0)
-    scatter.taken(3)
-    for j in scatter.order:
-        scatter.near(j, 1)
-    scatter.taken(2)
-    for j in range(half, chunks):
-        scatter.near(j, 0)
-    scatter.taken(1)
-    for j in range(half):
-        scatter.near(j, 0)
+    scatter.take(out_part, load_sems)
     gather.start()
-    lax.fori_loop(width // 2, width * parts, step, 0)
+    lax.fori_loop(0, width * parts, step, 0)
 
     def block_of(which, b):
         return grad_kv.at[pl.ds(which * count, count), pl.ds(b * tok, tok)]
 
     def trade(b):
-        return remote(block_of(1 - core, b), from_sib.at[b], (to_sib, at_sib), b, scatter.sibling)
-
-    def down(b):
-        return along_line(outbox.at[b], inbox.at[b], (to_line, at_line), b, below)
-
-    def own(b):
+        return remote(block_of(1 - core, b), from_sib.at[b], (to_sib, at_sib), b, gather.sibling)
+
+    def down(b, i):
+        return along_line(outbox.at[b, i], inbox.at[b, i], (to_line, at_line), (b, i), below)
+
+    def own(b, i):
         part = pl.ds(b * tok, tok)
-        return grad_kv[pl.ds(core * count, count), part, :].astype(f32) + from_sib[b].astype(f32)
+        return grad_kv[core * count + i, part, :].astype(f32) + from_sib[b, i].astype(f32)
 
     for b in range(planes):
 
@@ -1032,28 +1090,29 @@
         def _():
             trade(b).wait_recv()
 
-            @pl.when(z < planes - 1)
+        for i in range(count):
+
+            @pl.when((b <= z) & (z < planes - 1))
             def _():
-                down(b).wait_recv()
-
-        @pl.when((b < z) & (z < planes - 1))
-        def _():
-            outbox[b] = (own(b) + inbox[b].astype(f32)).astype(bf16)
-
-        @pl.when((b < z) & (z == planes - 1))
-        def _():
-            outbox[b] = own(b).astype(bf16)
-
-        @pl.when(b < z)
-        def _():
-            down(b).start()
+                down(b, i).wait_recv()
+
+            @pl.when((b < z) & (z < planes - 1))
+            def _():
+                outbox[b, i] = (own(b, i) + inbox[b, i].astype(f32)).astype(bf16)
+
+            @pl.when((b < z) & (z == planes - 1))
+            def _():
+                outbox[b, i] = own(b, i).astype(bf16)
+
+            @pl.when(b < z)
+            def _():
+                down(b, i).start()
 
         if b == 0:
-            for j in range(half, chunks):
+            for j in scatter.order[: chunks // 2]:
                 scatter.far(j)
         if b == 1:
-            gather.relay(0)
-            for j in range(half):
+            for j in scatter.order[chunks // 2 :]:
                 scatter.far(j)
 
     def keys(i, carry):
@@ -1065,10 +1124,47 @@
         return carry
 
     lax.fori_loop(0, count, keys, 0)
+    gather.far()
+    tiles = hidden.shape[1] // tok
+
+    def column_load(n):
+        part = pl.ds(pl.multiple_of(n * tok, tok), tok)
+        slot = lax.rem(n, 2)
+        return pltpu.make_async_copy(hidden.at[:, part], column_in.at[slot], column_sems.at[slot])
+
+    def weight_copy(n):
+        rows = pl.ds(pl.multiple_of(n * tok, tok), tok)
+        slot = lax.rem(n, 2)
+        return pltpu.make_async_copy(weight_stage.at[slot], weight_part.at[rows], weight_sem.at[slot])
+
+    def weight_tile(n, carry):
+        slot = lax.rem(n, 2)
+        column_load(n).wait()
+
+        @pl.when(n >= 2)
+        def _():
+            weight_copy(n - 2).wait()
+
+        weight_stage[slot] = dot(column_in[slot], grad_qkv[...], 0, 0).astype(bf16)
+        weight_copy(n).start()
+
+        @pl.when(n + 2 < tiles)
+        def _():
+            column_load(n + 2).start()
+
+        return carry
+
+    for n in (0, 1):
+        column_load(n).start()
+    lax.fori_loop(0, tiles, weight_tile, 0)
     for j in scatter.order:
         scatter.last(j)
-    gather.finish()
     scatter.finish()
+    for n in (tiles - 2, tiles - 1):
+        weight_copy(n).wait()
+    for kind in range(3, 7):
+        gather.from_sibling(kind)
+    gather.wait_sends()
     for b in range(planes):
 
         @pl.when(b <= z)
@@ -1077,32 +1173,35 @@
 
         @pl.when(b < z)
         def _():
-            down(b).wait_send()
+            for i in range(count):
+                down(b, i).wait_send()
 
     for copy in [kept, w_kept] + w_copies:
         copy.wait()
 
 
 def attention_back(
-    heads, q, kv, starts, places, grad, mixed, log_total, cosine, sine, out_part, down_rows, w_part, call,
-    chunks=4,
+    heads, q, kv, starts, places, grad, mixed, log_total, cosine, sine, hidden, out_part, down_rows, w_part,
+    call, chunks=4,
 ):
     planes, width = lax.axis_size(F), lax.axis_size(R)
     f32, bf16 = jnp.float32, jnp.bfloat16
-    tok, model = out_part.shape[1:]
+    tok, model = hidden.shape[0] // width, hidden.shape[1]
+    columns = q.shape[1] + 2 * HEAD_DIM
     length = kv.shape[1]
     vmem = pl.BlockSpec(memory_space=pltpu.VMEM)
     blocks = pltpu.VMEM((planes, width // 2, tok, 2 * HEAD_DIM), bf16)
     return pl.pallas_call(
         functools.partial(back_kernel, chunks, heads),
         out_shape=[
-            jax.ShapeDtypeStruct((q.shape[0], q.shape[1] + 2 * HEAD_DIM), bf16),
+            jax.ShapeDtypeStruct((q.shape[0], columns), bf16),
+            jax.ShapeDtypeStruct((model, columns), bf16),
             jax.ShapeDtypeStruct((tok, model), f32),
             jax.ShapeDtypeStruct((width,) + down_rows.shape, bf16),
             jax.ShapeDtypeStruct((width, w_part.shape[0], w_part.shape[1] // width), bf16),
         ],
-        in_specs=[vmem] * 9 + [ANY] * 3,
-        out_specs=[vmem] + [ANY] * 3,
+        in_specs=[vmem] * 9 + [ANY] * 4,
+        out_specs=[vmem] + [ANY] * 4,
         scratch_shapes=[
             pltpu.VMEM((length, 2 * HEAD_DIM), f32),
             pltpu.VMEM((width, length, 2 * HEAD_DIM), bf16),
@@ -1110,14 +1209,17 @@
             blocks,
             blocks,
         ]
-        + [DMA((planes,))] * 4
-        + [DMA, DMA, DMA((width - 1,)), DMA((width - 1,)), DMA((4,))]
+        + [DMA((planes,))] * 2
+        + [DMA((planes, width // 2))] * 2
+        + [DMA, DMA, DMA((width - 1,)), DMA((width - 1,))]
+        + [pltpu.VMEM((2, width * tok, tok), bf16), pltpu.VMEM((2, tok, columns), bf16)]
+        + [DMA((2,)), DMA((2,)), DMA((4,))]
         + Scatter.scratch(tok, model, chunks)
         + Gather.scratch(1),
         compiler_params=pltpu.CompilerParams(
             collective_id=call, has_side_effects=True, vmem_limit_bytes=60 << 20
         ),
-    )(q, kv, starts, places, grad, mixed, log_total, cosine, sine, out_part, down_rows, w_part)
+    )(q, kv, starts, places, grad, mixed, log_total, cosine, sine, hidden, out_part, down_rows, w_part)
 
 
 def hidden_kernel(chunks, grad_qkv, weight, feed_rows, grad_hidden, all_feed, feed_sem, *refs):
@@ -1190,7 +1292,7 @@
     )(tokens, gains, ids)
 
 
-def project(hidden, weight, cosine, sine, cotangent, call, chunks=4):
+def project(hidden, weight, cosine, sine, cotangent, query_width, call, chunks=4):
     planes, width = lax.axis_size(F), lax.axis_size(R)
     tok, model = cotangent.shape
     bf16 = jnp.bfloat16
@@ -1198,20 +1300,30 @@
     return pl.pallas_call(
         functools.partial(project_kernel, chunks),
         out_shape=[
-            jax.ShapeDtypeStruct((width * tok, weight.shape[1] - 2 * HEAD_DIM), bf16),
+            jax.ShapeDtypeStruct((width * tok, query_width), bf16),
             jax.ShapeDtypeStruct((width, planes, tok, 2 * HEAD_DIM), bf16),
             jax.ShapeDtypeStruct((width, tok, model), bf16),
+            jax.ShapeDtypeStruct((model // width, model), bf16),
         ],
-        in_specs=[vmem] * 4 + [ANY],
-        out_specs=[vmem, ANY, ANY],
-        scratch_shapes=[pltpu.VMEM((width, tok, 2 * HEAD_DIM), bf16), DMA, DMA]
+        in_specs=[ANY] + [vmem] * 3 + [ANY, ANY],
+        out_specs=[vmem, ANY, ANY, ANY],
+        scratch_shapes=[
+            pltpu.VMEM((width, tok, 2 * HEAD_DIM), bf16),
+            pltpu.VMEM((2, tok, model), bf16),
+            DMA((2,)),
+            DMA,
+            DMA,
+            DMA,
+            DMA((width - 1,)),
+            DMA((width - 1,)),
+        ]
         + [DMA((planes, width // 2))] * 2
         + [DMA((planes,))] * 2
         + Gather.scratch(chunks),
         compiler_params=pltpu.CompilerParams(
             collective_id=call, has_side_effects=True, vmem_limit_bytes=40 << 20
         ),
-    )(hidden, weight, cosine, sine, cotangent)
+    )(hidden, weight, cosine, sine, cotangent, weight)
 
 
 def scatter_kernel(
@@ -1532,9 +1644,6 @@
         )
     )
     w_qkv = w_attention[:, : qw + 2 * HEAD_DIM]
-    w_out = lax.all_to_all(
-        w_attention[:, qw + 2 * HEAD_DIM :], R, split_axis=0, concat_axis=1, tiled=True
-    )
     own_gains = jnp.stack([attention_gain, feed_gain]).astype(f32)
     tok_float = tokens.astype(f32)
     scale_in = inverse_rms(tok_float)
@@ -1574,7 +1683,15 @@
     if plane_kernels:
         wide_cosine, wide_sine = rope_tables(own_positions, 4)
         wide_sine = wide_sine * jnp.where(jnp.arange(2 * HEAD_DIM) // (HEAD_DIM // 2) % 2, 1.0, -1.0)
-        query, kv_rows, cot_all = project(hidden_in, w_qkv, wide_cosine, wide_sine, cotangent, 3)
+        query, kv_rows, cot_all, w_out = project(
+            hidden_in.reshape(width, tok, model),
+            w_attention,
+            wide_cosine,
+            wide_sine,
+            cotangent,
+            qw,
+            3,
+        )
         kv_rows = kv_rows.reshape(width, length, 2 * HEAD_DIM)
         cot_all = cot_all.reshape(all_tok, model)
     else:
@@ -1591,6 +1708,9 @@
             .reshape(width, length, 2 * HEAD_DIM)
         )
         cot_all = lax.all_gather(cotangent, R, axis=0, tiled=True)
+        w_out = lax.all_to_all(
+            w_attention[:, qw + 2 * HEAD_DIM :], R, split_axis=0, concat_axis=1, tiled=True
+        )
     common = [("tokens", query), ("sequence", kv_rows), ("row", starts), ("row", query_places)]
     mixed, log_totals = attention_call(
         attention_kernel,
@@ -1605,9 +1725,8 @@
     )
     if plane_kernels:
         cot_blocks = cot_all.reshape(width, tok, model)
-        middle, hidden_blocks, acts, down_part = middle_layer(
-            mixed, w_out, tokens, gain_mid[None], w_feed, cot_blocks, 1
-        )
+        middle = branch_layer(mixed, w_out, tokens, 1)
+        hidden_blocks, acts, down_part = middle_layer(middle, gain_mid[None], w_feed, cot_blocks, 2)
     else:
         middle = tok_float + plane_scatter(dot(mixed, w_out).astype(bf16), 1)
     scale_mid = inverse_rms(middle)
@@ -1650,7 +1769,7 @@
     w_out_part = dot(mixed, grad_branch, 0, 0).astype(bf16)
 
     if plane_kernels:
-        grad_qkv, feed_out, down_all, w_out_part = attention_back(
+        grad_qkv, qkv_part, feed_out, down_all, w_out_part = attention_back(
             heads,
             query,
             kv_rows,
@@ -1661,6 +1780,7 @@
             log_totals,
             wide_cosine,
             wide_sine,
+            hidden_in,
             out_part,
             down_rows,
             w_out_part,
@@ -1686,11 +1806,11 @@
         gk = rotate(gkv[:, None, :HEAD_DIM], cosine, sine, -1.0)[:, 0]
         grad_qkv = jnp.concatenate([gq.reshape(all_tok, qw), gk, gkv[:, HEAD_DIM:]], axis=1)
         grad_qkv = grad_qkv.astype(bf16)
+        qkv_part = dot(hidden_in, grad_qkv, 0, 0).astype(bf16)
         down_all = lax.all_gather(down_rows, R, axis=0, tiled=True)
         w_out_part = lax.all_to_all(w_out_part, R, split_axis=1, concat_axis=0, tiled=True)
     out_rows = line_scatter(w_out_part)
     activations = (middle + feed_out).astype(bf16)
-    qkv_part = dot(hidden_in, grad_qkv, 0, 0).astype(bf16)
     grad_qkv, qkv_part, feed_rows = lax.optimization_barrier((grad_qkv, qkv_part, feed_rows))
     qkv_rows = line_scatter(qkv_part)
     if plane_kernels:

time: 679 us -> 640 us (0.943)
  waiting for transfers between devices: 29.2 us -> 5.01 us
  matrix products: 20 us -> 10.5 us
    pallas_call x0 -> x1, Pallas kernels: none -> 42 us  [branch_layer(): pl.pallas_call(functools.partial(branch_kernel, chunks), out_shape=jax.Sh...]
    pallas_call x1, Pallas kernels: 94.5 us -> 53 us  [middle_layer(): pl.pallas_call(functools.partial(middle_kernel, chunks), out_shape=[jax.S...]
    all_gather x3, waiting for transfers between devices: 29.1 us -> 4.76 us  [line_gather(): return lax.all_gather(x, F, axis=0, tiled=True)]
    dot_general x3 -> x2, matrix products: 20 us -> 10.5 us  [dot(): lax.dot_general(a, b, (((ca,), (cb,)), ((), ())), preferred_element_type=...]
    pallas_call x1, Pallas kernels: 112 us -> 103 us  [attention_back(): pl.pallas_call(functools.partial(back_kernel, chunks, heads), out_shape=[...]
    pallas_call x1, Pallas kernels: 45.5 us -> 53 us  [project(): pl.pallas_call(functools.partial(project_kernel, chunks), out_shape=[jax....]
  transfers between devices with their start and end apart: 8 -> 7, of which waited for: 1 -> 1; matrix products, arithmetic and copies ran while one was open for 8% -> 7% of each run, Pallas kernels for 76% -> 80%
where the time goes in v6:
time: 640 us; the launch traced here: 636 us
  Pallas kernels  544 us (85%)
  local copies, waits for them, and re-layouts  36 us (6%)
  other arithmetic  23.6 us (4%)
  between operations  14.9 us (2%)
  matrix products  10.5 us (2%)
    pallas_call x1, Pallas kernels, attention_back(): pl.pallas_call(functools.partial(back_kernel, chunks, heads), out_shape=[...  103 us
    pallas_call x1, Pallas kernels, scatter_hidden(): pl.pallas_call(functools.partial(hidden_kernel, chunks), out_shape=[jax.S...  84 us
    pallas_call x1, Pallas kernels, feed_forward(): pl.pallas_call(functools.partial(feed_kernel, chunks), out_shape=[jax.Sha...  68.5 us
    pallas_call x1, Pallas kernels, middle_layer(): pl.pallas_call(functools.partial(middle_kernel, chunks), out_shape=[jax.S...  53 us
    pallas_call x1, Pallas kernels, project(): pl.pallas_call(functools.partial(project_kernel, chunks), out_shape=[jax....  53 us
    pallas_call x1, Pallas kernels, enter(): pl.pallas_call(functools.partial(enter_kernel, chunks), out_shape=[jax.Sh...  45.7 us
    pallas_call x1, Pallas kernels, branch_layer(): pl.pallas_call(functools.partial(branch_kernel, chunks), out_shape=jax.Sh...  42 us
    pallas_call x1, Pallas kernels, plane_gather(): pl.pallas_call(functools.partial(gather_kernel, chunks), out_shape=jax.Sh...  38.9 us
  transfers between devices with their start and end apart: 7, of which 1 were waited for; matrix products, arithmetic and copies ran while one was open for 7% of the time, Pallas kernels for 80%

profile of v6, /device:TPU:0, one launch (start us, length us, event | category | flops | bytes accessed | tf_op | source)
XLA Modules:
  0.0 635.7 jit_solution(7153252135805720703)
XLA Ops:
  7.2 0.0 all-gather.4.cloned.1.call-start
  7.3 1.2 constant_dynamic-slice_fusion.10
  8.5 1.1 constant_dynamic-slice_fusion.9
  9.6 1.0 pad_maximum_fusion
  10.6 0.0 all-gather.6.cloned.1.call-start
  10.7 45.7 %shard_map.203 = (bf16[8,256,2048]{2,1,0:T(8,128)(2,1)S(1)}, f32[4,8,512]{2,1,0:T(8,128)S(1)}, s32[8,8,128]{2,1,0:T(8,128)S(1)}) custom-call(bf16[256,2048]{1,0:T(8,128)(2,1)S(1)} %copy-done.3, f32[8,512]{1,0:T(8,128)S(1)} %fusion.14.gains, s32[8,128]{1,0:T(8,128)S(1)} %bitcast.45), custom_call_target="tpu_custom_call" | custom-call | tf_op jit(solution)/shard_map/pallas_call | solution.py:1277
  56.5 3.4 copy-done.2
  59.9 2.9 constant_dynamic-slice_fusion.1
  62.8 2.4 concatenate.12
  65.2 0.0 all-gather.8.cloned.1.call-start
  65.2 2.1 constant_dynamic-slice_fusion
  67.4 0.6 reduce-scatter.5.cloned.1.call-start
  68.0 0.1 slice_compare_fusion
  68.1 0.1 select_bitcast_fusion
  68.2 2.3 reduce-window.6
  70.4 0.3 slice_reduce_fusion
  70.7 0.2 reduce-window.9
  70.9 0.1 maximum_bitcast_fusion
  71.1 0.4 slice_reduce_fusion.2
  71.5 0.5 slice_reduce_fusion.1
  72.0 0.6 fusion.25
  72.6 5.0 fusion.10
  77.5 2.2 copy-done.4
  79.8 1.3 copy-done.12
  81.1 53.0 %shard_map.204 = (bf16[2048,256]{1,0:T(8,128)(2,1)S(1)}, bf16[8,4,256,128]{3,2,1,0:T(8,128)(2,1)S(1)}, bf16[8,256,2048]{2,1,0:T(8,128)(2,1)}, bf16[256,2048]{1,0:T(8,128)(2,1)S(1)}) custom-call(bf16[8,256,2048]{2,1,0:T(8,128)(2,1)} %copy-done.2, bf16[2048,640]{1,0:T(8,128)(2,1)S(1)} %copy-done.4, f32[2048,128]{1,0:T(8,128)S(1)} %copy-done.12, ...), custom_call_target="tpu_custom_call" | custom-call | tf_op jit(solution)/shard_map/pallas_call | solution.py:1300
  134.2 13.1 %shard_map.205 = (bf16[2048,256]{1,0:T(8,128)(2,1)S(1)}, f32[16,1,512]{2,1,0:T(1,128)S(1)}) custom-call(s32[16]{0:T(128)S(1)} %get-tuple-element.111.low, s32[16]{0:T(128)S(1)} %get-tuple-element.112.high, bf16[2048,256]{1,0:T(8,128)(2,1)S(1)} %get-tuple-element.52.q, bf16[8,1024,128]{2,1,0:T(8,128)(2,1)S(1)} %bitcast.42, s32[16,1,128]{2,1,0:T(1,128)S(1)} %fusion.22.starts, ...), custom_call_target="tpu_custom_call" | custom-call | tf_op jit(solution)/shard_map/pallas_call | solution.py:1551
  147.3 0.6 copy-done.23
  147.9 42.0 %shard_map.206.middle = f32[256,2048]{1,0:T(8,128)S(1)} custom-call(bf16[2048,256]{1,0:T(8,128)(2,1)S(1)} %get-tuple-element.54.mixed, bf16[256,2048]{1,0:T(8,128)(2,1)S(1)} %get-tuple-element.55.w_out, bf16[256,2048]{1,0:T(8,128)(2,1)S(1)} %copy-done.3), custom_call_target="tpu_custom_call" | custom-call | tf_op jit(solution)/shard_map/pallas_call | solution.py:759
  190.0 1.3 copy-done
  191.3 1.0 copy-done.6
  192.3 1.0 copy-done.19
  193.2 53.0 %shard_map.207 = (bf16[8,256,2048]{2,1,0:T(8,128)(2,1)}, f32[8,256,1408]{2,1,0:T(8,128)}, bf16[704,2048]{1,0:T(8,128)(2,1)}) custom-call(f32[256,2048]{1,0:T(8,128)} %copy-done, f32[1,2048]{1,0:T(1,128)} %bitcast.50, bf16[2048,1408]{1,0:T(8,128)(2,1)} %all-gather.6.cloned.1.call-done.w_feed, bf16[8,256,2048]{2,1,0:T(8,128)(2,1)} %get-tuple-element.59.cotangent), custom_call_target="tpu_custom_call" | custom-call | tf_op jit(solution)/shard_map/pallas_call | solution.py:777
  246.3 0.0 reduce-scatter.5.cloned.1.call-update
  246.3 0.2 reduce-scatter.7.cloned.1.call-start
  246.5 4.8 all-gather.8.cloned.1.call-done.w_down
  251.3 68.5 %shard_map.208 = (bf16[8,256,2048]{2,1,0:T(8,128)(2,1)}, f32[256,2048]{1,0:T(8,128)}, bf16[2048,1408]{1,0:T(8,128)(2,1)}) custom-call(bf16[8,256,2048]{2,1,0:T(8,128)(2,1)} %get-tuple-element.60.hidden, bf16[8,256,2048]{2,1,0:T(8,128)(2,1)} %get-tuple-element.59.cotangent, f32[8,256,1408]{2,1,0:T(8,128)} %get-tuple-element.61.acts, ...), custom_call_target="tpu_custom_call" | custom-call | tf_op jit(solution)/shard_map/pallas_call | solution.py:932
  319.8 0.3 reduce-scatter.11.cloned.1.call-start
  320.1 1.3 copy-done.1
  321.4 0.2 multiply_reduce_fusion.2
  321.6 1.4 copy-done.26
  323.0 0.7 multiply_reduce_fusion
  323.7 0.6 copy-done.9
  324.2 1.6 fusion.23.x
  325.9 38.9 %shard_map.209 = bf16[8,256,2048]{2,1,0:T(8,128)(2,1)} custom-call(bf16[256,2048]{1,0:T(8,128)(2,1)} %fusion.23.x), custom_call_target="tpu_custom_call" | custom-call | tf_op jit(solution)/shard_map/pallas_call | solution.py:1402
  364.8 7.2 %convolution_convert_fusion.w_part = bf16[256,2048]{1,0:T(8,128)(2,1)} fusion(bf16[2048,256]{1,0:T(8,128)(2,1)} %copy-done.6, bf16[2048,2048]{1,0:T(8,128)(2,1)} %bitcast.46), kind=kOutput, calls=%fused_computation.6 | convolution fusion | flops 2148007936 | bytes 10485760 | tf_op jit(solution)/shard_map/dot_general | solution.py:50
  371.9 3.4 convolution_convert_fusion.1.grad
  375.3 103.0 %shard_map.210 = (bf16[2048,384]{1,0:T(8,128)(2,1)}, bf16[2048,384]{1,0:T(8,128)(2,1)}, f32[256,2048]{1,0:T(8,128)}, bf16[8,176,2048]{2,1,0:T(8,128)(2,1)}, bf16[8,256,256]{2,1,0:T(8,128)(2,1)}) custom-call(bf16[2048,256]{1,0:T(8,128)(2,1)} %copy-done.14, bf16[8,1024,128]{2,1,0:T(8,128)(2,1)} %bitcast.43, s32[16,1,128]{2,1,0:T(1,128)} %copy-done.22, ...), custom_call_target="tpu_custom_call" | custom-call | tf_op jit(solution)/shard_map/pallas_call | solution.py:1194
  478.4 0.3 reduce-scatter.9.cloned.1.call-start
  478.7 0.3 fusion.9
  478.9 0.0 reduce-scatter.7.cloned.1.call-done.feed_rows
  479.0 0.1 reduce-scatter.9.cloned.1.call-update
  479.2 8.8 %bitcast_convert_fusion = f32[1408,2048]{1,0:T(8,128)} fusion(bf16[8,176,2048]{2,1,0:T(8,128)(2,1)} %get-tuple-element.86), kind=kLoop, calls=%fused_computation | loop fusion | flops 2883584 | bytes 17301504 | tf_op jit(solution)/shard_map/convert_element_type | solution.py:1841
  488.0 84.0 %shard_map.211 = (f32[256,2048]{1,0:T(8,128)S(1)}, bf16[8,512,1408]{2,1,0:T(8,128)(2,1)}) custom-call(bf16[2048,384]{1,0:T(8,128)(2,1)S(1)} %copy-done.17, bf16[2048,640]{1,0:T(8,128)(2,1)S(1)} %copy-done.5, bf16[512,1408]{1,0:T(8,128)(2,1)S(1)} %copy-done.18), custom_call_target="tpu_custom_call" | custom-call | tf_op jit(solution)/shard_map/pallas_call | solution.py:1258
  572.0 4.3 copy-done.7
  576.3 9.0 %shard_map.214 = (f32[512,5632]{1,0:T(8,128)}, f32[512,5632]{1,0:T(8,128)}) custom-call(bf16[8,512,1408]{2,1,0:T(8,128)(2,1)S(1)} %copy-done.7), custom_call_target="tpu_custom_call" | custom-call | tf_op jit(solution)/shard_map/pallas_call | solution.py:1590
  585.3 0.7 fusion.8
  586.0 0.6 pad.13.terms
  586.6 0.6 copy-done.27
  587.2 2.6 fusion.7
  589.8 29.2 %shard_map.212 = (bf16[8,512,384]{2,1,0:T(8,128)(2,1)}, bf16[8,512,256]{2,1,0:T(8,128)(2,1)}, f32[8,512]{1,0:T(8,128)}) custom-call(bf16[512,384]{1,0:T(8,128)(2,1)} %reduce-scatter.9.cloned.1.call-done.qkv, bf16[512,256]{1,0:T(8,128)(2,1)} %reduce-scatter.11.cloned.1.call-done.out_rows, f32[4,8,512]{2,1,0:T(8,128)} %pad.13.terms), custom_call_target="tpu_custom_call" | custom-call | tf_op jit(solution)/shard_map/pallas_call | solution.py:434
  618.9 1.4 fusion.24
  620.3 1.9 copy-done.15
  622.2 1.6 copy-done.16
  623.8 4.8 shard_map.213
  (79 shorter events, 0.4 us)
Async XLA Ops:
  7.2 3.5 copy-start.30
  7.2 3.5 copy-start.31
  7.2 3.5 copy-start.24
  7.2 3.5 copy-start.3
  7.2 70.3 %all-gather.4.cloned.1.call-start = ((), (), s32[]{:S(2)}) async-start(), calls=%async_computation.4 | async-start | bytes 3276800 | tf_op jit(solution)/shard_map/all_gather | solution.py:1446
  10.6 182.7 %all-gather.6.cloned.1.call-start = ((), (), s32[]{:S(2)}) async-start(), calls=%async_computation.5 | async-start | bytes 7208960 | tf_op jit(solution)/shard_map/all_gather | solution.py:1446
  56.5 3.4 copy-start.2
  65.2 186.1 %all-gather.8.cloned.1.call-start = ((), (), s32[]{:S(2)}) async-start(), calls=%async_computation.6 | async-start | bytes 3604480 | tf_op jit(solution)/shard_map/all_gather | solution.py:1446
  65.2 12.3 %copy-start.8 = (bf16[256,2048]{1,0:T(8,128)(2,1)S(1)}, bf16[256,2048]{1,0:T(8,128)(2,1)}, u32[]{:S(2)}) copy-start(bf16[256,2048]{1,0:T(8,128)(2,1)} %cotangent.1) | copy-start | bytes 3145732
  67.4 307.9 %reduce-scatter.5.cloned.1.call-start = ((), (), s32[]{:S(2)}) async-start(), calls=%async_computation.7 | async-start | bytes 3604480 | tf_op jit(solution)/shard_map/reduce_scatter | solution.py:1450
  71.1 63.1 %copy-start.21 = (s32[16,1,128]{2,1,0:T(1,128)}, s32[16,1,128]{2,1,0:T(1,128)S(1)}, u32[]{:S(2)}) copy-start(s32[16,1,128]{2,1,0:T(1,128)S(1)} %fusion.15.places) | copy-start | bytes 24580
  71.1 63.1 %copy-start.22 = (s32[16,1,128]{2,1,0:T(1,128)}, s32[16,1,128]{2,1,0:T(1,128)S(1)}, u32[]{:S(2)}) copy-start(s32[16,1,128]{2,1,0:T(1,128)S(1)} %fusion.22.starts) | copy-start | bytes 24580
  77.5 56.6 %copy-start.11 = (f32[2048,128]{1,0:T(8,128)}, f32[2048,128]{1,0:T(8,128)S(1)}, u32[]{:S(2)}) copy-start(f32[2048,128]{1,0:T(8,128)S(1)} %get-tuple-element.107.sine) | copy-start | bytes 3145732
  77.5 2.3 copy-start.4
  79.8 1.3 copy-start.12
  134.2 13.8 %copy-start.13 = (bf16[8,4,256,128]{3,2,1,0:T(8,128)(2,1)}, bf16[8,4,256,128]{3,2,1,0:T(8,128)(2,1)S(1)}, u32[]{:S(2)}) copy-start(bf16[8,4,256,128]{3,2,1,0:T(8,128)(2,1)S(1)} %get-tuple-element.53) | copy-start | bytes 6291460
  134.2 13.7 %copy-start.14 = (bf16[2048,256]{1,0:T(8,128)(2,1)}, bf16[2048,256]{1,0:T(8,128)(2,1)S(1)}, u32[]{:S(2)}) copy-start(bf16[2048,256]{1,0:T(8,128)(2,1)S(1)} %get-tuple-element.52.q) | copy-start | bytes 3145732
  147.3 0.6 copy-start.23
  189.9 1.3 copy-start
  191.3 1.0 copy-start.6
  192.3 1.0 copy-start.19
  246.3 232.7 %reduce-scatter.7.cloned.1.call-start = ((), (), s32[]{:S(2)}) async-start(), calls=%async_computation.8 | async-start | bytes 7208960 | tf_op jit(solution)/shard_map/reduce_scatter | solution.py:1450
  319.8 1.6 copy-start.1
  319.8 1.8 copy-start.29
  319.8 269.9 %reduce-scatter.11.cloned.1.call-start = ((), (), s32[]{:S(2)}) async-start(), calls=%async_computation.10 | async-start | bytes 1310720 | tf_op jit(solution)/shard_map/reduce_scatter | solution.py:1450
  321.4 1.6 copy-start.26
  323.0 1.3 copy-start.9
  364.7 7.2 %copy-start.20 = (bf16[256,2048]{1,0:T(8,128)(2,1)S(1)}, bf16[256,2048]{1,0:T(8,128)(2,1)}, u32[]{:S(2)}) copy-start(bf16[256,2048]{1,0:T(8,128)(2,1)} %copy-done.19) | copy-start | bytes 3145732
  364.7 7.2 %copy-start.25 = (bf16[8,256,2048]{2,1,0:T(8,128)(2,1)S(1)}, bf16[8,256,2048]{2,1,0:T(8,128)(2,1)}, u32[]{:S(2)}) copy-start(bf16[8,256,2048]{2,1,0:T(8,128)(2,1)} %shard_map.209) | copy-start | bytes 25165828
  478.4 111.4 %reduce-scatter.9.cloned.1.call-start = ((), (), s32[]{:S(2)}) async-start(), calls=%async_computation.9 | async-start | bytes 1966080 | tf_op jit(solution)/shard_map/reduce_scatter | solution.py:1450
  479.1 8.9 %copy-start.5 = (bf16[2048,640]{1,0:T(8,128)(2,1)S(1)}, bf16[2048,640]{1,0:T(8,128)(2,1)}, u32[]{:S(2)}) copy-start(bf16[2048,640]{1,0:T(8,128)(2,1)} %all-gather.4.cloned.1.call-done.weight.w_cols) | copy-start | bytes 7864324
  479.1 8.8 %copy-start.17 = (bf16[2048,384]{1,0:T(8,128)(2,1)S(1)}, bf16[2048,384]{1,0:T(8,128)(2,1)}, u32[]{:S(2)}) copy-start(bf16[2048,384]{1,0:T(8,128)(2,1)} %get-tuple-element.71.grad_qkv) | copy-start | bytes 4718596
  479.1 8.8 %copy-start.18 = (bf16[512,1408]{1,0:T(8,128)(2,1)S(1)}, bf16[512,1408]{1,0:T(8,128)(2,1)}, u32[]{:S(2)}) copy-start(bf16[512,1408]{1,0:T(8,128)(2,1)} %reduce-scatter.7.cloned.1.call-done.feed_rows) | copy-start | bytes 4325380
  572.0 4.3 copy-start.7
  576.3 10.3 %copy-start.28 = (f32[256,2048]{1,0:T(8,128)S(1)}, f32[256,2048]{1,0:T(8,128)}, u32[]{:S(2)}) copy-start(f32[256,2048]{1,0:T(8,128)} %get-tuple-element.67) | copy-start | bytes 6291460
  585.3 1.3 copy-start.10
  585.3 1.9 copy-start.27
  620.3 1.9 copy-start.15
  622.2 1.6 copy-start.16
Sparse Core Ops, SparseCore 0:
  10.7 57.5 all-gather.3
  70.4 106.8 all-gather.5
  178.9 72.2 all-gather.7
  253.4 70.0 reduce-scatter.4
  325.7 112.3 reduce-scatter.6
  478.5 26.9 reduce-scatter.10
  507.9 33.9 reduce-scatter.8

commit v7 on v6

--- a/solution.py
+++ b/solution.py
@@ -631,7 +631,7 @@
 
 def middle_kernel(
     chunks, middle, gain, w_feed, cotangent, hidden, acts, down_part,
-    blocks, act_stage, inner_turned, column_in, down_stage, out_sems, act_sems, column_sems, down_sem, *sems,
+    blocks, act_stage, cot_in, down_sum, down_stage, out_sems, act_sems, cot_sems, down_sem, *sems,
 ):
     f32, bf16 = jnp.float32, jnp.bfloat16
     width, tok, _ = blocks.shape
@@ -644,24 +644,14 @@
 
     gather = Gather([item(j) for j in range(chunks)], sems)
     units = w_feed.shape[1] // 2
-    tiles = middle.shape[1] // tok
     order = [*range(chunks // 2, chunks), *range(chunks // 2)]
 
-    def column_loads(n):
-        slot = lax.rem(n, 2)
-        part = pl.ds(pl.multiple_of(n * tok, tok), tok)
-        return [
-            pltpu.make_async_copy(
-                cotangent.at[me ^ i, :, part],
-                column_in.at[slot, pl.ds(i * tok, tok)],
-                column_sems.at[slot, i],
-            )
-            for i in range(width)
-        ]
-
-    for n in (0, 1):
-        for copy in column_loads(n):
-            copy.start()
+    def cot_load(i):
+        slot = lax.rem(i, 2)
+        return pltpu.make_async_copy(cotangent.at[me ^ i], cot_in.at[slot], cot_sems.at[slot])
+
+    for i in (0, 1):
+        cot_load(i).start()
     greet(gather.sibling, gather.x, gather.y)
     for j in order:
         part = pl.ds(j * size, size)
@@ -713,40 +703,28 @@
         act_copy(i).start()
         hidden_copy(i).start()
         gate, up = acc[:, :units], acc[:, units:]
-        inner_turned[i] = (gate / (1.0 + jnp.exp(-gate)) * up).astype(bf16).T
+        inner_turned = (gate / (1.0 + jnp.exp(-gate)) * up).astype(bf16).T
+        cot_load(i).wait()
+
+        @pl.when(i == 0)
+        def _():
+            down_sum[...] = dot(inner_turned, cot_in[0])
+
+        @pl.when(i > 0)
+        def _():
+            down_sum[...] += dot(inner_turned, cot_in[lax.rem(i, 2)])
+
+        @pl.when(i + 2 < width)
+        def _():
+            cot_load(i + 2).start()
+
         return carry
 
-    def down_copy(n):
-        part = pl.ds(pl.multiple_of(n * tok, tok), tok)
-        slot = lax.rem(n, 2)
-        return pltpu.make_async_copy(down_stage.at[slot], down_part.at[:, part], down_sem.at[slot])
-
-    def down_tile(n, carry):
-        slot = lax.rem(n, 2)
-        for copy in column_loads(n):
-            copy.wait()
-
-        @pl.when(n >= 2)
-        def _():
-            down_copy(n - 2).wait()
-
-        acc = dot(inner_turned[0], column_in[slot, :tok])
-        for i in range(1, width):
-            acc = acc + dot(inner_turned[i], column_in[slot, i * tok : (i + 1) * tok])
-        down_stage[slot] = acc.astype(bf16)
-        down_copy(n).start()
-
-        @pl.when(n + 2 < tiles)
-        def _():
-            for copy in column_loads(n + 2):
-                copy.start()
-
-        return carry
-
     lax.fori_loop(0, width, block, 0)
-    lax.fori_loop(0, tiles, down_tile, 0)
-    for n in (tiles - 2, tiles - 1):
-        down_copy(n).wait()
+    down_stage[...] = down_sum[...].astype(bf16)
+    down_copy = pltpu.make_async_copy(down_stage, down_part, down_sem)
+    down_copy.start()
+    down_copy.wait()
     gather.wait_sends()
     for i in (width - 2, width - 1):
         act_copy(i).wait()
@@ -786,13 +764,13 @@
         scratch_shapes=[
             pltpu.VMEM((width, tok, model), bf16),
             pltpu.VMEM((2, tok, 2 * units), f32),
-            pltpu.VMEM((width, units, tok), bf16),
-            pltpu.VMEM((2, width * tok, tok), bf16),
-            pltpu.VMEM((2, units, tok), bf16),
+            pltpu.VMEM((2, tok, model), bf16),
+            pltpu.VMEM((units, model), f32),
+            pltpu.VMEM((units, model), bf16),
             DMA((width,)),
             DMA((2,)),
-            DMA((2, width)),
             DMA((2,)),
+            DMA,
         ]
         + Gather.scratch(chunks),
         compiler_params=pltpu.CompilerParams(
@@ -897,12 +875,12 @@
             for copy in column_loads(n + 2):
                 copy.start()
 
-        @pl.when(n == 2)
+        @pl.when(n == 0)
         def _():
             for j in second_half:
                 scatter.far(j)
 
-        @pl.when(n == 5)
+        @pl.when(n == 3)
         def _():
             for j in first_half:
                 scatter.far(j)
@@ -955,6 +933,142 @@
             collective_id=call, has_side_effects=True, vmem_limit_bytes=62 << 20
         ),
     )(hidden, cotangent, acts, w_feed, w_down)
+
+
+def gradient_kernel(
+    chunks, gain, grad_hidden_hbm, middle_hbm, cotangent_hbm, w_out_hbm, mixed_hbm,
+    grad_mixed, w_part, grad_middle, term,
+    blocks, total, grad_hidden, middle, cotangent, w_out, mixed, chunk_sems, whole_sems, *sems,
+):
+    f32, bf16 = jnp.float32, jnp.bfloat16
+    width, tok, _ = blocks.shape
+    me = lax.axis_index(R)
+    size = tok // chunks
+
+    def item(j):
+        part = pl.ds(j * size, size)
+        return blocks.at[me, part], lambda owner: blocks.at[owner, part]
+
+    gather = Gather([item(j) for j in range(chunks)], sems)
+    order = [x for j in range(chunks // 2) for x in (j, chunks // 2 + j)]
+
+    def chunk_loads(j):
+        part = pl.ds(j * size, size)
+        pairs = (grad_hidden_hbm, grad_hidden), (middle_hbm, middle), (cotangent_hbm, cotangent)
+        return [
+            pltpu.make_async_copy(src.at[part], dst.at[part], chunk_sems.at[j, n])
+            for n, (src, dst) in enumerate(pairs)
+        ]
+
+    loads = {j: chunk_loads(j) for j in order}
+    whole = [
+        pltpu.make_async_copy(w_out_hbm, w_out, whole_sems.at[0]),
+        pltpu.make_async_copy(mixed_hbm, mixed, whole_sems.at[1]),
+    ]
+    for j in order:
+        for copy in loads[j]:
+            copy.start()
+    for copy in whole:
+        copy.start()
+    greet(gather.sibling, gather.x, gather.y)
+    terms = jnp.zeros(gain.shape, f32)
+    for j in order:
+        part = pl.ds(j * size, size)
+        for copy in loads[j]:
+            copy.wait()
+        residual = middle[part, :]
+        scale = inverse_rms(residual)
+        normed = residual * scale
+        grad = grad_hidden[part, :]
+        terms = terms + jnp.sum(grad * normed, axis=0, keepdims=True)
+        grad = grad * gain[...]
+        inner = jnp.mean(grad * normed, axis=1, keepdims=True)
+        result = cotangent[part, :].astype(f32) + scale * (grad - normed * inner)
+        grad_middle[part, :] = result
+        blocks[me, part] = result.astype(bf16)
+        gather.start_items((j,))
+    term[...] = terms
+    for copy in whole:
+        copy.wait()
+
+    def block(i, carry):
+        @pl.when(i == 1)
+        def _():
+            gather.from_sibling(3)
+
+        @pl.when(i == 2)
+        def _():
+            for j in order:
+                gather.pass_on(0, j)
+                gather.pass_on(1, j)
+
+        @pl.when(i == 3)
+        def _():
+            gather.from_sibling(4)
+
+        @pl.when(i == 5)
+        def _():
+            gather.from_sibling(5)
+
+        @pl.when(i == 6)
+        def _():
+            for j in order:
+                gather.pass_on(2, j)
+
+        @pl.when(i == 7)
+        def _():
+            gather.from_sibling(6)
+
+        rows = pl.ds(pl.multiple_of((me ^ i) * tok, tok), tok)
+        grad_mixed[rows, :] = dot(blocks[me ^ i], w_out[...], 1, 1).astype(bf16)
+        product = dot(mixed[rows, :], blocks[me ^ i], 0, 0)
+
+        @pl.when(i == 0)
+        def _():
+            total[...] = product
+
+        @pl.when(i > 0)
+        def _():
+            total[...] += product
+
+        return carry
+
+    lax.fori_loop(0, width, block, 0)
+    w_part[...] = total[...].astype(bf16)
+    gather.wait_sends()
+
+
+def gradient_layer(grad_hidden, middle, cotangent, gain, w_out, mixed, call, chunks=4):
+    width = lax.axis_size(R)
+    f32, bf16 = jnp.float32, jnp.bfloat16
+    tok, model = middle.shape
+    vmem = pl.BlockSpec(memory_space=pltpu.VMEM)
+    return pl.pallas_call(
+        functools.partial(gradient_kernel, chunks),
+        out_shape=[
+            jax.ShapeDtypeStruct(mixed.shape, bf16),
+            jax.ShapeDtypeStruct(w_out.shape, bf16),
+            jax.ShapeDtypeStruct((tok, model), f32),
+            jax.ShapeDtypeStruct((1, model), f32),
+        ],
+        in_specs=[vmem] + [ANY] * 5,
+        out_specs=[vmem] * 4,
+        scratch_shapes=[
+            pltpu.VMEM((width, tok, model), bf16),
+            pltpu.VMEM(w_out.shape, f32),
+            pltpu.VMEM((tok, model), f32),
+            pltpu.VMEM((tok, model), f32),
+            pltpu.VMEM((tok, model), bf16),
+            pltpu.VMEM(w_out.shape, bf16),
+            pltpu.VMEM(mixed.shape, bf16),
+            DMA((chunks, 3)),
+            DMA((2,)),
+        ]
+        + Gather.scratch(chunks),
+        compiler_params=pltpu.CompilerParams(
+            collective_id=call, has_side_effects=True, vmem_limit_bytes=60 << 20
+        ),
+    )(gain, grad_hidden, middle, cotangent, w_out, mixed)
 
 
 def back_kernel(
@@ -1583,6 +1697,22 @@
         to = slice(head * HEAD_DIM, (head + 1) * HEAD_DIM)
         key[:, to] = both[:, :HEAD_DIM]
         value[:, to] = both[:, HEAD_DIM:]
+
+
+def widen_kernel(x, out):
+    out[...] = x[0].astype(jnp.float32)
+
+
+def widen(x):
+    count, rows, columns = x.shape
+    return pl.pallas_call(
+        widen_kernel,
+        grid=(count,),
+        in_specs=[pl.BlockSpec((1, rows, columns), lambda i: (i, 0, 0))],
+        out_specs=pl.BlockSpec((rows, columns), lambda i: (i, 0)),
+        out_shape=jax.ShapeDtypeStruct((count * rows, columns), jnp.float32),
+        compiler_params=pltpu.CompilerParams(vmem_limit_bytes=60 << 20),
+    )(x)
 
 
 def join_call(kernel, arrays, outs, block=64):
@@ -1729,8 +1859,6 @@
         hidden_blocks, acts, down_part = middle_layer(middle, gain_mid[None], w_feed, cot_blocks, 2)
     else:
         middle = tok_float + plane_scatter(dot(mixed, w_out).astype(bf16), 1)
-    scale_mid = inverse_rms(middle)
-    normed_mid = middle * scale_mid
 
     if plane_kernels:
         out_part, grad_hidden_mid, feed_part = feed_forward(
@@ -1738,6 +1866,8 @@
         )
     else:
         w_gate, w_up = w_feed[:, :hidden_units], w_feed[:, hidden_units:]
+        scale_mid = inverse_rms(middle)
+        normed_mid = middle * scale_mid
         hidden_mid = plane_gather((normed_mid * gain_mid).astype(bf16), 2)
         gate_acc = dot(hidden_mid, w_gate)
         up_acc = dot(hidden_mid, w_up)
@@ -1758,15 +1888,19 @@
         feed_out = plane_scatter(out_part, 4)
     down_rows = line_scatter(down_part)
     feed_rows = line_scatter(feed_part)
-    gain_mid_term = jnp.sum(grad_hidden_mid * normed_mid, axis=0)
-    grad_normed_mid = grad_hidden_mid * gain_mid
-    grad_middle = cotangent.astype(f32) + scale_mid * (
-        grad_normed_mid - normed_mid * jnp.mean(grad_normed_mid * normed_mid, axis=1, keepdims=True)
-    )
-
-    grad_branch = plane_gather(grad_middle.astype(bf16), 6)
-    grad_mixed = dot(grad_branch, w_out, 1, 1).astype(bf16)
-    w_out_part = dot(mixed, grad_branch, 0, 0).astype(bf16)
+    if plane_kernels:
+        grad_mixed, w_out_part, grad_middle, gain_mid_term = gradient_layer(
+            grad_hidden_mid, middle, cotangent, gain_mid[None], w_out, mixed, 6
+        )
+        gain_mid_term = gain_mid_term[0]
+    else:
+        gain_mid_term = jnp.sum(grad_hidden_mid * normed_mid, axis=0)
+        grad_normed_mid = grad_hidden_mid * gain_mid
+        inner = jnp.mean(grad_normed_mid * normed_mid, axis=1, keepdims=True)
+        grad_middle = cotangent.astype(f32) + scale_mid * (grad_normed_mid - normed_mid * inner)
+        grad_branch = plane_gather(grad_middle.astype(bf16), 6)
+        grad_mixed = dot(grad_branch, w_out, 1, 1).astype(bf16)
+        w_out_part = dot(mixed, grad_branch, 0, 0).astype(bf16)
 
     if plane_kernels:
         grad_qkv, qkv_part, feed_out, down_all, w_out_part = attention_back(
@@ -1838,7 +1972,10 @@
         qkv_all = lax.all_gather(qkv_rows, R, axis=0, tiled=False)
         out_all = lax.all_gather(out_rows, R, axis=0, tiled=False)
         gain_terms = lax.psum(lax.psum_scatter(terms, F, scatter_dimension=1, tiled=True), R)
-    down_grad = down_all.reshape(feed // planes, model).astype(f32)
+    if plane_kernels:
+        down_grad = widen(down_all)
+    else:
+        down_grad = down_all.reshape(feed // planes, model).astype(f32)
     gate_grad, up_grad = join_call(
         functools.partial(join_feed_kernel, planes, piece), [feed_all], [feed, feed]
     )

time: 640 us -> 628 us (0.981)
  matrix products: 10.5 us -> 0 us
  other arithmetic: 23.6 us -> 14.2 us
  Pallas kernels: 544 us -> 551 us
    pallas_call x1 -> x2, Pallas kernels: 38.9 us -> 51 us  [the longest x1 42.5 us: gradient_layer(): pl.pallas_call(functools.partial(gradient_kernel, chunks), out_shape=[jax...]
    dot_general x2 -> x0, matrix products: 10.5 us -> none  [dot(): lax.dot_general(a, b, (((ca,), (cb,)), ((), ())), preferred_element_type=...]
    convert_element_type x2 -> x1, other arithmetic: 10.5 us -> 2.98 us  [per_device(): activations = (middle + feed_out).astype(bf16)]
    unnamed x68 -> x56, local copies, waits for them, and re-layouts: 22.5 us -> 21.6 us
  transfers between devices with their start and end apart: 7 -> 7, of which waited for: 1 -> 1; matrix products, arithmetic and copies ran while one was open for 7% -> 4% of each run, Pallas kernels for 80% -> 83%
where the time goes in v7:
time: 628 us; the launch traced here: 624 us
  Pallas kernels  551 us (88%)
  local copies, waits for them, and re-layouts  35 us (6%)
  between operations  15 us (2%)
  other arithmetic  14.2 us (2%)
  waiting for transfers between devices  7.89 us (1%)
    pallas_call x1, Pallas kernels, attention_back(): pl.pallas_call(functools.partial(back_kernel, chunks, heads), out_shape=[...  104 us
    pallas_call x1, Pallas kernels, scatter_hidden(): pl.pallas_call(functools.partial(hidden_kernel, chunks), out_shape=[jax.S...  84.6 us
    pallas_call x1, Pallas kernels, feed_forward(): pl.pallas_call(functools.partial(feed_kernel, chunks), out_shape=[jax.Sha...  64.8 us
    pallas_call x1, Pallas kernels, project(): pl.pallas_call(functools.partial(project_kernel, chunks), out_shape=[jax....  53.1 us
    pallas_call x1, Pallas kernels, middle_layer(): pl.pallas_call(functools.partial(middle_kernel, chunks), out_shape=[jax.S...  49.8 us
    pallas_call x1, Pallas kernels, enter(): pl.pallas_call(functools.partial(enter_kernel, chunks), out_shape=[jax.Sh...  45.7 us
    pallas_call x1, Pallas kernels, gradient_layer(): pl.pallas_call(functools.partial(gradient_kernel, chunks), out_shape=[jax...  42.5 us
    pallas_call x1, Pallas kernels, branch_layer(): pl.pallas_call(functools.partial(branch_kernel, chunks), out_shape=jax.Sh...  42 us
  transfers between devices with their start and end apart: 7, of which 1 were waited for; matrix products, arithmetic and copies ran while one was open for 4% of the time, Pallas kernels for 83%

profile of v7, /device:TPU:0, one launch (start us, length us, event | category | flops | bytes accessed | tf_op | source)
XLA Modules:
  0.0 624.0 jit_solution(2291926522461680598)
XLA Ops:
  7.2 0.0 all-gather.4.cloned.1.call-start
  7.3 1.2 constant_dynamic-slice_fusion.10
  8.5 1.1 constant_dynamic-slice_fusion.9
  9.6 1.0 pad_maximum_fusion
  10.6 0.0 all-gather.4.cloned.1.call-update
  10.6 0.0 all-gather.6.cloned.1.call-start
  10.7 45.7 %shard_map.203 = (bf16[8,256,2048]{2,1,0:T(8,128)(2,1)S(1)}, f32[4,8,512]{2,1,0:T(8,128)S(1)}, s32[8,8,128]{2,1,0:T(8,128)S(1)}) custom-call(bf16[256,2048]{1,0:T(8,128)(2,1)S(1)} %copy-done.3, f32[8,512]{1,0:T(8,128)S(1)} %fusion.14.gains, s32[8,128]{1,0:T(8,128)S(1)} %bitcast.36), custom_call_target="tpu_custom_call" | custom-call | tf_op jit(solution)/shard_map/pallas_call | solution.py:1391
  56.5 3.4 copy-done
  59.9 2.9 constant_dynamic-slice_fusion.1
  62.8 2.4 concatenate.12
  65.2 0.0 all-gather.8.cloned.1.call-start
  65.2 2.1 constant_dynamic-slice_fusion
  67.3 0.2 reduce-scatter.5.cloned.1.call-start
  67.5 0.1 slice_compare_fusion
  67.6 0.1 select_bitcast_fusion
  67.7 2.3 reduce-window.6
  70.0 0.3 slice_reduce_fusion
  70.3 0.2 reduce-window.9
  70.4 0.1 maximum_bitcast_fusion
  70.6 0.4 slice_reduce_fusion.2
  71.0 0.5 slice_reduce_fusion.1
  71.5 0.6 fusion.24
  72.1 5.0 fusion.10
  77.1 2.3 copy-done.4
  79.4 1.3 copy-done.8
  80.7 1.2 copy-done.12
  81.9 53.1 %shard_map.204 = (bf16[2048,256]{1,0:T(8,128)(2,1)S(1)}, bf16[8,4,256,128]{3,2,1,0:T(8,128)(2,1)S(1)}, bf16[8,256,2048]{2,1,0:T(8,128)(2,1)}, bf16[256,2048]{1,0:T(8,128)(2,1)S(1)}) custom-call(bf16[8,256,2048]{2,1,0:T(8,128)(2,1)} %copy-done, bf16[2048,640]{1,0:T(8,128)(2,1)S(1)} %copy-done.4, f32[2048,128]{1,0:T(8,128)S(1)} %copy-done.8, ...), custom_call_target="tpu_custom_call" | custom-call | tf_op jit(solution)/shard_map/pallas_call | solution.py:1414
  135.1 13.1 %shard_map.205 = (bf16[2048,256]{1,0:T(8,128)(2,1)S(1)}, f32[16,1,512]{2,1,0:T(1,128)S(1)}) custom-call(s32[16]{0:T(128)S(1)} %and_select_fusion.5.low, s32[16]{0:T(128)S(1)} %fusion.21.high, bf16[2048,256]{1,0:T(8,128)(2,1)S(1)} %get-tuple-element.56.q, bf16[8,1024,128]{2,1,0:T(8,128)(2,1)S(1)} %bitcast.33, s32[16,1,128]{2,1,0:T(1,128)S(1)} %get-tuple-element.118.starts, ...), custom_call_target="tpu_custom_call" | custom-call | tf_op jit(solution)/shard_map/pallas_call | solution.py:1665
  148.2 0.6 copy-done.20
  148.8 42.0 %shard_map.206.middle.middle_hbm = f32[256,2048]{1,0:T(8,128)S(1)} custom-call(bf16[2048,256]{1,0:T(8,128)(2,1)S(1)} %get-tuple-element.58.mixed.mixed_hbm, bf16[256,2048]{1,0:T(8,128)(2,1)S(1)} %get-tuple-element.59.w_out.w_out_hbm, bf16[256,2048]{1,0:T(8,128)(2,1)S(1)} %copy-done.3), custom_call_target="tpu_custom_call" | custom-call | tf_op jit(solution)/shard_map/pallas_call | solution.py:737
  190.8 1.3 copy-done.1
  192.1 1.0 copy-done.9
  193.1 1.0 copy-done.13
  194.1 49.8 %shard_map.207 = (bf16[8,256,2048]{2,1,0:T(8,128)(2,1)}, f32[8,256,1408]{2,1,0:T(8,128)}, bf16[704,2048]{1,0:T(8,128)(2,1)}) custom-call(f32[256,2048]{1,0:T(8,128)} %copy-done.1, f32[1,2048]{1,0:T(1,128)} %bitcast.40, bf16[2048,1408]{1,0:T(8,128)(2,1)} %all-gather.6.cloned.1.call-done.w_feed, bf16[8,256,2048]{2,1,0:T(8,128)(2,1)} %get-tuple-element.63.cotangent), custom_call_target="tpu_custom_call" | custom-call | tf_op jit(solution)/shard_map/pallas_call | solution.py:755
  243.9 0.0 reduce-scatter.5.cloned.1.call-update
  243.9 0.3 reduce-scatter.7.cloned.1.call-start
  244.2 7.1 %all-gather.8.cloned.1.call-done.w_down = bf16[704,2048]{1,0:T(8,128)(2,1)} async-done(((bf16[176,2048]{1,0:T(8,128)(2,1)}), bf16[704,2048]{1,0:T(8,128)(2,1)}) %all-gather.8.cloned.1.call-update) | async-done | bytes 2883600 | tf_op jit(solution)/shard_map/all_gather | solution.py:1560
  251.3 64.8 %shard_map.208 = (bf16[8,256,2048]{2,1,0:T(8,128)(2,1)}, f32[256,2048]{1,0:T(8,128)}, bf16[2048,1408]{1,0:T(8,128)(2,1)}) custom-call(bf16[8,256,2048]{2,1,0:T(8,128)(2,1)} %get-tuple-element.64.hidden, bf16[8,256,2048]{2,1,0:T(8,128)(2,1)} %get-tuple-element.63.cotangent, f32[8,256,1408]{2,1,0:T(8,128)} %get-tuple-element.65.acts, ...), custom_call_target="tpu_custom_call" | custom-call | tf_op jit(solution)/shard_map/pallas_call | solution.py:910
  316.1 0.0 reduce-scatter.7.cloned.1.call-update
  316.1 0.0 reduce-scatter.11.cloned.1.call-start
  316.2 42.5 %shard_map.209 = (bf16[2048,256]{1,0:T(8,128)(2,1)}, bf16[256,2048]{1,0:T(8,128)(2,1)}, f32[256,2048]{1,0:T(8,128)}, f32[1,2048]{1,0:T(1,128)}) custom-call(f32[1,2048]{1,0:T(1,128)} %bitcast.41, f32[256,2048]{1,0:T(8,128)} %get-tuple-element.67.grad_hidden_hbm, f32[256,2048]{1,0:T(8,128)} %copy-done.1, bf16[256,2048]{1,0:T(8,128)(2,1)} %cotangent_hbm.1, ...), custom_call_target="tpu_custom_call" | custom-call | tf_op jit(solution)/shard_map/pallas_call | solution.py:1046
  358.7 0.0 reduce-scatter.5.cloned.1.call-done.down_rows
  358.7 103.9 %shard_map.210 = (bf16[2048,384]{1,0:T(8,128)(2,1)}, bf16[2048,384]{1,0:T(8,128)(2,1)}, f32[256,2048]{1,0:T(8,128)}, bf16[8,176,2048]{2,1,0:T(8,128)(2,1)}, bf16[8,256,256]{2,1,0:T(8,128)(2,1)}) custom-call(bf16[2048,256]{1,0:T(8,128)(2,1)} %copy-done.11, bf16[8,1024,128]{2,1,0:T(8,128)(2,1)} %bitcast.34, s32[16,1,128]{2,1,0:T(1,128)} %copy-done.19, ...), custom_call_target="tpu_custom_call" | custom-call | tf_op jit(solution)/shard_map/pallas_call | solution.py:1308
  462.7 0.0 reduce-scatter.11.cloned.1.call-update
  462.7 0.0 reduce-scatter.9.cloned.1.call-start
  462.7 0.0 reduce-scatter.7.cloned.1.call-done.feed_rows
  462.8 0.7 reduce-scatter.9.cloned.1.call-update
  463.4 0.3 fusion.9
  463.7 8.5 %shard_map.215 = f32[1408,2048]{1,0:T(8,128)} custom-call(bf16[8,176,2048]{2,1,0:T(8,128)(2,1)} %get-tuple-element.94.x), custom_call_target="tpu_custom_call" | custom-call | tf_op jit(solution)/shard_map/pallas_call | solution.py:1708
  472.3 3.0 add_convert_fusion
  475.3 1.4 copy-done.17
  476.6 84.6 %shard_map.211 = (f32[256,2048]{1,0:T(8,128)S(1)}, bf16[8,512,1408]{2,1,0:T(8,128)(2,1)}) custom-call(bf16[2048,384]{1,0:T(8,128)(2,1)S(1)} %copy-done.16, bf16[2048,640]{1,0:T(8,128)(2,1)S(1)} %copy-done.5, bf16[512,1408]{1,0:T(8,128)(2,1)S(1)} %copy-done.17), custom_call_target="tpu_custom_call" | custom-call | tf_op jit(solution)/shard_map/pallas_call | solution.py:1372
  561.3 4.3 copy-done.6
  565.5 9.0 %shard_map.214 = (f32[512,5632]{1,0:T(8,128)}, f32[512,5632]{1,0:T(8,128)}) custom-call(bf16[8,512,1408]{2,1,0:T(8,128)(2,1)S(1)} %copy-done.6), custom_call_target="tpu_custom_call" | custom-call | tf_op jit(solution)/shard_map/pallas_call | solution.py:1720
  574.5 0.7 fusion.8
  575.2 0.0 copy-done.23
  575.2 0.6 pad.13.terms
  575.9 0.2 copy-done.22
  576.1 1.6 fusion.7
  577.7 29.4 %shard_map.212 = (bf16[8,512,384]{2,1,0:T(8,128)(2,1)}, bf16[8,512,256]{2,1,0:T(8,128)(2,1)}, f32[8,512]{1,0:T(8,128)}) custom-call(bf16[512,384]{1,0:T(8,128)(2,1)} %reduce-scatter.9.cloned.1.call-done.qkv, bf16[512,256]{1,0:T(8,128)(2,1)} %reduce-scatter.11.cloned.1.call-done.out_rows, f32[4,8,512]{2,1,0:T(8,128)} %pad.13.terms), custom_call_target="tpu_custom_call" | custom-call | tf_op jit(solution)/shard_map/pallas_call | solution.py:434
  607.1 1.4 fusion.23
  608.5 1.9 copy-done.14
  610.4 1.6 copy-done.15
  612.0 4.8 shard_map.213
  (61 shorter events, 0.3 us)
Async XLA Ops:
  7.2 3.5 copy-start.24
  7.2 3.5 copy-start.25
  7.2 3.5 copy-start.21
  7.2 3.5 copy-start.3
  7.2 69.9 %all-gather.4.cloned.1.call-start = ((), (), s32[]{:S(2)}) async-start(), calls=%async_computation.4 | async-start | bytes 3276800 | tf_op jit(solution)/shard_map/all_gather | solution.py:1560
  10.6 183.5 %all-gather.6.cloned.1.call-start = ((), (), s32[]{:S(2)}) async-start(), calls=%async_computation.5 | async-start | bytes 7208960 | tf_op jit(solution)/shard_map/all_gather | solution.py:1560
  56.5 3.4 copy-start
  65.2 186.1 %all-gather.8.cloned.1.call-start = ((), (), s32[]{:S(2)}) async-start(), calls=%async_computation.6 | async-start | bytes 3604480 | tf_op jit(solution)/shard_map/all_gather | solution.py:1560
  67.3 291.4 %reduce-scatter.5.cloned.1.call-start = ((), (), s32[]{:S(2)}) async-start(), calls=%async_computation.7 | async-start | bytes 3604480 | tf_op jit(solution)/shard_map/reduce_scatter | solution.py:1564
  70.6 64.4 %copy-start.18 = (s32[16,1,128]{2,1,0:T(1,128)}, s32[16,1,128]{2,1,0:T(1,128)S(1)}, u32[]{:S(2)}) copy-start(s32[16,1,128]{2,1,0:T(1,128)S(1)} %get-tuple-element.117.places) | copy-start | bytes 24580
  70.6 64.4 %copy-start.19 = (s32[16,1,128]{2,1,0:T(1,128)}, s32[16,1,128]{2,1,0:T(1,128)S(1)}, u32[]{:S(2)}) copy-start(s32[16,1,128]{2,1,0:T(1,128)S(1)} %get-tuple-element.118.starts) | copy-start | bytes 24580
  77.1 57.9 %copy-start.7 = (f32[2048,128]{1,0:T(8,128)}, f32[2048,128]{1,0:T(8,128)S(1)}, u32[]{:S(2)}) copy-start(f32[2048,128]{1,0:T(8,128)S(1)} %get-tuple-element.111.sine) | copy-start | bytes 3145732
  77.1 2.3 copy-start.4
  79.4 1.3 copy-start.8
  80.7 1.2 copy-start.12
  135.0 13.8 %copy-start.10 = (bf16[8,4,256,128]{3,2,1,0:T(8,128)(2,1)}, bf16[8,4,256,128]{3,2,1,0:T(8,128)(2,1)S(1)}, u32[]{:S(2)}) copy-start(bf16[8,4,256,128]{3,2,1,0:T(8,128)(2,1)S(1)} %get-tuple-element.57) | copy-start | bytes 6291460
  135.0 13.8 %copy-start.11 = (bf16[2048,256]{1,0:T(8,128)(2,1)}, bf16[2048,256]{1,0:T(8,128)(2,1)S(1)}, u32[]{:S(2)}) copy-start(bf16[2048,256]{1,0:T(8,128)(2,1)S(1)} %get-tuple-element.56.q) | copy-start | bytes 3145732
  148.2 0.6 copy-start.20
  190.8 1.3 copy-start.1
  192.1 1.0 copy-start.9
  193.1 1.0 copy-start.13
  243.9 218.8 %reduce-scatter.7.cloned.1.call-start = ((), (), s32[]{:S(2)}) async-start(), calls=%async_computation.8 | async-start | bytes 7208960 | tf_op jit(solution)/shard_map/reduce_scatter | solution.py:1564
  316.1 261.6 %reduce-scatter.11.cloned.1.call-start = ((), (), s32[]{:S(2)}) async-start(), calls=%async_computation.10 | async-start | bytes 1310720 | tf_op jit(solution)/shard_map/reduce_scatter | solution.py:1564
  462.7 115.0 %reduce-scatter.9.cloned.1.call-start = ((), (), s32[]{:S(2)}) async-start(), calls=%async_computation.9 | async-start | bytes 1966080 | tf_op jit(solution)/shard_map/reduce_scatter | solution.py:1564
  463.7 8.5 %copy-start.2 = (f32[256,2048]{1,0:T(8,128)S(1)}, f32[256,2048]{1,0:T(8,128)}, u32[]{:S(2)}) copy-start(f32[256,2048]{1,0:T(8,128)} %copy-done.1) | copy-start | bytes 6291460
  472.3 3.0 copy-start.5
  472.3 3.0 copy-start.16
  475.2 1.4 copy-start.17
  561.3 4.3 copy-start.6
  574.5 0.7 copy-start.23
  574.5 1.6 copy-start.22
  608.5 1.9 copy-start.14
  610.4 1.6 copy-start.15
Sparse Core Ops, SparseCore 0:
  10.7 57.4 all-gather.3
  70.4 106.9 all-gather.5
  178.9 72.2 all-gather.7
  253.4 70.3 reduce-scatter.4
  326.0 114.3 reduce-scatter.6
  462.8 27.4 reduce-scatter.10
  492.7 33.9 reduce-scatter.8

commit v8 on v7

--- a/solution.py
+++ b/solution.py
@@ -164,10 +164,32 @@
     own.wait()
 
 
-def enter_kernel(chunks, tokens, gains, ids, hidden, all_gains, all_ids, own, own_sem, to_z, at_z, *sems):
+def enter_kernel(
+    chunks, piece, tokens, gains, ids, gate, up, down, hidden, all_gains, all_ids, feed_cols, down_rows,
+    own, windows, joined, window_sems, rows_sem, own_sem, to_z, at_z, *sems,
+):
     f32 = jnp.float32
     planes = all_gains.shape[0]
     z = lax.axis_index(F)
+    me = lax.axis_index(R)
+    count, span = windows.shape[0], windows.shape[2]
+    total = gate.shape[1]
+
+    def window(k):
+        first = (k % planes) * (total // planes) + me * piece
+        start = jnp.minimum(first // 128 * 128, total - span)
+        return pl.multiple_of(start, 128), first - start
+
+    cuts = []
+    for k in range(count):
+        source = gate if k < planes else up
+        src = source.at[:, pl.ds(window(k)[0], span)]
+        cuts.append(pltpu.make_async_copy(src, windows.at[k], window_sems.at[k]))
+        cuts[-1].start()
+    own_rows = pltpu.make_async_copy(
+        down.at[pl.ds(pl.multiple_of(me * piece, 16), piece)], down_rows, rows_sem
+    )
+    own_rows.start()
     items = row_items(own, hidden, chunks) + [(ids, lambda owner: all_ids.at[owner])]
     gather = Gather(items, sems)
     others = [lax.rem(z + i, planes) for i in range(1, planes)]
@@ -205,10 +227,29 @@
     kept = pltpu.make_async_copy(own, hidden.at[gather.me], own_sem)
     kept.start()
     gather.start()
+
+    def cut(k):
+        cuts[k].wait()
+        shift = lax.rem(span - window(k)[1], span)
+
+        def some(n, carry):
+            rows = pl.ds(pl.multiple_of(n * 64, 64), 64)
+            turned = pltpu.roll(windows[k, rows, :].astype(f32), shift, 1)
+            joined[rows, k * piece : (k + 1) * piece] = turned[:, :piece]
+            return carry
+
+        lax.fori_loop(0, joined.shape[0] // 64, some, 0)
+
+    done = 0
     for i in range(gather.count):
+        while done < count * (i + 1) // gather.count:
+            cut(done)
+            done += 1
         gather.relay(i)
+    feed_cols[...] = joined[...].astype(jnp.bfloat16)
     gather.finish()
     kept.wait()
+    own_rows.wait()
 
 
 def turn(x, cosine, sine):
@@ -1085,7 +1126,13 @@
     core = lax.rem(me, 2)
     above, below = lax.rem(z + 1, planes), lax.rem(z + planes - 1, planes)
     scatter = Scatter(feed_out, chunks, refs[:12])
-    gather = Gather(row_items(down_rows, all_down, 1), refs[12:])
+    cut = (down_rows.shape[0] // 2 + 15) // 16 * 16
+
+    def down_item(first, count):
+        part = pl.ds(first, count)
+        return down_rows.at[part], lambda owner: all_down.at[owner, part]
+
+    gather = Gather([down_item(0, cut), down_item(cut, down_rows.shape[0] - cut)], refs[12:])
     barrier = pltpu.get_barrier_semaphore()
     for other in (above, below):
         pl.semaphore_signal(barrier, inc=1, device_id={F: other}, device_id_type=MESH)
@@ -1171,6 +1218,7 @@
         @pl.when(n == 11)
         def _():
             gather.relay(0)
+            gather.relay(1)
 
         return carry
 
@@ -1329,7 +1377,7 @@
         + [pltpu.VMEM((2, width * tok, tok), bf16), pltpu.VMEM((2, tok, columns), bf16)]
         + [DMA((2,)), DMA((2,)), DMA((4,))]
         + Scatter.scratch(tok, model, chunks)
-        + Gather.scratch(1),
+        + Gather.scratch(2),
         compiler_params=pltpu.CompilerParams(
             collective_id=call, has_side_effects=True, vmem_limit_bytes=60 << 20
         ),
@@ -1384,26 +1432,39 @@
     )(grad_qkv, weight, feed_rows)
 
 
-def enter(tokens, gains, ids, call, chunks=4):
+def enter(tokens, gains, ids, gate, up, down, piece, call, chunks=4):
     planes, rows = lax.axis_size(F), lax.axis_size(R)
     tok, model = tokens.shape
+    bf16, f32 = jnp.bfloat16, jnp.float32
+    depth = gate.shape[0]
+    span = (-(-piece // 128) + 1) * 128
     vmem = pl.BlockSpec(memory_space=pltpu.VMEM)
     return pl.pallas_call(
-        functools.partial(enter_kernel, chunks),
+        functools.partial(enter_kernel, chunks, piece),
         out_shape=[
-            jax.ShapeDtypeStruct((rows, tok, model), jnp.bfloat16),
-            jax.ShapeDtypeStruct((planes,) + gains.shape, jnp.float32),
+            jax.ShapeDtypeStruct((rows, tok, model), bf16),
+            jax.ShapeDtypeStruct((planes,) + gains.shape, f32),
             jax.ShapeDtypeStruct((rows,) + ids.shape, jnp.int32),
+            jax.ShapeDtypeStruct((depth, 2 * planes * piece), bf16),
+            jax.ShapeDtypeStruct((piece, down.shape[1]), bf16),
         ],
-        in_specs=[vmem] * 3,
-        out_specs=[ANY, vmem, vmem],
-        scratch_shapes=[pltpu.VMEM((tok, model), jnp.bfloat16), DMA]
-        + [DMA((planes - 1,))] * 2
+        in_specs=[vmem] * 3 + [ANY] * 3,
+        out_specs=[ANY, vmem, vmem, vmem, ANY],
+        scratch_shapes=[
+            pltpu.VMEM((tok, model), bf16),
+            pltpu.VMEM((2 * planes, depth, span), bf16),
+            pltpu.VMEM((depth, 2 * planes * piece), f32),
+            DMA((2 * planes,)),
+            DMA,
+            DMA,
+            DMA((planes - 1,)),
+            DMA((planes - 1,)),
+        ]
         + Gather.scratch(chunks + 1),
         compiler_params=pltpu.CompilerParams(
-            collective_id=call, has_side_effects=True, vmem_limit_bytes=32 << 20
+            collective_id=call, has_side_effects=True, vmem_limit_bytes=60 << 20
         ),
-    )(tokens, gains, ids)
+    )(tokens, gains, ids, gate, up, down)
 
 
 def project(hidden, weight, cosine, sine, cotangent, query_width, call, chunks=4):
@@ -1779,8 +1840,15 @@
     scale_in = inverse_rms(tok_float)
     normed_in = tok_float * scale_in
     if plane_kernels:
-        hidden_in, gains, ids = enter(
-            tokens, jnp.pad(own_gains, ((0, 6), (0, 0))), segment_ids.reshape(8, length // 8), 0
+        hidden_in, gains, ids, feed_cut, down_cut = enter(
+            tokens,
+            jnp.pad(own_gains, ((0, 6), (0, 0))),
+            segment_ids.reshape(8, length // 8),
+            gate_weight,
+            up_weight,
+            down_weight,
+            piece,
+            0,
         )
         hidden_in = hidden_in.reshape(all_tok, model)
         gains = gains[:, :2].transpose(1, 0, 2).reshape(2, model)
@@ -1789,21 +1857,15 @@
         gains = lax.all_gather(own_gains, F, axis=1, tiled=True)
         hidden_in = lax.all_gather((normed_in * gains[0]).astype(bf16), R, axis=0, tiled=True)
         ids = lax.all_gather(segment_ids, R, axis=0, tiled=True)
+        feed_cut = jnp.concatenate(feed_cols(gate_weight) + feed_cols(up_weight), axis=1)
+        down_cut = lax.dynamic_slice_in_dim(down_weight, r * piece, piece, 0)
     gain_in, gain_mid = gains[0], gains[1]
-    gate_weight, up_weight, down_weight, ids = lax.optimization_barrier(
-        (gate_weight, up_weight, down_weight, ids)
-    )
-    w_feed = line_gather(jnp.concatenate(feed_cols(gate_weight) + feed_cols(up_weight), axis=1))
-    w_down = line_gather(lax.dynamic_slice_in_dim(down_weight, r * piece, piece, 0))
-
-    places = jnp.arange(length, dtype=jnp.int32)
-    fresh = jnp.concatenate(
-        [jnp.ones((width, 1), dtype=jnp.bool_), ids[:, 1:] != ids[:, :-1]], axis=1
-    )
-    positions = places[None] - lax.cummax(jnp.where(fresh, places[None], 0), axis=1)
-    own_positions = lax.dynamic_slice_in_dim(positions, z * tok, tok, 1).reshape(all_tok)
+    w_feed, w_down = line_gather(feed_cut), line_gather(down_cut)
+
+    own_ids = lax.dynamic_slice_in_dim(ids, z * tok, tok, 1)
+    own_starts = jnp.sum(ids[:, None, :] < own_ids[:, :, None], axis=2, dtype=jnp.int32).reshape(all_tok)
     own_places = z * tok + jnp.arange(all_tok, dtype=jnp.int32) % tok
-    own_starts = own_places - own_positions
+    own_positions = own_places - own_starts
     steps = all_tok // QUERY_BLOCK
     starts = own_starts.reshape(steps, 1, QUERY_BLOCK)
     query_places = own_places.reshape(steps, 1, QUERY_BLOCK)

time: 628 us -> 612 us (0.975)
  local copies, waits for them, and re-layouts: 35 us -> 22.3 us
  Pallas kernels: 551 us -> 542 us
  waiting for transfers between devices: 7.89 us -> 16.1 us
    pallas_call x1, Pallas kernels: 104 us -> 89 us  [attention_back(): pl.pallas_call(functools.partial(back_kernel, chunks, heads), out_shape=[...]
    all_gather x3, waiting for transfers between devices: 7.08 us -> 14.8 us  [line_gather(): return lax.all_gather(x, F, axis=0, tiled=True)]
    unnamed x56 -> x52, local copies, waits for them, and re-layouts: 21.6 us -> 15.8 us
  transfers between devices with their start and end apart: 7 -> 7, of which waited for: 1 -> 1; matrix products, arithmetic and copies ran while one was open for 4% -> 2% of each run, Pallas kernels for 83% -> 83%
where the time goes in v8:
time: 612 us; the launch traced here: 609 us
  Pallas kernels  542 us (89%)
  local copies, waits for them, and re-layouts  22.3 us (4%)
  waiting for transfers between devices  16.1 us (3%)
  between operations  14.8 us (2%)
  other arithmetic  12.1 us (2%)
    pallas_call x1, Pallas kernels, attention_back(): pl.pallas_call(functools.partial(back_kernel, chunks, heads), out_shape=[...  89 us
    pallas_call x1, Pallas kernels, scatter_hidden(): pl.pallas_call(functools.partial(hidden_kernel, chunks), out_shape=[jax.S...  84.1 us
    pallas_call x1, Pallas kernels, feed_forward(): pl.pallas_call(functools.partial(feed_kernel, chunks), out_shape=[jax.Sha...  64.8 us
    pallas_call x1, Pallas kernels, project(): pl.pallas_call(functools.partial(project_kernel, chunks), out_shape=[jax....  52.9 us
    pallas_call x1, Pallas kernels, middle_layer(): pl.pallas_call(functools.partial(middle_kernel, chunks), out_shape=[jax.S...  49.8 us
    pallas_call x1, Pallas kernels, enter(): pl.pallas_call(functools.partial(enter_kernel, chunks, piece), out_shape=...  48.5 us
    pallas_call x1, Pallas kernels, gradient_layer(): pl.pallas_call(functools.partial(gradient_kernel, chunks), out_shape=[jax...  42.4 us
    pallas_call x1, Pallas kernels, branch_layer(): pl.pallas_call(functools.partial(branch_kernel, chunks), out_shape=jax.Sh...  42.1 us
  transfers between devices with their start and end apart: 7, of which 1 were waited for; matrix products, arithmetic and copies ran while one was open for 2% of the time, Pallas kernels for 83%

profile of v8, /device:TPU:0, one launch (start us, length us, event | category | flops | bytes accessed | tf_op | source)
XLA Modules:
  0.0 608.8 jit_solution(14159908370986553943)
XLA Ops:
  7.2 0.0 all-gather.4.cloned.1.call-start
  7.3 1.1 constant_dynamic-slice_fusion.1
  8.4 1.1 constant_dynamic-slice_fusion
  9.5 1.0 pad_maximum_fusion
  10.5 0.0 all-gather.4.cloned.1.call-update
  10.5 0.0 all-gather.6.cloned.1.call-start
  10.6 0.6 fusion.17.gains
  11.2 48.5 %shard_map.203 = (bf16[8,256,2048]{2,1,0:T(8,128)(2,1)}, f32[4,8,512]{2,1,0:T(8,128)}, s32[8,8,128]{2,1,0:T(8,128)}, bf16[512,1408]{1,0:T(8,128)(2,1)}, bf16[176,2048]{1,0:T(8,128)(2,1)}) custom-call(bf16[256,2048]{1,0:T(8,128)(2,1)} %tokens.3, f32[8,512]{1,0:T(8,128)} %fusion.17.gains, s32[8,128]{1,0:T(8,128)} %bitcast.35, bf16[512,5632]{1,0:T(8,128)(2,1)} %gate.1, ...), custom_call_target="tpu_custom_call" | custom-call | tf_op jit(solution)/shard_map/pallas_call | solution.py:1442
  59.7 0.0 copy-start.11
  59.7 0.0 all-gather.6.cloned.1.call-update
  59.7 0.0 all-gather.8.cloned.1.call-start
  59.8 0.7 all-gather.8.cloned.1.call-update
  60.5 0.6 reduce-scatter.5.cloned.1.call-start
  61.1 1.1 convert_reduce_fusion
  62.3 0.0 copy-start.17
  62.3 0.4 slice_reduce_fusion.1
  62.7 0.5 slice_reduce_fusion
  63.2 0.8 slice_bitcast_fusion
  64.0 0.6 fusion.29
  64.6 3.7 fusion.10
  68.4 0.0 copy-start.6
  68.4 0.0 all-gather.4.cloned.1.call-done.weight.w_cols
  68.4 2.1 copy-done.3
  70.5 52.9 %shard_map.204 = (bf16[2048,256]{1,0:T(8,128)(2,1)S(1)}, bf16[8,4,256,128]{3,2,1,0:T(8,128)(2,1)S(1)}, bf16[8,256,2048]{2,1,0:T(8,128)(2,1)}, bf16[256,2048]{1,0:T(8,128)(2,1)S(1)}) custom-call(bf16[8,256,2048]{2,1,0:T(8,128)(2,1)} %get-tuple-element.52.hidden, bf16[2048,640]{1,0:T(8,128)(2,1)S(1)} %copy-done.3, f32[2048,128]{1,0:T(8,128)S(1)} %get-tuple-element.98.cosine, ...), custom_call_target="tpu_custom_call" | custom-call | tf_op jit(solution)/shard_map/pallas_call | solution.py:1475
  123.4 0.0 copy-start.7
  123.4 1.0 copy-done.7
  124.4 13.1 %shard_map.205 = (bf16[2048,256]{1,0:T(8,128)(2,1)S(1)}, f32[16,1,512]{2,1,0:T(1,128)S(1)}) custom-call(s32[16]{0:T(128)S(1)} %get-tuple-element.101.low, s32[16]{0:T(128)S(1)} %get-tuple-element.102.high, bf16[2048,256]{1,0:T(8,128)(2,1)S(1)} %get-tuple-element.53.q, bf16[8,1024,128]{2,1,0:T(8,128)(2,1)S(1)} %bitcast.20, ...), custom_call_target="tpu_custom_call" | custom-call | tf_op jit(solution)/shard_map/pallas_call | solution.py:1726
  137.5 0.0 copy-start.19
  137.5 42.1 %shard_map.206.middle.middle_hbm = f32[256,2048]{1,0:T(8,128)S(1)} custom-call(bf16[2048,256]{1,0:T(8,128)(2,1)S(1)} %get-tuple-element.55.mixed.mixed_hbm, bf16[256,2048]{1,0:T(8,128)(2,1)S(1)} %get-tuple-element.56.w_out.w_out_hbm, bf16[256,2048]{1,0:T(8,128)(2,1)S(1)} %copy-done.2), custom_call_target="tpu_custom_call" | custom-call | tf_op jit(solution)/shard_map/pallas_call | solution.py:778
  179.7 0.0 copy-start
  179.7 1.3 copy-done
  181.0 1.0 copy-done.8
  182.0 1.0 copy-done.12
  182.9 49.8 %shard_map.207 = (bf16[8,256,2048]{2,1,0:T(8,128)(2,1)}, f32[8,256,1408]{2,1,0:T(8,128)}, bf16[704,2048]{1,0:T(8,128)(2,1)}) custom-call(f32[256,2048]{1,0:T(8,128)} %copy-done, f32[1,2048]{1,0:T(1,128)} %bitcast.26, bf16[2048,1408]{1,0:T(8,128)(2,1)} %all-gather.6.cloned.1.call-done.w_feed, bf16[8,256,2048]{2,1,0:T(8,128)(2,1)} %get-tuple-element.59.cotangent), custom_call_target="tpu_custom_call" | custom-call | tf_op jit(solution)/shard_map/pallas_call | solution.py:796
  232.8 0.0 reduce-scatter.5.cloned.1.call-update
  232.8 0.0 reduce-scatter.7.cloned.1.call-start
  232.8 14.8 %all-gather.8.cloned.1.call-done.w_down = bf16[704,2048]{1,0:T(8,128)(2,1)} async-done(((bf16[176,2048]{1,0:T(8,128)(2,1)}), bf16[704,2048]{1,0:T(8,128)(2,1)}) %all-gather.8.cloned.1.call-update) | async-done | bytes 2883600 | tf_op jit(solution)/shard_map/all_gather | solution.py:1621
  247.6 64.8 %shard_map.208 = (bf16[8,256,2048]{2,1,0:T(8,128)(2,1)}, f32[256,2048]{1,0:T(8,128)}, bf16[2048,1408]{1,0:T(8,128)(2,1)}) custom-call(bf16[8,256,2048]{2,1,0:T(8,128)(2,1)} %get-tuple-element.60.hidden, bf16[8,256,2048]{2,1,0:T(8,128)(2,1)} %get-tuple-element.59.cotangent, f32[8,256,1408]{2,1,0:T(8,128)} %get-tuple-element.61.acts, ...), custom_call_target="tpu_custom_call" | custom-call | tf_op jit(solution)/shard_map/pallas_call | solution.py:951
  312.5 0.0 reduce-scatter.7.cloned.1.call-update
  312.5 0.3 reduce-scatter.11.cloned.1.call-start
  312.8 42.4 %shard_map.209 = (bf16[2048,256]{1,0:T(8,128)(2,1)}, bf16[256,2048]{1,0:T(8,128)(2,1)}, f32[256,2048]{1,0:T(8,128)}, f32[1,2048]{1,0:T(1,128)}) custom-call(f32[1,2048]{1,0:T(1,128)} %bitcast.27, f32[256,2048]{1,0:T(8,128)} %get-tuple-element.63.grad_hidden_hbm, f32[256,2048]{1,0:T(8,128)} %copy-done, bf16[256,2048]{1,0:T(8,128)(2,1)} %cotangent_hbm.1, ...), custom_call_target="tpu_custom_call" | custom-call | tf_op jit(solution)/shard_map/pallas_call | solution.py:1087
  355.2 0.0 reduce-scatter.5.cloned.1.call-done.down_rows
  355.2 89.0 %shard_map.210 = (bf16[2048,384]{1,0:T(8,128)(2,1)}, bf16[2048,384]{1,0:T(8,128)(2,1)}, f32[256,2048]{1,0:T(8,128)}, bf16[8,176,2048]{2,1,0:T(8,128)(2,1)}, bf16[8,256,256]{2,1,0:T(8,128)(2,1)}) custom-call(bf16[2048,256]{1,0:T(8,128)(2,1)} %copy-done.10, bf16[8,1024,128]{2,1,0:T(8,128)(2,1)} %bitcast.21, s32[16,1,128]{2,1,0:T(1,128)} %copy-done.17, ...), custom_call_target="tpu_custom_call" | custom-call | tf_op jit(solution)/shard_map/pallas_call | solution.py:1356
  444.2 0.0 reduce-scatter.11.cloned.1.call-update
  444.2 0.3 reduce-scatter.9.cloned.1.call-start
  444.5 0.0 reduce-scatter.7.cloned.1.call-done.feed_rows
  444.5 0.4 reduce-scatter.9.cloned.1.call-update
  445.0 0.3 fusion.9
  445.3 8.5 %shard_map.215 = f32[1408,2048]{1,0:T(8,128)} custom-call(bf16[8,176,2048]{2,1,0:T(8,128)(2,1)} %get-tuple-element.90.x), custom_call_target="tpu_custom_call" | custom-call | tf_op jit(solution)/shard_map/pallas_call | solution.py:1769
  453.7 3.0 add_convert_fusion
  456.8 1.4 copy-done.16
  458.1 84.1 %shard_map.211 = (f32[256,2048]{1,0:T(8,128)S(1)}, bf16[8,512,1408]{2,1,0:T(8,128)(2,1)}) custom-call(bf16[2048,384]{1,0:T(8,128)(2,1)S(1)} %copy-done.15, bf16[2048,640]{1,0:T(8,128)(2,1)S(1)} %copy-done.4, bf16[512,1408]{1,0:T(8,128)(2,1)S(1)} %copy-done.16), custom_call_target="tpu_custom_call" | custom-call | tf_op jit(solution)/shard_map/pallas_call | solution.py:1420
  542.2 4.3 copy-done.5
  546.5 9.0 %shard_map.214 = (f32[512,5632]{1,0:T(8,128)}, f32[512,5632]{1,0:T(8,128)}) custom-call(bf16[8,512,1408]{2,1,0:T(8,128)(2,1)S(1)} %copy-done.5), custom_call_target="tpu_custom_call" | custom-call | tf_op jit(solution)/shard_map/pallas_call | solution.py:1781
  555.4 0.7 fusion.8
  556.1 0.0 copy-done.22
  556.1 0.6 pad.12.terms
  556.8 0.2 copy-done.20
  557.0 1.6 fusion.7
  558.6 33.5 %shard_map.212 = (bf16[8,512,384]{2,1,0:T(8,128)(2,1)}, bf16[8,512,256]{2,1,0:T(8,128)(2,1)}, f32[8,512]{1,0:T(8,128)}) custom-call(bf16[512,384]{1,0:T(8,128)(2,1)} %reduce-scatter.9.cloned.1.call-done.qkv, bf16[512,256]{1,0:T(8,128)(2,1)} %reduce-scatter.11.cloned.1.call-done.out_rows, f32[4,8,512]{2,1,0:T(8,128)} %pad.12.terms), custom_call_target="tpu_custom_call" | custom-call | tf_op jit(solution)/shard_map/pallas_call | solution.py:475
  592.1 1.4 fusion.28
  593.5 1.9 copy-done.13
  595.4 1.6 copy-done.14
  597.0 4.8 shard_map.213
  (49 shorter events, 0.2 us)
Async XLA Ops:
  7.2 3.4 copy-start.23
  7.2 3.4 copy-start.24
  7.2 61.2 %all-gather.4.cloned.1.call-start = ((), (), s32[]{:S(2)}) async-start(), calls=%async_computation.4 | async-start | bytes 3276800 | tf_op jit(solution)/shard_map/all_gather | solution.py:1621
  10.5 172.5 %all-gather.6.cloned.1.call-start = ((), (), s32[]{:S(2)}) async-start(), calls=%async_computation.5 | async-start | bytes 7208960 | tf_op jit(solution)/shard_map/all_gather | solution.py:1621
  59.7 1.4 copy-start.21
  59.7 8.7 %copy-start.11 = (bf16[256,2048]{1,0:T(8,128)(2,1)S(1)}, bf16[256,2048]{1,0:T(8,128)(2,1)}, u32[]{:S(2)}) copy-start(bf16[256,2048]{1,0:T(8,128)(2,1)} %cotangent_hbm.1) | copy-start | bytes 3145732
  59.7 187.9 %all-gather.8.cloned.1.call-start = ((), (), s32[]{:S(2)}) async-start(), calls=%async_computation.6 | async-start | bytes 3604480 | tf_op jit(solution)/shard_map/all_gather | solution.py:1621
  60.5 294.7 %reduce-scatter.5.cloned.1.call-start = ((), (), s32[]{:S(2)}) async-start(), calls=%async_computation.7 | async-start | bytes 3604480 | tf_op jit(solution)/shard_map/reduce_scatter | solution.py:1625
  62.3 62.1 %copy-start.17 = (s32[16,1,128]{2,1,0:T(1,128)}, s32[16,1,128]{2,1,0:T(1,128)S(1)}, u32[]{:S(2)}) copy-start(s32[16,1,128]{2,1,0:T(1,128)S(1)} %reshape_reshape.3.starts) | copy-start | bytes 24580
  62.3 62.0 %copy-start.18 = (s32[16,1,128]{2,1,0:T(1,128)}, s32[16,1,128]{2,1,0:T(1,128)S(1)}, u32[]{:S(2)}) copy-start(s32[16,1,128]{2,1,0:T(1,128)S(1)} %fusion.18.places) | copy-start | bytes 24580
  68.4 55.0 %copy-start.6 = (f32[2048,128]{1,0:T(8,128)}, f32[2048,128]{1,0:T(8,128)S(1)}, u32[]{:S(2)}) copy-start(f32[2048,128]{1,0:T(8,128)S(1)} %get-tuple-element.97.sine) | copy-start | bytes 3145732
  68.4 2.1 copy-start.3
  123.4 1.0 copy-start.7
  124.4 13.1 %copy-start.9 = (bf16[8,4,256,128]{3,2,1,0:T(8,128)(2,1)}, bf16[8,4,256,128]{3,2,1,0:T(8,128)(2,1)S(1)}, u32[]{:S(2)}) copy-start(bf16[8,4,256,128]{3,2,1,0:T(8,128)(2,1)S(1)} %get-tuple-element.54) | copy-start | bytes 6291460
  124.4 13.2 %copy-start.10 = (bf16[2048,256]{1,0:T(8,128)(2,1)}, bf16[2048,256]{1,0:T(8,128)(2,1)S(1)}, u32[]{:S(2)}) copy-start(bf16[2048,256]{1,0:T(8,128)(2,1)S(1)} %get-tuple-element.53.q) | copy-start | bytes 3145732
  124.4 13.2 %copy-start.2 = (bf16[256,2048]{1,0:T(8,128)(2,1)S(1)}, bf16[256,2048]{1,0:T(8,128)(2,1)}, u32[]{:S(2)}) copy-start(bf16[256,2048]{1,0:T(8,128)(2,1)} %tokens.3) | copy-start | bytes 3145732
  137.5 42.2 %copy-start.19 = (f32[16,1,512]{2,1,0:T(1,128)}, f32[16,1,512]{2,1,0:T(1,128)S(1)}, u32[]{:S(2)}) copy-start(f32[16,1,512]{2,1,0:T(1,128)S(1)} %get-tuple-element.65.log_total) | copy-start | bytes 98308
  179.7 1.3 copy-start
  181.0 1.0 copy-start.8
  182.0 1.0 copy-start.12
  232.8 211.7 %reduce-scatter.7.cloned.1.call-start = ((), (), s32[]{:S(2)}) async-start(), calls=%async_computation.8 | async-start | bytes 7208960 | tf_op jit(solution)/shard_map/reduce_scatter | solution.py:1625
  312.5 246.1 %reduce-scatter.11.cloned.1.call-start = ((), (), s32[]{:S(2)}) async-start(), calls=%async_computation.10 | async-start | bytes 1310720 | tf_op jit(solution)/shard_map/reduce_scatter | solution.py:1625
  444.2 114.4 %reduce-scatter.9.cloned.1.call-start = ((), (), s32[]{:S(2)}) async-start(), calls=%async_computation.9 | async-start | bytes 1966080 | tf_op jit(solution)/shard_map/reduce_scatter | solution.py:1625
  445.3 8.5 %copy-start.1 = (f32[256,2048]{1,0:T(8,128)S(1)}, f32[256,2048]{1,0:T(8,128)}, u32[]{:S(2)}) copy-start(f32[256,2048]{1,0:T(8,128)} %copy-done) | copy-start | bytes 6291460
  453.7 3.0 copy-start.4
  453.7 3.0 copy-start.15
  456.8 1.4 copy-start.16
  542.2 4.3 copy-start.5
  555.4 0.7 copy-start.22
  555.4 1.6 copy-start.20
  593.5 1.9 copy-start.13
  595.4 1.6 copy-start.14
Sparse Core Ops, SparseCore 0:
  10.6 57.5 all-gather.3
  69.8 106.8 all-gather.5
  178.3 69.3 all-gather.7
  249.8 58.9 reduce-scatter.4
  312.6 112.0 reduce-scatter.6
  444.3 30.8 reduce-scatter.10
  477.6 33.9 reduce-scatter.8

commit v9 on v8

--- a/solution.py
+++ b/solution.py
@@ -671,8 +671,8 @@
 
 
 def middle_kernel(
-    chunks, middle, gain, w_feed, cotangent, hidden, acts, down_part,
-    blocks, act_stage, cot_in, down_sum, down_stage, out_sems, act_sems, cot_sems, down_sem, *sems,
+    chunks, gain, w_feed, middle_hbm, cotangent, hidden, acts, down_part,
+    middle, middle_sems, blocks, act_stage, cot_in, down_sum, down_stage, out_sems, act_sems, cot_sems, down_sem, *sems,
 ):
     f32, bf16 = jnp.float32, jnp.bfloat16
     width, tok, _ = blocks.shape
@@ -691,11 +691,17 @@
         slot = lax.rem(i, 2)
         return pltpu.make_async_copy(cotangent.at[me ^ i], cot_in.at[slot], cot_sems.at[slot])
 
+    loads = {}
+    for j in order:
+        part = pl.ds(j * size, size)
+        loads[j] = pltpu.make_async_copy(middle_hbm.at[part], middle.at[part], middle_sems.at[j])
+        loads[j].start()
     for i in (0, 1):
         cot_load(i).start()
     greet(gather.sibling, gather.x, gather.y)
     for j in order:
         part = pl.ds(j * size, size)
+        loads[j].wait()
         total = middle[part, :]
         blocks[me, part] = (total * inverse_rms(total) * gain[...]).astype(bf16)
         gather.start_items((j,))
@@ -800,9 +806,11 @@
             jax.ShapeDtypeStruct((width, tok, 2 * units), f32),
             jax.ShapeDtypeStruct((units, model), bf16),
         ],
-        in_specs=[vmem] * 3 + [ANY],
+        in_specs=[vmem] * 2 + [ANY] * 2,
         out_specs=[ANY] * 3,
         scratch_shapes=[
+            pltpu.VMEM((tok, model), f32),
+            DMA((chunks,)),
             pltpu.VMEM((width, tok, model), bf16),
             pltpu.VMEM((2, tok, 2 * units), f32),
             pltpu.VMEM((2, tok, model), bf16),
@@ -817,7 +825,7 @@
         compiler_params=pltpu.CompilerParams(
             collective_id=call, has_side_effects=True, vmem_limit_bytes=56 << 20
         ),
-    )(middle, gain, w_feed, cotangent)
+    )(gain, w_feed, middle, cotangent)
 
 
 def feed_kernel(
@@ -1156,6 +1164,23 @@
     kept.start()
     parts = tok // QUERY_BLOCK
 
+    top = z == planes - 1
+    early = top & (core == 0)
+    late = jnp.logical_not(early)
+
+    def block_of(which, b):
+        return grad_kv.at[pl.ds(which * count, count), pl.ds(b * tok, tok)]
+
+    def trade(b):
+        return remote(block_of(1 - core, b), from_sib.at[b], (to_sib, at_sib), b, gather.sibling)
+
+    def down(b, i):
+        return along_line(outbox.at[b, i], inbox.at[b, i], (to_line, at_line), (b, i), below)
+
+    def own(b, i):
+        part = pl.ds(b * tok, tok)
+        return grad_kv[core * count + i, part, :].astype(f32) + from_sib[b, i].astype(f32)
+
     def step(n, carry):
         s, sub = n // parts, lax.rem(n, parts)
         rows = pl.ds(pl.multiple_of(n * QUERY_BLOCK, QUERY_BLOCK), QUERY_BLOCK)
@@ -1215,6 +1240,19 @@
             for j in scatter.order[chunks // 2 :]:
                 scatter.near(j, 0)
 
+        @pl.when((n == count * parts) & top & (core == 1))
+        def _():
+            for b in range(planes):
+                trade(b).start()
+
+        @pl.when((n == count * parts + 2) & early)
+        def _():
+            for b in range(planes - 1):
+                trade(b).wait_recv()
+                for i in range(count):
+                    outbox[b, i] = own(b, i).astype(bf16)
+                    down(b, i).start()
+
         @pl.when(n == 11)
         def _():
             gather.relay(0)
@@ -1226,47 +1264,34 @@
     gather.start()
     lax.fori_loop(0, width * parts, step, 0)
 
-    def block_of(which, b):
-        return grad_kv.at[pl.ds(which * count, count), pl.ds(b * tok, tok)]
-
-    def trade(b):
-        return remote(block_of(1 - core, b), from_sib.at[b], (to_sib, at_sib), b, gather.sibling)
-
-    def down(b, i):
-        return along_line(outbox.at[b, i], inbox.at[b, i], (to_line, at_line), (b, i), below)
-
-    def own(b, i):
-        part = pl.ds(b * tok, tok)
-        return grad_kv[core * count + i, part, :].astype(f32) + from_sib[b, i].astype(f32)
-
     for b in range(planes):
 
-        @pl.when(b <= z)
+        @pl.when((b <= z) & jnp.logical_not(top & (core == 1)))
         def _():
             trade(b).start()
 
     scatter.taken(0)
     for b in range(planes):
 
-        @pl.when(b <= z)
+        @pl.when((b <= z) & (late if b < planes - 1 else top))
         def _():
             trade(b).wait_recv()
 
         for i in range(count):
 
-            @pl.when((b <= z) & (z < planes - 1))
+            @pl.when((b <= z) & jnp.logical_not(top))
             def _():
                 down(b, i).wait_recv()
 
-            @pl.when((b < z) & (z < planes - 1))
+            @pl.when((b < z) & jnp.logical_not(top))
             def _():
                 outbox[b, i] = (own(b, i) + inbox[b, i].astype(f32)).astype(bf16)
 
-            @pl.when((b < z) & (z == planes - 1))
+            @pl.when((b < z) & top & late)
             def _():
                 outbox[b, i] = own(b, i).astype(bf16)
 
-            @pl.when(b < z)
+            @pl.when((b < z) & late)
             def _():
                 down(b, i).start()
 

time: 612 us -> 612 us (level)
  transfers between devices with their start and end apart: 7 -> 7, of which waited for: 1 -> 1; matrix products, arithmetic and copies ran while one was open for 2% -> 2% of each run, Pallas kernels for 83% -> 82%
where the time goes in v9:
time: 612 us; the launch traced here: 609 us
  Pallas kernels  543 us (89%)
  local copies, waits for them, and re-layouts  22.3 us (4%)
  waiting for transfers between devices  16.1 us (3%)
  between operations  14.8 us (2%)
  other arithmetic  12 us (2%)
    pallas_call x1, Pallas kernels, scatter_hidden(): pl.pallas_call(functools.partial(hidden_kernel, chunks), out_shape=[jax.S...  85.1 us
    pallas_call x1, Pallas kernels, attention_back(): pl.pallas_call(functools.partial(back_kernel, chunks, heads), out_shape=[...  83.6 us
    pallas_call x1, Pallas kernels, feed_forward(): pl.pallas_call(functools.partial(feed_kernel, chunks), out_shape=[jax.Sha...  64.8 us
    pallas_call x1, Pallas kernels, project(): pl.pallas_call(functools.partial(project_kernel, chunks), out_shape=[jax....  52.9 us
    pallas_call x1, Pallas kernels, middle_layer(): pl.pallas_call(functools.partial(middle_kernel, chunks), out_shape=[jax.S...  49.8 us
    pallas_call x1, Pallas kernels, enter(): pl.pallas_call(functools.partial(enter_kernel, chunks, piece), out_shape=...  48.5 us
    pallas_call x1, Pallas kernels, gradient_layer(): pl.pallas_call(functools.partial(gradient_kernel, chunks), out_shape=[jax...  42.4 us
    pallas_call x1, Pallas kernels, branch_layer(): pl.pallas_call(functools.partial(branch_kernel, chunks), out_shape=jax.Sh...  42.1 us
  transfers between devices with their start and end apart: 7, of which 1 were waited for; matrix products, arithmetic and copies ran while one was open for 2% of the time, Pallas kernels for 82%

profile of v9, /device:TPU:0, one launch (start us, length us, event | category | flops | bytes accessed | tf_op | source)
XLA Modules:
  0.0 609.1 jit_solution(12482728827138758197)
XLA Ops:
  7.2 0.0 all-gather.4.cloned.1.call-start
  7.3 1.1 constant_dynamic-slice_fusion.1
  8.4 1.1 constant_dynamic-slice_fusion
  9.5 1.0 pad_maximum_fusion
  10.5 0.0 all-gather.4.cloned.1.call-update
  10.5 0.0 all-gather.6.cloned.1.call-start
  10.6 0.6 fusion.17.gains
  11.2 48.5 %shard_map.203 = (bf16[8,256,2048]{2,1,0:T(8,128)(2,1)}, f32[4,8,512]{2,1,0:T(8,128)}, s32[8,8,128]{2,1,0:T(8,128)}, bf16[512,1408]{1,0:T(8,128)(2,1)}, bf16[176,2048]{1,0:T(8,128)(2,1)}) custom-call(bf16[256,2048]{1,0:T(8,128)(2,1)} %tokens.3, f32[8,512]{1,0:T(8,128)} %fusion.17.gains, s32[8,128]{1,0:T(8,128)} %bitcast.35, bf16[512,5632]{1,0:T(8,128)(2,1)} %gate.1, ...), custom_call_target="tpu_custom_call" | custom-call | tf_op jit(solution)/shard_map/pallas_call | solution.py:1467
  59.7 0.0 copy-start.11
  59.7 0.0 all-gather.6.cloned.1.call-update
  59.7 0.0 all-gather.8.cloned.1.call-start
  59.8 0.7 all-gather.8.cloned.1.call-update
  60.5 0.6 reduce-scatter.5.cloned.1.call-start
  61.1 1.1 convert_reduce_fusion
  62.3 0.0 copy-start.17
  62.3 0.4 slice_reduce_fusion.1
  62.7 0.5 slice_reduce_fusion
  63.2 0.8 slice_bitcast_fusion
  64.0 0.6 fusion.29
  64.6 3.7 fusion.10
  68.4 0.0 copy-start.6
  68.4 0.0 all-gather.4.cloned.1.call-done.weight.w_cols
  68.4 2.1 copy-done.3
  70.5 52.9 %shard_map.204 = (bf16[2048,256]{1,0:T(8,128)(2,1)S(1)}, bf16[8,4,256,128]{3,2,1,0:T(8,128)(2,1)S(1)}, bf16[8,256,2048]{2,1,0:T(8,128)(2,1)}, bf16[256,2048]{1,0:T(8,128)(2,1)S(1)}) custom-call(bf16[8,256,2048]{2,1,0:T(8,128)(2,1)} %get-tuple-element.52.hidden, bf16[2048,640]{1,0:T(8,128)(2,1)S(1)} %copy-done.3, f32[2048,128]{1,0:T(8,128)S(1)} %get-tuple-element.98.cosine, ...), custom_call_target="tpu_custom_call" | custom-call | tf_op jit(solution)/shard_map/pallas_call | solution.py:1500
  123.4 1.0 copy-done.7
  124.4 13.1 %shard_map.205 = (bf16[2048,256]{1,0:T(8,128)(2,1)S(1)}, f32[16,1,512]{2,1,0:T(1,128)S(1)}) custom-call(s32[16]{0:T(128)S(1)} %get-tuple-element.101.low, s32[16]{0:T(128)S(1)} %get-tuple-element.102.high, bf16[2048,256]{1,0:T(8,128)(2,1)S(1)} %get-tuple-element.53.q, bf16[8,1024,128]{2,1,0:T(8,128)(2,1)S(1)} %bitcast.20, ...), custom_call_target="tpu_custom_call" | custom-call | tf_op jit(solution)/shard_map/pallas_call | solution.py:1751
  137.5 0.0 copy-start.19
  137.5 42.1 %shard_map.206.middle_hbm = f32[256,2048]{1,0:T(8,128)S(1)} custom-call(bf16[2048,256]{1,0:T(8,128)(2,1)S(1)} %get-tuple-element.55.mixed.mixed_hbm, bf16[256,2048]{1,0:T(8,128)(2,1)S(1)} %get-tuple-element.56.w_out.w_out_hbm, bf16[256,2048]{1,0:T(8,128)(2,1)S(1)} %copy-done.2), custom_call_target="tpu_custom_call" | custom-call | tf_op jit(solution)/shard_map/pallas_call | solution.py:784
  179.7 0.0 copy-start
  179.7 1.3 copy-done
  181.0 1.0 copy-done.8
  182.0 1.0 copy-done.12
  182.9 49.8 %shard_map.207 = (bf16[8,256,2048]{2,1,0:T(8,128)(2,1)}, f32[8,256,1408]{2,1,0:T(8,128)}, bf16[704,2048]{1,0:T(8,128)(2,1)}) custom-call(f32[1,2048]{1,0:T(1,128)} %bitcast.26, bf16[2048,1408]{1,0:T(8,128)(2,1)} %all-gather.6.cloned.1.call-done.w_feed, f32[256,2048]{1,0:T(8,128)} %copy-done, bf16[8,256,2048]{2,1,0:T(8,128)(2,1)} %get-tuple-element.59.cotangent), custom_call_target="tpu_custom_call" | custom-call | tf_op jit(solution)/shard_map/pallas_call | solution.py:802
  232.7 0.0 reduce-scatter.5.cloned.1.call-update
  232.8 0.0 reduce-scatter.7.cloned.1.call-start
  232.8 14.8 %all-gather.8.cloned.1.call-done.w_down = bf16[704,2048]{1,0:T(8,128)(2,1)} async-done(((bf16[176,2048]{1,0:T(8,128)(2,1)}), bf16[704,2048]{1,0:T(8,128)(2,1)}) %all-gather.8.cloned.1.call-update) | async-done | bytes 2883600 | tf_op jit(solution)/shard_map/all_gather | solution.py:1646
  247.6 64.8 %shard_map.208 = (bf16[8,256,2048]{2,1,0:T(8,128)(2,1)}, f32[256,2048]{1,0:T(8,128)}, bf16[2048,1408]{1,0:T(8,128)(2,1)}) custom-call(bf16[8,256,2048]{2,1,0:T(8,128)(2,1)} %get-tuple-element.60.hidden, bf16[8,256,2048]{2,1,0:T(8,128)(2,1)} %get-tuple-element.59.cotangent, f32[8,256,1408]{2,1,0:T(8,128)} %get-tuple-element.61.acts, ...), custom_call_target="tpu_custom_call" | custom-call | tf_op jit(solution)/shard_map/pallas_call | solution.py:959
  312.5 0.0 reduce-scatter.7.cloned.1.call-update
  312.5 0.3 reduce-scatter.11.cloned.1.call-start
  312.8 42.4 %shard_map.209 = (bf16[2048,256]{1,0:T(8,128)(2,1)}, bf16[256,2048]{1,0:T(8,128)(2,1)}, f32[256,2048]{1,0:T(8,128)}, f32[1,2048]{1,0:T(1,128)}) custom-call(f32[1,2048]{1,0:T(1,128)} %bitcast.27, f32[256,2048]{1,0:T(8,128)} %get-tuple-element.63.grad_hidden_hbm, f32[256,2048]{1,0:T(8,128)} %copy-done, bf16[256,2048]{1,0:T(8,128)(2,1)} %cotangent_hbm.1, ...), custom_call_target="tpu_custom_call" | custom-call | tf_op jit(solution)/shard_map/pallas_call | solution.py:1095
  355.2 0.0 reduce-scatter.5.cloned.1.call-done.down_rows
  355.2 83.6 %shard_map.210 = (bf16[2048,384]{1,0:T(8,128)(2,1)}, bf16[2048,384]{1,0:T(8,128)(2,1)}, f32[256,2048]{1,0:T(8,128)}, bf16[8,176,2048]{2,1,0:T(8,128)(2,1)}, bf16[8,256,256]{2,1,0:T(8,128)(2,1)}) custom-call(bf16[2048,256]{1,0:T(8,128)(2,1)} %copy-done.10, bf16[8,1024,128]{2,1,0:T(8,128)(2,1)} %bitcast.21, s32[16,1,128]{2,1,0:T(1,128)} %copy-done.17, ...), custom_call_target="tpu_custom_call" | custom-call | tf_op jit(solution)/shard_map/pallas_call | solution.py:1381
  438.8 0.0 reduce-scatter.11.cloned.1.call-update
  438.8 0.3 reduce-scatter.9.cloned.1.call-start
  439.1 0.0 reduce-scatter.7.cloned.1.call-done.feed_rows
  439.2 0.4 reduce-scatter.9.cloned.1.call-update
  439.6 0.3 fusion.9
  439.9 0.0 copy-start.1
  439.9 8.5 %shard_map.215 = f32[1408,2048]{1,0:T(8,128)} custom-call(bf16[8,176,2048]{2,1,0:T(8,128)(2,1)} %get-tuple-element.90.x), custom_call_target="tpu_custom_call" | custom-call | tf_op jit(solution)/shard_map/pallas_call | solution.py:1794
  448.4 3.0 add_convert_fusion
  451.4 1.4 copy-done.16
  452.7 85.1 %shard_map.211 = (f32[256,2048]{1,0:T(8,128)S(1)}, bf16[8,512,1408]{2,1,0:T(8,128)(2,1)}) custom-call(bf16[2048,384]{1,0:T(8,128)(2,1)S(1)} %copy-done.15, bf16[2048,640]{1,0:T(8,128)(2,1)S(1)} %copy-done.4, bf16[512,1408]{1,0:T(8,128)(2,1)S(1)} %copy-done.16), custom_call_target="tpu_custom_call" | custom-call | tf_op jit(solution)/shard_map/pallas_call | solution.py:1445
  537.8 4.3 copy-done.5
  542.1 9.0 %shard_map.214 = (f32[512,5632]{1,0:T(8,128)}, f32[512,5632]{1,0:T(8,128)}) custom-call(bf16[8,512,1408]{2,1,0:T(8,128)(2,1)S(1)} %copy-done.5), custom_call_target="tpu_custom_call" | custom-call | tf_op jit(solution)/shard_map/pallas_call | solution.py:1806
  551.1 0.7 fusion.8
  551.7 0.0 copy-done.22
  551.8 0.6 pad.12.terms
  552.4 0.2 copy-done.20
  552.7 1.6 fusion.7
  554.3 38.1 %shard_map.212 = (bf16[8,512,384]{2,1,0:T(8,128)(2,1)}, bf16[8,512,256]{2,1,0:T(8,128)(2,1)}, f32[8,512]{1,0:T(8,128)}) custom-call(bf16[512,384]{1,0:T(8,128)(2,1)} %reduce-scatter.9.cloned.1.call-done.qkv, bf16[512,256]{1,0:T(8,128)(2,1)} %reduce-scatter.11.cloned.1.call-done.out_rows, f32[4,8,512]{2,1,0:T(8,128)} %pad.12.terms), custom_call_target="tpu_custom_call" | custom-call | tf_op jit(solution)/shard_map/pallas_call | solution.py:475
  592.4 1.4 fusion.28
  593.8 1.9 copy-done.13
  595.7 1.6 copy-done.14
  597.2 4.8 shard_map.213
  (49 shorter events, 0.2 us)
Async XLA Ops:
  7.2 3.4 copy-start.23
  7.2 3.4 copy-start.24
  7.2 61.2 %all-gather.4.cloned.1.call-start = ((), (), s32[]{:S(2)}) async-start(), calls=%async_computation.4 | async-start | bytes 3276800 | tf_op jit(solution)/shard_map/all_gather | solution.py:1646
  10.5 172.5 %all-gather.6.cloned.1.call-start = ((), (), s32[]{:S(2)}) async-start(), calls=%async_computation.5 | async-start | bytes 7208960 | tf_op jit(solution)/shard_map/all_gather | solution.py:1646
  59.7 1.4 copy-start.21
  59.7 8.7 %copy-start.11 = (bf16[256,2048]{1,0:T(8,128)(2,1)S(1)}, bf16[256,2048]{1,0:T(8,128)(2,1)}, u32[]{:S(2)}) copy-start(bf16[256,2048]{1,0:T(8,128)(2,1)} %cotangent_hbm.1) | copy-start | bytes 3145732
  59.7 187.9 %all-gather.8.cloned.1.call-start = ((), (), s32[]{:S(2)}) async-start(), calls=%async_computation.6 | async-start | bytes 3604480 | tf_op jit(solution)/shard_map/all_gather | solution.py:1646
  60.5 294.7 %reduce-scatter.5.cloned.1.call-start = ((), (), s32[]{:S(2)}) async-start(), calls=%async_computation.7 | async-start | bytes 3604480 | tf_op jit(solution)/shard_map/reduce_scatter | solution.py:1650
  62.3 62.1 %copy-start.17 = (s32[16,1,128]{2,1,0:T(1,128)}, s32[16,1,128]{2,1,0:T(1,128)S(1)}, u32[]{:S(2)}) copy-start(s32[16,1,128]{2,1,0:T(1,128)S(1)} %reshape_reshape.3.starts) | copy-start | bytes 24580
  62.3 62.0 %copy-start.18 = (s32[16,1,128]{2,1,0:T(1,128)}, s32[16,1,128]{2,1,0:T(1,128)S(1)}, u32[]{:S(2)}) copy-start(s32[16,1,128]{2,1,0:T(1,128)S(1)} %fusion.18.places) | copy-start | bytes 24580
  68.4 55.0 %copy-start.6 = (f32[2048,128]{1,0:T(8,128)}, f32[2048,128]{1,0:T(8,128)S(1)}, u32[]{:S(2)}) copy-start(f32[2048,128]{1,0:T(8,128)S(1)} %get-tuple-element.97.sine) | copy-start | bytes 3145732
  68.4 2.1 copy-start.3
  123.4 1.0 copy-start.7
  124.3 13.1 %copy-start.9 = (bf16[8,4,256,128]{3,2,1,0:T(8,128)(2,1)}, bf16[8,4,256,128]{3,2,1,0:T(8,128)(2,1)S(1)}, u32[]{:S(2)}) copy-start(bf16[8,4,256,128]{3,2,1,0:T(8,128)(2,1)S(1)} %get-tuple-element.54) | copy-start | bytes 6291460
  124.4 13.2 %copy-start.10 = (bf16[2048,256]{1,0:T(8,128)(2,1)}, bf16[2048,256]{1,0:T(8,128)(2,1)S(1)}, u32[]{:S(2)}) copy-start(bf16[2048,256]{1,0:T(8,128)(2,1)S(1)} %get-tuple-element.53.q) | copy-start | bytes 3145732
  124.4 13.2 %copy-start.2 = (bf16[256,2048]{1,0:T(8,128)(2,1)S(1)}, bf16[256,2048]{1,0:T(8,128)(2,1)}, u32[]{:S(2)}) copy-start(bf16[256,2048]{1,0:T(8,128)(2,1)} %tokens.3) | copy-start | bytes 3145732
  137.5 42.2 %copy-start.19 = (f32[16,1,512]{2,1,0:T(1,128)}, f32[16,1,512]{2,1,0:T(1,128)S(1)}, u32[]{:S(2)}) copy-start(f32[16,1,512]{2,1,0:T(1,128)S(1)} %get-tuple-element.65.log_total) | copy-start | bytes 98308
  179.7 1.3 copy-start
  181.0 1.0 copy-start.8
  182.0 1.0 copy-start.12
  232.8 206.4 %reduce-scatter.7.cloned.1.call-start = ((), (), s32[]{:S(2)}) async-start(), calls=%async_computation.8 | async-start | bytes 7208960 | tf_op jit(solution)/shard_map/reduce_scatter | solution.py:1650
  312.5 241.8 %reduce-scatter.11.cloned.1.call-start = ((), (), s32[]{:S(2)}) async-start(), calls=%async_computation.10 | async-start | bytes 1310720 | tf_op jit(solution)/shard_map/reduce_scatter | solution.py:1650
  438.8 115.4 %reduce-scatter.9.cloned.1.call-start = ((), (), s32[]{:S(2)}) async-start(), calls=%async_computation.9 | async-start | bytes 1966080 | tf_op jit(solution)/shard_map/reduce_scatter | solution.py:1650
  439.9 8.5 %copy-start.1 = (f32[256,2048]{1,0:T(8,128)S(1)}, f32[256,2048]{1,0:T(8,128)}, u32[]{:S(2)}) copy-start(f32[256,2048]{1,0:T(8,128)} %copy-done) | copy-start | bytes 6291460
  448.4 3.0 copy-start.4
  448.4 3.0 copy-start.15
  451.4 1.4 copy-start.16
  537.8 4.3 copy-start.5
  551.1 0.7 copy-start.22
  551.1 1.6 copy-start.20
  593.8 1.9 copy-start.13
  595.6 1.6 copy-start.14
Sparse Core Ops, SparseCore 0:
  10.6 57.5 all-gather.3
  69.8 106.8 all-gather.5
  178.3 69.3 all-gather.7
  249.8 58.4 reduce-scatter.4
  312.6 119.4 reduce-scatter.6
  439.0 35.2 reduce-scatter.10
  476.7 33.9 reduce-scatter.8
